TPU v7x, 32 devices: a whole 2x2x4 slice. The times are simulated.
32 devices in a mesh: gx: 4 (over z), gy: 8 (over y, x, core).
Axes of the slice: x: 2, y: 2, z: 4, core: 2. Of those that a mesh axis runs over, the one named last changes fastest.
Arguments:
- populations: float32 [27, 128, 8192], P(None, 'gx', 'gy'), may hold values from 0.002 to 0.42, as said below
- adjoint_in: float32 [27, 128, 8192], P(None, 'gx', 'gy'), may hold values from -6 to 6
- porosity: float32 [128, 8192], P('gx', 'gy'), may hold values from 0.1 to 10
- solid: int32 [128, 8192], P('gx', 'gy'), may hold values 0 or 1
- labels: int32 [128, 8192], P('gx', 'gy'), may hold values from 0 to 2
Outputs:
- final_pops: float32 [27, 128, 8192], P(None, 'gx', 'gy')
- adjoint_out: float32 [27, 128, 8192], P(None, 'gx', 'gy')
- sensitivity: float32 [128, 8192], P('gx', 'gy')
Inputs may be any that keep to these rules, and one draw needn't show every extreme that they name: `populations`: every population is between 0.6 and 1.4 times its weight w_i.
All inputs are finite; a program needn't handle non-finite values. Where the computation divides by a largest or mean magnitude, that divisor is 1e-20 or more. No bound on the sum of `solid` on one device may be relied on, other than what follows from the above.
Results may differ from a plain program's by a relative error of at most 0.0001.
Values sent between devices are 32-bit elements; how exact they have to be, the bound alone decides.
No kernel may reach another device: no remote copies, remote signals or barrier semaphores. Data moves between devices by JAX's collectives and lax.ppermute only.
A program may use at most 128 MiB of HBM per device.

v0:
```python
import functools

import jax
import jax.numpy as jnp
from jax import lax
from jax.experimental import pallas as pl
from jax.experimental.pallas import tpu as pltpu
from jax.sharding import PartitionSpec as P

NZ = 64
RELAX = 0.8
PUSH = 0.2
EPS = 1e-06
LANES = 128
VELOCITY = [(a, b, c) for a in (-1, 0, 1) for b in (-1, 0, 1) for c in (-1, 0, 1)]
INDEX = {v: i for i, v in enumerate(VELOCITY)}
WEIGHT = [
    [8.0 / 27, 2.0 / 27, 1.0 / 54, 1.0 / 216][abs(v[0]) + abs(v[1]) + abs(v[2])]
    for v in VELOCITY
]
NORM = [abs(v[0]) + abs(v[1]) + abs(v[2]) for v in VELOCITY]
F32 = jnp.float32
VMEM_LIMIT = 6 * 1024 * 1024
FLIGHT = 12 * 1024 * 1024


class Grid:
    def __init__(self, rows, width):
        self.rows = rows
        self.cols = width // LANES
        self.panel = rows + 16
        self.halo = self.cols + 1
        self.local = self.cols * rows
        self.extended = self.halo * rows + 24
        self.outer = ((0, 8), (rows - 8, 8))
        self.inner = tuple(((r, 16),) for r in range(8, rows - 8, 16))

    def at(self, i, k, r):
        return self.field(i) + k * self.panel + r

    def field(self, i):
        return i * (self.cols + 2) * self.panel + 8

    def padded(self, fields):
        return (fields * (self.cols + 2) * self.panel + 8, LANES)


def velocity(i, sign):
    return tuple(sign * n for n in VELOCITY[i]) if i < 27 else (0, 0, 0)


def moving(fields, sign, axis, side):
    return [i for i in range(fields) if velocity(i, sign)[axis] == side]


def lane_masks(height):
    lane = lax.broadcasted_iota(jnp.int32, (height, LANES), 1)
    return lane >= NZ, lane % NZ == 0, lane % NZ == NZ - 1


def shift_lanes(here, d, masks):
    first, last = masks[1:]
    dy, dz = d[1:]
    if dz == 0:
        return here if dy == 0 else pltpu.roll(here, NZ, 1)
    if dz == 1:
        one, other, edge = 1, NZ + 1, first
    else:
        one, other, edge = LANES - 1, NZ - 1, last
    inner, wrapped = (one, other) if dy == 0 else (other, one)
    return jnp.where(edge, pltpu.roll(here, wrapped, 1), pltpu.roll(here, inner, 1))


def pull(load, d, masks):
    high = masks[0]
    here = load(0)
    if d[1] == 1:
        here = jnp.where(high, load(-1), here)
    elif d[1] == -1:
        here = jnp.where(high, here, load(1))
    return shift_lanes(here, d, masks)


def stacked(parts):
    return parts[0] if len(parts) == 1 else jnp.concatenate(parts, 0)


def read_rows(ref, base, pieces):
    return stacked([ref[pl.ds(base + r, n), :] for r, n in pieces])


def write_rows(ref, base, pieces, value):
    done = 0
    for r, n in pieces:
        ref[pl.ds(base + r, n), :] = value[done : done + n]
        done += n


def pull_block(g, buf, sign, k, pieces, masks, fields=27):
    base = pl.multiple_of(k * g.panel, 8)
    after = pl.multiple_of(jnp.where(k == g.halo, g.panel, base + g.panel), 8)
    out = []
    for i in range(fields):
        d = velocity(i, sign)

        def load(n, i=i, d=d):
            start = {-1: base - g.panel, 0: base, 1: after}[n]
            return read_rows(buf, start + (g.field(i) - d[0]), pieces)

        out.append(pull(load, d, masks))
    return out


def pull_edge(g, buf, sign, side, masks, fields=27):
    out = []
    for i in range(fields):
        d = velocity(i, sign)
        if side == 1:
            row = g.rows - d[0]
        else:
            row = {1: g.rows, 0: g.rows + 1, -1: 0}[d[0]]

        def load(n, i=i, row=row):
            return buf[pl.ds(g.at(i, 1 + n, row), g.cols, stride=g.panel), :]

        out.append(pull(load, d, masks))
    return out


def moments(f):
    flat = {}
    along_z = None
    for a in (-1, 0, 1):
        for b in (-1, 0, 1):
            lo, mid, hi = (f[INDEX[(a, b, c)]] for c in (-1, 0, 1))
            flat[a, b] = lo + mid + hi
            diff = hi - lo
            along_z = diff if along_z is None else along_z + diff
    line = {}
    along_y = None
    for a in (-1, 0, 1):
        line[a] = flat[a, -1] + flat[a, 0] + flat[a, 1]
        diff = flat[a, 1] - flat[a, -1]
        along_y = diff if along_y is None else along_y + diff
    return line[-1] + line[0] + line[1], line[1] - line[-1], along_y, along_z


def combos(x, y, z):
    plane = {}
    for a in (-1, 0, 1):
        for b in (-1, 0, 1):
            if (a, b) > (0, 0):
                continue
            if a == 0:
                plane[a, b] = -y if b else None
            else:
                plane[a, b] = -x if b == 0 else (-x - y if b < 0 else y - x)
    out = []
    for a, b, c in VELOCITY[:13]:
        base = plane[a, b]
        if base is None:
            out.append(-z)
        else:
            out.append(base if c == 0 else (base - z if c < 0 else base + z))
    return out


def relax(f, rho, wx, wy, wz, damp, push, solid):
    ux, uy, uz = (wx + push) * damp, wy * damp, wz * damp
    base = 1.0 - 1.5 * (ux * ux + uy * uy + uz * uz)
    keep = 1.0 - 1.0 / RELAX
    gain = rho * (1.0 / RELAX)
    level = [gain * w for w in (8.0 / 27, 2.0 / 27, 1.0 / 54, 1.0 / 216)]
    along = combos(3.0 * ux, 3.0 * uy, 3.0 * uz)
    out = [None] * 27
    for i in range(13):
        j = 26 - i
        even = base + 0.5 * (along[i] * along[i])
        lift = level[NORM[i]]
        out[i] = jnp.where(solid, f[j], keep * f[i] + lift * (even + along[i]))
        out[j] = jnp.where(solid, f[i], keep * f[j] + lift * (even - along[i]))
    out[13] = jnp.where(solid, f[13], keep * f[13] + level[0] * base)
    return out


def pulled_moments(p):
    first = {}
    for a in (-1, 0, 1):
        for b in (-1, 0, 1):
            lo, mid, hi = (p[INDEX[(a, b, c)]] for c in (-1, 0, 1))
            both = lo + hi
            first[a, b] = (4.0 * mid + both, hi - lo, both)
    second = {}
    for a in (-1, 0, 1):
        lo, mid, hi = (first[a, b] for b in (-1, 0, 1))
        b0 = lo[0] + hi[0]
        b1 = lo[1] + hi[1]
        second[a] = dict(
            one=4.0 * mid[0] + b0,
            y=hi[0] - lo[0],
            yy=b0,
            z=4.0 * mid[1] + b1,
            yz=hi[1] - lo[1],
            zz=4.0 * mid[2] + lo[2] + hi[2],
        )
    lo, mid, hi = (second[a] for a in (-1, 0, 1))

    def full(key):
        return 4.0 * mid[key] + lo[key] + hi[key]

    xx = lo["one"] + hi["one"]
    return dict(
        one=4.0 * mid["one"] + xx,
        x=hi["one"] - lo["one"],
        xx=xx,
        y=full("y"),
        xy=hi["y"] - lo["y"],
        yy=full("yy"),
        z=full("z"),
        xz=hi["z"] - lo["z"],
        yz=full("yz"),
        zz=full("zz"),
    )


def adjoint_scalars(p, rho, wx, wy, wz, damp, push, solid):
    ux, uy, uz = (wx + push) * damp, wy * damp, wz * damp
    s = pulled_moments(p)
    scale = 1.0 / (216.0 * RELAX)
    one = s["one"] * scale
    b = [s[k] * (3.0 * scale) for k in ("x", "y", "z")]
    d = {k: s[k] * (9.0 * scale) for k in ("xx", "xy", "yy", "xz", "yz", "zz")}
    qx = d["xx"] * ux + d["xy"] * uy + d["xz"] * uz
    qy = d["xy"] * ux + d["yy"] * uy + d["yz"] * uz
    qz = d["xz"] * ux + d["yz"] * uy + d["zz"] * uz
    linear = b[0] * ux + b[1] * uy + b[2] * uz
    square = ux * ux + uy * uy + uz * uz
    even = one + linear + 0.5 * (qx * ux + qy * uy + qz * uz) - 1.5 * one * square
    three = 3.0 * one
    gx = (b[0] + qx - three * ux) * damp
    gy = (b[1] + qy - three * uy) * damp
    gz = (b[2] + qz - three * uz) * damp
    even = even - (gx * wx + gy * wy + gz * wz)
    porous = jnp.where(solid, 0.0, -rho * (gx * ux + gy * uy + gz * uz))
    return even, gx, gy, gz, porous


def adjoint_spread(p, even, gx, gy, gz, solid):
    keep = 1.0 - 1.0 / RELAX
    along = combos(gx, gy, gz)
    out = [None] * 27
    for i in range(13):
        j = 26 - i
        out[i] = jnp.where(solid, p[j], keep * p[i] + (even + along[i]))
        out[j] = jnp.where(solid, p[i], keep * p[j] + (even - along[i]))
    out[13] = jnp.where(solid, p[13], keep * p[13] + even)
    return out


def x_lines(g, sign, fields, side):
    lines = []
    for i in moving(fields, sign, 0, side):
        if side == 1:
            lines.append((i, g.rows - 1, (-1, g.rows + 1)))
            lines.append((i, g.rows - 2, (g.rows,)))
        else:
            lines += [(i, 0, (g.rows,)), (i, 1, (g.rows + 1,))]
    edge, target = (g.rows - 1, g.rows + 1) if side == 1 else (0, g.rows)
    return lines + [(i, edge, (target,)) for i in moving(fields, sign, 0, 0)]


def pack_x(g, buf, sign, fields, up, down):
    for side, ref in ((1, up), (-1, down)):
        for n, (i, r, _) in enumerate(x_lines(g, sign, fields, side)):
            ref[n * g.cols : (n + 1) * g.cols, :] = buf[
                pl.ds(g.at(i, 1, r), g.cols, stride=g.panel), :
            ]


def unpack_x(g, buf, sign, fields, up, down):
    for side, ref in ((1, up), (-1, down)):
        for n, (i, _, targets) in enumerate(x_lines(g, sign, fields, side)):
            value = ref[n * g.cols : (n + 1) * g.cols, :]
            for r in targets:
                buf[pl.ds(g.at(i, 1, r), g.cols, stride=g.panel), :] = value
    for i in moving(fields, sign, 0, -1):
        buf[pl.ds(g.at(i, 1, g.rows + 2), g.cols, stride=g.panel), :] = buf[
            pl.ds(g.at(i, 1, 0), g.cols, stride=g.panel), :
        ]


def halo_panels(g, i, sign):
    return (0, g.halo) if velocity(i, sign)[1] == 1 else (g.halo,)


def pack_corners(g, buf, sign, fields, up, down):
    for side, ref in ((1, up), (-1, down)):
        for n, (i, r, _) in enumerate(x_lines(g, sign, fields, side)):
            ref[n : n + 1, :] = buf[pl.ds(g.at(i, g.halo, r), 1), :]


def unpack_corners(g, buf, sign, fields, up, down):
    for side, ref in ((1, up), (-1, down)):
        for n, (i, _, targets) in enumerate(x_lines(g, sign, fields, side)):
            value = ref[n : n + 1, :]
            for r in targets:
                for k in halo_panels(g, i, sign):
                    buf[pl.ds(g.at(i, k, r), 1), :] = value
    for i in moving(fields, sign, 0, -1):
        for k in halo_panels(g, i, sign):
            buf[pl.ds(g.at(i, k, g.rows + 2), 1), :] = buf[pl.ds(g.at(i, k, 0), 1), :]


def still_pairs(fields, sign):
    still = moving(fields, sign, 1, 0)
    half = (len(still) + 1) // 2
    return [(still[n], still[n + half] if n + half < len(still) else None) for n in range(half)]


def y_slots(fields, sign):
    return 9 + len(still_pairs(fields, sign))


def pack_y(g, buf, sign, fields, high, up, down):
    for side, ref in ((1, up), (-1, down)):
        k = g.cols if side == 1 else 1
        for n, i in enumerate(moving(fields, sign, 1, side)):
            ref[n * g.rows : (n + 1) * g.rows, :] = buf[pl.ds(g.at(i, k, 0), g.rows), :]
        for n, (i, j) in enumerate(still_pairs(fields, sign)):
            value = buf[pl.ds(g.at(i, k, 0), g.rows), :]
            if j is not None:
                other = pltpu.roll(buf[pl.ds(g.at(j, k, 0), g.rows), :], NZ, 1)
                pair = (value, other) if side == 1 else (other, value)
                value = jnp.where(high, *pair)
            ref[(9 + n) * g.rows : (10 + n) * g.rows, :] = value


def unpack_y(g, buf, sign, fields, high, up, down):
    for side, ref in ((1, up), (-1, down)):
        for n, i in enumerate(moving(fields, sign, 1, side)):
            value = ref[n * g.rows : (n + 1) * g.rows, :]
            for k in halo_panels(g, i, sign):
                buf[pl.ds(g.at(i, k, 0), g.rows), :] = value
    for n, (i, j) in enumerate(still_pairs(fields, sign)):
        spot = slice((9 + n) * g.rows, (10 + n) * g.rows)
        before, after = up[spot, :], down[spot, :]
        buf[pl.ds(g.at(i, g.halo, 0), g.rows), :] = jnp.where(high, before, after)
        if j is not None:
            value = pltpu.roll(jnp.where(high, after, before), NZ, 1)
            buf[pl.ds(g.at(j, g.halo, 0), g.rows), :] = value


def by_parity(axis, first, second, act):
    even = lax.rem(lax.axis_index(axis), 2) == 0

    @pl.when(even)
    def _():
        act(first, second)

    @pl.when(jnp.logical_not(even))
    def _():
        act(second, first)


def load_fields(ref, rows, base, pieces, count):
    return [read_rows(ref, base + n * rows, pieces) for n in range(count)]


def save_fields(ref, rows, base, pieces, values):
    for n, value in enumerate(values):
        write_rows(ref, base + n * rows, pieces, value)


def save_populations(g, out, k, pieces, values):
    base = pl.multiple_of(k * g.panel, 8)
    for i, value in enumerate(values):
        write_rows(out, base + g.field(i), pieces, value)


def spot_of(g, k):
    return pl.multiple_of((k - 1) * g.rows, 8)


def lanes_of(k):
    return pl.ds(pl.multiple_of((k - 1) * LANES, LANES), LANES)


def every(first, last, act):
    def step(k, carry):
        act(k)
        return carry

    lax.fori_loop(first, last + 1, step, 0)


def side_panels(g, act, count):
    def step(n, carry):
        act(jnp.where(n == 0, 1, g.cols - 1 + n))
        return carry

    lax.fori_loop(0, count, step, 0)


def interior_tiles(g, act):
    for pieces in g.inner:
        every(2, g.cols - 1, functools.partial(act, pieces=pieces))


def middle_tiles(g, act):
    for pieces in g.inner:
        side_panels(g, functools.partial(act, pieces=pieces), 3)
    every(2, g.cols - 1, functools.partial(act, pieces=g.outer))


def rim_tiles(g, act):
    every(1, g.cols, functools.partial(act, pieces=g.outer))
    for pieces in g.inner:
        side_panels(g, functools.partial(act, pieces=pieces), 2)


def step_tile(g, buf, out, sign, fields, masks, compute):
    def act(k, pieces):
        values = compute(
            pull_block(g, buf, sign, k, pieces, masks, fields), spot_of(g, k), pieces
        )
        save_populations(g, out, k, pieces, values)

    return act


def corner_tiles(g, buf, out, sign, fields, masks, compute):
    small = tuple(mask[:8] for mask in masks)
    act = step_tile(g, buf, out, sign, fields, masks, compute)
    side_panels(g, functools.partial(act, pieces=g.outer), 3)
    spot = g.halo * g.rows
    pieces = ((g.rows, 8),)
    values = compute(pull_block(g, buf, sign, g.halo, pieces, small, fields), spot, ((0, 8),))
    for i in range(27):
        dx = velocity(i, sign)[0]
        if dx == -1:
            out[pl.ds(g.at(i, g.halo, g.rows), 1), :] = values[i][0:1]
        elif dx == 1:
            out[pl.ds(g.at(i, g.halo, -1), 1), :] = values[i][1:2]
    edges = [pull_edge(g, buf, sign, side, small, fields) for side in (1, -1)]
    both = [stacked(pair) for pair in zip(*edges)]
    values = compute(both, spot, ((8, 16),))
    for i in moving(27, sign, 0, -1):
        out[pl.ds(g.at(i, 1, g.rows), g.cols, stride=g.panel), :] = values[i][:8]
    for i in moving(27, sign, 0, 1):
        out[pl.ds(g.at(i, 1, -1), g.cols, stride=g.panel), :] = values[i][8:]
    for i in moving(27, sign, 1, 1):
        out[pl.ds(g.at(i, 0, 0), g.rows), :] = out[pl.ds(g.at(i, g.halo, 0), g.rows), :]
        for r in (-1, g.rows):
            out[pl.ds(g.at(i, 0, r), 1), :] = out[pl.ds(g.at(i, g.halo, r), 1), :]


def flow_of(f):
    rho, mx, my, mz = moments(f)
    inverse = 1.0 / rho
    return inverse, rho, mx * inverse, my * inverse, mz * inverse


def collide_first(g, state, out):
    def act(k, pieces, f):
        base = pl.multiple_of(k * g.panel, 8)
        damp, push, wall = (read_rows(out, base + g.field(i), pieces) for i in (27, 28, 29))
        flow = flow_of(f)[1:] + (damp, push)
        save_fields(state, g.local, spot_of(g, k), pieces, flow + (wall,))
        save_populations(g, out, k, pieces, relax(f, *flow, wall > 0.5))

    return act


def collide_second(g, state):
    def compute(values, spot, pieces):
        f, (damp, push, wall) = values[:27], values[27:]
        flow = flow_of(f)[1:] + (damp, push)
        save_fields(state, g.extended, spot, pieces, flow + (wall,))
        return relax(f, *flow, wall > 0.5)

    return compute


def adjoint_second(g, state, total):
    def compute(p, spot, pieces):
        *flow, wall = load_fields(state, g.extended, spot, pieces, 7)
        *spread, porous = adjoint_scalars(p, *flow, wall > 0.5)
        save_fields(total, g.extended, spot, pieces, [porous])
        return adjoint_spread(p, *spread, wall > 0.5)

    return compute


def seed_tile(g, buf, adjoint, stage, out, masks):
    def act(k, pieces):
        f = pull_block(g, buf, 1, k, pieces, masks)
        for i in range(27):
            write_rows(stage.at[k - 1, i], 0, pieces, f[i])
        inverse, _, wx, wy, wz = flow_of(f)
        even = -(wx * wx + wy * wy + wz * wz) * inverse
        along = combos(wx * inverse, wy * inverse, wz * inverse)
        lanes = lanes_of(k)
        seeded = [
            stacked([adjoint[i, pl.ds(r, n), lanes] for r, n in pieces]) + even for i in range(27)
        ]
        for i in range(13):
            seeded[i] = seeded[i] + along[i]
            seeded[26 - i] = seeded[26 - i] - along[i]
        save_populations(g, out, k, pieces, seeded)

    return act


def block_of(ref, k):
    return ref.at[:, :, lanes_of(k)]


def pack_faces(g, buf, sign, fields, x_first, x_second, y_first, y_second):
    high = lane_masks(g.rows)[0]
    by_parity("gx", x_first, x_second, functools.partial(pack_x, g, buf, sign, fields))
    by_parity("gy", y_first, y_second, functools.partial(pack_y, g, buf, sign, fields, high))


def rim_first_kernel(g, pops, *refs):
    flat, (out, state, stage, *faces), near, (sems, flat_sems) = (
        refs[:3],
        refs[3:10],
        refs[10:13],
        refs[13:],
    )
    porosity, solid, labels = near

    def copy(k):
        return pltpu.make_async_copy(block_of(pops, k), stage.at[k - 1], sems.at[k - 1])

    flat_copies = [
        pltpu.make_async_copy(source, target, flat_sems.at[n])
        for n, (source, target) in enumerate(zip(flat, near))
    ]
    for each in flat_copies:
        each.start()
    for k in range(1, g.cols + 1):
        copy(k).start()
    for each in flat_copies:
        each.wait()

    def fields_of(k):
        lanes = lanes_of(k)
        label = labels[:, lanes]
        damp = 1.0 / (1.0 + porosity[:, lanes])
        push = jnp.where(label == 1, PUSH, jnp.where(label == 2, -PUSH, 0.0))
        base = pl.multiple_of(k * g.panel, 8)
        for i, value in ((27, damp), (28, push), (29, solid[:, lanes].astype(F32))):
            out[pl.ds(base + g.field(i), g.rows), :] = value

    every(1, g.cols, fields_of)
    collide = collide_first(g, state, out)

    def act(k, pieces):
        collide(k, pieces, [read_rows(stage.at[k - 1, i], 0, pieces) for i in range(27)])

    def column(k):
        copy(k).wait()
        act(k, g.outer)

    every(1, g.cols, column)
    for pieces in g.inner:
        side_panels(g, functools.partial(act, pieces=pieces), 2)
    pack_faces(g, out, 1, 30, *faces)


def inner_first_kernel(g, _, _state, stage, post, state0, out, state1):
    masks = lane_masks(16)
    collide = collide_first(g, state0, post)

    def act(k, pieces):
        collide(k, pieces, [read_rows(stage.at[k - 1, i], 0, pieces) for i in range(27)])

    interior_tiles(g, act)
    interior_tiles(g, step_tile(g, post, out, 1, 30, masks, collide_second(g, state1)))


def relay_kernel(g, sign, fields, _, y_second, y_first, buf, first, second):
    high = lane_masks(g.rows)[0]
    by_parity("gy", y_second, y_first, functools.partial(unpack_y, g, buf, sign, fields, high))
    by_parity("gx", first, second, functools.partial(pack_corners, g, buf, sign, fields))


def middle_second_kernel(g, post, out, state1, x_second, x_first):
    masks = lane_masks(16)
    by_parity("gx", x_second, x_first, functools.partial(unpack_x, g, post, 1, 30))
    middle_tiles(g, step_tile(g, post, out, 1, 30, masks, collide_second(g, state1)))


def rim_seed_kernel(g, _post, _out, _state, first, second, adjoint, *refs):
    post, out, state1, stage, field, *faces = refs
    masks = lane_masks(16)
    by_parity("gx", second, first, functools.partial(unpack_corners, g, post, 1, 30))
    corner_tiles(g, post, out, 1, 30, masks, collide_second(g, state1))
    rim_tiles(g, seed_tile(g, out, adjoint, stage, field, masks))
    pack_faces(g, field, -1, 27, *faces)


def inner_seed_kernel(
    g, post, _stage, _field, state1, adjoint, stage, field, out, total, final, sems
):
    masks = lane_masks(16)

    def copy(k):
        return pltpu.make_async_copy(stage.at[k - 1], block_of(final, k), sems.at[k - 1])

    copy(1).start()
    copy(g.cols).start()
    seed = seed_tile(g, post, adjoint, stage, field, masks)

    def column(k):
        for pieces in g.inner:
            seed(k, pieces)
        copy(k).start()

    every(2, g.cols - 1, column)
    interior_tiles(g, step_tile(g, field, out, -1, 27, masks, adjoint_second(g, state1, total)))
    every(1, g.cols, lambda k: copy(k).wait())


def middle_adjoint_kernel(g, field, out, total, state1, x_second, x_first):
    masks = lane_masks(16)
    by_parity("gx", x_second, x_first, functools.partial(unpack_x, g, field, -1, 27))
    middle_tiles(g, step_tile(g, field, out, -1, 27, masks, adjoint_second(g, state1, total)))


def total_kernel(g, _field, out, before, state1, state0, first, second, *refs):
    field, out, before, total, peak, parts = refs
    masks = lane_masks(16)
    by_parity("gx", second, first, functools.partial(unpack_corners, g, field, -1, 27))
    corner_tiles(g, field, out, -1, 27, masks, adjoint_second(g, state1, before))
    peak[...] = jnp.zeros((8, LANES), F32)

    def act(k, pieces):
        p = pull_block(g, out, -1, k, pieces, masks)
        spot = spot_of(g, k)
        *flow, wall = load_fields(state0, g.local, spot, pieces, 7)
        *spread, porous = adjoint_scalars(p, *flow, wall > 0.5)
        here = load_fields(before, g.extended, spot, pieces, 1)[0] + porous
        save_fields(total, g.local, spot, pieces, [here])
        save_fields(parts, g.local, spot, pieces, spread + [wall])
        largest = jnp.maximum(jnp.abs(here[:8]), jnp.abs(here[8:]))
        peak[...] = jnp.maximum(peak[...], largest)

    for pieces in (g.outer,) + g.inner:
        every(1, g.cols, functools.partial(act, pieces=pieces))


def adjoint_kernel(g, first, last, buf, parts, result, stage, sems):
    masks = lane_masks(16)

    def copy(k):
        return pltpu.make_async_copy(stage.at[k - first], block_of(result, k), sems.at[k - first])

    def column(k):
        for pieces in (g.outer,) + g.inner:
            p = pull_block(g, buf, -1, k, pieces, masks)
            *spread, wall = load_fields(parts, g.local, spot_of(g, k), pieces, 5)
            for i, value in enumerate(adjoint_spread(p, *spread, wall > 0.5)):
                write_rows(stage.at[k - first, i], 0, pieces, value)
        copy(k).start()

    every(first, last, column)
    every(first, last, lambda k: copy(k).wait())


def scale_kernel(g, total, peak, out):
    largest = jnp.max(peak[...])
    factor = 1.0 / (jnp.full((g.rows, LANES), largest, F32) + EPS)
    for c in range(g.cols):
        value = total[c * g.rows : (c + 1) * g.rows, :] * factor
        out[:, c * LANES : (c + 1) * LANES] = value


def swap_pairs(count, start):
    pairs = []
    for i in range(start, count, 2):
        j = (i + 1) % count
        pairs += [(i, j), (j, i)]
    return pairs


def swap(axis, count, first, second):
    return (
        lax.ppermute(first, axis, swap_pairs(count, 0)),
        lax.ppermute(second, axis, swap_pairs(count, 1)),
    )


def largest_of_all(peak, sizes, beside):
    groups = 0
    for axis, count, widths in (("gy", sizes[1], (2, 4, 4)), ("gx", sizes[0], (4, 2))):
        step = 1
        for width in widths:
            width = min(width, count // step)
            parts = [
                lax.ppermute(peak, axis, [(i, i ^ (n * step)) for i in range(count)])
                for n in range(1, width)
            ]
            groups += 1
            if groups == 2:
                peak = beside(peak)
            peak = functools.reduce(jnp.maximum, parts, peak)
            step *= width
    return peak


def on_device(sizes, populations, adjoint_in, porosity, solid, labels):
    rows, width = porosity.shape
    g = Grid(rows, width)
    in_vmem = pl.BlockSpec(memory_space=pltpu.VMEM)
    in_hbm = pl.BlockSpec(memory_space=pltpu.HBM)
    nx, ny = sizes

    def vmem(*shape):
        return pltpu.VMEM(shape, F32)

    def fields(count, size):
        return vmem(count * size, LANES)

    def padded(count):
        return vmem(*g.padded(count))

    def faces(count, sign):
        along_x = vmem(count * g.cols, LANES)
        along_y = vmem(y_slots(count, sign) * rows, LANES)
        return [along_x, along_x, along_y, along_y]

    def corners(count):
        return [vmem(-(-count // 8) * 8, LANES)] * 2

    whole = pltpu.HBM(populations.shape, F32)
    stage = vmem(g.cols, 27, rows, LANES)
    sems = pltpu.SemaphoreType.DMA((g.cols,))

    def call(name, kernel, operands, out_shape, scratch=(), kept=0, load=0, result=None):
        out_shape = [pltpu.VMEM(x.shape, x.dtype) for x in operands[:kept]] + out_shape
        aliases = {n: n for n in range(kept)}
        space = pltpu.HBM if name == "rim_first" else pltpu.VMEM
        pinned = [pltpu.with_memory_space_constraint(x, space) for x in operands]
        in_specs = [pl.BlockSpec(memory_space=space)] * len(operands)
        if result is not None:
            aliases[len(operands)] = len(out_shape) - 1
            pinned.append(pltpu.with_memory_space_constraint(result, pltpu.HBM))
            in_specs.append(in_hbm)
        return pl.pallas_call(
            functools.partial(kernel, g),
            in_specs=in_specs,
            out_shape=out_shape,
            out_specs=[in_hbm if x is whole else in_vmem for x in out_shape],
            scratch_shapes=list(scratch),
            input_output_aliases=aliases,
            compiler_params=pltpu.CompilerParams(vmem_limit_bytes=VMEM_LIMIT),
            cost_estimate=pl.CostEstimate(flops=0, bytes_accessed=load, transcendentals=0)
            if load
            else None,
            name=name,
        )(*pinned)

    def swap_faces(parcels):
        x_first, x_second = swap("gx", nx, *parcels[:2])
        y_first, y_second = swap("gy", ny, *parcels[2:])
        return [x_second, x_first], [y_second, y_first]

    def relay(buf, parcels, sign, count):
        def kernel(grid, *refs):
            relay_kernel(grid, sign, count, *refs)

        buf, *parcels = call("relay", kernel, [buf, *parcels], corners(count), kept=1)
        return buf, swap("gx", nx, *parcels)

    post, state0, staged, *parcels = call(
        "rim_first",
        rim_first_kernel,
        [populations, porosity, solid, labels],
        [padded(30), fields(7, g.local), stage] + faces(30, 1),
        [vmem(*porosity.shape)]
        + [pltpu.VMEM(porosity.shape, jnp.int32)] * 2
        + [sems, pltpu.SemaphoreType.DMA((3,))],
    )
    along_x, along_y = swap_faces(parcels)
    post, state0, second, state1 = call(
        "inner_first",
        inner_first_kernel,
        [post, state0, staged],
        [padded(27), fields(7, g.extended)],
        kept=2,
        load=FLIGHT,
    )
    post, parcels = relay(post, along_y, 1, 30)
    post, second, state1 = call(
        "middle_second",
        lambda grid, _post, _out, _state, b, a, *refs: middle_second_kernel(grid, *refs, b, a),
        [post, second, state1, *along_x],
        [],
        kept=3,
        load=FLIGHT,
    )
    _, second, state1, staged, field, *parcels = call(
        "rim_seed",
        rim_seed_kernel,
        [post, second, state1, *parcels, adjoint_in],
        [stage, padded(27)] + faces(27, -1),
        kept=3,
    )
    along_x, along_y = swap_faces(parcels)
    _, field, pulled, total, final = call(
        "inner_seed",
        lambda grid, kept, into, buf, *refs: inner_seed_kernel(grid, buf, kept, into, *refs),
        [staged, field, second, state1, adjoint_in],
        [padded(27), fields(1, g.extended), whole],
        [sems],
        kept=2,
        load=FLIGHT,
    )
    field, parcels = relay(field, along_y, -1, 27)
    field, pulled, total = call(
        "middle_adjoint",
        lambda grid, _field, _out, _total, state, b, a, *refs: middle_adjoint_kernel(
            grid, *refs, state, b, a
        ),
        [field, pulled, total, state1, *along_x],
        [],
        kept=3,
        load=FLIGHT,
    )
    _, pulled, _, total, peak, parts = call(
        "total",
        total_kernel,
        [field, pulled, total, state1, state0, *parcels],
        [fields(1, g.local), vmem(8, LANES), fields(5, g.local)],
        kept=3,
    )
    half = g.cols // 2
    scratch = [vmem(half, 27, rows, LANES), pltpu.SemaphoreType.DMA((half,))]
    halves = []

    def first_half(peak):
        def kernel(grid, buf, fields, near, echo, *refs):
            echo[...] = near[...]
            adjoint_kernel(grid, 1, half, buf, fields, *refs)

        echo, result = call(
            "adjoint_low",
            kernel,
            [pulled, parts, peak],
            [vmem(8, LANES), whole],
            scratch,
            load=FLIGHT // 2,
        )
        halves.append(result)
        return echo

    largest = largest_of_all(peak, sizes, first_half)
    (adjoint_out,) = call(
        "adjoint_high",
        lambda grid, buf, fields, _, *refs: adjoint_kernel(
            grid, 1 + half, g.cols, buf, fields, *refs
        ),
        [pulled, parts],
        [whole],
        scratch,
        load=FLIGHT // 2,
        result=halves[0],
    )
    (sensitivity,) = call(
        "normalize",
        scale_kernel,
        [total, largest],
        [jax.ShapeDtypeStruct(porosity.shape, F32)],
    )
    return final, adjoint_out, sensitivity


def solution(mesh):
    sizes = (mesh.shape["gx"], mesh.shape["gy"])
    whole, flat = P(None, "gx", "gy"), P("gx", "gy")
    return jax.shard_map(
        functools.partial(on_device, sizes),
        mesh=mesh,
        in_specs=(whole, whole, flat, flat, flat),
        out_specs=(whole, whole, flat),
        check_vma=False,
    )
```

profile of v0, /device:TPU:0, one launch (start us, length us, event | category | flops | bytes accessed | tf_op | source)
XLA Modules:
  0.0 57.7 jit_solution(5292584592762275897)
XLA Ops:
  0.6 3.3 %rim_first.1 = (f32[14408,128]{1,0:T(8,128)S(1)}, f32[1792,128]{1,0:T(8,128)S(1)}, f32[8,27,32,128]{3,2,1,0:T(8,128)S(1)}, f32[240,128]{1,0:T(8,128)S(1)}, f32[2...) custom-call(f32[27,32,1024]{2,1,0:T(8,128)} %pops.1, f32[32,1024]{1,0:T(8,128)} %refs_0_.1, ...), custom_call_target="tpu_custom_call" | custom-call | tf_op jit(solution)/shard_map/rim_first/pallas_call | solution.py:751
  3.9 3.4 %collective-permute-start = (f32[480,128]{1,0:T(8,128)S(1)}, f32[480,128]{1,0:T(8,128)S(1)}, u32[]{:S(2)}, u32[]{:S(2)}) collective-permute-start(f32[480,128]{1,0:T(8,128)S(1)} %get-tuple-element.48), channel_id=1, source_target_pairs={{1,2},{2,1},{3,4},{4,3},{5,6},{6,5},{7,0},{0,7},{9,10},{10,9},{11,... | collective-permute-start | bytes 737288 | tf_op jit(solution)/shard_map/ppermute | solution.py:691
  7.3 0.0 collective-permute-start.1
  7.3 3.6 %collective-permute-start.2 = (f32[240,128]{1,0:T(8,128)S(1)}, f32[240,128]{1,0:T(8,128)S(1)}, u32[]{:S(2)}, u32[]{:S(2)}) collective-permute-start(f32[240,128]{1,0:T(8,128)S(1)} %get-tuple-element.53), channel_id=1, source_target_pairs={{8,16},{16,8},{24,0},{0,24},{9,17},{17,9},{25,1},{1,25},{10,18},{1... | collective-permute-start | bytes 368648 | tf_op jit(solution)/shard_map/ppermute | solution.py:691
  10.9 0.0 collective-permute-start.3
  10.9 1.9 %inner_first.1 = (f32[14408,128]{1,0:T(8,128)S(1)}, f32[1792,128]{1,0:T(8,128)S(1)}, f32[12968,128]{1,0:T(8,128)S(1)}, f32[2184,128]{1,0:T(8,128)S(1)}) custom-call(f32[14408,128]{1,0:T(8,128)S(1)} %get-tuple-element.44._, f32[1792,128]{1,0:T(8,128)S(1)} %get-tuple-element.45._state, ...), custom_call_target="tpu_custom_call", output_to_operand_aliasing={{0}: (0, {}), {1}: (1, {})} | custom-call | bytes 12582912 | tf_op jit(solution)/shard_map/inner_first/pallas_call | solution.py:751
  12.9 0.1 collective-permute-done.refs_1_
  13.0 0.0 collective-permute-done.1.refs_2_
  13.0 0.1 relay.2
  13.2 3.1 %collective-permute-start.4 = (f32[32,128]{1,0:T(8,128)S(1)}, f32[32,128]{1,0:T(8,128)S(1)}, u32[]{:S(2)}, u32[]{:S(2)}) collective-permute-start(f32[32,128]{1,0:T(8,128)S(1)} %get-tuple-element.58), channel_id=1, source_target_pairs={{0,8},{8,0},{16,24},{24,16},{1,9},{9,1},{17,25},{25,17},{2,10},{10... | collective-permute-start | bytes 49160 | tf_op jit(solution)/shard_map/ppermute | solution.py:690
  16.3 2.5 %collective-permute-start.5 = (f32[32,128]{1,0:T(8,128)S(1)}, f32[32,128]{1,0:T(8,128)S(1)}, u32[]{:S(2)}, u32[]{:S(2)}) collective-permute-start(f32[32,128]{1,0:T(8,128)S(1)} %get-tuple-element.59), channel_id=1, source_target_pairs={{8,16},{16,8},{24,0},{0,24},{9,17},{17,9},{25,1},{1,25},{10,18},{1... | collective-permute-start | bytes 49160 | tf_op jit(solution)/shard_map/ppermute | solution.py:691
  18.7 0.0 collective-permute-done.2.b
  18.8 0.0 collective-permute-done.3.a
  18.8 0.0 copy-start
  18.8 2.2 %middle_second.1 = (f32[14408,128]{1,0:T(8,128)S(1)}, f32[12968,128]{1,0:T(8,128)S(1)}, f32[2184,128]{1,0:T(8,128)S(1)}) custom-call(f32[14408,128]{1,0:T(8,128)S(1)} %get-tuple-element.50._post, f32[12968,128]{1,0:T(8,128)S(1)} %get-tuple-element.51._out, ...), custom_call_target="tpu_custom_call", output_to_operand_aliasing={{0}: (0, {}), {1}: (1, {}), {2}: (2, {})} | custom-call | bytes 12582912 | tf_op jit(solution)/shard_map/middle_second/pallas_call | solution.py:751
  21.0 0.0 collective-permute-done.4.first
  21.0 0.8 %collective-permute-done.5.second = f32[32,128]{1,0:T(8,128)S(1)} collective-permute-done((f32[32,128]{1,0:T(8,128)S(1)}, f32[32,128]{1,0:T(8,128)S(1)}, u32[]{:S(2)}, u32[]{:S(2)}) %collective-permute-start.5) | collective-permute-done | bytes 16416 | tf_op jit(solution)/shard_map/ppermute | solution.py:691
  21.8 0.0 copy-done
  21.8 3.2 %rim_seed.1 = (f32[14408,128]{1,0:T(8,128)S(1)}, f32[12968,128]{1,0:T(8,128)S(1)}, f32[2184,128]{1,0:T(8,128)S(1)}, f32[8,27,32,128]{3,2,1,0:T(8,128)S(1)}, f32[...) custom-call(f32[14408,128]{1,0:T(8,128)S(1)} %get-tuple-element.55._, ...), custom_call_target="tpu_custom_call", output_to_operand_aliasing={{0}: (0, {}), {1}: (1, {}), {2}: (2, {})} | custom-call | tf_op jit(solution)/shard_map/rim_seed/pallas_call | solution.py:751
  25.1 0.1 collective-permute-start.6
  25.1 0.3 collective-permute-start.7
  25.4 2.3 %collective-permute-start.8 = (f32[216,128]{1,0:T(8,128)S(1)}, f32[216,128]{1,0:T(8,128)S(1)}, u32[]{:S(2)}, u32[]{:S(2)}) collective-permute-start(f32[216,128]{1,0:T(8,128)S(1)} %get-tuple-element.71), channel_id=1, source_target_pairs={{8,16},{16,8},{24,0},{0,24},{9,17},{17,9},{25,1},{1,25},{10,18},{1... | collective-permute-start | bytes 331784 | tf_op jit(solution)/shard_map/ppermute | solution.py:691
  27.8 0.0 collective-permute-start.9
  27.8 2.7 %inner_seed.1 = (f32[8,27,32,128]{3,2,1,0:T(8,128)S(1)}, f32[12968,128]{1,0:T(8,128)S(1)}, f32[12968,128]{1,0:T(8,128)S(1)}, f32[312,128]{1,0:T(8,128)S(1)}, f32[27,32,1024]{2,1,0:T(8,128)}) custom-call(f32[8,27,32,128]{3,2,1,0:T(8,128)S(1)} %get-tuple-element.60.kept, ...), custom_call_target="tpu_custom_call", output_to_operand_aliasing={{0}: (0, {}), {1}: (1, {})} | custom-call | bytes 12582912 | tf_op jit(solution)/shard_map/inner_seed/pallas_call | solution.py:751
  30.5 2.7 %collective-permute-done.6.refs_1_ = f32[448,128]{1,0:T(8,128)S(1)} collective-permute-done((f32[448,128]{1,0:T(8,128)S(1)}, f32[448,128]{1,0:T(8,128)S(1)}, u32[]{:S(2)}, u32[]{:S(2)}) %collective-permute-start.6) | collective-permute-done | bytes 229408 | tf_op jit(solution)/shard_map/ppermute | solution.py:691
  33.2 0.0 collective-permute-done.7.refs_2_
  33.2 0.1 relay.3
  33.3 0.1 collective-permute-start.10
  33.4 2.5 %collective-permute-start.11 = (f32[32,128]{1,0:T(8,128)S(1)}, f32[32,128]{1,0:T(8,128)S(1)}, u32[]{:S(2)}, u32[]{:S(2)}) collective-permute-start(f32[32,128]{1,0:T(8,128)S(1)} %get-tuple-element.78), channel_id=1, source_target_pairs={{8,16},{16,8},{24,0},{0,24},{9,17},{17,9},{25,1},{1,25},{10,18},{1... | collective-permute-start | bytes 49160 | tf_op jit(solution)/shard_map/ppermute | solution.py:691
  35.9 0.0 collective-permute-done.8.b
  35.9 0.0 collective-permute-done.9.a
  35.9 2.1 %middle_adjoint.1 = (f32[12968,128]{1,0:T(8,128)S(1)}, f32[12968,128]{1,0:T(8,128)S(1)}, f32[312,128]{1,0:T(8,128)S(1)}) custom-call(f32[12968,128]{1,0:T(8,128)S(1)} %get-tuple-element.68._field, f32[12968,128]{1,0:T(8,128)S(1)} %get-tuple-element.69._out, ...), custom_call_target="tpu_custom_call", output_to_operand_aliasing={{0}: (0, {}), {1}: (1, {}), {2}: (2, {})} | custom-call | bytes 12582912 | tf_op jit(solution)/shard_map/middle_adjoint/pallas_call | solution.py:751
  38.1 0.0 collective-permute-done.10.first
  38.1 0.9 %collective-permute-done.11.second = f32[32,128]{1,0:T(8,128)S(1)} collective-permute-done((f32[32,128]{1,0:T(8,128)S(1)}, f32[32,128]{1,0:T(8,128)S(1)}, u32[]{:S(2)}, u32[]{:S(2)}) %collective-permute-start.11) | collective-permute-done | bytes 16416 | tf_op jit(solution)/shard_map/ppermute | solution.py:691
  39.0 3.9 %total.1 = (f32[12968,128]{1,0:T(8,128)S(1)}, f32[12968,128]{1,0:T(8,128)S(1)}, f32[312,128]{1,0:T(8,128)S(1)}, f32[256,128]{1,0:T(8,128)S(1)}, f32[8,128]{1,0:T(8,128)S(1)}, /*index=5*/f32[1280,128]{1,0:T(8,128)S(1)}) custom-call(f32[12968,128]{1,0:T(8,128)S(1)} %get-tuple-element.73._field, ...), custom_call_target="tpu_custom_call", output_to_operand_aliasing={{0}: (0, {}), {1}: (1, {}), {2}: (2, {})} | custom-call | tf_op jit(solution)/shard_map/total/pallas_call | solution.py:751
  42.9 0.1 collective-permute-start.12
  43.0 1.2 %collective-permute-done.12 = f32[8,128]{1,0:T(8,128)S(1)} collective-permute-done((f32[8,128]{1,0:T(8,128)S(1)}, f32[8,128]{1,0:T(8,128)S(1)}, u32[]{:S(2)}, u32[]{:S(2)}) %collective-permute-start.12) | collective-permute-done | bytes 4128 | tf_op jit(solution)/shard_map/ppermute | solution.py:702
  44.2 2.1 %collective-permute-start.15 = (f32[8,128]{1,0:T(8,128)S(1)}, f32[8,128]{1,0:T(8,128)S(1)}, u32[]{:S(2)}, u32[]{:S(2)}) collective-permute-start(f32[8,128]{1,0:T(8,128)S(1)} %max.21.near), channel_id=1, source_target_pairs={{0,6},{1,7},{2,4},{3,5},{4,2},{5,3},{6,0},{7,1},{8,14},{9,15},{10,... | collective-permute-start | bytes 12296 | tf_op jit(solution)/shard_map/ppermute | solution.py:702
  46.3 0.7 %collective-permute-start.14 = (f32[8,128]{1,0:T(8,128)S(1)}, f32[8,128]{1,0:T(8,128)S(1)}, u32[]{:S(2)}, u32[]{:S(2)}) collective-permute-start(f32[8,128]{1,0:T(8,128)S(1)} %max.21.near), channel_id=1, source_target_pairs={{0,4},{1,5},{2,6},{3,7},{4,0},{5,1},{6,2},{7,3},{8,12},{9,13},{10,... | collective-permute-start | bytes 12296 | tf_op jit(solution)/shard_map/ppermute | solution.py:702
  47.0 0.7 %collective-permute-start.13 = (f32[8,128]{1,0:T(8,128)S(1)}, f32[8,128]{1,0:T(8,128)S(1)}, u32[]{:S(2)}, u32[]{:S(2)}) collective-permute-start(f32[8,128]{1,0:T(8,128)S(1)} %max.21.near), channel_id=1, source_target_pairs={{0,2},{1,3},{2,0},{3,1},{4,6},{5,7},{6,4},{7,5},{8,10},{9,11},{10,... | collective-permute-start | bytes 12296 | tf_op jit(solution)/shard_map/ppermute | solution.py:702
  47.7 1.8 %adjoint_low.1 = (f32[8,128]{1,0:T(8,128)S(1)}, f32[27,32,1024]{2,1,0:T(8,128)}) custom-call(f32[12968,128]{1,0:T(8,128)S(1)} %get-tuple-element.79.buf, f32[1280,128]{1,0:T(8,128)S(1)} %get-tuple-element.80.fields, f32[8,128]{1,0:T(8,128)S(1)} %max.21.near), custom_call_target="tpu_custom_call" | custom-call | bytes 6291456 | tf_op jit(solution)/shard_map/adjoint_low/pallas_call | solution.py:751
  49.5 0.0 collective-permute-done.15
  49.5 0.4 collective-permute-done.14
  49.9 0.7 %collective-permute-done.13 = f32[8,128]{1,0:T(8,128)S(1)} collective-permute-done((f32[8,128]{1,0:T(8,128)S(1)}, f32[8,128]{1,0:T(8,128)S(1)}, u32[]{:S(2)}, u32[]{:S(2)}) %collective-permute-start.13) | collective-permute-done | bytes 4128 | tf_op jit(solution)/shard_map/ppermute | solution.py:702
  50.6 1.4 %collective-permute-start.18 = (f32[8,128]{1,0:T(8,128)S(1)}, f32[8,128]{1,0:T(8,128)S(1)}, u32[]{:S(2)}, u32[]{:S(2)}) collective-permute-start(f32[8,128]{1,0:T(8,128)S(1)} %maximum_maximum_fusion.1), channel_id=1, source_target_pairs={{0,24},{8,16},{16,8},{24,0},{1,25},{9,17},{17,9},{25,1},{2,26},{10... | collective-permute-start | bytes 12296 | tf_op jit(solution)/shard_map/ppermute | solution.py:702
  52.1 0.0 collective-permute-start.17
  52.1 2.9 %collective-permute-start.16 = (f32[8,128]{1,0:T(8,128)S(1)}, f32[8,128]{1,0:T(8,128)S(1)}, u32[]{:S(2)}, u32[]{:S(2)}) collective-permute-start(f32[8,128]{1,0:T(8,128)S(1)} %maximum_maximum_fusion.1), channel_id=1, source_target_pairs={{0,8},{8,0},{16,24},{24,16},{1,9},{9,1},{17,25},{25,17},{2,10},{10... | collective-permute-start | bytes 12296 | tf_op jit(solution)/shard_map/ppermute | solution.py:702
  55.0 1.8 %adjoint_high.1 = f32[27,32,1024]{2,1,0:T(8,128)} custom-call(f32[12968,128]{1,0:T(8,128)S(1)} %get-tuple-element.79.buf, f32[1280,128]{1,0:T(8,128)S(1)} %get-tuple-element.80.fields, f32[27,32,1024]{2,1,0:T(8,128)} %get-tuple-element.82._), custom_call_target="tpu_custom_call", output_to_operand_aliasing={{}: (2, {})} | custom-call | bytes 6291456 | tf_op jit(solution)/shard_map/adjoint_high/pallas_call | solution.py:751
  56.8 0.0 collective-permute-done.18
  56.8 0.0 collective-permute-done.17
  56.8 0.0 collective-permute-done.16
  56.9 0.8 %normalize.1 = f32[32,1024]{1,0:T(8,128)} custom-call(f32[256,128]{1,0:T(8,128)S(1)} %get-tuple-element.83.total, f32[8,128]{1,0:T(8,128)S(1)} %maximum_maximum_fusion.peak), custom_call_target="tpu_custom_call" | custom-call | tf_op jit(solution)/shard_map/normalize/pallas_call | solution.py:751
  (3 shorter events, 0.0 us)
Async XLA Ops:
  3.9 9.1 %collective-permute-start = (f32[480,128]{1,0:T(8,128)S(1)}, f32[480,128]{1,0:T(8,128)S(1)}, u32[]{:S(2)}, u32[]{:S(2)}) collective-permute-start(f32[480,128]{1,0:T(8,128)S(1)} %get-tuple-element.48), channel_id=1, source_target_pairs={{1,2},{2,1},{3,4},{4,3},{5,6},{6,5},{7,0},{0,7},{9,10},{10,9},{11,... | collective-permute-start | bytes 737288 | tf_op jit(solution)/shard_map/ppermute | solution.py:691
  7.3 5.7 %collective-permute-start.1 = (f32[480,128]{1,0:T(8,128)S(1)}, f32[480,128]{1,0:T(8,128)S(1)}, u32[]{:S(2)}, u32[]{:S(2)}) collective-permute-start(f32[480,128]{1,0:T(8,128)S(1)} %get-tuple-element.49), channel_id=1, source_target_pairs={{0,1},{1,0},{2,3},{3,2},{4,5},{5,4},{6,7},{7,6},{8,9},{9,8},{10,11... | collective-permute-start | bytes 737288 | tf_op jit(solution)/shard_map/ppermute | solution.py:690
  7.3 11.4 %collective-permute-start.2 = (f32[240,128]{1,0:T(8,128)S(1)}, f32[240,128]{1,0:T(8,128)S(1)}, u32[]{:S(2)}, u32[]{:S(2)}) collective-permute-start(f32[240,128]{1,0:T(8,128)S(1)} %get-tuple-element.53), channel_id=1, source_target_pairs={{8,16},{16,8},{24,0},{0,24},{9,17},{17,9},{25,1},{1,25},{10,18},{1... | collective-permute-start | bytes 368648 | tf_op jit(solution)/shard_map/ppermute | solution.py:691
  10.9 7.8 %collective-permute-start.3 = (f32[240,128]{1,0:T(8,128)S(1)}, f32[240,128]{1,0:T(8,128)S(1)}, u32[]{:S(2)}, u32[]{:S(2)}) collective-permute-start(f32[240,128]{1,0:T(8,128)S(1)} %get-tuple-element.54), channel_id=1, source_target_pairs={{0,8},{8,0},{16,24},{24,16},{1,9},{9,1},{17,25},{25,17},{2,10},{10... | collective-permute-start | bytes 368648 | tf_op jit(solution)/shard_map/ppermute | solution.py:690
  13.2 7.8 %collective-permute-start.4 = (f32[32,128]{1,0:T(8,128)S(1)}, f32[32,128]{1,0:T(8,128)S(1)}, u32[]{:S(2)}, u32[]{:S(2)}) collective-permute-start(f32[32,128]{1,0:T(8,128)S(1)} %get-tuple-element.58), channel_id=1, source_target_pairs={{0,8},{8,0},{16,24},{24,16},{1,9},{9,1},{17,25},{25,17},{2,10},{10... | collective-permute-start | bytes 49160 | tf_op jit(solution)/shard_map/ppermute | solution.py:690
  16.3 5.5 %collective-permute-start.5 = (f32[32,128]{1,0:T(8,128)S(1)}, f32[32,128]{1,0:T(8,128)S(1)}, u32[]{:S(2)}, u32[]{:S(2)}) collective-permute-start(f32[32,128]{1,0:T(8,128)S(1)} %get-tuple-element.59), channel_id=1, source_target_pairs={{8,16},{16,8},{24,0},{0,24},{9,17},{17,9},{25,1},{1,25},{10,18},{1... | collective-permute-start | bytes 49160 | tf_op jit(solution)/shard_map/ppermute | solution.py:691
  18.8 3.1 %copy-start = (f32[27,32,1024]{2,1,0:T(8,128)S(1)}, f32[27,32,1024]{2,1,0:T(8,128)}, u32[]{:S(2)}) copy-start(f32[27,32,1024]{2,1,0:T(8,128)} %refs_1_.3) | copy-start | bytes 10616836
  25.1 8.1 %collective-permute-start.6 = (f32[448,128]{1,0:T(8,128)S(1)}, f32[448,128]{1,0:T(8,128)S(1)}, u32[]{:S(2)}, u32[]{:S(2)}) collective-permute-start(f32[448,128]{1,0:T(8,128)S(1)} %get-tuple-element.66), channel_id=1, source_target_pairs={{1,2},{2,1},{3,4},{4,3},{5,6},{6,5},{7,0},{0,7},{9,10},{10,9},{11,... | collective-permute-start | bytes 688136 | tf_op jit(solution)/shard_map/ppermute | solution.py:691
  25.1 8.1 %collective-permute-start.7 = (f32[448,128]{1,0:T(8,128)S(1)}, f32[448,128]{1,0:T(8,128)S(1)}, u32[]{:S(2)}, u32[]{:S(2)}) collective-permute-start(f32[448,128]{1,0:T(8,128)S(1)} %get-tuple-element.67), channel_id=1, source_target_pairs={{0,1},{1,0},{2,3},{3,2},{4,5},{5,4},{6,7},{7,6},{8,9},{9,8},{10,11... | collective-permute-start | bytes 688136 | tf_op jit(solution)/shard_map/ppermute | solution.py:690
  25.4 10.5 %collective-permute-start.8 = (f32[216,128]{1,0:T(8,128)S(1)}, f32[216,128]{1,0:T(8,128)S(1)}, u32[]{:S(2)}, u32[]{:S(2)}) collective-permute-start(f32[216,128]{1,0:T(8,128)S(1)} %get-tuple-element.71), channel_id=1, source_target_pairs={{8,16},{16,8},{24,0},{0,24},{9,17},{17,9},{25,1},{1,25},{10,18},{1... | collective-permute-start | bytes 331784 | tf_op jit(solution)/shard_map/ppermute | solution.py:691
  27.8 8.2 %collective-permute-start.9 = (f32[216,128]{1,0:T(8,128)S(1)}, f32[216,128]{1,0:T(8,128)S(1)}, u32[]{:S(2)}, u32[]{:S(2)}) collective-permute-start(f32[216,128]{1,0:T(8,128)S(1)} %get-tuple-element.72), channel_id=1, source_target_pairs={{0,8},{8,0},{16,24},{24,16},{1,9},{9,1},{17,25},{25,17},{2,10},{10... | collective-permute-start | bytes 331784 | tf_op jit(solution)/shard_map/ppermute | solution.py:690
  33.3 4.7 %collective-permute-start.10 = (f32[32,128]{1,0:T(8,128)S(1)}, f32[32,128]{1,0:T(8,128)S(1)}, u32[]{:S(2)}, u32[]{:S(2)}) collective-permute-start(f32[32,128]{1,0:T(8,128)S(1)} %get-tuple-element.77), channel_id=1, source_target_pairs={{0,8},{8,0},{16,24},{24,16},{1,9},{9,1},{17,25},{25,17},{2,10},{10... | collective-permute-start | bytes 49160 | tf_op jit(solution)/shard_map/ppermute | solution.py:690
  33.4 5.6 %collective-permute-start.11 = (f32[32,128]{1,0:T(8,128)S(1)}, f32[32,128]{1,0:T(8,128)S(1)}, u32[]{:S(2)}, u32[]{:S(2)}) collective-permute-start(f32[32,128]{1,0:T(8,128)S(1)} %get-tuple-element.78), channel_id=1, source_target_pairs={{8,16},{16,8},{24,0},{0,24},{9,17},{17,9},{25,1},{1,25},{10,18},{1... | collective-permute-start | bytes 49160 | tf_op jit(solution)/shard_map/ppermute | solution.py:691
  42.9 1.2 %collective-permute-start.12 = (f32[8,128]{1,0:T(8,128)S(1)}, f32[8,128]{1,0:T(8,128)S(1)}, u32[]{:S(2)}, u32[]{:S(2)}) collective-permute-start(f32[8,128]{1,0:T(8,128)S(1)} %get-tuple-element.81), channel_id=1, source_target_pairs={{0,1},{1,0},{2,3},{3,2},{4,5},{5,4},{6,7},{7,6},{8,9},{9,8},{10,11... | collective-permute-start | bytes 12296 | tf_op jit(solution)/shard_map/ppermute | solution.py:702
  44.2 5.3 %collective-permute-start.15 = (f32[8,128]{1,0:T(8,128)S(1)}, f32[8,128]{1,0:T(8,128)S(1)}, u32[]{:S(2)}, u32[]{:S(2)}) collective-permute-start(f32[8,128]{1,0:T(8,128)S(1)} %max.21.near), channel_id=1, source_target_pairs={{0,6},{1,7},{2,4},{3,5},{4,2},{5,3},{6,0},{7,1},{8,14},{9,15},{10,... | collective-permute-start | bytes 12296 | tf_op jit(solution)/shard_map/ppermute | solution.py:702
  46.3 3.6 %collective-permute-start.14 = (f32[8,128]{1,0:T(8,128)S(1)}, f32[8,128]{1,0:T(8,128)S(1)}, u32[]{:S(2)}, u32[]{:S(2)}) collective-permute-start(f32[8,128]{1,0:T(8,128)S(1)} %max.21.near), channel_id=1, source_target_pairs={{0,4},{1,5},{2,6},{3,7},{4,0},{5,1},{6,2},{7,3},{8,12},{9,13},{10,... | collective-permute-start | bytes 12296 | tf_op jit(solution)/shard_map/ppermute | solution.py:702
  47.0 3.6 %collective-permute-start.13 = (f32[8,128]{1,0:T(8,128)S(1)}, f32[8,128]{1,0:T(8,128)S(1)}, u32[]{:S(2)}, u32[]{:S(2)}) collective-permute-start(f32[8,128]{1,0:T(8,128)S(1)} %max.21.near), channel_id=1, source_target_pairs={{0,2},{1,3},{2,0},{3,1},{4,6},{5,7},{6,4},{7,5},{8,10},{9,11},{10,... | collective-permute-start | bytes 12296 | tf_op jit(solution)/shard_map/ppermute | solution.py:702
  50.6 6.2 %collective-permute-start.18 = (f32[8,128]{1,0:T(8,128)S(1)}, f32[8,128]{1,0:T(8,128)S(1)}, u32[]{:S(2)}, u32[]{:S(2)}) collective-permute-start(f32[8,128]{1,0:T(8,128)S(1)} %maximum_maximum_fusion.1), channel_id=1, source_target_pairs={{0,24},{8,16},{16,8},{24,0},{1,25},{9,17},{17,9},{25,1},{2,26},{10... | collective-permute-start | bytes 12296 | tf_op jit(solution)/shard_map/ppermute | solution.py:702
  52.1 4.8 %collective-permute-start.17 = (f32[8,128]{1,0:T(8,128)S(1)}, f32[8,128]{1,0:T(8,128)S(1)}, u32[]{:S(2)}, u32[]{:S(2)}) collective-permute-start(f32[8,128]{1,0:T(8,128)S(1)} %maximum_maximum_fusion.1), channel_id=1, source_target_pairs={{0,16},{8,24},{16,0},{24,8},{1,17},{9,25},{17,1},{25,9},{2,18},{10... | collective-permute-start | bytes 12296 | tf_op jit(solution)/shard_map/ppermute | solution.py:702
  52.1 4.8 %collective-permute-start.16 = (f32[8,128]{1,0:T(8,128)S(1)}, f32[8,128]{1,0:T(8,128)S(1)}, u32[]{:S(2)}, u32[]{:S(2)}) collective-permute-start(f32[8,128]{1,0:T(8,128)S(1)} %maximum_maximum_fusion.1), channel_id=1, source_target_pairs={{0,8},{8,0},{16,24},{24,16},{1,9},{9,1},{17,25},{25,17},{2,10},{10... | collective-permute-start | bytes 12296 | tf_op jit(solution)/shard_map/ppermute | solution.py:702
where the time goes:
time: 57.8 us; the launch traced here: 57.7 us
  starting transfers between devices  25.8 us (45%)
  Pallas kernels  24.1 us (42%)
  waiting for transfers between devices  6.91 us (12%)
  between operations  0.81 us (1%)
    pallas_call x12, Pallas kernels, call(): pl.pallas_call(functools.partial(kernel, g), in_specs=in_specs, out_shape...  24.1 us
    ppermute x6, starting transfers between devices, swap(): lax.ppermute(second, axis, swap_pairs(count, 1))  14.4 us
    ppermute x7, starting transfers between devices, largest_of_all(): lax.ppermute(peak, axis, [(i, i ^ n * step) for i in range(count)])  7.95 us
    ppermute x6, waiting for transfers between devices, swap(): lax.ppermute(second, axis, swap_pairs(count, 1))  4.61 us
    ppermute x6, starting transfers between devices, swap(): lax.ppermute(first, axis, swap_pairs(count, 0))  3.46 us
    ppermute x7, waiting for transfers between devices, largest_of_all(): lax.ppermute(peak, axis, [(i, i ^ n * step) for i in range(count)])  2.28 us
  transfers between devices with their start and end apart: 19, of which 7 were waited for; matrix products, arithmetic and copies ran while one was open for 0% of the time, Pallas kernels for 22%

commit v1 on v0

--- a/solution.py
+++ b/solution.py
@@ -55,20 +55,19 @@
 
 def lane_masks(height):
     lane = lax.broadcasted_iota(jnp.int32, (height, LANES), 1)
-    return lane >= NZ, lane % NZ == 0, lane % NZ == NZ - 1
+    level = lane % NZ
+    below = jnp.where(level == 0, lane + (NZ - 1), lane - 1)
+    above = jnp.where(level == NZ - 1, lane - (NZ - 1), lane + 1)
+    other = lane ^ NZ
+    return lane >= NZ, below, above, below ^ NZ, above ^ NZ, other
 
 
 def shift_lanes(here, d, masks):
-    first, last = masks[1:]
     dy, dz = d[1:]
     if dz == 0:
         return here if dy == 0 else pltpu.roll(here, NZ, 1)
-    if dz == 1:
-        one, other, edge = 1, NZ + 1, first
-    else:
-        one, other, edge = LANES - 1, NZ - 1, last
-    inner, wrapped = (one, other) if dy == 0 else (other, one)
-    return jnp.where(edge, pltpu.roll(here, wrapped, 1), pltpu.roll(here, inner, 1))
+    source = masks[(1 if dz == 1 else 2) + (0 if dy == 0 else 2)]
+    return jnp.take_along_axis(here, source, axis=1, mode="promise_in_bounds")
 
 
 def pull(load, d, masks):

time: 57.8 us -> 58.1 us (level)
  transfers between devices with their start and end apart: 19 -> 19, of which waited for: 7 -> 7; matrix products, arithmetic and copies ran while one was open for 0% -> 0% of each run, Pallas kernels for 22% -> 23%
where the time goes in v1:
time: 58.1 us; the launch traced here: 57.9 us
  starting transfers between devices  25.8 us (44%)
  Pallas kernels  24.4 us (42%)
  waiting for transfers between devices  6.84 us (12%)
  between operations  0.82 us (1%)
    pallas_call x12, Pallas kernels, call(): pl.pallas_call(functools.partial(kernel, g), in_specs=in_specs, out_shape...  24.4 us
    ppermute x6, starting transfers between devices, swap(): lax.ppermute(second, axis, swap_pairs(count, 1))  14.5 us
    ppermute x7, starting transfers between devices, largest_of_all(): lax.ppermute(peak, axis, [(i, i ^ n * step) for i in range(count)])  7.95 us
    ppermute x6, waiting for transfers between devices, swap(): lax.ppermute(second, axis, swap_pairs(count, 1))  4.6 us
    ppermute x6, starting transfers between devices, swap(): lax.ppermute(first, axis, swap_pairs(count, 0))  3.4 us
    ppermute x7, waiting for transfers between devices, largest_of_all(): lax.ppermute(peak, axis, [(i, i ^ n * step) for i in range(count)])  2.23 us
  transfers between devices with their start and end apart: 19, of which 7 were waited for; matrix products, arithmetic and copies ran while one was open for 0% of the time, Pallas kernels for 23%

profile of v1, /device:TPU:0, one launch (start us, length us, event | category | flops | bytes accessed | tf_op | source)
XLA Modules:
  0.0 57.9 jit_solution(12422898076696340906)
XLA Ops:
  0.6 3.3 %rim_first.1 = (f32[14408,128]{1,0:T(8,128)S(1)}, f32[1792,128]{1,0:T(8,128)S(1)}, f32[8,27,32,128]{3,2,1,0:T(8,128)S(1)}, f32[240,128]{1,0:T(8,128)S(1)}, f32[2...) custom-call(f32[27,32,1024]{2,1,0:T(8,128)} %pops.1, f32[32,1024]{1,0:T(8,128)} %refs_0_.1, ...), custom_call_target="tpu_custom_call" | custom-call | tf_op jit(solution)/shard_map/rim_first/pallas_call | solution.py:750
  3.9 3.4 %collective-permute-start = (f32[480,128]{1,0:T(8,128)S(1)}, f32[480,128]{1,0:T(8,128)S(1)}, u32[]{:S(2)}, u32[]{:S(2)}) collective-permute-start(f32[480,128]{1,0:T(8,128)S(1)} %get-tuple-element.48), channel_id=1, source_target_pairs={{1,2},{2,1},{3,4},{4,3},{5,6},{6,5},{7,0},{0,7},{9,10},{10,9},{11,... | collective-permute-start | bytes 737288 | tf_op jit(solution)/shard_map/ppermute | solution.py:690
  7.3 0.0 collective-permute-start.1
  7.3 3.6 %collective-permute-start.2 = (f32[240,128]{1,0:T(8,128)S(1)}, f32[240,128]{1,0:T(8,128)S(1)}, u32[]{:S(2)}, u32[]{:S(2)}) collective-permute-start(f32[240,128]{1,0:T(8,128)S(1)} %get-tuple-element.53), channel_id=1, source_target_pairs={{8,16},{16,8},{24,0},{0,24},{9,17},{17,9},{25,1},{1,25},{10,18},{1... | collective-permute-start | bytes 368648 | tf_op jit(solution)/shard_map/ppermute | solution.py:690
  10.9 0.0 collective-permute-start.3
  10.9 1.9 %inner_first.1 = (f32[14408,128]{1,0:T(8,128)S(1)}, f32[1792,128]{1,0:T(8,128)S(1)}, f32[12968,128]{1,0:T(8,128)S(1)}, f32[2184,128]{1,0:T(8,128)S(1)}) custom-call(f32[14408,128]{1,0:T(8,128)S(1)} %get-tuple-element.44._, f32[1792,128]{1,0:T(8,128)S(1)} %get-tuple-element.45._state, ...), custom_call_target="tpu_custom_call", output_to_operand_aliasing={{0}: (0, {}), {1}: (1, {})} | custom-call | bytes 12582912 | tf_op jit(solution)/shard_map/inner_first/pallas_call | solution.py:750
  12.8 0.2 collective-permute-done.refs_1_
  13.0 0.0 collective-permute-done.1.refs_2_
  13.0 0.1 relay.2
  13.2 3.1 %collective-permute-start.4 = (f32[32,128]{1,0:T(8,128)S(1)}, f32[32,128]{1,0:T(8,128)S(1)}, u32[]{:S(2)}, u32[]{:S(2)}) collective-permute-start(f32[32,128]{1,0:T(8,128)S(1)} %get-tuple-element.58), channel_id=1, source_target_pairs={{0,8},{8,0},{16,24},{24,16},{1,9},{9,1},{17,25},{25,17},{2,10},{10... | collective-permute-start | bytes 49160 | tf_op jit(solution)/shard_map/ppermute | solution.py:689
  16.3 2.5 %collective-permute-start.5 = (f32[32,128]{1,0:T(8,128)S(1)}, f32[32,128]{1,0:T(8,128)S(1)}, u32[]{:S(2)}, u32[]{:S(2)}) collective-permute-start(f32[32,128]{1,0:T(8,128)S(1)} %get-tuple-element.59), channel_id=1, source_target_pairs={{8,16},{16,8},{24,0},{0,24},{9,17},{17,9},{25,1},{1,25},{10,18},{1... | collective-permute-start | bytes 49160 | tf_op jit(solution)/shard_map/ppermute | solution.py:690
  18.7 0.0 collective-permute-done.2.b
  18.8 0.0 collective-permute-done.3.a
  18.8 0.0 copy-start
  18.8 2.2 %middle_second.1 = (f32[14408,128]{1,0:T(8,128)S(1)}, f32[12968,128]{1,0:T(8,128)S(1)}, f32[2184,128]{1,0:T(8,128)S(1)}) custom-call(f32[14408,128]{1,0:T(8,128)S(1)} %get-tuple-element.50._post, f32[12968,128]{1,0:T(8,128)S(1)} %get-tuple-element.51._out, ...), custom_call_target="tpu_custom_call", output_to_operand_aliasing={{0}: (0, {}), {1}: (1, {}), {2}: (2, {})} | custom-call | bytes 12582912 | tf_op jit(solution)/shard_map/middle_second/pallas_call | solution.py:750
  20.9 0.0 collective-permute-done.4.first
  20.9 0.9 %collective-permute-done.5.second = f32[32,128]{1,0:T(8,128)S(1)} collective-permute-done((f32[32,128]{1,0:T(8,128)S(1)}, f32[32,128]{1,0:T(8,128)S(1)}, u32[]{:S(2)}, u32[]{:S(2)}) %collective-permute-start.5) | collective-permute-done | bytes 16416 | tf_op jit(solution)/shard_map/ppermute | solution.py:690
  21.8 0.0 copy-done
  21.8 3.3 %rim_seed.1 = (f32[14408,128]{1,0:T(8,128)S(1)}, f32[12968,128]{1,0:T(8,128)S(1)}, f32[2184,128]{1,0:T(8,128)S(1)}, f32[8,27,32,128]{3,2,1,0:T(8,128)S(1)}, f32[...) custom-call(f32[14408,128]{1,0:T(8,128)S(1)} %get-tuple-element.55._, ...), custom_call_target="tpu_custom_call", output_to_operand_aliasing={{0}: (0, {}), {1}: (1, {}), {2}: (2, {})} | custom-call | tf_op jit(solution)/shard_map/rim_seed/pallas_call | solution.py:750
  25.1 0.1 collective-permute-start.6
  25.2 0.2 collective-permute-start.7
  25.4 2.4 %collective-permute-start.8 = (f32[216,128]{1,0:T(8,128)S(1)}, f32[216,128]{1,0:T(8,128)S(1)}, u32[]{:S(2)}, u32[]{:S(2)}) collective-permute-start(f32[216,128]{1,0:T(8,128)S(1)} %get-tuple-element.71), channel_id=1, source_target_pairs={{8,16},{16,8},{24,0},{0,24},{9,17},{17,9},{25,1},{1,25},{10,18},{1... | collective-permute-start | bytes 331784 | tf_op jit(solution)/shard_map/ppermute | solution.py:690
  27.8 0.0 collective-permute-start.9
  27.8 2.7 %inner_seed.1 = (f32[8,27,32,128]{3,2,1,0:T(8,128)S(1)}, f32[12968,128]{1,0:T(8,128)S(1)}, f32[12968,128]{1,0:T(8,128)S(1)}, f32[312,128]{1,0:T(8,128)S(1)}, f32[27,32,1024]{2,1,0:T(8,128)}) custom-call(f32[8,27,32,128]{3,2,1,0:T(8,128)S(1)} %get-tuple-element.60.kept, ...), custom_call_target="tpu_custom_call", output_to_operand_aliasing={{0}: (0, {}), {1}: (1, {})} | custom-call | bytes 12582912 | tf_op jit(solution)/shard_map/inner_seed/pallas_call | solution.py:750
  30.5 2.7 %collective-permute-done.6.refs_1_ = f32[448,128]{1,0:T(8,128)S(1)} collective-permute-done((f32[448,128]{1,0:T(8,128)S(1)}, f32[448,128]{1,0:T(8,128)S(1)}, u32[]{:S(2)}, u32[]{:S(2)}) %collective-permute-start.6) | collective-permute-done | bytes 229408 | tf_op jit(solution)/shard_map/ppermute | solution.py:690
  33.2 0.0 collective-permute-done.7.refs_2_
  33.2 0.1 relay.3
  33.3 0.1 collective-permute-start.10
  33.4 2.5 %collective-permute-start.11 = (f32[32,128]{1,0:T(8,128)S(1)}, f32[32,128]{1,0:T(8,128)S(1)}, u32[]{:S(2)}, u32[]{:S(2)}) collective-permute-start(f32[32,128]{1,0:T(8,128)S(1)} %get-tuple-element.78), channel_id=1, source_target_pairs={{8,16},{16,8},{24,0},{0,24},{9,17},{17,9},{25,1},{1,25},{10,18},{1... | collective-permute-start | bytes 49160 | tf_op jit(solution)/shard_map/ppermute | solution.py:690
  36.0 0.0 collective-permute-done.8.b
  36.0 0.0 collective-permute-done.9.a
  36.0 2.2 %middle_adjoint.1 = (f32[12968,128]{1,0:T(8,128)S(1)}, f32[12968,128]{1,0:T(8,128)S(1)}, f32[312,128]{1,0:T(8,128)S(1)}) custom-call(f32[12968,128]{1,0:T(8,128)S(1)} %get-tuple-element.68._field, f32[12968,128]{1,0:T(8,128)S(1)} %get-tuple-element.69._out, ...), custom_call_target="tpu_custom_call", output_to_operand_aliasing={{0}: (0, {}), {1}: (1, {}), {2}: (2, {})} | custom-call | bytes 12582912 | tf_op jit(solution)/shard_map/middle_adjoint/pallas_call | solution.py:750
  38.2 0.0 collective-permute-done.10.first
  38.2 0.9 %collective-permute-done.11.second = f32[32,128]{1,0:T(8,128)S(1)} collective-permute-done((f32[32,128]{1,0:T(8,128)S(1)}, f32[32,128]{1,0:T(8,128)S(1)}, u32[]{:S(2)}, u32[]{:S(2)}) %collective-permute-start.11) | collective-permute-done | bytes 16416 | tf_op jit(solution)/shard_map/ppermute | solution.py:690
  39.0 4.1 %total.1 = (f32[12968,128]{1,0:T(8,128)S(1)}, f32[12968,128]{1,0:T(8,128)S(1)}, f32[312,128]{1,0:T(8,128)S(1)}, f32[256,128]{1,0:T(8,128)S(1)}, f32[8,128]{1,0:T(8,128)S(1)}, /*index=5*/f32[1280,128]{1,0:T(8,128)S(1)}) custom-call(f32[12968,128]{1,0:T(8,128)S(1)} %get-tuple-element.73._field, ...), custom_call_target="tpu_custom_call", output_to_operand_aliasing={{0}: (0, {}), {1}: (1, {}), {2}: (2, {})} | custom-call | tf_op jit(solution)/shard_map/total/pallas_call | solution.py:750
  43.1 0.1 collective-permute-start.12
  43.2 1.2 %collective-permute-done.12 = f32[8,128]{1,0:T(8,128)S(1)} collective-permute-done((f32[8,128]{1,0:T(8,128)S(1)}, f32[8,128]{1,0:T(8,128)S(1)}, u32[]{:S(2)}, u32[]{:S(2)}) %collective-permute-start.12) | collective-permute-done | bytes 4128 | tf_op jit(solution)/shard_map/ppermute | solution.py:701
  44.3 2.2 %collective-permute-start.15 = (f32[8,128]{1,0:T(8,128)S(1)}, f32[8,128]{1,0:T(8,128)S(1)}, u32[]{:S(2)}, u32[]{:S(2)}) collective-permute-start(f32[8,128]{1,0:T(8,128)S(1)} %max.21.near), channel_id=1, source_target_pairs={{0,6},{1,7},{2,4},{3,5},{4,2},{5,3},{6,0},{7,1},{8,14},{9,15},{10,... | collective-permute-start | bytes 12296 | tf_op jit(solution)/shard_map/ppermute | solution.py:701
  46.5 0.7 %collective-permute-start.14 = (f32[8,128]{1,0:T(8,128)S(1)}, f32[8,128]{1,0:T(8,128)S(1)}, u32[]{:S(2)}, u32[]{:S(2)}) collective-permute-start(f32[8,128]{1,0:T(8,128)S(1)} %max.21.near), channel_id=1, source_target_pairs={{0,4},{1,5},{2,6},{3,7},{4,0},{5,1},{6,2},{7,3},{8,12},{9,13},{10,... | collective-permute-start | bytes 12296 | tf_op jit(solution)/shard_map/ppermute | solution.py:701
  47.2 0.6 %collective-permute-start.13 = (f32[8,128]{1,0:T(8,128)S(1)}, f32[8,128]{1,0:T(8,128)S(1)}, u32[]{:S(2)}, u32[]{:S(2)}) collective-permute-start(f32[8,128]{1,0:T(8,128)S(1)} %max.21.near), channel_id=1, source_target_pairs={{0,2},{1,3},{2,0},{3,1},{4,6},{5,7},{6,4},{7,5},{8,10},{9,11},{10,... | collective-permute-start | bytes 12296 | tf_op jit(solution)/shard_map/ppermute | solution.py:701
  47.8 1.9 %adjoint_low.1 = (f32[8,128]{1,0:T(8,128)S(1)}, f32[27,32,1024]{2,1,0:T(8,128)}) custom-call(f32[12968,128]{1,0:T(8,128)S(1)} %get-tuple-element.79.buf, f32[1280,128]{1,0:T(8,128)S(1)} %get-tuple-element.80.fields, f32[8,128]{1,0:T(8,128)S(1)} %max.21.near), custom_call_target="tpu_custom_call" | custom-call | bytes 6291456 | tf_op jit(solution)/shard_map/adjoint_low/pallas_call | solution.py:750
  49.7 0.0 collective-permute-done.15
  49.7 0.4 collective-permute-done.14
  50.1 0.7 %collective-permute-done.13 = f32[8,128]{1,0:T(8,128)S(1)} collective-permute-done((f32[8,128]{1,0:T(8,128)S(1)}, f32[8,128]{1,0:T(8,128)S(1)}, u32[]{:S(2)}, u32[]{:S(2)}) %collective-permute-start.13) | collective-permute-done | bytes 4128 | tf_op jit(solution)/shard_map/ppermute | solution.py:701
  50.8 1.5 %collective-permute-start.18 = (f32[8,128]{1,0:T(8,128)S(1)}, f32[8,128]{1,0:T(8,128)S(1)}, u32[]{:S(2)}, u32[]{:S(2)}) collective-permute-start(f32[8,128]{1,0:T(8,128)S(1)} %maximum_maximum_fusion.1), channel_id=1, source_target_pairs={{0,24},{8,16},{16,8},{24,0},{1,25},{9,17},{17,9},{25,1},{2,26},{10... | collective-permute-start | bytes 12296 | tf_op jit(solution)/shard_map/ppermute | solution.py:701
  52.3 0.0 collective-permute-start.17
  52.3 2.9 %collective-permute-start.16 = (f32[8,128]{1,0:T(8,128)S(1)}, f32[8,128]{1,0:T(8,128)S(1)}, u32[]{:S(2)}, u32[]{:S(2)}) collective-permute-start(f32[8,128]{1,0:T(8,128)S(1)} %maximum_maximum_fusion.1), channel_id=1, source_target_pairs={{0,8},{8,0},{16,24},{24,16},{1,9},{9,1},{17,25},{25,17},{2,10},{10... | collective-permute-start | bytes 12296 | tf_op jit(solution)/shard_map/ppermute | solution.py:701
  55.2 1.9 %adjoint_high.1 = f32[27,32,1024]{2,1,0:T(8,128)} custom-call(f32[12968,128]{1,0:T(8,128)S(1)} %get-tuple-element.79.buf, f32[1280,128]{1,0:T(8,128)S(1)} %get-tuple-element.80.fields, f32[27,32,1024]{2,1,0:T(8,128)} %get-tuple-element.82._), custom_call_target="tpu_custom_call", output_to_operand_aliasing={{}: (2, {})} | custom-call | bytes 6291456 | tf_op jit(solution)/shard_map/adjoint_high/pallas_call | solution.py:750
  57.1 0.0 collective-permute-done.18
  57.1 0.0 collective-permute-done.17
  57.1 0.0 collective-permute-done.16
  57.1 0.8 %normalize.1 = f32[32,1024]{1,0:T(8,128)} custom-call(f32[256,128]{1,0:T(8,128)S(1)} %get-tuple-element.83.total, f32[8,128]{1,0:T(8,128)S(1)} %maximum_maximum_fusion.peak), custom_call_target="tpu_custom_call" | custom-call | tf_op jit(solution)/shard_map/normalize/pallas_call | solution.py:750
  (3 shorter events, 0.0 us)
Async XLA Ops:
  3.9 9.1 %collective-permute-start = (f32[480,128]{1,0:T(8,128)S(1)}, f32[480,128]{1,0:T(8,128)S(1)}, u32[]{:S(2)}, u32[]{:S(2)}) collective-permute-start(f32[480,128]{1,0:T(8,128)S(1)} %get-tuple-element.48), channel_id=1, source_target_pairs={{1,2},{2,1},{3,4},{4,3},{5,6},{6,5},{7,0},{0,7},{9,10},{10,9},{11,... | collective-permute-start | bytes 737288 | tf_op jit(solution)/shard_map/ppermute | solution.py:690
  7.3 5.7 %collective-permute-start.1 = (f32[480,128]{1,0:T(8,128)S(1)}, f32[480,128]{1,0:T(8,128)S(1)}, u32[]{:S(2)}, u32[]{:S(2)}) collective-permute-start(f32[480,128]{1,0:T(8,128)S(1)} %get-tuple-element.49), channel_id=1, source_target_pairs={{0,1},{1,0},{2,3},{3,2},{4,5},{5,4},{6,7},{7,6},{8,9},{9,8},{10,11... | collective-permute-start | bytes 737288 | tf_op jit(solution)/shard_map/ppermute | solution.py:689
  7.3 11.4 %collective-permute-start.2 = (f32[240,128]{1,0:T(8,128)S(1)}, f32[240,128]{1,0:T(8,128)S(1)}, u32[]{:S(2)}, u32[]{:S(2)}) collective-permute-start(f32[240,128]{1,0:T(8,128)S(1)} %get-tuple-element.53), channel_id=1, source_target_pairs={{8,16},{16,8},{24,0},{0,24},{9,17},{17,9},{25,1},{1,25},{10,18},{1... | collective-permute-start | bytes 368648 | tf_op jit(solution)/shard_map/ppermute | solution.py:690
  10.9 7.8 %collective-permute-start.3 = (f32[240,128]{1,0:T(8,128)S(1)}, f32[240,128]{1,0:T(8,128)S(1)}, u32[]{:S(2)}, u32[]{:S(2)}) collective-permute-start(f32[240,128]{1,0:T(8,128)S(1)} %get-tuple-element.54), channel_id=1, source_target_pairs={{0,8},{8,0},{16,24},{24,16},{1,9},{9,1},{17,25},{25,17},{2,10},{10... | collective-permute-start | bytes 368648 | tf_op jit(solution)/shard_map/ppermute | solution.py:689
  13.2 7.8 %collective-permute-start.4 = (f32[32,128]{1,0:T(8,128)S(1)}, f32[32,128]{1,0:T(8,128)S(1)}, u32[]{:S(2)}, u32[]{:S(2)}) collective-permute-start(f32[32,128]{1,0:T(8,128)S(1)} %get-tuple-element.58), channel_id=1, source_target_pairs={{0,8},{8,0},{16,24},{24,16},{1,9},{9,1},{17,25},{25,17},{2,10},{10... | collective-permute-start | bytes 49160 | tf_op jit(solution)/shard_map/ppermute | solution.py:689
  16.3 5.5 %collective-permute-start.5 = (f32[32,128]{1,0:T(8,128)S(1)}, f32[32,128]{1,0:T(8,128)S(1)}, u32[]{:S(2)}, u32[]{:S(2)}) collective-permute-start(f32[32,128]{1,0:T(8,128)S(1)} %get-tuple-element.59), channel_id=1, source_target_pairs={{8,16},{16,8},{24,0},{0,24},{9,17},{17,9},{25,1},{1,25},{10,18},{1... | collective-permute-start | bytes 49160 | tf_op jit(solution)/shard_map/ppermute | solution.py:690
  18.8 3.1 %copy-start = (f32[27,32,1024]{2,1,0:T(8,128)S(1)}, f32[27,32,1024]{2,1,0:T(8,128)}, u32[]{:S(2)}) copy-start(f32[27,32,1024]{2,1,0:T(8,128)} %refs_1_.3) | copy-start | bytes 10616836
  25.1 8.1 %collective-permute-start.6 = (f32[448,128]{1,0:T(8,128)S(1)}, f32[448,128]{1,0:T(8,128)S(1)}, u32[]{:S(2)}, u32[]{:S(2)}) collective-permute-start(f32[448,128]{1,0:T(8,128)S(1)} %get-tuple-element.66), channel_id=1, source_target_pairs={{1,2},{2,1},{3,4},{4,3},{5,6},{6,5},{7,0},{0,7},{9,10},{10,9},{11,... | collective-permute-start | bytes 688136 | tf_op jit(solution)/shard_map/ppermute | solution.py:690
  25.2 8.1 %collective-permute-start.7 = (f32[448,128]{1,0:T(8,128)S(1)}, f32[448,128]{1,0:T(8,128)S(1)}, u32[]{:S(2)}, u32[]{:S(2)}) collective-permute-start(f32[448,128]{1,0:T(8,128)S(1)} %get-tuple-element.67), channel_id=1, source_target_pairs={{0,1},{1,0},{2,3},{3,2},{4,5},{5,4},{6,7},{7,6},{8,9},{9,8},{10,11... | collective-permute-start | bytes 688136 | tf_op jit(solution)/shard_map/ppermute | solution.py:689
  25.4 10.6 %collective-permute-start.8 = (f32[216,128]{1,0:T(8,128)S(1)}, f32[216,128]{1,0:T(8,128)S(1)}, u32[]{:S(2)}, u32[]{:S(2)}) collective-permute-start(f32[216,128]{1,0:T(8,128)S(1)} %get-tuple-element.71), channel_id=1, source_target_pairs={{8,16},{16,8},{24,0},{0,24},{9,17},{17,9},{25,1},{1,25},{10,18},{1... | collective-permute-start | bytes 331784 | tf_op jit(solution)/shard_map/ppermute | solution.py:690
  27.8 8.2 %collective-permute-start.9 = (f32[216,128]{1,0:T(8,128)S(1)}, f32[216,128]{1,0:T(8,128)S(1)}, u32[]{:S(2)}, u32[]{:S(2)}) collective-permute-start(f32[216,128]{1,0:T(8,128)S(1)} %get-tuple-element.72), channel_id=1, source_target_pairs={{0,8},{8,0},{16,24},{24,16},{1,9},{9,1},{17,25},{25,17},{2,10},{10... | collective-permute-start | bytes 331784 | tf_op jit(solution)/shard_map/ppermute | solution.py:689
  33.3 4.8 %collective-permute-start.10 = (f32[32,128]{1,0:T(8,128)S(1)}, f32[32,128]{1,0:T(8,128)S(1)}, u32[]{:S(2)}, u32[]{:S(2)}) collective-permute-start(f32[32,128]{1,0:T(8,128)S(1)} %get-tuple-element.77), channel_id=1, source_target_pairs={{0,8},{8,0},{16,24},{24,16},{1,9},{9,1},{17,25},{25,17},{2,10},{10... | collective-permute-start | bytes 49160 | tf_op jit(solution)/shard_map/ppermute | solution.py:689
  33.4 5.6 %collective-permute-start.11 = (f32[32,128]{1,0:T(8,128)S(1)}, f32[32,128]{1,0:T(8,128)S(1)}, u32[]{:S(2)}, u32[]{:S(2)}) collective-permute-start(f32[32,128]{1,0:T(8,128)S(1)} %get-tuple-element.78), channel_id=1, source_target_pairs={{8,16},{16,8},{24,0},{0,24},{9,17},{17,9},{25,1},{1,25},{10,18},{1... | collective-permute-start | bytes 49160 | tf_op jit(solution)/shard_map/ppermute | solution.py:690
  43.1 1.2 %collective-permute-start.12 = (f32[8,128]{1,0:T(8,128)S(1)}, f32[8,128]{1,0:T(8,128)S(1)}, u32[]{:S(2)}, u32[]{:S(2)}) collective-permute-start(f32[8,128]{1,0:T(8,128)S(1)} %get-tuple-element.81), channel_id=1, source_target_pairs={{0,1},{1,0},{2,3},{3,2},{4,5},{5,4},{6,7},{7,6},{8,9},{9,8},{10,11... | collective-permute-start | bytes 12296 | tf_op jit(solution)/shard_map/ppermute | solution.py:701
  44.3 5.4 %collective-permute-start.15 = (f32[8,128]{1,0:T(8,128)S(1)}, f32[8,128]{1,0:T(8,128)S(1)}, u32[]{:S(2)}, u32[]{:S(2)}) collective-permute-start(f32[8,128]{1,0:T(8,128)S(1)} %max.21.near), channel_id=1, source_target_pairs={{0,6},{1,7},{2,4},{3,5},{4,2},{5,3},{6,0},{7,1},{8,14},{9,15},{10,... | collective-permute-start | bytes 12296 | tf_op jit(solution)/shard_map/ppermute | solution.py:701
  46.5 3.6 %collective-permute-start.14 = (f32[8,128]{1,0:T(8,128)S(1)}, f32[8,128]{1,0:T(8,128)S(1)}, u32[]{:S(2)}, u32[]{:S(2)}) collective-permute-start(f32[8,128]{1,0:T(8,128)S(1)} %max.21.near), channel_id=1, source_target_pairs={{0,4},{1,5},{2,6},{3,7},{4,0},{5,1},{6,2},{7,3},{8,12},{9,13},{10,... | collective-permute-start | bytes 12296 | tf_op jit(solution)/shard_map/ppermute | solution.py:701
  47.2 3.6 %collective-permute-start.13 = (f32[8,128]{1,0:T(8,128)S(1)}, f32[8,128]{1,0:T(8,128)S(1)}, u32[]{:S(2)}, u32[]{:S(2)}) collective-permute-start(f32[8,128]{1,0:T(8,128)S(1)} %max.21.near), channel_id=1, source_target_pairs={{0,2},{1,3},{2,0},{3,1},{4,6},{5,7},{6,4},{7,5},{8,10},{9,11},{10,... | collective-permute-start | bytes 12296 | tf_op jit(solution)/shard_map/ppermute | solution.py:701
  50.8 6.3 %collective-permute-start.18 = (f32[8,128]{1,0:T(8,128)S(1)}, f32[8,128]{1,0:T(8,128)S(1)}, u32[]{:S(2)}, u32[]{:S(2)}) collective-permute-start(f32[8,128]{1,0:T(8,128)S(1)} %maximum_maximum_fusion.1), channel_id=1, source_target_pairs={{0,24},{8,16},{16,8},{24,0},{1,25},{9,17},{17,9},{25,1},{2,26},{10... | collective-permute-start | bytes 12296 | tf_op jit(solution)/shard_map/ppermute | solution.py:701
  52.3 4.8 %collective-permute-start.17 = (f32[8,128]{1,0:T(8,128)S(1)}, f32[8,128]{1,0:T(8,128)S(1)}, u32[]{:S(2)}, u32[]{:S(2)}) collective-permute-start(f32[8,128]{1,0:T(8,128)S(1)} %maximum_maximum_fusion.1), channel_id=1, source_target_pairs={{0,16},{8,24},{16,0},{24,8},{1,17},{9,25},{17,1},{25,9},{2,18},{10... | collective-permute-start | bytes 12296 | tf_op jit(solution)/shard_map/ppermute | solution.py:701
  52.3 4.8 %collective-permute-start.16 = (f32[8,128]{1,0:T(8,128)S(1)}, f32[8,128]{1,0:T(8,128)S(1)}, u32[]{:S(2)}, u32[]{:S(2)}) collective-permute-start(f32[8,128]{1,0:T(8,128)S(1)} %maximum_maximum_fusion.1), channel_id=1, source_target_pairs={{0,8},{8,0},{16,24},{24,16},{1,9},{9,1},{17,25},{25,17},{2,10},{10... | collective-permute-start | bytes 12296 | tf_op jit(solution)/shard_map/ppermute | solution.py:701

commit v2 on v0

--- a/solution.py
+++ b/solution.py
@@ -390,7 +390,7 @@
         act(k)
         return carry
 
-    lax.fori_loop(first, last + 1, step, 0)
+    lax.fori_loop(first, last + 1, step, 0, unroll=2 - (last + 1 - first) % 2)
 
 
 def side_panels(g, act, count):
@@ -398,7 +398,7 @@
         act(jnp.where(n == 0, 1, g.cols - 1 + n))
         return carry
 
-    lax.fori_loop(0, count, step, 0)
+    lax.fori_loop(0, count, step, 0, unroll=count)
 
 
 def interior_tiles(g, act):

time: 57.8 us -> 55.6 us (0.962)
  Pallas kernels: 24.1 us -> 19.7 us
  waiting for transfers between devices: 6.91 us -> 9.07 us
    pallas_call x12, Pallas kernels: 24.1 us -> 19.7 us  [call(): pl.pallas_call(functools.partial(kernel, g), in_specs=in_specs, out_shape...]
    ppermute x6, waiting for transfers between devices: 4.61 us -> 6.89 us  [swap(): lax.ppermute(second, axis, swap_pairs(count, 1))]
  transfers between devices with their start and end apart: 19 -> 19, of which waited for: 7 -> 7; matrix products, arithmetic and copies ran while one was open for 0% -> 0% of each run, Pallas kernels for 22% -> 18%
where the time goes in v2:
time: 55.6 us; the launch traced here: 55.4 us
  starting transfers between devices  25.8 us (46%)
  Pallas kernels  19.7 us (35%)
  waiting for transfers between devices  9.07 us (16%)
  between operations  0.81 us (1%)
    pallas_call x12, Pallas kernels, call(): pl.pallas_call(functools.partial(kernel, g), in_specs=in_specs, out_shape...  19.7 us
    ppermute x6, starting transfers between devices, swap(): lax.ppermute(second, axis, swap_pairs(count, 1))  14.6 us
    ppermute x7, starting transfers between devices, largest_of_all(): lax.ppermute(peak, axis, [(i, i ^ n * step) for i in range(count)])  7.95 us
    ppermute x6, waiting for transfers between devices, swap(): lax.ppermute(second, axis, swap_pairs(count, 1))  6.89 us
    ppermute x6, starting transfers between devices, swap(): lax.ppermute(first, axis, swap_pairs(count, 0))  3.26 us
    ppermute x7, waiting for transfers between devices, largest_of_all(): lax.ppermute(peak, axis, [(i, i ^ n * step) for i in range(count)])  2.17 us
  transfers between devices with their start and end apart: 19, of which 7 were waited for; matrix products, arithmetic and copies ran while one was open for 0% of the time, Pallas kernels for 18%

profile of v2, /device:TPU:0, one launch (start us, length us, event | category | flops | bytes accessed | tf_op | source)
XLA Modules:
  0.0 55.4 jit_solution(6109613981756809645)
XLA Ops:
  0.6 3.2 %rim_first.1 = (f32[14408,128]{1,0:T(8,128)S(1)}, f32[1792,128]{1,0:T(8,128)S(1)}, f32[8,27,32,128]{3,2,1,0:T(8,128)S(1)}, f32[240,128]{1,0:T(8,128)S(1)}, f32[2...) custom-call(f32[27,32,1024]{2,1,0:T(8,128)} %pops.1, f32[32,1024]{1,0:T(8,128)} %refs_0_.1, ...), custom_call_target="tpu_custom_call" | custom-call | tf_op jit(solution)/shard_map/rim_first/pallas_call | solution.py:751
  3.9 3.4 %collective-permute-start = (f32[480,128]{1,0:T(8,128)S(1)}, f32[480,128]{1,0:T(8,128)S(1)}, u32[]{:S(2)}, u32[]{:S(2)}) collective-permute-start(f32[480,128]{1,0:T(8,128)S(1)} %get-tuple-element.48), channel_id=1, source_target_pairs={{1,2},{2,1},{3,4},{4,3},{5,6},{6,5},{7,0},{0,7},{9,10},{10,9},{11,... | collective-permute-start | bytes 737288 | tf_op jit(solution)/shard_map/ppermute | solution.py:691
  7.3 0.0 collective-permute-start.1
  7.3 3.6 %collective-permute-start.2 = (f32[240,128]{1,0:T(8,128)S(1)}, f32[240,128]{1,0:T(8,128)S(1)}, u32[]{:S(2)}, u32[]{:S(2)}) collective-permute-start(f32[240,128]{1,0:T(8,128)S(1)} %get-tuple-element.53), channel_id=1, source_target_pairs={{8,16},{16,8},{24,0},{0,24},{9,17},{17,9},{25,1},{1,25},{10,18},{1... | collective-permute-start | bytes 368648 | tf_op jit(solution)/shard_map/ppermute | solution.py:691
  10.9 0.0 collective-permute-start.3
  10.9 1.5 %inner_first.1 = (f32[14408,128]{1,0:T(8,128)S(1)}, f32[1792,128]{1,0:T(8,128)S(1)}, f32[12968,128]{1,0:T(8,128)S(1)}, f32[2184,128]{1,0:T(8,128)S(1)}) custom-call(f32[14408,128]{1,0:T(8,128)S(1)} %get-tuple-element.44._, f32[1792,128]{1,0:T(8,128)S(1)} %get-tuple-element.45._state, ...), custom_call_target="tpu_custom_call", output_to_operand_aliasing={{0}: (0, {}), {1}: (1, {})} | custom-call | bytes 12582912 | tf_op jit(solution)/shard_map/inner_first/pallas_call | solution.py:751
  12.4 0.5 collective-permute-done.refs_1_
  13.0 0.0 collective-permute-done.1.refs_2_
  13.0 0.1 relay.2
  13.1 3.1 %collective-permute-start.4 = (f32[32,128]{1,0:T(8,128)S(1)}, f32[32,128]{1,0:T(8,128)S(1)}, u32[]{:S(2)}, u32[]{:S(2)}) collective-permute-start(f32[32,128]{1,0:T(8,128)S(1)} %get-tuple-element.58), channel_id=1, source_target_pairs={{0,8},{8,0},{16,24},{24,16},{1,9},{9,1},{17,25},{25,17},{2,10},{10... | collective-permute-start | bytes 49160 | tf_op jit(solution)/shard_map/ppermute | solution.py:690
  16.2 2.5 %collective-permute-start.5 = (f32[32,128]{1,0:T(8,128)S(1)}, f32[32,128]{1,0:T(8,128)S(1)}, u32[]{:S(2)}, u32[]{:S(2)}) collective-permute-start(f32[32,128]{1,0:T(8,128)S(1)} %get-tuple-element.59), channel_id=1, source_target_pairs={{8,16},{16,8},{24,0},{0,24},{9,17},{17,9},{25,1},{1,25},{10,18},{1... | collective-permute-start | bytes 49160 | tf_op jit(solution)/shard_map/ppermute | solution.py:691
  18.7 0.0 collective-permute-done.2.b
  18.7 0.0 collective-permute-done.3.a
  18.7 0.0 copy-start
  18.7 1.6 %middle_second.1 = (f32[14408,128]{1,0:T(8,128)S(1)}, f32[12968,128]{1,0:T(8,128)S(1)}, f32[2184,128]{1,0:T(8,128)S(1)}) custom-call(f32[14408,128]{1,0:T(8,128)S(1)} %get-tuple-element.50._post, f32[12968,128]{1,0:T(8,128)S(1)} %get-tuple-element.51._out, ...), custom_call_target="tpu_custom_call", output_to_operand_aliasing={{0}: (0, {}), {1}: (1, {}), {2}: (2, {})} | custom-call | bytes 12582912 | tf_op jit(solution)/shard_map/middle_second/pallas_call | solution.py:751
  20.3 0.0 collective-permute-done.4.first
  20.3 1.5 %collective-permute-done.5.second = f32[32,128]{1,0:T(8,128)S(1)} collective-permute-done((f32[32,128]{1,0:T(8,128)S(1)}, f32[32,128]{1,0:T(8,128)S(1)}, u32[]{:S(2)}, u32[]{:S(2)}) %collective-permute-start.5) | collective-permute-done | bytes 16416 | tf_op jit(solution)/shard_map/ppermute | solution.py:691
  21.8 0.0 copy-done
  21.8 2.5 %rim_seed.1 = (f32[14408,128]{1,0:T(8,128)S(1)}, f32[12968,128]{1,0:T(8,128)S(1)}, f32[2184,128]{1,0:T(8,128)S(1)}, f32[8,27,32,128]{3,2,1,0:T(8,128)S(1)}, f32[...) custom-call(f32[14408,128]{1,0:T(8,128)S(1)} %get-tuple-element.55._, ...), custom_call_target="tpu_custom_call", output_to_operand_aliasing={{0}: (0, {}), {1}: (1, {}), {2}: (2, {})} | custom-call | tf_op jit(solution)/shard_map/rim_seed/pallas_call | solution.py:751
  24.2 0.1 collective-permute-start.6
  24.3 0.1 collective-permute-start.7
  24.4 2.5 %collective-permute-start.8 = (f32[216,128]{1,0:T(8,128)S(1)}, f32[216,128]{1,0:T(8,128)S(1)}, u32[]{:S(2)}, u32[]{:S(2)}) collective-permute-start(f32[216,128]{1,0:T(8,128)S(1)} %get-tuple-element.71), channel_id=1, source_target_pairs={{8,16},{16,8},{24,0},{0,24},{9,17},{17,9},{25,1},{1,25},{10,18},{1... | collective-permute-start | bytes 331784 | tf_op jit(solution)/shard_map/ppermute | solution.py:691
  26.9 0.0 collective-permute-start.9
  26.9 2.0 %inner_seed.1 = (f32[8,27,32,128]{3,2,1,0:T(8,128)S(1)}, f32[12968,128]{1,0:T(8,128)S(1)}, f32[12968,128]{1,0:T(8,128)S(1)}, f32[312,128]{1,0:T(8,128)S(1)}, f32[27,32,1024]{2,1,0:T(8,128)}) custom-call(f32[8,27,32,128]{3,2,1,0:T(8,128)S(1)} %get-tuple-element.60.kept, ...), custom_call_target="tpu_custom_call", output_to_operand_aliasing={{0}: (0, {}), {1}: (1, {})} | custom-call | bytes 12582912 | tf_op jit(solution)/shard_map/inner_seed/pallas_call | solution.py:751
  29.0 3.4 %collective-permute-done.6.refs_1_ = f32[448,128]{1,0:T(8,128)S(1)} collective-permute-done((f32[448,128]{1,0:T(8,128)S(1)}, f32[448,128]{1,0:T(8,128)S(1)}, u32[]{:S(2)}, u32[]{:S(2)}) %collective-permute-start.6) | collective-permute-done | bytes 229408 | tf_op jit(solution)/shard_map/ppermute | solution.py:691
  32.4 0.0 collective-permute-done.7.refs_2_
  32.4 0.1 relay.3
  32.5 0.1 collective-permute-start.10
  32.6 2.5 %collective-permute-start.11 = (f32[32,128]{1,0:T(8,128)S(1)}, f32[32,128]{1,0:T(8,128)S(1)}, u32[]{:S(2)}, u32[]{:S(2)}) collective-permute-start(f32[32,128]{1,0:T(8,128)S(1)} %get-tuple-element.78), channel_id=1, source_target_pairs={{8,16},{16,8},{24,0},{0,24},{9,17},{17,9},{25,1},{1,25},{10,18},{1... | collective-permute-start | bytes 49160 | tf_op jit(solution)/shard_map/ppermute | solution.py:691
  35.1 0.0 collective-permute-done.8.b
  35.1 0.0 collective-permute-done.9.a
  35.1 1.5 %middle_adjoint.1 = (f32[12968,128]{1,0:T(8,128)S(1)}, f32[12968,128]{1,0:T(8,128)S(1)}, f32[312,128]{1,0:T(8,128)S(1)}) custom-call(f32[12968,128]{1,0:T(8,128)S(1)} %get-tuple-element.68._field, f32[12968,128]{1,0:T(8,128)S(1)} %get-tuple-element.69._out, ...), custom_call_target="tpu_custom_call", output_to_operand_aliasing={{0}: (0, {}), {1}: (1, {}), {2}: (2, {})} | custom-call | bytes 12582912 | tf_op jit(solution)/shard_map/middle_adjoint/pallas_call | solution.py:751
  36.7 0.0 collective-permute-done.10.first
  36.7 1.5 %collective-permute-done.11.second = f32[32,128]{1,0:T(8,128)S(1)} collective-permute-done((f32[32,128]{1,0:T(8,128)S(1)}, f32[32,128]{1,0:T(8,128)S(1)}, u32[]{:S(2)}, u32[]{:S(2)}) %collective-permute-start.11) | collective-permute-done | bytes 16416 | tf_op jit(solution)/shard_map/ppermute | solution.py:691
  38.2 2.9 %total.1 = (f32[12968,128]{1,0:T(8,128)S(1)}, f32[12968,128]{1,0:T(8,128)S(1)}, f32[312,128]{1,0:T(8,128)S(1)}, f32[256,128]{1,0:T(8,128)S(1)}, f32[8,128]{1,0:T(8,128)S(1)}, /*index=5*/f32[1280,128]{1,0:T(8,128)S(1)}) custom-call(f32[12968,128]{1,0:T(8,128)S(1)} %get-tuple-element.73._field, ...), custom_call_target="tpu_custom_call", output_to_operand_aliasing={{0}: (0, {}), {1}: (1, {}), {2}: (2, {})} | custom-call | tf_op jit(solution)/shard_map/total/pallas_call | solution.py:751
  41.1 0.1 collective-permute-start.12
  41.2 1.2 %collective-permute-done.12 = f32[8,128]{1,0:T(8,128)S(1)} collective-permute-done((f32[8,128]{1,0:T(8,128)S(1)}, f32[8,128]{1,0:T(8,128)S(1)}, u32[]{:S(2)}, u32[]{:S(2)}) %collective-permute-start.12) | collective-permute-done | bytes 4128 | tf_op jit(solution)/shard_map/ppermute | solution.py:702
  42.4 1.4 %collective-permute-start.15 = (f32[8,128]{1,0:T(8,128)S(1)}, f32[8,128]{1,0:T(8,128)S(1)}, u32[]{:S(2)}, u32[]{:S(2)}) collective-permute-start(f32[8,128]{1,0:T(8,128)S(1)} %max.21.near), channel_id=1, source_target_pairs={{0,6},{1,7},{2,4},{3,5},{4,2},{5,3},{6,0},{7,1},{8,14},{9,15},{10,... | collective-permute-start | bytes 12296 | tf_op jit(solution)/shard_map/ppermute | solution.py:702
  43.8 0.7 %collective-permute-start.14 = (f32[8,128]{1,0:T(8,128)S(1)}, f32[8,128]{1,0:T(8,128)S(1)}, u32[]{:S(2)}, u32[]{:S(2)}) collective-permute-start(f32[8,128]{1,0:T(8,128)S(1)} %max.21.near), channel_id=1, source_target_pairs={{0,4},{1,5},{2,6},{3,7},{4,0},{5,1},{6,2},{7,3},{8,12},{9,13},{10,... | collective-permute-start | bytes 12296 | tf_op jit(solution)/shard_map/ppermute | solution.py:702
  44.5 1.3 %collective-permute-start.13 = (f32[8,128]{1,0:T(8,128)S(1)}, f32[8,128]{1,0:T(8,128)S(1)}, u32[]{:S(2)}, u32[]{:S(2)}) collective-permute-start(f32[8,128]{1,0:T(8,128)S(1)} %max.21.near), channel_id=1, source_target_pairs={{0,2},{1,3},{2,0},{3,1},{4,6},{5,7},{6,4},{7,5},{8,10},{9,11},{10,... | collective-permute-start | bytes 12296 | tf_op jit(solution)/shard_map/ppermute | solution.py:702
  45.9 1.7 %adjoint_low.1 = (f32[8,128]{1,0:T(8,128)S(1)}, f32[27,32,1024]{2,1,0:T(8,128)}) custom-call(f32[12968,128]{1,0:T(8,128)S(1)} %get-tuple-element.79.buf, f32[1280,128]{1,0:T(8,128)S(1)} %get-tuple-element.80.fields, f32[8,128]{1,0:T(8,128)S(1)} %max.21.near), custom_call_target="tpu_custom_call" | custom-call | bytes 6291456 | tf_op jit(solution)/shard_map/adjoint_low/pallas_call | solution.py:751
  47.5 0.0 collective-permute-done.15
  47.5 0.0 collective-permute-done.14
  47.5 0.6 %collective-permute-done.13 = f32[8,128]{1,0:T(8,128)S(1)} collective-permute-done((f32[8,128]{1,0:T(8,128)S(1)}, f32[8,128]{1,0:T(8,128)S(1)}, u32[]{:S(2)}, u32[]{:S(2)}) %collective-permute-start.13) | collective-permute-done | bytes 4128 | tf_op jit(solution)/shard_map/ppermute | solution.py:702
  48.1 2.0 %collective-permute-start.18 = (f32[8,128]{1,0:T(8,128)S(1)}, f32[8,128]{1,0:T(8,128)S(1)}, u32[]{:S(2)}, u32[]{:S(2)}) collective-permute-start(f32[8,128]{1,0:T(8,128)S(1)} %maximum_maximum_fusion.1), channel_id=1, source_target_pairs={{0,24},{8,16},{16,8},{24,0},{1,25},{9,17},{17,9},{25,1},{2,26},{10... | collective-permute-start | bytes 12296 | tf_op jit(solution)/shard_map/ppermute | solution.py:702
  50.1 0.0 collective-permute-start.17
  50.1 2.4 %collective-permute-start.16 = (f32[8,128]{1,0:T(8,128)S(1)}, f32[8,128]{1,0:T(8,128)S(1)}, u32[]{:S(2)}, u32[]{:S(2)}) collective-permute-start(f32[8,128]{1,0:T(8,128)S(1)} %maximum_maximum_fusion.1), channel_id=1, source_target_pairs={{0,8},{8,0},{16,24},{24,16},{1,9},{9,1},{17,25},{25,17},{2,10},{10... | collective-permute-start | bytes 12296 | tf_op jit(solution)/shard_map/ppermute | solution.py:702
  52.5 1.7 %adjoint_high.1 = f32[27,32,1024]{2,1,0:T(8,128)} custom-call(f32[12968,128]{1,0:T(8,128)S(1)} %get-tuple-element.79.buf, f32[1280,128]{1,0:T(8,128)S(1)} %get-tuple-element.80.fields, f32[27,32,1024]{2,1,0:T(8,128)} %get-tuple-element.82._), custom_call_target="tpu_custom_call", output_to_operand_aliasing={{}: (2, {})} | custom-call | bytes 6291456 | tf_op jit(solution)/shard_map/adjoint_high/pallas_call | solution.py:751
  54.2 0.0 collective-permute-done.18
  54.2 0.4 collective-permute-done.17
  54.6 0.0 collective-permute-done.16
  54.6 0.8 %normalize.1 = f32[32,1024]{1,0:T(8,128)} custom-call(f32[256,128]{1,0:T(8,128)S(1)} %get-tuple-element.83.total, f32[8,128]{1,0:T(8,128)S(1)} %maximum_maximum_fusion.peak), custom_call_target="tpu_custom_call" | custom-call | tf_op jit(solution)/shard_map/normalize/pallas_call | solution.py:751
  (3 shorter events, 0.0 us)
Async XLA Ops:
  3.9 9.1 %collective-permute-start = (f32[480,128]{1,0:T(8,128)S(1)}, f32[480,128]{1,0:T(8,128)S(1)}, u32[]{:S(2)}, u32[]{:S(2)}) collective-permute-start(f32[480,128]{1,0:T(8,128)S(1)} %get-tuple-element.48), channel_id=1, source_target_pairs={{1,2},{2,1},{3,4},{4,3},{5,6},{6,5},{7,0},{0,7},{9,10},{10,9},{11,... | collective-permute-start | bytes 737288 | tf_op jit(solution)/shard_map/ppermute | solution.py:691
  7.3 5.7 %collective-permute-start.1 = (f32[480,128]{1,0:T(8,128)S(1)}, f32[480,128]{1,0:T(8,128)S(1)}, u32[]{:S(2)}, u32[]{:S(2)}) collective-permute-start(f32[480,128]{1,0:T(8,128)S(1)} %get-tuple-element.49), channel_id=1, source_target_pairs={{0,1},{1,0},{2,3},{3,2},{4,5},{5,4},{6,7},{7,6},{8,9},{9,8},{10,11... | collective-permute-start | bytes 737288 | tf_op jit(solution)/shard_map/ppermute | solution.py:690
  7.3 11.4 %collective-permute-start.2 = (f32[240,128]{1,0:T(8,128)S(1)}, f32[240,128]{1,0:T(8,128)S(1)}, u32[]{:S(2)}, u32[]{:S(2)}) collective-permute-start(f32[240,128]{1,0:T(8,128)S(1)} %get-tuple-element.53), channel_id=1, source_target_pairs={{8,16},{16,8},{24,0},{0,24},{9,17},{17,9},{25,1},{1,25},{10,18},{1... | collective-permute-start | bytes 368648 | tf_op jit(solution)/shard_map/ppermute | solution.py:691
  10.9 7.8 %collective-permute-start.3 = (f32[240,128]{1,0:T(8,128)S(1)}, f32[240,128]{1,0:T(8,128)S(1)}, u32[]{:S(2)}, u32[]{:S(2)}) collective-permute-start(f32[240,128]{1,0:T(8,128)S(1)} %get-tuple-element.54), channel_id=1, source_target_pairs={{0,8},{8,0},{16,24},{24,16},{1,9},{9,1},{17,25},{25,17},{2,10},{10... | collective-permute-start | bytes 368648 | tf_op jit(solution)/shard_map/ppermute | solution.py:690
  13.1 7.2 %collective-permute-start.4 = (f32[32,128]{1,0:T(8,128)S(1)}, f32[32,128]{1,0:T(8,128)S(1)}, u32[]{:S(2)}, u32[]{:S(2)}) collective-permute-start(f32[32,128]{1,0:T(8,128)S(1)} %get-tuple-element.58), channel_id=1, source_target_pairs={{0,8},{8,0},{16,24},{24,16},{1,9},{9,1},{17,25},{25,17},{2,10},{10... | collective-permute-start | bytes 49160 | tf_op jit(solution)/shard_map/ppermute | solution.py:690
  16.2 5.5 %collective-permute-start.5 = (f32[32,128]{1,0:T(8,128)S(1)}, f32[32,128]{1,0:T(8,128)S(1)}, u32[]{:S(2)}, u32[]{:S(2)}) collective-permute-start(f32[32,128]{1,0:T(8,128)S(1)} %get-tuple-element.59), channel_id=1, source_target_pairs={{8,16},{16,8},{24,0},{0,24},{9,17},{17,9},{25,1},{1,25},{10,18},{1... | collective-permute-start | bytes 49160 | tf_op jit(solution)/shard_map/ppermute | solution.py:691
  18.7 3.1 %copy-start = (f32[27,32,1024]{2,1,0:T(8,128)S(1)}, f32[27,32,1024]{2,1,0:T(8,128)}, u32[]{:S(2)}) copy-start(f32[27,32,1024]{2,1,0:T(8,128)} %refs_1_.3) | copy-start | bytes 10616836
  24.2 8.1 %collective-permute-start.6 = (f32[448,128]{1,0:T(8,128)S(1)}, f32[448,128]{1,0:T(8,128)S(1)}, u32[]{:S(2)}, u32[]{:S(2)}) collective-permute-start(f32[448,128]{1,0:T(8,128)S(1)} %get-tuple-element.66), channel_id=1, source_target_pairs={{1,2},{2,1},{3,4},{4,3},{5,6},{6,5},{7,0},{0,7},{9,10},{10,9},{11,... | collective-permute-start | bytes 688136 | tf_op jit(solution)/shard_map/ppermute | solution.py:691
  24.3 8.1 %collective-permute-start.7 = (f32[448,128]{1,0:T(8,128)S(1)}, f32[448,128]{1,0:T(8,128)S(1)}, u32[]{:S(2)}, u32[]{:S(2)}) collective-permute-start(f32[448,128]{1,0:T(8,128)S(1)} %get-tuple-element.67), channel_id=1, source_target_pairs={{0,1},{1,0},{2,3},{3,2},{4,5},{5,4},{6,7},{7,6},{8,9},{9,8},{10,11... | collective-permute-start | bytes 688136 | tf_op jit(solution)/shard_map/ppermute | solution.py:690
  24.4 10.7 %collective-permute-start.8 = (f32[216,128]{1,0:T(8,128)S(1)}, f32[216,128]{1,0:T(8,128)S(1)}, u32[]{:S(2)}, u32[]{:S(2)}) collective-permute-start(f32[216,128]{1,0:T(8,128)S(1)} %get-tuple-element.71), channel_id=1, source_target_pairs={{8,16},{16,8},{24,0},{0,24},{9,17},{17,9},{25,1},{1,25},{10,18},{1... | collective-permute-start | bytes 331784 | tf_op jit(solution)/shard_map/ppermute | solution.py:691
  26.9 8.2 %collective-permute-start.9 = (f32[216,128]{1,0:T(8,128)S(1)}, f32[216,128]{1,0:T(8,128)S(1)}, u32[]{:S(2)}, u32[]{:S(2)}) collective-permute-start(f32[216,128]{1,0:T(8,128)S(1)} %get-tuple-element.72), channel_id=1, source_target_pairs={{0,8},{8,0},{16,24},{24,16},{1,9},{9,1},{17,25},{25,17},{2,10},{10... | collective-permute-start | bytes 331784 | tf_op jit(solution)/shard_map/ppermute | solution.py:690
  32.5 4.2 %collective-permute-start.10 = (f32[32,128]{1,0:T(8,128)S(1)}, f32[32,128]{1,0:T(8,128)S(1)}, u32[]{:S(2)}, u32[]{:S(2)}) collective-permute-start(f32[32,128]{1,0:T(8,128)S(1)} %get-tuple-element.77), channel_id=1, source_target_pairs={{0,8},{8,0},{16,24},{24,16},{1,9},{9,1},{17,25},{25,17},{2,10},{10... | collective-permute-start | bytes 49160 | tf_op jit(solution)/shard_map/ppermute | solution.py:690
  32.6 5.6 %collective-permute-start.11 = (f32[32,128]{1,0:T(8,128)S(1)}, f32[32,128]{1,0:T(8,128)S(1)}, u32[]{:S(2)}, u32[]{:S(2)}) collective-permute-start(f32[32,128]{1,0:T(8,128)S(1)} %get-tuple-element.78), channel_id=1, source_target_pairs={{8,16},{16,8},{24,0},{0,24},{9,17},{17,9},{25,1},{1,25},{10,18},{1... | collective-permute-start | bytes 49160 | tf_op jit(solution)/shard_map/ppermute | solution.py:691
  41.1 1.2 %collective-permute-start.12 = (f32[8,128]{1,0:T(8,128)S(1)}, f32[8,128]{1,0:T(8,128)S(1)}, u32[]{:S(2)}, u32[]{:S(2)}) collective-permute-start(f32[8,128]{1,0:T(8,128)S(1)} %get-tuple-element.81), channel_id=1, source_target_pairs={{0,1},{1,0},{2,3},{3,2},{4,5},{5,4},{6,7},{7,6},{8,9},{9,8},{10,11... | collective-permute-start | bytes 12296 | tf_op jit(solution)/shard_map/ppermute | solution.py:702
  42.4 5.2 %collective-permute-start.15 = (f32[8,128]{1,0:T(8,128)S(1)}, f32[8,128]{1,0:T(8,128)S(1)}, u32[]{:S(2)}, u32[]{:S(2)}) collective-permute-start(f32[8,128]{1,0:T(8,128)S(1)} %max.21.near), channel_id=1, source_target_pairs={{0,6},{1,7},{2,4},{3,5},{4,2},{5,3},{6,0},{7,1},{8,14},{9,15},{10,... | collective-permute-start | bytes 12296 | tf_op jit(solution)/shard_map/ppermute | solution.py:702
  43.8 3.7 %collective-permute-start.14 = (f32[8,128]{1,0:T(8,128)S(1)}, f32[8,128]{1,0:T(8,128)S(1)}, u32[]{:S(2)}, u32[]{:S(2)}) collective-permute-start(f32[8,128]{1,0:T(8,128)S(1)} %max.21.near), channel_id=1, source_target_pairs={{0,4},{1,5},{2,6},{3,7},{4,0},{5,1},{6,2},{7,3},{8,12},{9,13},{10,... | collective-permute-start | bytes 12296 | tf_op jit(solution)/shard_map/ppermute | solution.py:702
  44.5 3.6 %collective-permute-start.13 = (f32[8,128]{1,0:T(8,128)S(1)}, f32[8,128]{1,0:T(8,128)S(1)}, u32[]{:S(2)}, u32[]{:S(2)}) collective-permute-start(f32[8,128]{1,0:T(8,128)S(1)} %max.21.near), channel_id=1, source_target_pairs={{0,2},{1,3},{2,0},{3,1},{4,6},{5,7},{6,4},{7,5},{8,10},{9,11},{10,... | collective-permute-start | bytes 12296 | tf_op jit(solution)/shard_map/ppermute | solution.py:702
  48.1 6.1 %collective-permute-start.18 = (f32[8,128]{1,0:T(8,128)S(1)}, f32[8,128]{1,0:T(8,128)S(1)}, u32[]{:S(2)}, u32[]{:S(2)}) collective-permute-start(f32[8,128]{1,0:T(8,128)S(1)} %maximum_maximum_fusion.1), channel_id=1, source_target_pairs={{0,24},{8,16},{16,8},{24,0},{1,25},{9,17},{17,9},{25,1},{2,26},{10... | collective-permute-start | bytes 12296 | tf_op jit(solution)/shard_map/ppermute | solution.py:702
  50.1 4.5 %collective-permute-start.17 = (f32[8,128]{1,0:T(8,128)S(1)}, f32[8,128]{1,0:T(8,128)S(1)}, u32[]{:S(2)}, u32[]{:S(2)}) collective-permute-start(f32[8,128]{1,0:T(8,128)S(1)} %maximum_maximum_fusion.1), channel_id=1, source_target_pairs={{0,16},{8,24},{16,0},{24,8},{1,17},{9,25},{17,1},{25,9},{2,18},{10... | collective-permute-start | bytes 12296 | tf_op jit(solution)/shard_map/ppermute | solution.py:702
  50.1 4.5 %collective-permute-start.16 = (f32[8,128]{1,0:T(8,128)S(1)}, f32[8,128]{1,0:T(8,128)S(1)}, u32[]{:S(2)}, u32[]{:S(2)}) collective-permute-start(f32[8,128]{1,0:T(8,128)S(1)} %maximum_maximum_fusion.1), channel_id=1, source_target_pairs={{0,8},{8,0},{16,24},{24,16},{1,9},{9,1},{17,25},{25,17},{2,10},{10... | collective-permute-start | bytes 12296 | tf_op jit(solution)/shard_map/ppermute | solution.py:702

commit v3 on v2

--- a/solution.py
+++ b/solution.py
@@ -390,7 +390,9 @@
         act(k)
         return carry
 
-    lax.fori_loop(first, last + 1, step, 0, unroll=2 - (last + 1 - first) % 2)
+    count = last + 1 - first
+    unroll = max(n for n in (1, 2, 3, 4) if count % n == 0)
+    lax.fori_loop(first, last + 1, step, 0, unroll=unroll)
 
 
 def side_panels(g, act, count):
@@ -410,6 +412,20 @@
     for pieces in g.inner:
         side_panels(g, functools.partial(act, pieces=pieces), 3)
     every(2, g.cols - 1, functools.partial(act, pieces=g.outer))
+
+
+def core_tiles(g, act):
+    for pieces in g.inner:
+        every(3, g.cols - 2, functools.partial(act, pieces=pieces))
+
+
+def near_core_tiles(g, act):
+    def step(n, carry):
+        for pieces in g.inner:
+            act(jnp.where(n == 0, 2, g.cols - 1), pieces=pieces)
+        return carry
+
+    lax.fori_loop(0, 2, step, 0, unroll=2)
 
 
 def rim_tiles(g, act):
@@ -530,9 +546,13 @@
     )
     porosity, solid, labels = near
 
-    def copy(k):
-        return pltpu.make_async_copy(block_of(pops, k), stage.at[k - 1], sems.at[k - 1])
-
+    def copy(k, r, n):
+        rows = pl.ds(r, n)
+        source = pops.at[:, rows, lanes_of(k)]
+        part = 0 if r == 0 else 2 if r + n == g.rows else 1
+        return pltpu.make_async_copy(source, stage.at[k - 1, :, rows], sems.at[k - 1, part])
+
+    middle = (8, g.rows - 16)
     flat_copies = [
         pltpu.make_async_copy(source, target, flat_sems.at[n])
         for n, (source, target) in enumerate(zip(flat, near))
@@ -540,7 +560,10 @@
     for each in flat_copies:
         each.start()
     for k in range(1, g.cols + 1):
-        copy(k).start()
+        for piece in g.outer:
+            copy(k, *piece).start()
+    for k in (1, g.cols, *range(2, g.cols)):
+        copy(k, *middle).start()
     for each in flat_copies:
         each.wait()
 
@@ -560,13 +583,18 @@
         collide(k, pieces, [read_rows(stage.at[k - 1, i], 0, pieces) for i in range(27)])
 
     def column(k):
-        copy(k).wait()
+        for piece in g.outer:
+            copy(k, *piece).wait()
         act(k, g.outer)
 
     every(1, g.cols, column)
+    for k in (1, g.cols):
+        copy(k, *middle).wait()
     for pieces in g.inner:
         side_panels(g, functools.partial(act, pieces=pieces), 2)
     pack_faces(g, out, 1, 30, *faces)
+    for k in range(2, g.cols):
+        copy(k, *middle).wait()
 
 
 def inner_first_kernel(g, _, _state, stage, post, state0, out, state1):
@@ -586,13 +614,14 @@
     by_parity("gx", first, second, functools.partial(pack_corners, g, buf, sign, fields))
 
 
-def middle_second_kernel(g, post, out, state1, x_second, x_first):
+def middle_second_kernel(g, adjoint, post, out, state1, stage, field, x_second, x_first):
     masks = lane_masks(16)
     by_parity("gx", x_second, x_first, functools.partial(unpack_x, g, post, 1, 30))
     middle_tiles(g, step_tile(g, post, out, 1, 30, masks, collide_second(g, state1)))
-
-
-def rim_seed_kernel(g, _post, _out, _state, first, second, adjoint, *refs):
+    core_tiles(g, seed_tile(g, out, adjoint, stage, field, masks))
+
+
+def rim_seed_kernel(g, _post, _out, _state, _stage, _field, first, second, adjoint, *refs):
     post, out, state1, stage, field, *faces = refs
     masks = lane_masks(16)
     by_parity("gx", second, first, functools.partial(unpack_corners, g, post, 1, 30))
@@ -613,29 +642,13 @@
     copy(g.cols).start()
     seed = seed_tile(g, post, adjoint, stage, field, masks)
 
-    def column(k):
-        for pieces in g.inner:
-            seed(k, pieces)
-        copy(k).start()
-
-    every(2, g.cols - 1, column)
+    near_core_tiles(g, seed)
+    every(2, g.cols - 1, lambda k: copy(k).start())
     interior_tiles(g, step_tile(g, field, out, -1, 27, masks, adjoint_second(g, state1, total)))
     every(1, g.cols, lambda k: copy(k).wait())
 
 
-def middle_adjoint_kernel(g, field, out, total, state1, x_second, x_first):
-    masks = lane_masks(16)
-    by_parity("gx", x_second, x_first, functools.partial(unpack_x, g, field, -1, 27))
-    middle_tiles(g, step_tile(g, field, out, -1, 27, masks, adjoint_second(g, state1, total)))
-
-
-def total_kernel(g, _field, out, before, state1, state0, first, second, *refs):
-    field, out, before, total, peak, parts = refs
-    masks = lane_masks(16)
-    by_parity("gx", second, first, functools.partial(unpack_corners, g, field, -1, 27))
-    corner_tiles(g, field, out, -1, 27, masks, adjoint_second(g, state1, before))
-    peak[...] = jnp.zeros((8, LANES), F32)
-
+def total_tile(g, out, before, state0, total, parts, masks):
     def act(k, pieces):
         p = pull_block(g, out, -1, k, pieces, masks)
         spot = spot_of(g, k)
@@ -644,11 +657,31 @@
         here = load_fields(before, g.extended, spot, pieces, 1)[0] + porous
         save_fields(total, g.local, spot, pieces, [here])
         save_fields(parts, g.local, spot, pieces, spread + [wall])
-        largest = jnp.maximum(jnp.abs(here[:8]), jnp.abs(here[8:]))
-        peak[...] = jnp.maximum(peak[...], largest)
-
-    for pieces in (g.outer,) + g.inner:
-        every(1, g.cols, functools.partial(act, pieces=pieces))
+
+    return act
+
+
+def middle_adjoint_kernel(g, field, out, before, total, parts, state1, state0, x_second, x_first):
+    masks = lane_masks(16)
+    by_parity("gx", x_second, x_first, functools.partial(unpack_x, g, field, -1, 27))
+    middle_tiles(g, step_tile(g, field, out, -1, 27, masks, adjoint_second(g, state1, before)))
+    core_tiles(g, total_tile(g, out, before, state0, total, parts, masks))
+
+
+def total_kernel(g, *refs):
+    state1, state0, first, second, field, out, before, total, parts, peak = refs[5:]
+    masks = lane_masks(16)
+    by_parity("gx", second, first, functools.partial(unpack_corners, g, field, -1, 27))
+    corner_tiles(g, field, out, -1, 27, masks, adjoint_second(g, state1, before))
+    act = total_tile(g, out, before, state0, total, parts, masks)
+    near_core_tiles(g, act)
+    rim_tiles(g, act)
+    size = 8 * (g.local // 64)
+    largest = jnp.zeros((8, LANES), F32)
+    for start in range(0, g.local, size):
+        value = jnp.abs(total[start : start + size, :]).reshape(-1, 8, LANES)
+        largest = jnp.maximum(largest, jnp.max(value, 0))
+    peak[...] = largest
 
 
 def adjoint_kernel(g, first, last, buf, parts, result, stage, sems):
@@ -781,7 +814,7 @@
         [padded(30), fields(7, g.local), stage] + faces(30, 1),
         [vmem(*porosity.shape)]
         + [pltpu.VMEM(porosity.shape, jnp.int32)] * 2
-        + [sems, pltpu.SemaphoreType.DMA((3,))],
+        + [pltpu.SemaphoreType.DMA((g.cols, 3)), pltpu.SemaphoreType.DMA((3,))],
     )
     along_x, along_y = swap_faces(parcels)
     post, state0, second, state1 = call(
@@ -793,23 +826,25 @@
         load=FLIGHT,
     )
     post, parcels = relay(post, along_y, 1, 30)
-    post, second, state1 = call(
+    post, second, state1, staged, field = call(
         "middle_second",
-        lambda grid, _post, _out, _state, b, a, *refs: middle_second_kernel(grid, *refs, b, a),
-        [post, second, state1, *along_x],
-        [],
+        lambda grid, _post, _out, _state, b, a, source, *refs: middle_second_kernel(
+            grid, source, *refs, b, a
+        ),
+        [post, second, state1, *along_x, adjoint_in],
+        [stage, padded(27)],
         kept=3,
         load=FLIGHT,
     )
     _, second, state1, staged, field, *parcels = call(
         "rim_seed",
         rim_seed_kernel,
-        [post, second, state1, *parcels, adjoint_in],
-        [stage, padded(27)] + faces(27, -1),
-        kept=3,
+        [post, second, state1, staged, field, *parcels, adjoint_in],
+        faces(27, -1),
+        kept=5,
     )
     along_x, along_y = swap_faces(parcels)
-    _, field, pulled, total, final = call(
+    _, field, pulled, before, final = call(
         "inner_seed",
         lambda grid, kept, into, buf, *refs: inner_seed_kernel(grid, buf, kept, into, *refs),
         [staged, field, second, state1, adjoint_in],
@@ -819,22 +854,22 @@
         load=FLIGHT,
     )
     field, parcels = relay(field, along_y, -1, 27)
-    field, pulled, total = call(
+    field, pulled, before, total, parts = call(
         "middle_adjoint",
-        lambda grid, _field, _out, _total, state, b, a, *refs: middle_adjoint_kernel(
-            grid, *refs, state, b, a
+        lambda grid, _field, _out, _before, near, far, b, a, *refs: middle_adjoint_kernel(
+            grid, *refs, near, far, b, a
         ),
-        [field, pulled, total, state1, *along_x],
-        [],
+        [field, pulled, before, state1, state0, *along_x],
+        [fields(1, g.local), fields(5, g.local)],
         kept=3,
         load=FLIGHT,
     )
-    _, pulled, _, total, peak, parts = call(
+    _, pulled, _, total, parts, peak = call(
         "total",
         total_kernel,
-        [field, pulled, total, state1, state0, *parcels],
-        [fields(1, g.local), vmem(8, LANES), fields(5, g.local)],
-        kept=3,
+        [field, pulled, before, total, parts, state1, state0, *parcels],
+        [vmem(8, LANES)],
+        kept=5,
     )
     half = g.cols // 2
     scratch = [vmem(half, 27, rows, LANES), pltpu.SemaphoreType.DMA((half,))]

time: 55.6 us -> 54.3 us (0.977)
  Pallas kernels: 19.7 us -> 18.8 us
    pallas_call x12, Pallas kernels: 19.7 us -> 18.8 us  [call(): pl.pallas_call(functools.partial(kernel, g), in_specs=in_specs, out_shape...]
  transfers between devices with their start and end apart: 19 -> 19, of which waited for: 7 -> 7; matrix products, arithmetic and copies ran while one was open for 0% -> 0% of each run, Pallas kernels for 18% -> 20%
where the time goes in v3:
time: 54.3 us; the launch traced here: 54.1 us
  starting transfers between devices  25.8 us (48%)
  Pallas kernels  18.8 us (35%)
  waiting for transfers between devices  8.68 us (16%)
  between operations  0.81 us (1%)
    pallas_call x12, Pallas kernels, call(): pl.pallas_call(functools.partial(kernel, g), in_specs=in_specs, out_shape...  18.8 us
    ppermute x6, starting transfers between devices, swap(): lax.ppermute(second, axis, swap_pairs(count, 1))  14.6 us
    ppermute x7, starting transfers between devices, largest_of_all(): lax.ppermute(peak, axis, [(i, i ^ n * step) for i in range(count)])  7.95 us
    ppermute x6, waiting for transfers between devices, swap(): lax.ppermute(second, axis, swap_pairs(count, 1))  6.44 us
    ppermute x6, starting transfers between devices, swap(): lax.ppermute(first, axis, swap_pairs(count, 0))  3.26 us
    ppermute x7, waiting for transfers between devices, largest_of_all(): lax.ppermute(peak, axis, [(i, i ^ n * step) for i in range(count)])  2.23 us
  transfers between devices with their start and end apart: 19, of which 7 were waited for; matrix products, arithmetic and copies ran while one was open for 0% of the time, Pallas kernels for 20%

profile of v3, /device:TPU:0, one launch (start us, length us, event | category | flops | bytes accessed | tf_op | source)
XLA Modules:
  0.0 54.1 jit_solution(18203855875025220845)
XLA Ops:
  0.6 3.1 %rim_first.1 = (f32[14408,128]{1,0:T(8,128)S(1)}, f32[1792,128]{1,0:T(8,128)S(1)}, f32[8,27,32,128]{3,2,1,0:T(8,128)S(1)}, f32[240,128]{1,0:T(8,128)S(1)}, f32[2...) custom-call(f32[27,32,1024]{2,1,0:T(8,128)} %pops.1, f32[32,1024]{1,0:T(8,128)} %refs_0_.1, ...), custom_call_target="tpu_custom_call" | custom-call | tf_op jit(solution)/shard_map/rim_first/pallas_call | solution.py:784
  3.7 3.4 %collective-permute-start = (f32[480,128]{1,0:T(8,128)S(1)}, f32[480,128]{1,0:T(8,128)S(1)}, u32[]{:S(2)}, u32[]{:S(2)}) collective-permute-start(f32[480,128]{1,0:T(8,128)S(1)} %get-tuple-element.52), channel_id=1, source_target_pairs={{1,2},{2,1},{3,4},{4,3},{5,6},{6,5},{7,0},{0,7},{9,10},{10,9},{11,... | collective-permute-start | bytes 737288 | tf_op jit(solution)/shard_map/ppermute | solution.py:724
  7.1 0.0 collective-permute-start.1
  7.1 3.6 %collective-permute-start.2 = (f32[240,128]{1,0:T(8,128)S(1)}, f32[240,128]{1,0:T(8,128)S(1)}, u32[]{:S(2)}, u32[]{:S(2)}) collective-permute-start(f32[240,128]{1,0:T(8,128)S(1)} %get-tuple-element.57), channel_id=1, source_target_pairs={{8,16},{16,8},{24,0},{0,24},{9,17},{17,9},{25,1},{1,25},{10,18},{1... | collective-permute-start | bytes 368648 | tf_op jit(solution)/shard_map/ppermute | solution.py:724
  10.7 0.0 collective-permute-start.3
  10.7 1.4 %inner_first.1 = (f32[14408,128]{1,0:T(8,128)S(1)}, f32[1792,128]{1,0:T(8,128)S(1)}, f32[12968,128]{1,0:T(8,128)S(1)}, f32[2184,128]{1,0:T(8,128)S(1)}) custom-call(f32[14408,128]{1,0:T(8,128)S(1)} %get-tuple-element.48._, f32[1792,128]{1,0:T(8,128)S(1)} %get-tuple-element.49._state, ...), custom_call_target="tpu_custom_call", output_to_operand_aliasing={{0}: (0, {}), {1}: (1, {})} | custom-call | bytes 12582912 | tf_op jit(solution)/shard_map/inner_first/pallas_call | solution.py:784
  12.1 0.0 copy-start
  12.1 0.7 %collective-permute-done.refs_1_ = f32[480,128]{1,0:T(8,128)S(1)} collective-permute-done((f32[480,128]{1,0:T(8,128)S(1)}, f32[480,128]{1,0:T(8,128)S(1)}, u32[]{:S(2)}, u32[]{:S(2)}) %collective-permute-start) | collective-permute-done | bytes 245792 | tf_op jit(solution)/shard_map/ppermute | solution.py:724
  12.8 0.0 collective-permute-done.1.refs_2_
  12.8 0.1 relay.2
  12.9 3.1 %collective-permute-start.4 = (f32[32,128]{1,0:T(8,128)S(1)}, f32[32,128]{1,0:T(8,128)S(1)}, u32[]{:S(2)}, u32[]{:S(2)}) collective-permute-start(f32[32,128]{1,0:T(8,128)S(1)} %get-tuple-element.64), channel_id=1, source_target_pairs={{0,8},{8,0},{16,24},{24,16},{1,9},{9,1},{17,25},{25,17},{2,10},{10... | collective-permute-start | bytes 49160 | tf_op jit(solution)/shard_map/ppermute | solution.py:723
  16.1 2.5 %collective-permute-start.5 = (f32[32,128]{1,0:T(8,128)S(1)}, f32[32,128]{1,0:T(8,128)S(1)}, u32[]{:S(2)}, u32[]{:S(2)}) collective-permute-start(f32[32,128]{1,0:T(8,128)S(1)} %get-tuple-element.65), channel_id=1, source_target_pairs={{8,16},{16,8},{24,0},{0,24},{9,17},{17,9},{25,1},{1,25},{10,18},{1... | collective-permute-start | bytes 49160 | tf_op jit(solution)/shard_map/ppermute | solution.py:724
  18.5 0.0 collective-permute-done.2.b
  18.5 0.0 collective-permute-done.3.a
  18.5 0.0 copy-done
  18.5 2.0 %middle_second.1 = (f32[14408,128]{1,0:T(8,128)S(1)}, f32[12968,128]{1,0:T(8,128)S(1)}, f32[2184,128]{1,0:T(8,128)S(1)}, f32[8,27,32,128]{3,2,1,0:T(8,128)S(1)}, f32[12968,128]{1,0:T(8,128)S(1)}) custom-call(f32[14408,128]{1,0:T(8,128)S(1)} %get-tuple-element.54._post, ...), custom_call_target="tpu_custom_call", output_to_operand_aliasing={{0}: (0, {}), {1}: (1, {}), {2}: (2, {})} | custom-call | bytes 12582912 | tf_op jit(solution)/shard_map/middle_second/pallas_call | solution.py:784
  20.5 0.0 collective-permute-done.4.first
  20.5 1.1 %collective-permute-done.5.second = f32[32,128]{1,0:T(8,128)S(1)} collective-permute-done((f32[32,128]{1,0:T(8,128)S(1)}, f32[32,128]{1,0:T(8,128)S(1)}, u32[]{:S(2)}, u32[]{:S(2)}) %collective-permute-start.5) | collective-permute-done | bytes 16416 | tf_op jit(solution)/shard_map/ppermute | solution.py:724
  21.6 2.3 %rim_seed.1 = (f32[14408,128]{1,0:T(8,128)S(1)}, f32[12968,128]{1,0:T(8,128)S(1)}, f32[2184,128]{1,0:T(8,128)S(1)}, f32[8,27,32,128]{3,2,1,0:T(8,128)S(1)}, f32[...) custom-call(f32[14408,128]{1,0:T(8,128)S(1)} %get-tuple-element.59._, ...), custom_call_target="tpu_custom_call", output_to_operand_aliasing={{0}: (0, {}), {1}: (1, {}), {2}: (2, {}), {3}: (3, {}), {4}... | custom-call | tf_op jit(solution)/shard_map/rim_seed/pallas_call | solution.py:784
  23.9 0.1 collective-permute-start.6
  23.9 0.1 collective-permute-start.7
  24.0 2.5 %collective-permute-start.8 = (f32[216,128]{1,0:T(8,128)S(1)}, f32[216,128]{1,0:T(8,128)S(1)}, u32[]{:S(2)}, u32[]{:S(2)}) collective-permute-start(f32[216,128]{1,0:T(8,128)S(1)} %get-tuple-element.78), channel_id=1, source_target_pairs={{8,16},{16,8},{24,0},{0,24},{9,17},{17,9},{25,1},{1,25},{10,18},{1... | collective-permute-start | bytes 331784 | tf_op jit(solution)/shard_map/ppermute | solution.py:724
  26.6 0.0 collective-permute-start.9
  26.6 1.9 %inner_seed.1 = (f32[8,27,32,128]{3,2,1,0:T(8,128)S(1)}, f32[12968,128]{1,0:T(8,128)S(1)}, f32[12968,128]{1,0:T(8,128)S(1)}, f32[312,128]{1,0:T(8,128)S(1)}, f32[27,32,1024]{2,1,0:T(8,128)}) custom-call(f32[8,27,32,128]{3,2,1,0:T(8,128)S(1)} %get-tuple-element.66.kept, ...), custom_call_target="tpu_custom_call", output_to_operand_aliasing={{0}: (0, {}), {1}: (1, {})} | custom-call | bytes 12582912 | tf_op jit(solution)/shard_map/inner_seed/pallas_call | solution.py:784
  28.4 3.6 %collective-permute-done.6.refs_1_ = f32[448,128]{1,0:T(8,128)S(1)} collective-permute-done((f32[448,128]{1,0:T(8,128)S(1)}, f32[448,128]{1,0:T(8,128)S(1)}, u32[]{:S(2)}, u32[]{:S(2)}) %collective-permute-start.6) | collective-permute-done | bytes 229408 | tf_op jit(solution)/shard_map/ppermute | solution.py:724
  32.0 0.0 collective-permute-done.7.refs_2_
  32.0 0.1 relay.3
  32.1 0.1 collective-permute-start.10
  32.2 2.5 %collective-permute-start.11 = (f32[32,128]{1,0:T(8,128)S(1)}, f32[32,128]{1,0:T(8,128)S(1)}, u32[]{:S(2)}, u32[]{:S(2)}) collective-permute-start(f32[32,128]{1,0:T(8,128)S(1)} %get-tuple-element.86), channel_id=1, source_target_pairs={{8,16},{16,8},{24,0},{0,24},{9,17},{17,9},{25,1},{1,25},{10,18},{1... | collective-permute-start | bytes 49160 | tf_op jit(solution)/shard_map/ppermute | solution.py:724
  34.8 0.0 collective-permute-done.8.b
  34.8 0.0 collective-permute-done.9.a
  34.8 1.9 %middle_adjoint.1 = (f32[12968,128]{1,0:T(8,128)S(1)}, f32[12968,128]{1,0:T(8,128)S(1)}, f32[312,128]{1,0:T(8,128)S(1)}, f32[256,128]{1,0:T(8,128)S(1)}, f32[1280,128]{1,0:T(8,128)S(1)}) custom-call(f32[12968,128]{1,0:T(8,128)S(1)} %get-tuple-element.74._field, ...), custom_call_target="tpu_custom_call", output_to_operand_aliasing={{0}: (0, {}), {1}: (1, {}), {2}: (2, {})} | custom-call | bytes 12582912 | tf_op jit(solution)/shard_map/middle_adjoint/pallas_call | solution.py:784
  36.7 0.0 collective-permute-done.10.refs_7_
  36.7 1.1 %collective-permute-done.11.refs_8_ = f32[32,128]{1,0:T(8,128)S(1)} collective-permute-done((f32[32,128]{1,0:T(8,128)S(1)}, f32[32,128]{1,0:T(8,128)S(1)}, u32[]{:S(2)}, u32[]{:S(2)}) %collective-permute-start.11) | collective-permute-done | bytes 16416 | tf_op jit(solution)/shard_map/ppermute | solution.py:724
  37.8 2.1 %total.1 = (f32[12968,128]{1,0:T(8,128)S(1)}, f32[12968,128]{1,0:T(8,128)S(1)}, f32[312,128]{1,0:T(8,128)S(1)}, f32[256,128]{1,0:T(8,128)S(1)}, f32[1280,128]{1,0:T(8,128)S(1)}, /*index=5*/f32[8,128]{1,0:T(8,128)S(1)}) custom-call(f32[12968,128]{1,0:T(8,128)S(1)} %get-tuple-element.80.r, ...), custom_call_target="tpu_custom_call", output_to_operand_aliasing={{0}: (0, {}), {1}: (1, {}), {2}: (2, {}), {3}: (3, {}), {4}... | custom-call | tf_op jit(solution)/shard_map/total/pallas_call | solution.py:784
  39.9 0.1 collective-permute-start.12
  40.0 1.2 %collective-permute-done.12 = f32[8,128]{1,0:T(8,128)S(1)} collective-permute-done((f32[8,128]{1,0:T(8,128)S(1)}, f32[8,128]{1,0:T(8,128)S(1)}, u32[]{:S(2)}, u32[]{:S(2)}) %collective-permute-start.12) | collective-permute-done | bytes 4128 | tf_op jit(solution)/shard_map/ppermute | solution.py:735
  41.1 1.3 %collective-permute-start.15 = (f32[8,128]{1,0:T(8,128)S(1)}, f32[8,128]{1,0:T(8,128)S(1)}, u32[]{:S(2)}, u32[]{:S(2)}) collective-permute-start(f32[8,128]{1,0:T(8,128)S(1)} %max.21.near), channel_id=1, source_target_pairs={{0,6},{1,7},{2,4},{3,5},{4,2},{5,3},{6,0},{7,1},{8,14},{9,15},{10,... | collective-permute-start | bytes 12296 | tf_op jit(solution)/shard_map/ppermute | solution.py:735
  42.4 0.7 %collective-permute-start.14 = (f32[8,128]{1,0:T(8,128)S(1)}, f32[8,128]{1,0:T(8,128)S(1)}, u32[]{:S(2)}, u32[]{:S(2)}) collective-permute-start(f32[8,128]{1,0:T(8,128)S(1)} %max.21.near), channel_id=1, source_target_pairs={{0,4},{1,5},{2,6},{3,7},{4,0},{5,1},{6,2},{7,3},{8,12},{9,13},{10,... | collective-permute-start | bytes 12296 | tf_op jit(solution)/shard_map/ppermute | solution.py:735
  43.2 1.5 %collective-permute-start.13 = (f32[8,128]{1,0:T(8,128)S(1)}, f32[8,128]{1,0:T(8,128)S(1)}, u32[]{:S(2)}, u32[]{:S(2)}) collective-permute-start(f32[8,128]{1,0:T(8,128)S(1)} %max.21.near), channel_id=1, source_target_pairs={{0,2},{1,3},{2,0},{3,1},{4,6},{5,7},{6,4},{7,5},{8,10},{9,11},{10,... | collective-permute-start | bytes 12296 | tf_op jit(solution)/shard_map/ppermute | solution.py:735
  44.6 1.6 %adjoint_low.1 = (f32[8,128]{1,0:T(8,128)S(1)}, f32[27,32,1024]{2,1,0:T(8,128)}) custom-call(f32[12968,128]{1,0:T(8,128)S(1)} %get-tuple-element.87.buf, f32[1280,128]{1,0:T(8,128)S(1)} %get-tuple-element.88.fields, f32[8,128]{1,0:T(8,128)S(1)} %max.21.near), custom_call_target="tpu_custom_call" | custom-call | bytes 6291456 | tf_op jit(solution)/shard_map/adjoint_low/pallas_call | solution.py:784
  46.2 0.0 collective-permute-done.15
  46.3 0.0 collective-permute-done.14
  46.3 0.5 collective-permute-done.13
  46.8 2.1 %collective-permute-start.18 = (f32[8,128]{1,0:T(8,128)S(1)}, f32[8,128]{1,0:T(8,128)S(1)}, u32[]{:S(2)}, u32[]{:S(2)}) collective-permute-start(f32[8,128]{1,0:T(8,128)S(1)} %maximum_maximum_fusion.1), channel_id=1, source_target_pairs={{0,24},{8,16},{16,8},{24,0},{1,25},{9,17},{17,9},{25,1},{2,26},{10... | collective-permute-start | bytes 12296 | tf_op jit(solution)/shard_map/ppermute | solution.py:735
  48.8 0.0 collective-permute-start.17
  48.8 2.3 %collective-permute-start.16 = (f32[8,128]{1,0:T(8,128)S(1)}, f32[8,128]{1,0:T(8,128)S(1)}, u32[]{:S(2)}, u32[]{:S(2)}) collective-permute-start(f32[8,128]{1,0:T(8,128)S(1)} %maximum_maximum_fusion.1), channel_id=1, source_target_pairs={{0,8},{8,0},{16,24},{24,16},{1,9},{9,1},{17,25},{25,17},{2,10},{10... | collective-permute-start | bytes 12296 | tf_op jit(solution)/shard_map/ppermute | solution.py:735
  51.2 1.6 %adjoint_high.1 = f32[27,32,1024]{2,1,0:T(8,128)} custom-call(f32[12968,128]{1,0:T(8,128)S(1)} %get-tuple-element.87.buf, f32[1280,128]{1,0:T(8,128)S(1)} %get-tuple-element.88.fields, f32[27,32,1024]{2,1,0:T(8,128)} %get-tuple-element.90._), custom_call_target="tpu_custom_call", output_to_operand_aliasing={{}: (2, {})} | custom-call | bytes 6291456 | tf_op jit(solution)/shard_map/adjoint_high/pallas_call | solution.py:784
  52.8 0.0 collective-permute-done.18
  52.8 0.6 %collective-permute-done.17 = f32[8,128]{1,0:T(8,128)S(1)} collective-permute-done((f32[8,128]{1,0:T(8,128)S(1)}, f32[8,128]{1,0:T(8,128)S(1)}, u32[]{:S(2)}, u32[]{:S(2)}) %collective-permute-start.17) | collective-permute-done | bytes 4128 | tf_op jit(solution)/shard_map/ppermute | solution.py:735
  53.3 0.0 collective-permute-done.16
  53.3 0.8 %normalize.1 = f32[32,1024]{1,0:T(8,128)} custom-call(f32[256,128]{1,0:T(8,128)S(1)} %get-tuple-element.91.total, f32[8,128]{1,0:T(8,128)S(1)} %maximum_maximum_fusion.peak), custom_call_target="tpu_custom_call" | custom-call | tf_op jit(solution)/shard_map/normalize/pallas_call | solution.py:784
  (3 shorter events, 0.0 us)
Async XLA Ops:
  3.7 9.1 %collective-permute-start = (f32[480,128]{1,0:T(8,128)S(1)}, f32[480,128]{1,0:T(8,128)S(1)}, u32[]{:S(2)}, u32[]{:S(2)}) collective-permute-start(f32[480,128]{1,0:T(8,128)S(1)} %get-tuple-element.52), channel_id=1, source_target_pairs={{1,2},{2,1},{3,4},{4,3},{5,6},{6,5},{7,0},{0,7},{9,10},{10,9},{11,... | collective-permute-start | bytes 737288 | tf_op jit(solution)/shard_map/ppermute | solution.py:724
  7.1 5.7 %collective-permute-start.1 = (f32[480,128]{1,0:T(8,128)S(1)}, f32[480,128]{1,0:T(8,128)S(1)}, u32[]{:S(2)}, u32[]{:S(2)}) collective-permute-start(f32[480,128]{1,0:T(8,128)S(1)} %get-tuple-element.53), channel_id=1, source_target_pairs={{0,1},{1,0},{2,3},{3,2},{4,5},{5,4},{6,7},{7,6},{8,9},{9,8},{10,11... | collective-permute-start | bytes 737288 | tf_op jit(solution)/shard_map/ppermute | solution.py:723
  7.1 11.4 %collective-permute-start.2 = (f32[240,128]{1,0:T(8,128)S(1)}, f32[240,128]{1,0:T(8,128)S(1)}, u32[]{:S(2)}, u32[]{:S(2)}) collective-permute-start(f32[240,128]{1,0:T(8,128)S(1)} %get-tuple-element.57), channel_id=1, source_target_pairs={{8,16},{16,8},{24,0},{0,24},{9,17},{17,9},{25,1},{1,25},{10,18},{1... | collective-permute-start | bytes 368648 | tf_op jit(solution)/shard_map/ppermute | solution.py:724
  10.7 7.8 %collective-permute-start.3 = (f32[240,128]{1,0:T(8,128)S(1)}, f32[240,128]{1,0:T(8,128)S(1)}, u32[]{:S(2)}, u32[]{:S(2)}) collective-permute-start(f32[240,128]{1,0:T(8,128)S(1)} %get-tuple-element.58), channel_id=1, source_target_pairs={{0,8},{8,0},{16,24},{24,16},{1,9},{9,1},{17,25},{25,17},{2,10},{10... | collective-permute-start | bytes 368648 | tf_op jit(solution)/shard_map/ppermute | solution.py:723
  12.1 6.4 %copy-start = (f32[27,32,1024]{2,1,0:T(8,128)S(1)}, f32[27,32,1024]{2,1,0:T(8,128)}, u32[]{:S(2)}) copy-start(f32[27,32,1024]{2,1,0:T(8,128)} %refs_1_.3) | copy-start | bytes 10616836
  12.9 7.6 %collective-permute-start.4 = (f32[32,128]{1,0:T(8,128)S(1)}, f32[32,128]{1,0:T(8,128)S(1)}, u32[]{:S(2)}, u32[]{:S(2)}) collective-permute-start(f32[32,128]{1,0:T(8,128)S(1)} %get-tuple-element.64), channel_id=1, source_target_pairs={{0,8},{8,0},{16,24},{24,16},{1,9},{9,1},{17,25},{25,17},{2,10},{10... | collective-permute-start | bytes 49160 | tf_op jit(solution)/shard_map/ppermute | solution.py:723
  16.1 5.5 %collective-permute-start.5 = (f32[32,128]{1,0:T(8,128)S(1)}, f32[32,128]{1,0:T(8,128)S(1)}, u32[]{:S(2)}, u32[]{:S(2)}) collective-permute-start(f32[32,128]{1,0:T(8,128)S(1)} %get-tuple-element.65), channel_id=1, source_target_pairs={{8,16},{16,8},{24,0},{0,24},{9,17},{17,9},{25,1},{1,25},{10,18},{1... | collective-permute-start | bytes 49160 | tf_op jit(solution)/shard_map/ppermute | solution.py:724
  23.9 8.1 %collective-permute-start.6 = (f32[448,128]{1,0:T(8,128)S(1)}, f32[448,128]{1,0:T(8,128)S(1)}, u32[]{:S(2)}, u32[]{:S(2)}) collective-permute-start(f32[448,128]{1,0:T(8,128)S(1)} %get-tuple-element.72), channel_id=1, source_target_pairs={{1,2},{2,1},{3,4},{4,3},{5,6},{6,5},{7,0},{0,7},{9,10},{10,9},{11,... | collective-permute-start | bytes 688136 | tf_op jit(solution)/shard_map/ppermute | solution.py:724
  23.9 8.1 %collective-permute-start.7 = (f32[448,128]{1,0:T(8,128)S(1)}, f32[448,128]{1,0:T(8,128)S(1)}, u32[]{:S(2)}, u32[]{:S(2)}) collective-permute-start(f32[448,128]{1,0:T(8,128)S(1)} %get-tuple-element.73), channel_id=1, source_target_pairs={{0,1},{1,0},{2,3},{3,2},{4,5},{5,4},{6,7},{7,6},{8,9},{9,8},{10,11... | collective-permute-start | bytes 688136 | tf_op jit(solution)/shard_map/ppermute | solution.py:723
  24.0 10.7 %collective-permute-start.8 = (f32[216,128]{1,0:T(8,128)S(1)}, f32[216,128]{1,0:T(8,128)S(1)}, u32[]{:S(2)}, u32[]{:S(2)}) collective-permute-start(f32[216,128]{1,0:T(8,128)S(1)} %get-tuple-element.78), channel_id=1, source_target_pairs={{8,16},{16,8},{24,0},{0,24},{9,17},{17,9},{25,1},{1,25},{10,18},{1... | collective-permute-start | bytes 331784 | tf_op jit(solution)/shard_map/ppermute | solution.py:724
  26.6 8.2 %collective-permute-start.9 = (f32[216,128]{1,0:T(8,128)S(1)}, f32[216,128]{1,0:T(8,128)S(1)}, u32[]{:S(2)}, u32[]{:S(2)}) collective-permute-start(f32[216,128]{1,0:T(8,128)S(1)} %get-tuple-element.79), channel_id=1, source_target_pairs={{0,8},{8,0},{16,24},{24,16},{1,9},{9,1},{17,25},{25,17},{2,10},{10... | collective-permute-start | bytes 331784 | tf_op jit(solution)/shard_map/ppermute | solution.py:723
  32.1 4.5 %collective-permute-start.10 = (f32[32,128]{1,0:T(8,128)S(1)}, f32[32,128]{1,0:T(8,128)S(1)}, u32[]{:S(2)}, u32[]{:S(2)}) collective-permute-start(f32[32,128]{1,0:T(8,128)S(1)} %get-tuple-element.85), channel_id=1, source_target_pairs={{0,8},{8,0},{16,24},{24,16},{1,9},{9,1},{17,25},{25,17},{2,10},{10... | collective-permute-start | bytes 49160 | tf_op jit(solution)/shard_map/ppermute | solution.py:723
  32.2 5.6 %collective-permute-start.11 = (f32[32,128]{1,0:T(8,128)S(1)}, f32[32,128]{1,0:T(8,128)S(1)}, u32[]{:S(2)}, u32[]{:S(2)}) collective-permute-start(f32[32,128]{1,0:T(8,128)S(1)} %get-tuple-element.86), channel_id=1, source_target_pairs={{8,16},{16,8},{24,0},{0,24},{9,17},{17,9},{25,1},{1,25},{10,18},{1... | collective-permute-start | bytes 49160 | tf_op jit(solution)/shard_map/ppermute | solution.py:724
  39.9 1.2 %collective-permute-start.12 = (f32[8,128]{1,0:T(8,128)S(1)}, f32[8,128]{1,0:T(8,128)S(1)}, u32[]{:S(2)}, u32[]{:S(2)}) collective-permute-start(f32[8,128]{1,0:T(8,128)S(1)} %get-tuple-element.89), channel_id=1, source_target_pairs={{0,1},{1,0},{2,3},{3,2},{4,5},{5,4},{6,7},{7,6},{8,9},{9,8},{10,11... | collective-permute-start | bytes 12296 | tf_op jit(solution)/shard_map/ppermute | solution.py:735
  41.1 5.1 %collective-permute-start.15 = (f32[8,128]{1,0:T(8,128)S(1)}, f32[8,128]{1,0:T(8,128)S(1)}, u32[]{:S(2)}, u32[]{:S(2)}) collective-permute-start(f32[8,128]{1,0:T(8,128)S(1)} %max.21.near), channel_id=1, source_target_pairs={{0,6},{1,7},{2,4},{3,5},{4,2},{5,3},{6,0},{7,1},{8,14},{9,15},{10,... | collective-permute-start | bytes 12296 | tf_op jit(solution)/shard_map/ppermute | solution.py:735
  42.4 3.8 %collective-permute-start.14 = (f32[8,128]{1,0:T(8,128)S(1)}, f32[8,128]{1,0:T(8,128)S(1)}, u32[]{:S(2)}, u32[]{:S(2)}) collective-permute-start(f32[8,128]{1,0:T(8,128)S(1)} %max.21.near), channel_id=1, source_target_pairs={{0,4},{1,5},{2,6},{3,7},{4,0},{5,1},{6,2},{7,3},{8,12},{9,13},{10,... | collective-permute-start | bytes 12296 | tf_op jit(solution)/shard_map/ppermute | solution.py:735
  43.2 3.6 %collective-permute-start.13 = (f32[8,128]{1,0:T(8,128)S(1)}, f32[8,128]{1,0:T(8,128)S(1)}, u32[]{:S(2)}, u32[]{:S(2)}) collective-permute-start(f32[8,128]{1,0:T(8,128)S(1)} %max.21.near), channel_id=1, source_target_pairs={{0,2},{1,3},{2,0},{3,1},{4,6},{5,7},{6,4},{7,5},{8,10},{9,11},{10,... | collective-permute-start | bytes 12296 | tf_op jit(solution)/shard_map/ppermute | solution.py:735
  46.8 6.0 %collective-permute-start.18 = (f32[8,128]{1,0:T(8,128)S(1)}, f32[8,128]{1,0:T(8,128)S(1)}, u32[]{:S(2)}, u32[]{:S(2)}) collective-permute-start(f32[8,128]{1,0:T(8,128)S(1)} %maximum_maximum_fusion.1), channel_id=1, source_target_pairs={{0,24},{8,16},{16,8},{24,0},{1,25},{9,17},{17,9},{25,1},{2,26},{10... | collective-permute-start | bytes 12296 | tf_op jit(solution)/shard_map/ppermute | solution.py:735
  48.8 4.5 %collective-permute-start.17 = (f32[8,128]{1,0:T(8,128)S(1)}, f32[8,128]{1,0:T(8,128)S(1)}, u32[]{:S(2)}, u32[]{:S(2)}) collective-permute-start(f32[8,128]{1,0:T(8,128)S(1)} %maximum_maximum_fusion.1), channel_id=1, source_target_pairs={{0,16},{8,24},{16,0},{24,8},{1,17},{9,25},{17,1},{25,9},{2,18},{10... | collective-permute-start | bytes 12296 | tf_op jit(solution)/shard_map/ppermute | solution.py:735
  48.8 4.5 %collective-permute-start.16 = (f32[8,128]{1,0:T(8,128)S(1)}, f32[8,128]{1,0:T(8,128)S(1)}, u32[]{:S(2)}, u32[]{:S(2)}) collective-permute-start(f32[8,128]{1,0:T(8,128)S(1)} %maximum_maximum_fusion.1), channel_id=1, source_target_pairs={{0,8},{8,0},{16,24},{24,16},{1,9},{9,1},{17,25},{25,17},{2,10},{10... | collective-permute-start | bytes 12296 | tf_op jit(solution)/shard_map/ppermute | solution.py:735

commit v4 on v3

--- a/solution.py
+++ b/solution.py
@@ -293,24 +293,6 @@
     return (0, g.halo) if velocity(i, sign)[1] == 1 else (g.halo,)
 
 
-def pack_corners(g, buf, sign, fields, up, down):
-    for side, ref in ((1, up), (-1, down)):
-        for n, (i, r, _) in enumerate(x_lines(g, sign, fields, side)):
-            ref[n : n + 1, :] = buf[pl.ds(g.at(i, g.halo, r), 1), :]
-
-
-def unpack_corners(g, buf, sign, fields, up, down):
-    for side, ref in ((1, up), (-1, down)):
-        for n, (i, _, targets) in enumerate(x_lines(g, sign, fields, side)):
-            value = ref[n : n + 1, :]
-            for r in targets:
-                for k in halo_panels(g, i, sign):
-                    buf[pl.ds(g.at(i, k, r), 1), :] = value
-    for i in moving(fields, sign, 0, -1):
-        for k in halo_panels(g, i, sign):
-            buf[pl.ds(g.at(i, k, g.rows + 2), 1), :] = buf[pl.ds(g.at(i, k, 0), 1), :]
-
-
 def still_pairs(fields, sign):
     still = moving(fields, sign, 1, 0)
     half = (len(still) + 1) // 2
@@ -321,33 +303,49 @@
     return 9 + len(still_pairs(fields, sign))
 
 
-def pack_y(g, buf, sign, fields, high, up, down):
+def y_slot(g, n, part):
+    return (2 * n, g.rows, 2) if part == "corner" else (n * g.rows, 0, g.rows)
+
+
+def pack_y(g, buf, sign, fields, part, up, down):
     for side, ref in ((1, up), (-1, down)):
         k = g.cols if side == 1 else 1
         for n, i in enumerate(moving(fields, sign, 1, side)):
-            ref[n * g.rows : (n + 1) * g.rows, :] = buf[pl.ds(g.at(i, k, 0), g.rows), :]
+            to, r, count = y_slot(g, n, part)
+            ref[to : to + count, :] = buf[pl.ds(g.at(i, k, r), count), :]
         for n, (i, j) in enumerate(still_pairs(fields, sign)):
-            value = buf[pl.ds(g.at(i, k, 0), g.rows), :]
+            to, r, count = y_slot(g, 9 + n, part)
+            value = buf[pl.ds(g.at(i, k, r), count), :]
             if j is not None:
-                other = pltpu.roll(buf[pl.ds(g.at(j, k, 0), g.rows), :], NZ, 1)
+                other = pltpu.roll(buf[pl.ds(g.at(j, k, r), count), :], NZ, 1)
                 pair = (value, other) if side == 1 else (other, value)
-                value = jnp.where(high, *pair)
-            ref[(9 + n) * g.rows : (10 + n) * g.rows, :] = value
-
-
-def unpack_y(g, buf, sign, fields, high, up, down):
+                value = jnp.where(lane_masks(count)[0], *pair)
+            ref[to : to + count, :] = value
+
+
+def unpack_y(g, buf, sign, fields, part, up, down):
     for side, ref in ((1, up), (-1, down)):
         for n, i in enumerate(moving(fields, sign, 1, side)):
-            value = ref[n * g.rows : (n + 1) * g.rows, :]
+            to, r, count = y_slot(g, n, part)
+            value = ref[to : to + count, :]
             for k in halo_panels(g, i, sign):
-                buf[pl.ds(g.at(i, k, 0), g.rows), :] = value
+                buf[pl.ds(g.at(i, k, r), count), :] = value
     for n, (i, j) in enumerate(still_pairs(fields, sign)):
-        spot = slice((9 + n) * g.rows, (10 + n) * g.rows)
-        before, after = up[spot, :], down[spot, :]
-        buf[pl.ds(g.at(i, g.halo, 0), g.rows), :] = jnp.where(high, before, after)
+        to, r, count = y_slot(g, 9 + n, part)
+        high = lane_masks(count)[0]
+        before, after = up[to : to + count, :], down[to : to + count, :]
+        buf[pl.ds(g.at(i, g.halo, r), count), :] = jnp.where(high, before, after)
         if j is not None:
             value = pltpu.roll(jnp.where(high, after, before), NZ, 1)
-            buf[pl.ds(g.at(j, g.halo, 0), g.rows), :] = value
+            buf[pl.ds(g.at(j, g.halo, r), count), :] = value
+    if part != "corner":
+        return
+    for i in moving(fields, sign, 0, 1):
+        for k in halo_panels(g, i, sign):
+            buf[pl.ds(g.at(i, k, -1), 1), :] = buf[pl.ds(g.at(i, k, g.rows + 1), 1), :]
+    for i in moving(fields, sign, 0, -1):
+        for k in halo_panels(g, i, sign):
+            buf[pl.ds(g.at(i, k, g.rows + 2), 1), :] = buf[pl.ds(g.at(i, k, 0), 1), :]
 
 
 def by_parity(axis, first, second, act):
@@ -532,9 +530,8 @@
 
 
 def pack_faces(g, buf, sign, fields, x_first, x_second, y_first, y_second):
-    high = lane_masks(g.rows)[0]
     by_parity("gx", x_first, x_second, functools.partial(pack_x, g, buf, sign, fields))
-    by_parity("gy", y_first, y_second, functools.partial(pack_y, g, buf, sign, fields, high))
+    by_parity("gy", y_first, y_second, functools.partial(pack_y, g, buf, sign, fields, "face"))
 
 
 def rim_first_kernel(g, pops, *refs):
@@ -608,15 +605,14 @@
     interior_tiles(g, step_tile(g, post, out, 1, 30, masks, collide_second(g, state1)))
 
 
-def relay_kernel(g, sign, fields, _, y_second, y_first, buf, first, second):
-    high = lane_masks(g.rows)[0]
-    by_parity("gy", y_second, y_first, functools.partial(unpack_y, g, buf, sign, fields, high))
-    by_parity("gx", first, second, functools.partial(pack_corners, g, buf, sign, fields))
-
-
-def middle_second_kernel(g, adjoint, post, out, state1, stage, field, x_second, x_first):
+def relay_kernel(g, sign, fields, _, x_second, x_first, y_second, y_first, buf, first, second):
+    by_parity("gx", x_second, x_first, functools.partial(unpack_x, g, buf, sign, fields))
+    by_parity("gy", y_second, y_first, functools.partial(unpack_y, g, buf, sign, fields, "face"))
+    by_parity("gy", first, second, functools.partial(pack_y, g, buf, sign, fields, "corner"))
+
+
+def middle_second_kernel(g, _out, _state, post, adjoint, out, state1, stage, field):
     masks = lane_masks(16)
-    by_parity("gx", x_second, x_first, functools.partial(unpack_x, g, post, 1, 30))
     middle_tiles(g, step_tile(g, post, out, 1, 30, masks, collide_second(g, state1)))
     core_tiles(g, seed_tile(g, out, adjoint, stage, field, masks))
 
@@ -624,7 +620,7 @@
 def rim_seed_kernel(g, _post, _out, _state, _stage, _field, first, second, adjoint, *refs):
     post, out, state1, stage, field, *faces = refs
     masks = lane_masks(16)
-    by_parity("gx", second, first, functools.partial(unpack_corners, g, post, 1, 30))
+    by_parity("gy", second, first, functools.partial(unpack_y, g, post, 1, 30, "corner"))
     corner_tiles(g, post, out, 1, 30, masks, collide_second(g, state1))
     rim_tiles(g, seed_tile(g, out, adjoint, stage, field, masks))
     pack_faces(g, field, -1, 27, *faces)
@@ -661,9 +657,8 @@
     return act
 
 
-def middle_adjoint_kernel(g, field, out, before, total, parts, state1, state0, x_second, x_first):
+def middle_adjoint_kernel(g, _out, _before, field, state1, state0, out, before, total, parts):
     masks = lane_masks(16)
-    by_parity("gx", x_second, x_first, functools.partial(unpack_x, g, field, -1, 27))
     middle_tiles(g, step_tile(g, field, out, -1, 27, masks, adjoint_second(g, state1, before)))
     core_tiles(g, total_tile(g, out, before, state0, total, parts, masks))
 
@@ -671,7 +666,7 @@
 def total_kernel(g, *refs):
     state1, state0, first, second, field, out, before, total, parts, peak = refs[5:]
     masks = lane_masks(16)
-    by_parity("gx", second, first, functools.partial(unpack_corners, g, field, -1, 27))
+    by_parity("gy", second, first, functools.partial(unpack_y, g, field, -1, 27, "corner"))
     corner_tiles(g, field, out, -1, 27, masks, adjoint_second(g, state1, before))
     act = total_tile(g, out, before, state0, total, parts, masks)
     near_core_tiles(g, act)
@@ -726,21 +721,27 @@
 
 
 def largest_of_all(peak, sizes, beside):
+    nx, ny = sizes
+    peak = jnp.maximum(peak, lax.ppermute(peak, "gy", [(i, i + 1) for i in range(0, ny, 2)]))
     groups = 0
-    for axis, count, widths in (("gy", sizes[1], (2, 4, 4)), ("gx", sizes[0], (4, 2))):
-        step = 1
+    for axis, count, first, widths in (("gy", ny, 2, (4, 4)), ("gx", nx, 1, (4, 2))):
+        step = first
         for width in widths:
             width = min(width, count // step)
-            parts = [
-                lax.ppermute(peak, axis, [(i, i ^ (n * step)) for i in range(count)])
-                for n in range(1, width)
-            ]
+            parts = []
+            for n in range(1, width):
+                pairs = [(i, i ^ (n * step)) for i in range(count)]
+                if axis == "gy":
+                    parts.append(lax.ppermute(peak, "gy", [(i, j) for i, j in pairs if i % 2]))
+                else:
+                    pairs = [(i * ny + y, j * ny + y) for i, j in pairs for y in range(1, ny, 2)]
+                    parts.append(lax.ppermute(peak, ("gx", "gy"), pairs))
             groups += 1
-            if groups == 2:
-                peak = beside(peak)
+            if groups <= 2:
+                peak = beside(peak, groups)
             peak = functools.reduce(jnp.maximum, parts, peak)
             step *= width
-    return peak
+    return jnp.maximum(peak, lax.ppermute(peak, "gy", [(i + 1, i) for i in range(0, ny, 2)]))
 
 
 def on_device(sizes, populations, adjoint_in, porosity, solid, labels):
@@ -764,8 +765,8 @@
         along_y = vmem(y_slots(count, sign) * rows, LANES)
         return [along_x, along_x, along_y, along_y]
 
-    def corners(count):
-        return [vmem(-(-count // 8) * 8, LANES)] * 2
+    def corners(count, sign):
+        return [vmem(-(-2 * y_slots(count, sign) // 8) * 8, LANES)] * 2
 
     whole = pltpu.HBM(populations.shape, F32)
     stage = vmem(g.cols, 27, rows, LANES)
@@ -798,14 +799,14 @@
     def swap_faces(parcels):
         x_first, x_second = swap("gx", nx, *parcels[:2])
         y_first, y_second = swap("gy", ny, *parcels[2:])
-        return [x_second, x_first], [y_second, y_first]
+        return [x_second, x_first, y_second, y_first]
 
     def relay(buf, parcels, sign, count):
         def kernel(grid, *refs):
             relay_kernel(grid, sign, count, *refs)
 
-        buf, *parcels = call("relay", kernel, [buf, *parcels], corners(count), kept=1)
-        return buf, swap("gx", nx, *parcels)
+        buf, *parcels = call("relay", kernel, [buf, *parcels], corners(count, sign), kept=1)
+        return buf, swap("gy", ny, *parcels)
 
     post, state0, staged, *parcels = call(
         "rim_first",
@@ -816,7 +817,7 @@
         + [pltpu.VMEM(porosity.shape, jnp.int32)] * 2
         + [pltpu.SemaphoreType.DMA((g.cols, 3)), pltpu.SemaphoreType.DMA((3,))],
     )
-    along_x, along_y = swap_faces(parcels)
+    parcels = swap_faces(parcels)
     post, state0, second, state1 = call(
         "inner_first",
         inner_first_kernel,
@@ -825,15 +826,13 @@
         kept=2,
         load=FLIGHT,
     )
-    post, parcels = relay(post, along_y, 1, 30)
-    post, second, state1, staged, field = call(
+    post, parcels = relay(post, parcels, 1, 30)
+    second, state1, staged, field = call(
         "middle_second",
-        lambda grid, _post, _out, _state, b, a, source, *refs: middle_second_kernel(
-            grid, source, *refs, b, a
-        ),
-        [post, second, state1, *along_x, adjoint_in],
+        middle_second_kernel,
+        [second, state1, post, adjoint_in],
         [stage, padded(27)],
-        kept=3,
+        kept=2,
         load=FLIGHT,
     )
     _, second, state1, staged, field, *parcels = call(
@@ -843,7 +842,7 @@
         faces(27, -1),
         kept=5,
     )
-    along_x, along_y = swap_faces(parcels)
+    parcels = swap_faces(parcels)
     _, field, pulled, before, final = call(
         "inner_seed",
         lambda grid, kept, into, buf, *refs: inner_seed_kernel(grid, buf, kept, into, *refs),
@@ -853,15 +852,13 @@
         kept=2,
         load=FLIGHT,
     )
-    field, parcels = relay(field, along_y, -1, 27)
-    field, pulled, before, total, parts = call(
+    field, parcels = relay(field, parcels, -1, 27)
+    pulled, before, total, parts = call(
         "middle_adjoint",
-        lambda grid, _field, _out, _before, near, far, b, a, *refs: middle_adjoint_kernel(
-            grid, *refs, near, far, b, a
-        ),
-        [field, pulled, before, state1, state0, *along_x],
+        middle_adjoint_kernel,
+        [pulled, before, field, state1, state0],
         [fields(1, g.local), fields(5, g.local)],
-        kept=3,
+        kept=2,
         load=FLIGHT,
     )
     _, pulled, _, total, parts, peak = call(
@@ -873,36 +870,30 @@
     )
     half = g.cols // 2
     scratch = [vmem(half, 27, rows, LANES), pltpu.SemaphoreType.DMA((half,))]
-    halves = []
-
-    def first_half(peak):
-        def kernel(grid, buf, fields, near, echo, *refs):
+    halves = [None]
+
+    def run_half(peak, n):
+        first, last = ((1, half), (1 + half, g.cols))[n - 1]
+
+        def kernel(grid, buf, fields, near, *refs):
+            echo, *refs = refs[-4:]
             echo[...] = near[...]
-            adjoint_kernel(grid, 1, half, buf, fields, *refs)
+            adjoint_kernel(grid, first, last, buf, fields, *refs)
 
         echo, result = call(
-            "adjoint_low",
+            ("adjoint_low", "adjoint_high")[n - 1],
             kernel,
             [pulled, parts, peak],
             [vmem(8, LANES), whole],
             scratch,
             load=FLIGHT // 2,
+            result=halves[-1],
         )
         halves.append(result)
         return echo
 
-    largest = largest_of_all(peak, sizes, first_half)
-    (adjoint_out,) = call(
-        "adjoint_high",
-        lambda grid, buf, fields, _, *refs: adjoint_kernel(
-            grid, 1 + half, g.cols, buf, fields, *refs
-        ),
-        [pulled, parts],
-        [whole],
-        scratch,
-        load=FLIGHT // 2,
-        result=halves[0],
-    )
+    largest = largest_of_all(peak, sizes, run_half)
+    adjoint_out = halves[-1]
     (sensitivity,) = call(
         "normalize",
         scale_kernel,

time: 54.3 us -> 69.6 us (1.28)
  waiting for transfers between devices: 8.68 us -> 30.2 us
  starting transfers between devices: 25.8 us -> 19.3 us
    ppermute x7 -> x8, waiting for transfers between devices: 2.23 us -> 17.2 us  [the longest x1 16.4 us: largest_of_all(): lax.ppermute(peak, 'gy', [(i + 1, i) for i in range(0, ny, 2)])]
    ppermute x6, waiting for transfers between devices: 0.02 us -> 4.07 us  [swap(): lax.ppermute(first, axis, swap_pairs(count, 0))]
    ppermute x6, starting transfers between devices: 3.26 us -> 0.17 us  [swap(): lax.ppermute(first, axis, swap_pairs(count, 0))]
    ppermute x6, waiting for transfers between devices: 6.44 us -> 9 us  [swap(): lax.ppermute(second, axis, swap_pairs(count, 1))]
    ppermute x6, starting transfers between devices: 14.6 us -> 12.1 us  [swap(): lax.ppermute(second, axis, swap_pairs(count, 1))]
    ppermute x7 -> x8, starting transfers between devices: 7.95 us -> 6.98 us  [the longest x3 1.98 us: largest_of_all(): parts.append(lax.ppermute(peak, ('gx', 'gy'), pairs))]
  transfers between devices with their start and end apart: 19 -> 20, of which waited for: 7 -> 8; matrix products, arithmetic and copies ran while one was open for 0% -> 0% of each run, Pallas kernels for 20% -> 12%
where the time goes in v4:
time: 69.6 us; the launch traced here: 69.3 us
  waiting for transfers between devices  30.2 us (43%)
  starting transfers between devices  19.3 us (28%)
  Pallas kernels  18.9 us (27%)
  between operations  0.87 us (1%)
    pallas_call x12, Pallas kernels, call(): pl.pallas_call(functools.partial(kernel, g), in_specs=in_specs, out_shape...  18.9 us
    ppermute x1, waiting for transfers between devices, largest_of_all(): lax.ppermute(peak, 'gy', [(i + 1, i) for i in range(0, ny, 2)])  16.4 us
    ppermute x6, starting transfers between devices, swap(): lax.ppermute(second, axis, swap_pairs(count, 1))  12.1 us
    ppermute x6, waiting for transfers between devices, swap(): lax.ppermute(second, axis, swap_pairs(count, 1))  9 us
    ppermute x6, waiting for transfers between devices, swap(): lax.ppermute(first, axis, swap_pairs(count, 0))  4.07 us
    ppermute x3, starting transfers between devices, largest_of_all(): parts.append(lax.ppermute(peak, ('gx', 'gy'), pairs))  1.98 us
    ppermute x3, starting transfers between devices, largest_of_all(): parts.append(lax.ppermute(peak, 'gy', [(i, j) for i, j in pairs if i % 2]))  1.97 us
    ppermute x1, starting transfers between devices, largest_of_all(): lax.ppermute(peak, 'gy', [(i, i + 1) for i in range(0, ny, 2)])  1.73 us
  transfers between devices with their start and end apart: 20, of which 8 were waited for; matrix products, arithmetic and copies ran while one was open for 0% of the time, Pallas kernels for 12%

profile of v4, /device:TPU:0, one launch (start us, length us, event | category | flops | bytes accessed | tf_op | source)
XLA Modules:
  0.0 69.3 jit_solution(14768443779181080975)
XLA Ops:
  0.6 3.1 %rim_first.1 = (f32[14408,128]{1,0:T(8,128)S(1)}, f32[1792,128]{1,0:T(8,128)S(1)}, f32[8,27,32,128]{3,2,1,0:T(8,128)S(1)}, f32[240,128]{1,0:T(8,128)S(1)}, f32[2...) custom-call(f32[27,32,1024]{2,1,0:T(8,128)} %pops.1, f32[32,1024]{1,0:T(8,128)} %refs_0_.1, ...), custom_call_target="tpu_custom_call" | custom-call | tf_op jit(solution)/shard_map/rim_first/pallas_call | solution.py:785
  3.7 3.4 %collective-permute-start.2 = (f32[480,128]{1,0:T(8,128)S(1)}, f32[480,128]{1,0:T(8,128)S(1)}, u32[]{:S(2)}, u32[]{:S(2)}) collective-permute-start(f32[480,128]{1,0:T(8,128)S(1)} %get-tuple-element.54), channel_id=1, source_target_pairs={{1,2},{2,1},{3,4},{4,3},{5,6},{6,5},{7,0},{0,7},{9,10},{10,9},{11,... | collective-permute-start | bytes 737288 | tf_op jit(solution)/shard_map/ppermute | solution.py:719
  7.1 0.0 collective-permute-start.3
  7.1 3.6 %collective-permute-start = (f32[240,128]{1,0:T(8,128)S(1)}, f32[240,128]{1,0:T(8,128)S(1)}, u32[]{:S(2)}, u32[]{:S(2)}) collective-permute-start(f32[240,128]{1,0:T(8,128)S(1)} %get-tuple-element.52), channel_id=1, source_target_pairs={{8,16},{16,8},{24,0},{0,24},{9,17},{17,9},{25,1},{1,25},{10,18},{1... | collective-permute-start | bytes 368648 | tf_op jit(solution)/shard_map/ppermute | solution.py:719
  10.7 0.0 collective-permute-start.1
  10.7 1.4 %inner_first.1 = (f32[14408,128]{1,0:T(8,128)S(1)}, f32[1792,128]{1,0:T(8,128)S(1)}, f32[12968,128]{1,0:T(8,128)S(1)}, f32[2184,128]{1,0:T(8,128)S(1)}) custom-call(f32[14408,128]{1,0:T(8,128)S(1)} %get-tuple-element.48._, f32[1792,128]{1,0:T(8,128)S(1)} %get-tuple-element.49._state, ...), custom_call_target="tpu_custom_call", output_to_operand_aliasing={{0}: (0, {}), {1}: (1, {})} | custom-call | bytes 12582912 | tf_op jit(solution)/shard_map/inner_first/pallas_call | solution.py:785
  12.1 0.0 copy-start
  12.1 3.0 %collective-permute-done.refs_1_ = f32[240,128]{1,0:T(8,128)S(1)} collective-permute-done((f32[240,128]{1,0:T(8,128)S(1)}, f32[240,128]{1,0:T(8,128)S(1)}, u32[]{:S(2)}, u32[]{:S(2)}) %collective-permute-start) | collective-permute-done | bytes 122912 | tf_op jit(solution)/shard_map/ppermute | solution.py:719
  15.1 2.4 %collective-permute-done.1.refs_2_ = f32[240,128]{1,0:T(8,128)S(1)} collective-permute-done((f32[240,128]{1,0:T(8,128)S(1)}, f32[240,128]{1,0:T(8,128)S(1)}, u32[]{:S(2)}, u32[]{:S(2)}) %collective-permute-start.1) | collective-permute-done | bytes 122912 | tf_op jit(solution)/shard_map/ppermute | solution.py:718
  17.5 0.0 collective-permute-done.2.refs_3_
  17.5 0.0 collective-permute-done.3.refs_4_
  17.5 0.3 relay.2
  17.8 0.1 collective-permute-start.4
  17.9 0.7 %collective-permute-start.5 = (f32[32,128]{1,0:T(8,128)S(1)}, f32[32,128]{1,0:T(8,128)S(1)}, u32[]{:S(2)}, u32[]{:S(2)}) collective-permute-start(f32[32,128]{1,0:T(8,128)S(1)} %get-tuple-element.64), channel_id=1, source_target_pairs={{1,2},{2,1},{3,4},{4,3},{5,6},{6,5},{7,0},{0,7},{9,10},{10,9},{11,... | collective-permute-start | bytes 49160 | tf_op jit(solution)/shard_map/ppermute | solution.py:719
  18.6 0.0 copy-done
  18.6 1.8 %middle_second.1 = (f32[12968,128]{1,0:T(8,128)S(1)}, f32[2184,128]{1,0:T(8,128)S(1)}, f32[8,27,32,128]{3,2,1,0:T(8,128)S(1)}, f32[12968,128]{1,0:T(8,128)S(1)}) custom-call(f32[12968,128]{1,0:T(8,128)S(1)} %get-tuple-element.57._out, f32[2184,128]{1,0:T(8,128)S(1)} %get-tuple-element.58._state, ...), custom_call_target="tpu_custom_call", output_to_operand_aliasing={{0}: (0, {}), {1}: (1, {})} | custom-call | bytes 12582912 | tf_op jit(solution)/shard_map/middle_second/pallas_call | solution.py:785
  20.4 0.0 collective-permute-done.4.first
  20.4 1.6 %collective-permute-done.5.second = f32[32,128]{1,0:T(8,128)S(1)} collective-permute-done((f32[32,128]{1,0:T(8,128)S(1)}, f32[32,128]{1,0:T(8,128)S(1)}, u32[]{:S(2)}, u32[]{:S(2)}) %collective-permute-start.5) | collective-permute-done | bytes 16416 | tf_op jit(solution)/shard_map/ppermute | solution.py:719
  22.0 2.3 %rim_seed.1 = (f32[14408,128]{1,0:T(8,128)S(1)}, f32[12968,128]{1,0:T(8,128)S(1)}, f32[2184,128]{1,0:T(8,128)S(1)}, f32[8,27,32,128]{3,2,1,0:T(8,128)S(1)}, f32[...) custom-call(f32[14408,128]{1,0:T(8,128)S(1)} %get-tuple-element.56.p, ...), custom_call_target="tpu_custom_call", output_to_operand_aliasing={{0}: (0, {}), {1}: (1, {}), {2}: (2, {}), {3}: (3, {}), {4}... | custom-call | tf_op jit(solution)/shard_map/rim_seed/pallas_call | solution.py:785
  24.3 0.7 collective-permute-start.8
  25.0 0.0 collective-permute-start.9
  25.0 1.8 %collective-permute-start.6 = (f32[216,128]{1,0:T(8,128)S(1)}, f32[216,128]{1,0:T(8,128)S(1)}, u32[]{:S(2)}, u32[]{:S(2)}) collective-permute-start(f32[216,128]{1,0:T(8,128)S(1)} %get-tuple-element.71), channel_id=1, source_target_pairs={{8,16},{16,8},{24,0},{0,24},{9,17},{17,9},{25,1},{1,25},{10,18},{1... | collective-permute-start | bytes 331784 | tf_op jit(solution)/shard_map/ppermute | solution.py:719
  26.9 0.0 collective-permute-start.7
  26.9 1.9 %inner_seed.1 = (f32[8,27,32,128]{3,2,1,0:T(8,128)S(1)}, f32[12968,128]{1,0:T(8,128)S(1)}, f32[12968,128]{1,0:T(8,128)S(1)}, f32[312,128]{1,0:T(8,128)S(1)}, f32[27,32,1024]{2,1,0:T(8,128)}) custom-call(f32[8,27,32,128]{3,2,1,0:T(8,128)S(1)} %get-tuple-element.65.kept, ...), custom_call_target="tpu_custom_call", output_to_operand_aliasing={{0}: (0, {}), {1}: (1, {})} | custom-call | bytes 12582912 | tf_op jit(solution)/shard_map/inner_seed/pallas_call | solution.py:785
  28.7 4.0 %collective-permute-done.6.refs_1_ = f32[216,128]{1,0:T(8,128)S(1)} collective-permute-done((f32[216,128]{1,0:T(8,128)S(1)}, f32[216,128]{1,0:T(8,128)S(1)}, u32[]{:S(2)}, u32[]{:S(2)}) %collective-permute-start.6) | collective-permute-done | bytes 110624 | tf_op jit(solution)/shard_map/ppermute | solution.py:719
  32.7 1.7 %collective-permute-done.7.refs_2_ = f32[216,128]{1,0:T(8,128)S(1)} collective-permute-done((f32[216,128]{1,0:T(8,128)S(1)}, f32[216,128]{1,0:T(8,128)S(1)}, u32[]{:S(2)}, u32[]{:S(2)}) %collective-permute-start.7) | collective-permute-done | bytes 110624 | tf_op jit(solution)/shard_map/ppermute | solution.py:718
  34.4 0.0 collective-permute-done.8.refs_3_
  34.4 0.0 collective-permute-done.9.refs_4_
  34.4 0.3 relay.3
  34.7 0.0 collective-permute-start.10
  34.8 1.9 %collective-permute-start.11 = (f32[32,128]{1,0:T(8,128)S(1)}, f32[32,128]{1,0:T(8,128)S(1)}, u32[]{:S(2)}, u32[]{:S(2)}) collective-permute-start(f32[32,128]{1,0:T(8,128)S(1)} %get-tuple-element.84), channel_id=1, source_target_pairs={{1,2},{2,1},{3,4},{4,3},{5,6},{6,5},{7,0},{0,7},{9,10},{10,9},{11,... | collective-permute-start | bytes 49160 | tf_op jit(solution)/shard_map/ppermute | solution.py:719
  36.6 1.8 %middle_adjoint.1 = (f32[12968,128]{1,0:T(8,128)S(1)}, f32[312,128]{1,0:T(8,128)S(1)}, f32[256,128]{1,0:T(8,128)S(1)}, f32[1280,128]{1,0:T(8,128)S(1)}) custom-call(f32[12968,128]{1,0:T(8,128)S(1)} %get-tuple-element.76._out, f32[312,128]{1,0:T(8,128)S(1)} %get-tuple-element.77._before, ...), custom_call_target="tpu_custom_call", output_to_operand_aliasing={{0}: (0, {}), {1}: (1, {})} | custom-call | bytes 12582912 | tf_op jit(solution)/shard_map/middle_adjoint/pallas_call | solution.py:785
  38.4 0.0 collective-permute-done.10.refs_7_
  38.4 0.5 collective-permute-done.11.refs_8_
  38.9 2.1 %total.1 = (f32[12968,128]{1,0:T(8,128)S(1)}, f32[12968,128]{1,0:T(8,128)S(1)}, f32[312,128]{1,0:T(8,128)S(1)}, f32[256,128]{1,0:T(8,128)S(1)}, f32[1280,128]{1,0:T(8,128)S(1)}, /*index=5*/f32[8,128]{1,0:T(8,128)S(1)}) custom-call(f32[12968,128]{1,0:T(8,128)S(1)} %get-tuple-element.75.f, ...), custom_call_target="tpu_custom_call", output_to_operand_aliasing={{0}: (0, {}), {1}: (1, {}), {2}: (2, {}), {3}: (3, {}), {4}... | custom-call | tf_op jit(solution)/shard_map/total/pallas_call | solution.py:785
  41.0 1.7 %collective-permute-start.12 = (f32[8,128]{1,0:T(8,128)S(1)}, f32[8,128]{1,0:T(8,128)S(1)}, u32[]{:S(2)}, u32[]{:S(2)}) collective-permute-start(f32[8,128]{1,0:T(8,128)S(1)} %get-tuple-element.87), channel_id=1, source_target_pairs={{0,1},{2,3},{4,5},{6,7},{8,9},{10,11},{12,13},{14,15},{16,17},{18,... | collective-permute-start | bytes 12296 | tf_op jit(solution)/shard_map/ppermute | solution.py:725
  42.8 0.8 %collective-permute-done.12 = f32[8,128]{1,0:T(8,128)S(1)} collective-permute-done((f32[8,128]{1,0:T(8,128)S(1)}, f32[8,128]{1,0:T(8,128)S(1)}, u32[]{:S(2)}, u32[]{:S(2)}) %collective-permute-start.12) | collective-permute-done | bytes 4128 | tf_op jit(solution)/shard_map/ppermute | solution.py:725
  43.6 0.6 collective-permute-start.15
  44.2 0.7 collective-permute-start.14
  44.9 0.7 collective-permute-start.13
  45.6 1.6 %adjoint_low.1 = (f32[8,128]{1,0:T(8,128)S(1)}, f32[27,32,1024]{2,1,0:T(8,128)}) custom-call(f32[12968,128]{1,0:T(8,128)S(1)} %get-tuple-element.85.buf, f32[1280,128]{1,0:T(8,128)S(1)} %get-tuple-element.86.fields, f32[8,128]{1,0:T(8,128)S(1)} %max.24.near), custom_call_target="tpu_custom_call" | custom-call | bytes 6291456 | tf_op jit(solution)/shard_map/adjoint_low/pallas_call | solution.py:785
  47.2 0.0 collective-permute-done.15
  47.2 0.0 collective-permute-done.14
  47.2 0.0 collective-permute-done.13
  47.2 1.6 %adjoint_high.1 = (f32[8,128]{1,0:T(8,128)S(1)}, f32[27,32,1024]{2,1,0:T(8,128)}) custom-call(f32[12968,128]{1,0:T(8,128)S(1)} %get-tuple-element.85.buf, f32[1280,128]{1,0:T(8,128)S(1)} %get-tuple-element.86.fields, f32[8,128]{1,0:T(8,128)S(1)} %maximum_maximum_fusion.1.near, f32[27,32,1024]{2,1,0:T(8,128)} %get-tuple-element.89.refs_0_), custom_call_target="tpu_custom_call", output_to_operand_aliasing={{1}: (3, {})} | custom-call | bytes 6291456 | tf_op jit(solution)/shard_map/adjoint_high/pallas_call | solution.py:785
  48.8 0.7 collective-permute-start.18
  49.5 0.7 collective-permute-start.17
  50.2 0.7 collective-permute-start.16
  50.8 0.0 collective-permute-done.18
  50.8 0.0 collective-permute-done.17
  50.9 0.0 collective-permute-done.16
  50.9 1.3 %collective-permute-start.19 = (f32[8,128]{1,0:T(8,128)S(1)}, f32[8,128]{1,0:T(8,128)S(1)}, u32[]{:S(2)}, u32[]{:S(2)}) collective-permute-start(f32[8,128]{1,0:T(8,128)S(1)} %maximum_maximum_fusion), channel_id=1, source_target_pairs={{1,0},{3,2},{5,4},{7,6},{9,8},{11,10},{13,12},{15,14},{17,16},{19,... | collective-permute-start | bytes 12296 | tf_op jit(solution)/shard_map/ppermute | solution.py:744
  52.2 16.4 %collective-permute-done.19 = f32[8,128]{1,0:T(8,128)S(1)} collective-permute-done((f32[8,128]{1,0:T(8,128)S(1)}, f32[8,128]{1,0:T(8,128)S(1)}, u32[]{:S(2)}, u32[]{:S(2)}) %collective-permute-start.19) | collective-permute-done | bytes 4128 | tf_op jit(solution)/shard_map/ppermute | solution.py:744
  68.5 0.8 %normalize.1 = f32[32,1024]{1,0:T(8,128)} custom-call(f32[256,128]{1,0:T(8,128)S(1)} %get-tuple-element.91.total, f32[8,128]{1,0:T(8,128)S(1)} %max.31.peak), custom_call_target="tpu_custom_call" | custom-call | tf_op jit(solution)/shard_map/normalize/pallas_call | solution.py:785
  (4 shorter events, 0.0 us)
Async XLA Ops:
  3.7 13.7 %collective-permute-start.2 = (f32[480,128]{1,0:T(8,128)S(1)}, f32[480,128]{1,0:T(8,128)S(1)}, u32[]{:S(2)}, u32[]{:S(2)}) collective-permute-start(f32[480,128]{1,0:T(8,128)S(1)} %get-tuple-element.54), channel_id=1, source_target_pairs={{1,2},{2,1},{3,4},{4,3},{5,6},{6,5},{7,0},{0,7},{9,10},{10,9},{11,... | collective-permute-start | bytes 737288 | tf_op jit(solution)/shard_map/ppermute | solution.py:719
  7.1 10.3 %collective-permute-start.3 = (f32[480,128]{1,0:T(8,128)S(1)}, f32[480,128]{1,0:T(8,128)S(1)}, u32[]{:S(2)}, u32[]{:S(2)}) collective-permute-start(f32[480,128]{1,0:T(8,128)S(1)} %get-tuple-element.55), channel_id=1, source_target_pairs={{0,1},{1,0},{2,3},{3,2},{4,5},{5,4},{6,7},{7,6},{8,9},{9,8},{10,11... | collective-permute-start | bytes 737288 | tf_op jit(solution)/shard_map/ppermute | solution.py:718
  7.1 8.0 %collective-permute-start = (f32[240,128]{1,0:T(8,128)S(1)}, f32[240,128]{1,0:T(8,128)S(1)}, u32[]{:S(2)}, u32[]{:S(2)}) collective-permute-start(f32[240,128]{1,0:T(8,128)S(1)} %get-tuple-element.52), channel_id=1, source_target_pairs={{8,16},{16,8},{24,0},{0,24},{9,17},{17,9},{25,1},{1,25},{10,18},{1... | collective-permute-start | bytes 368648 | tf_op jit(solution)/shard_map/ppermute | solution.py:719
  10.7 6.7 %collective-permute-start.1 = (f32[240,128]{1,0:T(8,128)S(1)}, f32[240,128]{1,0:T(8,128)S(1)}, u32[]{:S(2)}, u32[]{:S(2)}) collective-permute-start(f32[240,128]{1,0:T(8,128)S(1)} %get-tuple-element.53), channel_id=1, source_target_pairs={{0,8},{8,0},{16,24},{24,16},{1,9},{9,1},{17,25},{25,17},{2,10},{10... | collective-permute-start | bytes 368648 | tf_op jit(solution)/shard_map/ppermute | solution.py:718
  12.1 6.5 %copy-start = (f32[27,32,1024]{2,1,0:T(8,128)S(1)}, f32[27,32,1024]{2,1,0:T(8,128)}, u32[]{:S(2)}) copy-start(f32[27,32,1024]{2,1,0:T(8,128)} %refs_1_.3) | copy-start | bytes 10616836
  17.8 2.7 %collective-permute-start.4 = (f32[32,128]{1,0:T(8,128)S(1)}, f32[32,128]{1,0:T(8,128)S(1)}, u32[]{:S(2)}, u32[]{:S(2)}) collective-permute-start(f32[32,128]{1,0:T(8,128)S(1)} %get-tuple-element.63), channel_id=1, source_target_pairs={{0,1},{1,0},{2,3},{3,2},{4,5},{5,4},{6,7},{7,6},{8,9},{9,8},{10,11... | collective-permute-start | bytes 49160 | tf_op jit(solution)/shard_map/ppermute | solution.py:718
  17.9 4.1 %collective-permute-start.5 = (f32[32,128]{1,0:T(8,128)S(1)}, f32[32,128]{1,0:T(8,128)S(1)}, u32[]{:S(2)}, u32[]{:S(2)}) collective-permute-start(f32[32,128]{1,0:T(8,128)S(1)} %get-tuple-element.64), channel_id=1, source_target_pairs={{1,2},{2,1},{3,4},{4,3},{5,6},{6,5},{7,0},{0,7},{9,10},{10,9},{11,... | collective-permute-start | bytes 49160 | tf_op jit(solution)/shard_map/ppermute | solution.py:719
  24.3 10.1 %collective-permute-start.8 = (f32[448,128]{1,0:T(8,128)S(1)}, f32[448,128]{1,0:T(8,128)S(1)}, u32[]{:S(2)}, u32[]{:S(2)}) collective-permute-start(f32[448,128]{1,0:T(8,128)S(1)} %get-tuple-element.73), channel_id=1, source_target_pairs={{1,2},{2,1},{3,4},{4,3},{5,6},{6,5},{7,0},{0,7},{9,10},{10,9},{11,... | collective-permute-start | bytes 688136 | tf_op jit(solution)/shard_map/ppermute | solution.py:719
  25.0 9.4 %collective-permute-start.9 = (f32[448,128]{1,0:T(8,128)S(1)}, f32[448,128]{1,0:T(8,128)S(1)}, u32[]{:S(2)}, u32[]{:S(2)}) collective-permute-start(f32[448,128]{1,0:T(8,128)S(1)} %get-tuple-element.74), channel_id=1, source_target_pairs={{0,1},{1,0},{2,3},{3,2},{4,5},{5,4},{6,7},{7,6},{8,9},{9,8},{10,11... | collective-permute-start | bytes 688136 | tf_op jit(solution)/shard_map/ppermute | solution.py:718
  25.0 7.7 %collective-permute-start.6 = (f32[216,128]{1,0:T(8,128)S(1)}, f32[216,128]{1,0:T(8,128)S(1)}, u32[]{:S(2)}, u32[]{:S(2)}) collective-permute-start(f32[216,128]{1,0:T(8,128)S(1)} %get-tuple-element.71), channel_id=1, source_target_pairs={{8,16},{16,8},{24,0},{0,24},{9,17},{17,9},{25,1},{1,25},{10,18},{1... | collective-permute-start | bytes 331784 | tf_op jit(solution)/shard_map/ppermute | solution.py:719
  26.9 7.6 %collective-permute-start.7 = (f32[216,128]{1,0:T(8,128)S(1)}, f32[216,128]{1,0:T(8,128)S(1)}, u32[]{:S(2)}, u32[]{:S(2)}) collective-permute-start(f32[216,128]{1,0:T(8,128)S(1)} %get-tuple-element.72), channel_id=1, source_target_pairs={{0,8},{8,0},{16,24},{24,16},{1,9},{9,1},{17,25},{25,17},{2,10},{10... | collective-permute-start | bytes 331784 | tf_op jit(solution)/shard_map/ppermute | solution.py:718
  34.7 3.7 %collective-permute-start.10 = (f32[32,128]{1,0:T(8,128)S(1)}, f32[32,128]{1,0:T(8,128)S(1)}, u32[]{:S(2)}, u32[]{:S(2)}) collective-permute-start(f32[32,128]{1,0:T(8,128)S(1)} %get-tuple-element.83), channel_id=1, source_target_pairs={{0,1},{1,0},{2,3},{3,2},{4,5},{5,4},{6,7},{7,6},{8,9},{9,8},{10,11... | collective-permute-start | bytes 49160 | tf_op jit(solution)/shard_map/ppermute | solution.py:718
  34.8 4.1 %collective-permute-start.11 = (f32[32,128]{1,0:T(8,128)S(1)}, f32[32,128]{1,0:T(8,128)S(1)}, u32[]{:S(2)}, u32[]{:S(2)}) collective-permute-start(f32[32,128]{1,0:T(8,128)S(1)} %get-tuple-element.84), channel_id=1, source_target_pairs={{1,2},{2,1},{3,4},{4,3},{5,6},{6,5},{7,0},{0,7},{9,10},{10,9},{11,... | collective-permute-start | bytes 49160 | tf_op jit(solution)/shard_map/ppermute | solution.py:719
  41.0 2.5 %collective-permute-start.12 = (f32[8,128]{1,0:T(8,128)S(1)}, f32[8,128]{1,0:T(8,128)S(1)}, u32[]{:S(2)}, u32[]{:S(2)}) collective-permute-start(f32[8,128]{1,0:T(8,128)S(1)} %get-tuple-element.87), channel_id=1, source_target_pairs={{0,1},{2,3},{4,5},{6,7},{8,9},{10,11},{12,13},{14,15},{16,17},{18,... | collective-permute-start | bytes 12296 | tf_op jit(solution)/shard_map/ppermute | solution.py:725
  43.6 3.6 %collective-permute-start.15 = (f32[8,128]{1,0:T(8,128)S(1)}, f32[8,128]{1,0:T(8,128)S(1)}, u32[]{:S(2)}, u32[]{:S(2)}) collective-permute-start(f32[8,128]{1,0:T(8,128)S(1)} %max.24.near), channel_id=1, source_target_pairs={{1,7},{3,5},{5,3},{7,1},{9,15},{11,13},{13,11},{15,9},{17,23},{19,... | collective-permute-start | bytes 12296 | tf_op jit(solution)/shard_map/ppermute | solution.py:735
  44.2 3.0 %collective-permute-start.14 = (f32[8,128]{1,0:T(8,128)S(1)}, f32[8,128]{1,0:T(8,128)S(1)}, u32[]{:S(2)}, u32[]{:S(2)}) collective-permute-start(f32[8,128]{1,0:T(8,128)S(1)} %max.24.near), channel_id=1, source_target_pairs={{1,5},{3,7},{5,1},{7,3},{9,13},{11,15},{13,9},{15,11},{17,21},{19,... | collective-permute-start | bytes 12296 | tf_op jit(solution)/shard_map/ppermute | solution.py:735
  44.9 2.3 %collective-permute-start.13 = (f32[8,128]{1,0:T(8,128)S(1)}, f32[8,128]{1,0:T(8,128)S(1)}, u32[]{:S(2)}, u32[]{:S(2)}) collective-permute-start(f32[8,128]{1,0:T(8,128)S(1)} %max.24.near), channel_id=1, source_target_pairs={{1,3},{3,1},{5,7},{7,5},{9,11},{11,9},{13,15},{15,13},{17,19},{19,... | collective-permute-start | bytes 12296 | tf_op jit(solution)/shard_map/ppermute | solution.py:735
  48.8 2.0 %collective-permute-start.18 = (f32[8,128]{1,0:T(8,128)S(1)}, f32[8,128]{1,0:T(8,128)S(1)}, u32[]{:S(2)}, u32[]{:S(2)}) collective-permute-start(f32[8,128]{1,0:T(8,128)S(1)} %get-tuple-element.92), channel_id=1, source_target_pairs={{1,25},{3,27},{5,29},{7,31},{9,17},{11,19},{13,21},{15,23},{17,9},... | collective-permute-start | bytes 12296 | tf_op jit(solution)/shard_map/ppermute | solution.py:738
  49.5 1.4 %collective-permute-start.17 = (f32[8,128]{1,0:T(8,128)S(1)}, f32[8,128]{1,0:T(8,128)S(1)}, u32[]{:S(2)}, u32[]{:S(2)}) collective-permute-start(f32[8,128]{1,0:T(8,128)S(1)} %get-tuple-element.92), channel_id=1, source_target_pairs={{1,17},{3,19},{5,21},{7,23},{9,25},{11,27},{13,29},{15,31},{17,1},... | collective-permute-start | bytes 12296 | tf_op jit(solution)/shard_map/ppermute | solution.py:738
  50.2 0.7 collective-permute-start.16
  50.9 17.7 %collective-permute-start.19 = (f32[8,128]{1,0:T(8,128)S(1)}, f32[8,128]{1,0:T(8,128)S(1)}, u32[]{:S(2)}, u32[]{:S(2)}) collective-permute-start(f32[8,128]{1,0:T(8,128)S(1)} %maximum_maximum_fusion), channel_id=1, source_target_pairs={{1,0},{3,2},{5,4},{7,6},{9,8},{11,10},{13,12},{15,14},{17,16},{19,... | collective-permute-start | bytes 12296 | tf_op jit(solution)/shard_map/ppermute | solution.py:744

commit v5 on v3

--- a/solution.py
+++ b/solution.py
@@ -726,17 +726,27 @@
 
 
 def largest_of_all(peak, sizes, beside):
+    nx, ny = sizes
+    peak = jnp.maximum(peak, lax.ppermute(peak, "gy", [(i, i ^ 1) for i in range(ny)]))
     groups = 0
-    for axis, count, widths in (("gy", sizes[1], (2, 4, 4)), ("gx", sizes[0], (4, 2))):
-        step = 1
+    for axis, count, first, widths in (("gy", ny, 2, (4, 4)), ("gx", nx, 1, (4, 2))):
+        step = first
         for width in widths:
             width = min(width, count // step)
-            parts = [
-                lax.ppermute(peak, axis, [(i, i ^ (n * step)) for i in range(count)])
-                for n in range(1, width)
-            ]
+            parts = []
+            for n in range(1, width):
+                if axis == "gy":
+                    pairs = [(i, i ^ (n * step) ^ 1) for i in range(ny)]
+                    parts.append(lax.ppermute(peak, "gy", pairs))
+                else:
+                    pairs = [
+                        (i * ny + y, (i ^ (n * step)) * ny + (y ^ 1))
+                        for i in range(nx)
+                        for y in range(ny)
+                    ]
+                    parts.append(lax.ppermute(peak, ("gx", "gy"), pairs))
             groups += 1
-            if groups == 2:
+            if groups == 1:
                 peak = beside(peak)
             peak = functools.reduce(jnp.maximum, parts, peak)
             step *= width

time: 54.3 us -> 53.2 us (0.980)
  starting transfers between devices: 25.8 us -> 24.9 us
    ppermute x7, starting transfers between devices: 7.95 us -> 7.03 us  [the longest x3 3.98 us: largest_of_all(): parts.append(lax.ppermute(peak, ('gx', 'gy'), pairs))]
where the time goes in v5:
time: 53.2 us; the launch traced here: 53 us
  starting transfers between devices  24.9 us (47%)
  Pallas kernels  18.8 us (35%)
  waiting for transfers between devices  8.46 us (16%)
  between operations  0.81 us (2%)
    pallas_call x12, Pallas kernels, call(): pl.pallas_call(functools.partial(kernel, g), in_specs=in_specs, out_shape...  18.8 us
    ppermute x6, starting transfers between devices, swap(): lax.ppermute(second, axis, swap_pairs(count, 1))  14.6 us
    ppermute x6, waiting for transfers between devices, swap(): lax.ppermute(second, axis, swap_pairs(count, 1))  6.44 us
    ppermute x3, starting transfers between devices, largest_of_all(): parts.append(lax.ppermute(peak, ('gx', 'gy'), pairs))  3.98 us
    ppermute x6, starting transfers between devices, swap(): lax.ppermute(first, axis, swap_pairs(count, 0))  3.26 us
    ppermute x3, starting transfers between devices, largest_of_all(): parts.append(lax.ppermute(peak, 'gy', pairs))  2.98 us
    ppermute x1, waiting for transfers between devices, largest_of_all(): lax.ppermute(peak, 'gy', [(i, i ^ 1) for i in range(ny)])  1.15 us
  transfers between devices with their start and end apart: 19, of which 7 were waited for; matrix products, arithmetic and copies ran while one was open for 0% of the time, Pallas kernels for 20%

profile of v5, /device:TPU:0, one launch (start us, length us, event | category | flops | bytes accessed | tf_op | source)
XLA Modules:
  0.0 53.0 jit_solution(16224061043686033484)
XLA Ops:
  0.6 3.1 %rim_first.1 = (f32[14408,128]{1,0:T(8,128)S(1)}, f32[1792,128]{1,0:T(8,128)S(1)}, f32[8,27,32,128]{3,2,1,0:T(8,128)S(1)}, f32[240,128]{1,0:T(8,128)S(1)}, f32[2...) custom-call(f32[27,32,1024]{2,1,0:T(8,128)} %pops.1, f32[32,1024]{1,0:T(8,128)} %refs_0_.1, ...), custom_call_target="tpu_custom_call" | custom-call | tf_op jit(solution)/shard_map/rim_first/pallas_call | solution.py:794
  3.7 3.4 %collective-permute-start = (f32[480,128]{1,0:T(8,128)S(1)}, f32[480,128]{1,0:T(8,128)S(1)}, u32[]{:S(2)}, u32[]{:S(2)}) collective-permute-start(f32[480,128]{1,0:T(8,128)S(1)} %get-tuple-element.52), channel_id=1, source_target_pairs={{1,2},{2,1},{3,4},{4,3},{5,6},{6,5},{7,0},{0,7},{9,10},{10,9},{11,... | collective-permute-start | bytes 737288 | tf_op jit(solution)/shard_map/ppermute | solution.py:724
  7.1 0.0 collective-permute-start.1
  7.1 3.6 %collective-permute-start.2 = (f32[240,128]{1,0:T(8,128)S(1)}, f32[240,128]{1,0:T(8,128)S(1)}, u32[]{:S(2)}, u32[]{:S(2)}) collective-permute-start(f32[240,128]{1,0:T(8,128)S(1)} %get-tuple-element.57), channel_id=1, source_target_pairs={{8,16},{16,8},{24,0},{0,24},{9,17},{17,9},{25,1},{1,25},{10,18},{1... | collective-permute-start | bytes 368648 | tf_op jit(solution)/shard_map/ppermute | solution.py:724
  10.7 0.0 collective-permute-start.3
  10.7 1.4 %inner_first.1 = (f32[14408,128]{1,0:T(8,128)S(1)}, f32[1792,128]{1,0:T(8,128)S(1)}, f32[12968,128]{1,0:T(8,128)S(1)}, f32[2184,128]{1,0:T(8,128)S(1)}) custom-call(f32[14408,128]{1,0:T(8,128)S(1)} %get-tuple-element.48._, f32[1792,128]{1,0:T(8,128)S(1)} %get-tuple-element.49._state, ...), custom_call_target="tpu_custom_call", output_to_operand_aliasing={{0}: (0, {}), {1}: (1, {})} | custom-call | bytes 12582912 | tf_op jit(solution)/shard_map/inner_first/pallas_call | solution.py:794
  12.1 0.0 copy-start
  12.1 0.7 %collective-permute-done.refs_1_ = f32[480,128]{1,0:T(8,128)S(1)} collective-permute-done((f32[480,128]{1,0:T(8,128)S(1)}, f32[480,128]{1,0:T(8,128)S(1)}, u32[]{:S(2)}, u32[]{:S(2)}) %collective-permute-start) | collective-permute-done | bytes 245792 | tf_op jit(solution)/shard_map/ppermute | solution.py:724
  12.8 0.0 collective-permute-done.1.refs_2_
  12.8 0.1 relay.2
  12.9 3.1 %collective-permute-start.4 = (f32[32,128]{1,0:T(8,128)S(1)}, f32[32,128]{1,0:T(8,128)S(1)}, u32[]{:S(2)}, u32[]{:S(2)}) collective-permute-start(f32[32,128]{1,0:T(8,128)S(1)} %get-tuple-element.64), channel_id=1, source_target_pairs={{0,8},{8,0},{16,24},{24,16},{1,9},{9,1},{17,25},{25,17},{2,10},{10... | collective-permute-start | bytes 49160 | tf_op jit(solution)/shard_map/ppermute | solution.py:723
  16.1 2.5 %collective-permute-start.5 = (f32[32,128]{1,0:T(8,128)S(1)}, f32[32,128]{1,0:T(8,128)S(1)}, u32[]{:S(2)}, u32[]{:S(2)}) collective-permute-start(f32[32,128]{1,0:T(8,128)S(1)} %get-tuple-element.65), channel_id=1, source_target_pairs={{8,16},{16,8},{24,0},{0,24},{9,17},{17,9},{25,1},{1,25},{10,18},{1... | collective-permute-start | bytes 49160 | tf_op jit(solution)/shard_map/ppermute | solution.py:724
  18.5 0.0 collective-permute-done.2.b
  18.5 0.0 collective-permute-done.3.a
  18.5 0.0 copy-done
  18.5 2.0 %middle_second.1 = (f32[14408,128]{1,0:T(8,128)S(1)}, f32[12968,128]{1,0:T(8,128)S(1)}, f32[2184,128]{1,0:T(8,128)S(1)}, f32[8,27,32,128]{3,2,1,0:T(8,128)S(1)}, f32[12968,128]{1,0:T(8,128)S(1)}) custom-call(f32[14408,128]{1,0:T(8,128)S(1)} %get-tuple-element.54._post, ...), custom_call_target="tpu_custom_call", output_to_operand_aliasing={{0}: (0, {}), {1}: (1, {}), {2}: (2, {})} | custom-call | bytes 12582912 | tf_op jit(solution)/shard_map/middle_second/pallas_call | solution.py:794
  20.5 0.0 collective-permute-done.4.first
  20.5 1.1 %collective-permute-done.5.second = f32[32,128]{1,0:T(8,128)S(1)} collective-permute-done((f32[32,128]{1,0:T(8,128)S(1)}, f32[32,128]{1,0:T(8,128)S(1)}, u32[]{:S(2)}, u32[]{:S(2)}) %collective-permute-start.5) | collective-permute-done | bytes 16416 | tf_op jit(solution)/shard_map/ppermute | solution.py:724
  21.6 2.3 %rim_seed.1 = (f32[14408,128]{1,0:T(8,128)S(1)}, f32[12968,128]{1,0:T(8,128)S(1)}, f32[2184,128]{1,0:T(8,128)S(1)}, f32[8,27,32,128]{3,2,1,0:T(8,128)S(1)}, f32[...) custom-call(f32[14408,128]{1,0:T(8,128)S(1)} %get-tuple-element.59._, ...), custom_call_target="tpu_custom_call", output_to_operand_aliasing={{0}: (0, {}), {1}: (1, {}), {2}: (2, {}), {3}: (3, {}), {4}... | custom-call | tf_op jit(solution)/shard_map/rim_seed/pallas_call | solution.py:794
  23.9 0.1 collective-permute-start.6
  23.9 0.1 collective-permute-start.7
  24.0 2.5 %collective-permute-start.8 = (f32[216,128]{1,0:T(8,128)S(1)}, f32[216,128]{1,0:T(8,128)S(1)}, u32[]{:S(2)}, u32[]{:S(2)}) collective-permute-start(f32[216,128]{1,0:T(8,128)S(1)} %get-tuple-element.78), channel_id=1, source_target_pairs={{8,16},{16,8},{24,0},{0,24},{9,17},{17,9},{25,1},{1,25},{10,18},{1... | collective-permute-start | bytes 331784 | tf_op jit(solution)/shard_map/ppermute | solution.py:724
  26.6 0.0 collective-permute-start.9
  26.6 1.9 %inner_seed.1 = (f32[8,27,32,128]{3,2,1,0:T(8,128)S(1)}, f32[12968,128]{1,0:T(8,128)S(1)}, f32[12968,128]{1,0:T(8,128)S(1)}, f32[312,128]{1,0:T(8,128)S(1)}, f32[27,32,1024]{2,1,0:T(8,128)}) custom-call(f32[8,27,32,128]{3,2,1,0:T(8,128)S(1)} %get-tuple-element.66.kept, ...), custom_call_target="tpu_custom_call", output_to_operand_aliasing={{0}: (0, {}), {1}: (1, {})} | custom-call | bytes 12582912 | tf_op jit(solution)/shard_map/inner_seed/pallas_call | solution.py:794
  28.4 3.6 %collective-permute-done.6.refs_1_ = f32[448,128]{1,0:T(8,128)S(1)} collective-permute-done((f32[448,128]{1,0:T(8,128)S(1)}, f32[448,128]{1,0:T(8,128)S(1)}, u32[]{:S(2)}, u32[]{:S(2)}) %collective-permute-start.6) | collective-permute-done | bytes 229408 | tf_op jit(solution)/shard_map/ppermute | solution.py:724
  32.0 0.0 collective-permute-done.7.refs_2_
  32.0 0.1 relay.3
  32.1 0.1 collective-permute-start.10
  32.2 2.5 %collective-permute-start.11 = (f32[32,128]{1,0:T(8,128)S(1)}, f32[32,128]{1,0:T(8,128)S(1)}, u32[]{:S(2)}, u32[]{:S(2)}) collective-permute-start(f32[32,128]{1,0:T(8,128)S(1)} %get-tuple-element.86), channel_id=1, source_target_pairs={{8,16},{16,8},{24,0},{0,24},{9,17},{17,9},{25,1},{1,25},{10,18},{1... | collective-permute-start | bytes 49160 | tf_op jit(solution)/shard_map/ppermute | solution.py:724
  34.8 0.0 collective-permute-done.8.b
  34.8 0.0 collective-permute-done.9.a
  34.8 1.9 %middle_adjoint.1 = (f32[12968,128]{1,0:T(8,128)S(1)}, f32[12968,128]{1,0:T(8,128)S(1)}, f32[312,128]{1,0:T(8,128)S(1)}, f32[256,128]{1,0:T(8,128)S(1)}, f32[1280,128]{1,0:T(8,128)S(1)}) custom-call(f32[12968,128]{1,0:T(8,128)S(1)} %get-tuple-element.74._field, ...), custom_call_target="tpu_custom_call", output_to_operand_aliasing={{0}: (0, {}), {1}: (1, {}), {2}: (2, {})} | custom-call | bytes 12582912 | tf_op jit(solution)/shard_map/middle_adjoint/pallas_call | solution.py:794
  36.7 0.0 collective-permute-done.10.refs_7_
  36.7 1.1 %collective-permute-done.11.refs_8_ = f32[32,128]{1,0:T(8,128)S(1)} collective-permute-done((f32[32,128]{1,0:T(8,128)S(1)}, f32[32,128]{1,0:T(8,128)S(1)}, u32[]{:S(2)}, u32[]{:S(2)}) %collective-permute-start.11) | collective-permute-done | bytes 16416 | tf_op jit(solution)/shard_map/ppermute | solution.py:724
  37.8 2.1 %total.1 = (f32[12968,128]{1,0:T(8,128)S(1)}, f32[12968,128]{1,0:T(8,128)S(1)}, f32[312,128]{1,0:T(8,128)S(1)}, f32[256,128]{1,0:T(8,128)S(1)}, f32[1280,128]{1,0:T(8,128)S(1)}, /*index=5*/f32[8,128]{1,0:T(8,128)S(1)}) custom-call(f32[12968,128]{1,0:T(8,128)S(1)} %get-tuple-element.80.r, ...), custom_call_target="tpu_custom_call", output_to_operand_aliasing={{0}: (0, {}), {1}: (1, {}), {2}: (2, {}), {3}: (3, {}), {4}... | custom-call | tf_op jit(solution)/shard_map/total/pallas_call | solution.py:794
  39.9 0.1 collective-permute-start.12
  40.0 1.2 %collective-permute-done.12 = f32[8,128]{1,0:T(8,128)S(1)} collective-permute-done((f32[8,128]{1,0:T(8,128)S(1)}, f32[8,128]{1,0:T(8,128)S(1)}, u32[]{:S(2)}, u32[]{:S(2)}) %collective-permute-start.12) | collective-permute-done | bytes 4128 | tf_op jit(solution)/shard_map/ppermute | solution.py:730
  41.1 1.1 %collective-permute-start.15 = (f32[8,128]{1,0:T(8,128)S(1)}, f32[8,128]{1,0:T(8,128)S(1)}, u32[]{:S(2)}, u32[]{:S(2)}) collective-permute-start(f32[8,128]{1,0:T(8,128)S(1)} %max.21.near), channel_id=1, source_target_pairs={{0,7},{1,6},{2,5},{3,4},{4,3},{5,2},{6,1},{7,0},{8,15},{9,14},{10,... | collective-permute-start | bytes 12296 | tf_op jit(solution)/shard_map/ppermute | solution.py:740
  42.2 0.7 %collective-permute-start.14 = (f32[8,128]{1,0:T(8,128)S(1)}, f32[8,128]{1,0:T(8,128)S(1)}, u32[]{:S(2)}, u32[]{:S(2)}) collective-permute-start(f32[8,128]{1,0:T(8,128)S(1)} %max.21.near), channel_id=1, source_target_pairs={{0,5},{1,4},{2,7},{3,6},{4,1},{5,0},{6,3},{7,2},{8,13},{9,12},{10,... | collective-permute-start | bytes 12296 | tf_op jit(solution)/shard_map/ppermute | solution.py:740
  42.9 1.3 %collective-permute-start.13 = (f32[8,128]{1,0:T(8,128)S(1)}, f32[8,128]{1,0:T(8,128)S(1)}, u32[]{:S(2)}, u32[]{:S(2)}) collective-permute-start(f32[8,128]{1,0:T(8,128)S(1)} %max.21.near), channel_id=1, source_target_pairs={{0,3},{1,2},{2,1},{3,0},{4,7},{5,6},{6,5},{7,4},{8,11},{9,10},{10,... | collective-permute-start | bytes 12296 | tf_op jit(solution)/shard_map/ppermute | solution.py:740
  44.1 1.6 %adjoint_low.1 = (f32[8,128]{1,0:T(8,128)S(1)}, f32[27,32,1024]{2,1,0:T(8,128)}) custom-call(f32[12968,128]{1,0:T(8,128)S(1)} %get-tuple-element.87.buf, f32[1280,128]{1,0:T(8,128)S(1)} %get-tuple-element.88.fields, f32[8,128]{1,0:T(8,128)S(1)} %max.21.near), custom_call_target="tpu_custom_call" | custom-call | bytes 6291456 | tf_op jit(solution)/shard_map/adjoint_low/pallas_call | solution.py:794
  45.7 0.0 collective-permute-done.15
  45.7 0.0 collective-permute-done.14
  45.8 0.2 collective-permute-done.13
  45.9 2.4 %collective-permute-start.18 = (f32[8,128]{1,0:T(8,128)S(1)}, f32[8,128]{1,0:T(8,128)S(1)}, u32[]{:S(2)}, u32[]{:S(2)}) collective-permute-start(f32[8,128]{1,0:T(8,128)S(1)} %maximum_maximum_fusion.1), channel_id=1, source_target_pairs={{0,25},{1,24},{2,27},{3,26},{4,29},{5,28},{6,31},{7,30},{8,17},{9,... | collective-permute-start | bytes 12296 | tf_op jit(solution)/shard_map/ppermute | solution.py:747
  48.3 0.0 collective-permute-start.17
  48.3 1.6 %collective-permute-start.16 = (f32[8,128]{1,0:T(8,128)S(1)}, f32[8,128]{1,0:T(8,128)S(1)}, u32[]{:S(2)}, u32[]{:S(2)}) collective-permute-start(f32[8,128]{1,0:T(8,128)S(1)} %maximum_maximum_fusion.1), channel_id=1, source_target_pairs={{0,9},{1,8},{2,11},{3,10},{4,13},{5,12},{6,15},{7,14},{8,1},{9,0},... | collective-permute-start | bytes 12296 | tf_op jit(solution)/shard_map/ppermute | solution.py:747
  49.9 1.6 %adjoint_high.1 = f32[27,32,1024]{2,1,0:T(8,128)} custom-call(f32[12968,128]{1,0:T(8,128)S(1)} %get-tuple-element.87.buf, f32[1280,128]{1,0:T(8,128)S(1)} %get-tuple-element.88.fields, f32[27,32,1024]{2,1,0:T(8,128)} %get-tuple-element.90._), custom_call_target="tpu_custom_call", output_to_operand_aliasing={{}: (2, {})} | custom-call | bytes 6291456 | tf_op jit(solution)/shard_map/adjoint_high/pallas_call | solution.py:794
  51.5 0.0 collective-permute-done.18
  51.5 0.7 %collective-permute-done.17 = f32[8,128]{1,0:T(8,128)S(1)} collective-permute-done((f32[8,128]{1,0:T(8,128)S(1)}, f32[8,128]{1,0:T(8,128)S(1)}, u32[]{:S(2)}, u32[]{:S(2)}) %collective-permute-start.17) | collective-permute-done | bytes 4128 | tf_op jit(solution)/shard_map/ppermute | solution.py:747
  52.2 0.0 collective-permute-done.16
  52.2 0.8 %normalize.1 = f32[32,1024]{1,0:T(8,128)} custom-call(f32[256,128]{1,0:T(8,128)S(1)} %get-tuple-element.91.total, f32[8,128]{1,0:T(8,128)S(1)} %maximum_maximum_fusion.peak), custom_call_target="tpu_custom_call" | custom-call | tf_op jit(solution)/shard_map/normalize/pallas_call | solution.py:794
  (3 shorter events, 0.0 us)
Async XLA Ops:
  3.7 9.1 %collective-permute-start = (f32[480,128]{1,0:T(8,128)S(1)}, f32[480,128]{1,0:T(8,128)S(1)}, u32[]{:S(2)}, u32[]{:S(2)}) collective-permute-start(f32[480,128]{1,0:T(8,128)S(1)} %get-tuple-element.52), channel_id=1, source_target_pairs={{1,2},{2,1},{3,4},{4,3},{5,6},{6,5},{7,0},{0,7},{9,10},{10,9},{11,... | collective-permute-start | bytes 737288 | tf_op jit(solution)/shard_map/ppermute | solution.py:724
  7.1 5.7 %collective-permute-start.1 = (f32[480,128]{1,0:T(8,128)S(1)}, f32[480,128]{1,0:T(8,128)S(1)}, u32[]{:S(2)}, u32[]{:S(2)}) collective-permute-start(f32[480,128]{1,0:T(8,128)S(1)} %get-tuple-element.53), channel_id=1, source_target_pairs={{0,1},{1,0},{2,3},{3,2},{4,5},{5,4},{6,7},{7,6},{8,9},{9,8},{10,11... | collective-permute-start | bytes 737288 | tf_op jit(solution)/shard_map/ppermute | solution.py:723
  7.1 11.4 %collective-permute-start.2 = (f32[240,128]{1,0:T(8,128)S(1)}, f32[240,128]{1,0:T(8,128)S(1)}, u32[]{:S(2)}, u32[]{:S(2)}) collective-permute-start(f32[240,128]{1,0:T(8,128)S(1)} %get-tuple-element.57), channel_id=1, source_target_pairs={{8,16},{16,8},{24,0},{0,24},{9,17},{17,9},{25,1},{1,25},{10,18},{1... | collective-permute-start | bytes 368648 | tf_op jit(solution)/shard_map/ppermute | solution.py:724
  10.7 7.8 %collective-permute-start.3 = (f32[240,128]{1,0:T(8,128)S(1)}, f32[240,128]{1,0:T(8,128)S(1)}, u32[]{:S(2)}, u32[]{:S(2)}) collective-permute-start(f32[240,128]{1,0:T(8,128)S(1)} %get-tuple-element.58), channel_id=1, source_target_pairs={{0,8},{8,0},{16,24},{24,16},{1,9},{9,1},{17,25},{25,17},{2,10},{10... | collective-permute-start | bytes 368648 | tf_op jit(solution)/shard_map/ppermute | solution.py:723
  12.1 6.4 %copy-start = (f32[27,32,1024]{2,1,0:T(8,128)S(1)}, f32[27,32,1024]{2,1,0:T(8,128)}, u32[]{:S(2)}) copy-start(f32[27,32,1024]{2,1,0:T(8,128)} %refs_1_.3) | copy-start | bytes 10616836
  12.9 7.6 %collective-permute-start.4 = (f32[32,128]{1,0:T(8,128)S(1)}, f32[32,128]{1,0:T(8,128)S(1)}, u32[]{:S(2)}, u32[]{:S(2)}) collective-permute-start(f32[32,128]{1,0:T(8,128)S(1)} %get-tuple-element.64), channel_id=1, source_target_pairs={{0,8},{8,0},{16,24},{24,16},{1,9},{9,1},{17,25},{25,17},{2,10},{10... | collective-permute-start | bytes 49160 | tf_op jit(solution)/shard_map/ppermute | solution.py:723
  16.1 5.5 %collective-permute-start.5 = (f32[32,128]{1,0:T(8,128)S(1)}, f32[32,128]{1,0:T(8,128)S(1)}, u32[]{:S(2)}, u32[]{:S(2)}) collective-permute-start(f32[32,128]{1,0:T(8,128)S(1)} %get-tuple-element.65), channel_id=1, source_target_pairs={{8,16},{16,8},{24,0},{0,24},{9,17},{17,9},{25,1},{1,25},{10,18},{1... | collective-permute-start | bytes 49160 | tf_op jit(solution)/shard_map/ppermute | solution.py:724
  23.9 8.1 %collective-permute-start.6 = (f32[448,128]{1,0:T(8,128)S(1)}, f32[448,128]{1,0:T(8,128)S(1)}, u32[]{:S(2)}, u32[]{:S(2)}) collective-permute-start(f32[448,128]{1,0:T(8,128)S(1)} %get-tuple-element.72), channel_id=1, source_target_pairs={{1,2},{2,1},{3,4},{4,3},{5,6},{6,5},{7,0},{0,7},{9,10},{10,9},{11,... | collective-permute-start | bytes 688136 | tf_op jit(solution)/shard_map/ppermute | solution.py:724
  23.9 8.1 %collective-permute-start.7 = (f32[448,128]{1,0:T(8,128)S(1)}, f32[448,128]{1,0:T(8,128)S(1)}, u32[]{:S(2)}, u32[]{:S(2)}) collective-permute-start(f32[448,128]{1,0:T(8,128)S(1)} %get-tuple-element.73), channel_id=1, source_target_pairs={{0,1},{1,0},{2,3},{3,2},{4,5},{5,4},{6,7},{7,6},{8,9},{9,8},{10,11... | collective-permute-start | bytes 688136 | tf_op jit(solution)/shard_map/ppermute | solution.py:723
  24.0 10.7 %collective-permute-start.8 = (f32[216,128]{1,0:T(8,128)S(1)}, f32[216,128]{1,0:T(8,128)S(1)}, u32[]{:S(2)}, u32[]{:S(2)}) collective-permute-start(f32[216,128]{1,0:T(8,128)S(1)} %get-tuple-element.78), channel_id=1, source_target_pairs={{8,16},{16,8},{24,0},{0,24},{9,17},{17,9},{25,1},{1,25},{10,18},{1... | collective-permute-start | bytes 331784 | tf_op jit(solution)/shard_map/ppermute | solution.py:724
  26.6 8.2 %collective-permute-start.9 = (f32[216,128]{1,0:T(8,128)S(1)}, f32[216,128]{1,0:T(8,128)S(1)}, u32[]{:S(2)}, u32[]{:S(2)}) collective-permute-start(f32[216,128]{1,0:T(8,128)S(1)} %get-tuple-element.79), channel_id=1, source_target_pairs={{0,8},{8,0},{16,24},{24,16},{1,9},{9,1},{17,25},{25,17},{2,10},{10... | collective-permute-start | bytes 331784 | tf_op jit(solution)/shard_map/ppermute | solution.py:723
  32.1 4.5 %collective-permute-start.10 = (f32[32,128]{1,0:T(8,128)S(1)}, f32[32,128]{1,0:T(8,128)S(1)}, u32[]{:S(2)}, u32[]{:S(2)}) collective-permute-start(f32[32,128]{1,0:T(8,128)S(1)} %get-tuple-element.85), channel_id=1, source_target_pairs={{0,8},{8,0},{16,24},{24,16},{1,9},{9,1},{17,25},{25,17},{2,10},{10... | collective-permute-start | bytes 49160 | tf_op jit(solution)/shard_map/ppermute | solution.py:723
  32.2 5.6 %collective-permute-start.11 = (f32[32,128]{1,0:T(8,128)S(1)}, f32[32,128]{1,0:T(8,128)S(1)}, u32[]{:S(2)}, u32[]{:S(2)}) collective-permute-start(f32[32,128]{1,0:T(8,128)S(1)} %get-tuple-element.86), channel_id=1, source_target_pairs={{8,16},{16,8},{24,0},{0,24},{9,17},{17,9},{25,1},{1,25},{10,18},{1... | collective-permute-start | bytes 49160 | tf_op jit(solution)/shard_map/ppermute | solution.py:724
  39.9 1.2 %collective-permute-start.12 = (f32[8,128]{1,0:T(8,128)S(1)}, f32[8,128]{1,0:T(8,128)S(1)}, u32[]{:S(2)}, u32[]{:S(2)}) collective-permute-start(f32[8,128]{1,0:T(8,128)S(1)} %get-tuple-element.89), channel_id=1, source_target_pairs={{0,1},{1,0},{2,3},{3,2},{4,5},{5,4},{6,7},{7,6},{8,9},{9,8},{10,11... | collective-permute-start | bytes 12296 | tf_op jit(solution)/shard_map/ppermute | solution.py:730
  41.1 4.6 %collective-permute-start.15 = (f32[8,128]{1,0:T(8,128)S(1)}, f32[8,128]{1,0:T(8,128)S(1)}, u32[]{:S(2)}, u32[]{:S(2)}) collective-permute-start(f32[8,128]{1,0:T(8,128)S(1)} %max.21.near), channel_id=1, source_target_pairs={{0,7},{1,6},{2,5},{3,4},{4,3},{5,2},{6,1},{7,0},{8,15},{9,14},{10,... | collective-permute-start | bytes 12296 | tf_op jit(solution)/shard_map/ppermute | solution.py:740
  42.2 3.5 %collective-permute-start.14 = (f32[8,128]{1,0:T(8,128)S(1)}, f32[8,128]{1,0:T(8,128)S(1)}, u32[]{:S(2)}, u32[]{:S(2)}) collective-permute-start(f32[8,128]{1,0:T(8,128)S(1)} %max.21.near), channel_id=1, source_target_pairs={{0,5},{1,4},{2,7},{3,6},{4,1},{5,0},{6,3},{7,2},{8,13},{9,12},{10,... | collective-permute-start | bytes 12296 | tf_op jit(solution)/shard_map/ppermute | solution.py:740
  42.9 3.0 %collective-permute-start.13 = (f32[8,128]{1,0:T(8,128)S(1)}, f32[8,128]{1,0:T(8,128)S(1)}, u32[]{:S(2)}, u32[]{:S(2)}) collective-permute-start(f32[8,128]{1,0:T(8,128)S(1)} %max.21.near), channel_id=1, source_target_pairs={{0,3},{1,2},{2,1},{3,0},{4,7},{5,6},{6,5},{7,4},{8,11},{9,10},{10,... | collective-permute-start | bytes 12296 | tf_op jit(solution)/shard_map/ppermute | solution.py:740
  45.9 5.6 %collective-permute-start.18 = (f32[8,128]{1,0:T(8,128)S(1)}, f32[8,128]{1,0:T(8,128)S(1)}, u32[]{:S(2)}, u32[]{:S(2)}) collective-permute-start(f32[8,128]{1,0:T(8,128)S(1)} %maximum_maximum_fusion.1), channel_id=1, source_target_pairs={{0,25},{1,24},{2,27},{3,26},{4,29},{5,28},{6,31},{7,30},{8,17},{9,... | collective-permute-start | bytes 12296 | tf_op jit(solution)/shard_map/ppermute | solution.py:747
  48.3 3.9 %collective-permute-start.17 = (f32[8,128]{1,0:T(8,128)S(1)}, f32[8,128]{1,0:T(8,128)S(1)}, u32[]{:S(2)}, u32[]{:S(2)}) collective-permute-start(f32[8,128]{1,0:T(8,128)S(1)} %maximum_maximum_fusion.1), channel_id=1, source_target_pairs={{0,17},{1,16},{2,19},{3,18},{4,21},{5,20},{6,23},{7,22},{8,25},{9,... | collective-permute-start | bytes 12296 | tf_op jit(solution)/shard_map/ppermute | solution.py:747
  48.3 3.9 %collective-permute-start.16 = (f32[8,128]{1,0:T(8,128)S(1)}, f32[8,128]{1,0:T(8,128)S(1)}, u32[]{:S(2)}, u32[]{:S(2)}) collective-permute-start(f32[8,128]{1,0:T(8,128)S(1)} %maximum_maximum_fusion.1), channel_id=1, source_target_pairs={{0,9},{1,8},{2,11},{3,10},{4,13},{5,12},{6,15},{7,14},{8,1},{9,0},... | collective-permute-start | bytes 12296 | tf_op jit(solution)/shard_map/ppermute | solution.py:747

commit v6 on v5

--- a/solution.py
+++ b/solution.py
@@ -321,7 +321,8 @@
     return 9 + len(still_pairs(fields, sign))
 
 
-def pack_y(g, buf, sign, fields, high, up, down):
+def pack_y(g, buf, sign, fields, up, down):
+    high = lane_masks(g.rows)[0]
     for side, ref in ((1, up), (-1, down)):
         k = g.cols if side == 1 else 1
         for n, i in enumerate(moving(fields, sign, 1, side)):
@@ -531,80 +532,72 @@
     return ref.at[:, :, lanes_of(k)]
 
 
-def pack_faces(g, buf, sign, fields, x_first, x_second, y_first, y_second):
-    high = lane_masks(g.rows)[0]
-    by_parity("gx", x_first, x_second, functools.partial(pack_x, g, buf, sign, fields))
-    by_parity("gy", y_first, y_second, functools.partial(pack_y, g, buf, sign, fields, high))
-
-
-def rim_first_kernel(g, pops, *refs):
-    flat, (out, state, stage, *faces), near, (sems, flat_sems) = (
+def flat_fields(g, out, near, k):
+    porosity, solid, labels = near
+    lanes = lanes_of(k)
+    label = labels[:, lanes]
+    damp = 1.0 / (1.0 + porosity[:, lanes])
+    push = jnp.where(label == 1, PUSH, jnp.where(label == 2, -PUSH, 0.0))
+    base = pl.multiple_of(k * g.panel, 8)
+    for i, value in ((27, damp), (28, push), (29, solid[:, lanes].astype(F32))):
+        out[pl.ds(base + g.field(i), g.rows), :] = value
+
+
+def staged_tile(g, collide, stage):
+    def act(k, pieces):
+        collide(k, pieces, [read_rows(stage.at[k - 1, i], 0, pieces) for i in range(27)])
+
+    return act
+
+
+def side_tiles(g, act):
+    for pieces in (g.outer,) + g.inner:
+        side_panels(g, functools.partial(act, pieces=pieces), 2)
+
+
+def side_first_kernel(g, pops, *refs):
+    flat, (out, state, stage), near, faces, (sems, flat_sems) = (
         refs[:3],
-        refs[3:10],
-        refs[10:13],
-        refs[13:],
-    )
-    porosity, solid, labels = near
-
-    def copy(k, r, n):
-        rows = pl.ds(r, n)
-        source = pops.at[:, rows, lanes_of(k)]
-        part = 0 if r == 0 else 2 if r + n == g.rows else 1
-        return pltpu.make_async_copy(source, stage.at[k - 1, :, rows], sems.at[k - 1, part])
-
-    middle = (8, g.rows - 16)
+        refs[3:6],
+        refs[6:9],
+        refs[9:11],
+        refs[11:],
+    )
+
+    def copy(k):
+        return pltpu.make_async_copy(block_of(pops, k), stage.at[k - 1], sems.at[k - 1])
+
     flat_copies = [
         pltpu.make_async_copy(source, target, flat_sems.at[n])
         for n, (source, target) in enumerate(zip(flat, near))
     ]
     for each in flat_copies:
         each.start()
-    for k in range(1, g.cols + 1):
-        for piece in g.outer:
-            copy(k, *piece).start()
     for k in (1, g.cols, *range(2, g.cols)):
-        copy(k, *middle).start()
+        copy(k).start()
     for each in flat_copies:
         each.wait()
-
-    def fields_of(k):
-        lanes = lanes_of(k)
-        label = labels[:, lanes]
-        damp = 1.0 / (1.0 + porosity[:, lanes])
-        push = jnp.where(label == 1, PUSH, jnp.where(label == 2, -PUSH, 0.0))
-        base = pl.multiple_of(k * g.panel, 8)
-        for i, value in ((27, damp), (28, push), (29, solid[:, lanes].astype(F32))):
-            out[pl.ds(base + g.field(i), g.rows), :] = value
-
-    every(1, g.cols, fields_of)
-    collide = collide_first(g, state, out)
-
-    def act(k, pieces):
-        collide(k, pieces, [read_rows(stage.at[k - 1, i], 0, pieces) for i in range(27)])
-
-    def column(k):
-        for piece in g.outer:
-            copy(k, *piece).wait()
-        act(k, g.outer)
-
-    every(1, g.cols, column)
     for k in (1, g.cols):
-        copy(k, *middle).wait()
-    for pieces in g.inner:
-        side_panels(g, functools.partial(act, pieces=pieces), 2)
-    pack_faces(g, out, 1, 30, *faces)
+        flat_fields(g, out, near, k)
+    copy(1).wait()
+    copy(g.cols).wait()
+    side_tiles(g, staged_tile(g, collide_first(g, state, out), stage))
+    by_parity("gy", *faces, functools.partial(pack_y, g, out, 1, 30))
     for k in range(2, g.cols):
-        copy(k, *middle).wait()
+        copy(k).wait()
+
+
+def rim_first_kernel(g, _out, _state, stage, *refs):
+    near, (out, state), faces = refs[:3], refs[3:5], refs[5:]
+    every(2, g.cols - 1, functools.partial(flat_fields, g, out, near))
+    act = staged_tile(g, collide_first(g, state, out), stage)
+    every(2, g.cols - 1, functools.partial(act, pieces=g.outer))
+    by_parity("gx", *faces, functools.partial(pack_x, g, out, 1, 30))
 
 
 def inner_first_kernel(g, _, _state, stage, post, state0, out, state1):
     masks = lane_masks(16)
-    collide = collide_first(g, state0, post)
-
-    def act(k, pieces):
-        collide(k, pieces, [read_rows(stage.at[k - 1, i], 0, pieces) for i in range(27)])
-
-    interior_tiles(g, act)
+    interior_tiles(g, staged_tile(g, collide_first(g, state0, post), stage))
     interior_tiles(g, step_tile(g, post, out, 1, 30, masks, collide_second(g, state1)))
 
 
@@ -621,13 +614,19 @@
     core_tiles(g, seed_tile(g, out, adjoint, stage, field, masks))
 
 
-def rim_seed_kernel(g, _post, _out, _state, _stage, _field, first, second, adjoint, *refs):
+def side_seed_kernel(g, _post, _out, _state, _stage, _field, first, second, adjoint, *refs):
     post, out, state1, stage, field, *faces = refs
     masks = lane_masks(16)
     by_parity("gx", second, first, functools.partial(unpack_corners, g, post, 1, 30))
     corner_tiles(g, post, out, 1, 30, masks, collide_second(g, state1))
-    rim_tiles(g, seed_tile(g, out, adjoint, stage, field, masks))
-    pack_faces(g, field, -1, 27, *faces)
+    side_tiles(g, seed_tile(g, out, adjoint, stage, field, masks))
+    by_parity("gy", *faces, functools.partial(pack_y, g, field, -1, 27))
+
+
+def rim_seed_kernel(g, _stage, _field, out, adjoint, stage, field, *faces):
+    seed = seed_tile(g, out, adjoint, stage, field, lane_masks(16))
+    every(2, g.cols - 1, functools.partial(seed, pieces=g.outer))
+    by_parity("gx", *faces, functools.partial(pack_x, g, field, -1, 27))
 
 
 def inner_seed_kernel(
@@ -769,10 +768,11 @@
     def padded(count):
         return vmem(*g.padded(count))
 
-    def faces(count, sign):
-        along_x = vmem(count * g.cols, LANES)
-        along_y = vmem(y_slots(count, sign) * rows, LANES)
-        return [along_x, along_x, along_y, along_y]
+    def x_faces(count):
+        return [vmem(count * g.cols, LANES)] * 2
+
+    def y_faces(count, sign):
+        return [vmem(y_slots(count, sign) * rows, LANES)] * 2
 
     def corners(count):
         return [vmem(-(-count // 8) * 8, LANES)] * 2
@@ -784,7 +784,7 @@
     def call(name, kernel, operands, out_shape, scratch=(), kept=0, load=0, result=None):
         out_shape = [pltpu.VMEM(x.shape, x.dtype) for x in operands[:kept]] + out_shape
         aliases = {n: n for n in range(kept)}
-        space = pltpu.HBM if name == "rim_first" else pltpu.VMEM
+        space = pltpu.HBM if name == "side_first" else pltpu.VMEM
         pinned = [pltpu.with_memory_space_constraint(x, space) for x in operands]
         in_specs = [pl.BlockSpec(memory_space=space)] * len(operands)
         if result is not None:
@@ -805,10 +805,8 @@
             name=name,
         )(*pinned)
 
-    def swap_faces(parcels):
-        x_first, x_second = swap("gx", nx, *parcels[:2])
-        y_first, y_second = swap("gy", ny, *parcels[2:])
-        return [x_second, x_first], [y_second, y_first]
+    def swap_faces(axis, count, parcels):
+        return swap(axis, count, *parcels)[::-1]
 
     def relay(buf, parcels, sign, count):
         def kernel(grid, *refs):
@@ -817,16 +815,24 @@
         buf, *parcels = call("relay", kernel, [buf, *parcels], corners(count), kept=1)
         return buf, swap("gx", nx, *parcels)
 
-    post, state0, staged, *parcels = call(
+    flat_space = [vmem(*porosity.shape)] + [pltpu.VMEM(porosity.shape, jnp.int32)] * 2
+    post, state0, staged, *rest = call(
+        "side_first",
+        side_first_kernel,
+        [populations, porosity, solid, labels],
+        [padded(30), fields(7, g.local), stage] + flat_space + y_faces(30, 1),
+        [sems, pltpu.SemaphoreType.DMA((3,))],
+    )
+    along_y = swap_faces("gy", ny, rest[3:])
+    post, state0, *parcels = call(
         "rim_first",
         rim_first_kernel,
-        [populations, porosity, solid, labels],
-        [padded(30), fields(7, g.local), stage] + faces(30, 1),
-        [vmem(*porosity.shape)]
-        + [pltpu.VMEM(porosity.shape, jnp.int32)] * 2
-        + [pltpu.SemaphoreType.DMA((g.cols, 3)), pltpu.SemaphoreType.DMA((3,))],
-    )
-    along_x, along_y = swap_faces(parcels)
+        [post, state0, staged, *rest[:3]],
+        x_faces(30),
+        kept=2,
+        load=FLIGHT,
+    )
+    along_x = swap_faces("gx", nx, parcels)
     post, state0, second, state1 = call(
         "inner_first",
         inner_first_kernel,
@@ -847,13 +853,22 @@
         load=FLIGHT,
     )
     _, second, state1, staged, field, *parcels = call(
+        "side_seed",
+        side_seed_kernel,
+        [post, second, state1, staged, field, *parcels, adjoint_in],
+        y_faces(27, -1),
+        kept=5,
+    )
+    along_y = swap_faces("gy", ny, parcels)
+    staged, field, *parcels = call(
         "rim_seed",
         rim_seed_kernel,
-        [post, second, state1, staged, field, *parcels, adjoint_in],
-        faces(27, -1),
-        kept=5,
-    )
-    along_x, along_y = swap_faces(parcels)
+        [staged, field, second, adjoint_in],
+        x_faces(27),
+        kept=2,
+        load=FLIGHT,
+    )
+    along_x = swap_faces("gx", nx, parcels)
     _, field, pulled, before, final = call(
         "inner_seed",
         lambda grid, kept, into, buf, *refs: inner_seed_kernel(grid, buf, kept, into, *refs),

time: 53.2 us -> 52 us (0.977)
  waiting for transfers between devices: 8.46 us -> 7.2 us
    ppermute x6, waiting for transfers between devices: 6.44 us -> 4.78 us  [swap(): lax.ppermute(second, axis, swap_pairs(count, 1))]
    ppermute x3, waiting for transfers between devices: 0.16 us -> 1.18 us  [largest_of_all(): parts.append(lax.ppermute(peak, 'gy', pairs))]
    ppermute x3, waiting for transfers between devices: 0.69 us -> 0.01 us  [largest_of_all(): parts.append(lax.ppermute(peak, ('gx', 'gy'), pairs))]
    pallas_call x12 -> x14, Pallas kernels: 18.8 us -> 18.9 us  [call(): pl.pallas_call(functools.partial(kernel, g), in_specs=in_specs, out_shape...]
  transfers between devices with their start and end apart: 19 -> 19, of which waited for: 7 -> 7; matrix products, arithmetic and copies ran while one was open for 0% -> 0% of each run, Pallas kernels for 20% -> 23%
where the time goes in v6:
time: 52 us; the launch traced here: 51.8 us
  starting transfers between devices  24.8 us (48%)
  Pallas kernels  18.9 us (36%)
  waiting for transfers between devices  7.2 us (14%)
  between operations  0.85 us (2%)
    pallas_call x14, Pallas kernels, call(): pl.pallas_call(functools.partial(kernel, g), in_specs=in_specs, out_shape...  18.9 us
    ppermute x6, starting transfers between devices, swap(): lax.ppermute(second, axis, swap_pairs(count, 1))  14.4 us
    ppermute x6, waiting for transfers between devices, swap(): lax.ppermute(second, axis, swap_pairs(count, 1))  4.78 us
    ppermute x3, starting transfers between devices, largest_of_all(): parts.append(lax.ppermute(peak, ('gx', 'gy'), pairs))  3.88 us
    ppermute x6, starting transfers between devices, swap(): lax.ppermute(first, axis, swap_pairs(count, 0))  3.53 us
    ppermute x3, starting transfers between devices, largest_of_all(): parts.append(lax.ppermute(peak, 'gy', pairs))  2.98 us
    ppermute x3, waiting for transfers between devices, largest_of_all(): parts.append(lax.ppermute(peak, 'gy', pairs))  1.18 us
    ppermute x1, waiting for transfers between devices, largest_of_all(): lax.ppermute(peak, 'gy', [(i, i ^ 1) for i in range(ny)])  1.15 us
  transfers between devices with their start and end apart: 19, of which 7 were waited for; matrix products, arithmetic and copies ran while one was open for 0% of the time, Pallas kernels for 23%

profile of v6, /device:TPU:0, one launch (start us, length us, event | category | flops | bytes accessed | tf_op | source)
XLA Modules:
  0.0 51.8 jit_solution(17664817919817415283)
XLA Ops:
  0.6 2.6 %side_first.1 = (f32[14408,128]{1,0:T(8,128)S(1)}, f32[1792,128]{1,0:T(8,128)S(1)}, f32[8,27,32,128]{3,2,1,0:T(8,128)S(1)}, f32[32,1024]{1,0:T(8,128)S(1)}, s32[...) custom-call(f32[27,32,1024]{2,1,0:T(8,128)} %pops.1, ...), custom_call_target="tpu_custom_call" | custom-call | tf_op jit(solution)/shard_map/side_first/pallas_call | solution.py:794
  3.2 3.4 %collective-permute-start = (f32[480,128]{1,0:T(8,128)S(1)}, f32[480,128]{1,0:T(8,128)S(1)}, u32[]{:S(2)}, u32[]{:S(2)}) collective-permute-start(f32[480,128]{1,0:T(8,128)S(1)} %get-tuple-element.64), channel_id=1, source_target_pairs={{1,2},{2,1},{3,4},{4,3},{5,6},{6,5},{7,0},{0,7},{9,10},{10,9},{11,... | collective-permute-start | bytes 737288 | tf_op jit(solution)/shard_map/ppermute | solution.py:723
  6.6 0.0 collective-permute-start.1
  6.6 0.6 %rim_first.1 = (f32[14408,128]{1,0:T(8,128)S(1)}, f32[1792,128]{1,0:T(8,128)S(1)}, f32[240,128]{1,0:T(8,128)S(1)}, f32[240,128]{1,0:T(8,128)S(1)}) custom-call(f32[14408,128]{1,0:T(8,128)S(1)} %get-tuple-element.55._out, f32[1792,128]{1,0:T(8,128)S(1)} %get-tuple-element.56._state, ...), custom_call_target="tpu_custom_call", output_to_operand_aliasing={{0}: (0, {}), {1}: (1, {})} | custom-call | bytes 12582912 | tf_op jit(solution)/shard_map/rim_first/pallas_call | solution.py:794
  7.3 3.7 %collective-permute-start.2 = (f32[240,128]{1,0:T(8,128)S(1)}, f32[240,128]{1,0:T(8,128)S(1)}, u32[]{:S(2)}, u32[]{:S(2)}) collective-permute-start(f32[240,128]{1,0:T(8,128)S(1)} %get-tuple-element.69), channel_id=1, source_target_pairs={{8,16},{16,8},{24,0},{0,24},{9,17},{17,9},{25,1},{1,25},{10,18},{1... | collective-permute-start | bytes 368648 | tf_op jit(solution)/shard_map/ppermute | solution.py:723
  10.9 0.0 collective-permute-start.3
  10.9 1.4 %inner_first.1 = (f32[14408,128]{1,0:T(8,128)S(1)}, f32[1792,128]{1,0:T(8,128)S(1)}, f32[12968,128]{1,0:T(8,128)S(1)}, f32[2184,128]{1,0:T(8,128)S(1)}) custom-call(f32[14408,128]{1,0:T(8,128)S(1)} %get-tuple-element.61._, f32[1792,128]{1,0:T(8,128)S(1)} %get-tuple-element.62._state, ...), custom_call_target="tpu_custom_call", output_to_operand_aliasing={{0}: (0, {}), {1}: (1, {})} | custom-call | bytes 12582912 | tf_op jit(solution)/shard_map/inner_first/pallas_call | solution.py:794
  12.3 0.0 copy-start
  12.3 0.0 collective-permute-done.refs_1_
  12.3 0.0 collective-permute-done.1.refs_2_
  12.3 0.1 relay.2
  12.5 3.1 %collective-permute-start.4 = (f32[32,128]{1,0:T(8,128)S(1)}, f32[32,128]{1,0:T(8,128)S(1)}, u32[]{:S(2)}, u32[]{:S(2)}) collective-permute-start(f32[32,128]{1,0:T(8,128)S(1)} %get-tuple-element.76), channel_id=1, source_target_pairs={{0,8},{8,0},{16,24},{24,16},{1,9},{9,1},{17,25},{25,17},{2,10},{10... | collective-permute-start | bytes 49160 | tf_op jit(solution)/shard_map/ppermute | solution.py:722
  15.6 2.5 %collective-permute-start.5 = (f32[32,128]{1,0:T(8,128)S(1)}, f32[32,128]{1,0:T(8,128)S(1)}, u32[]{:S(2)}, u32[]{:S(2)}) collective-permute-start(f32[32,128]{1,0:T(8,128)S(1)} %get-tuple-element.77), channel_id=1, source_target_pairs={{8,16},{16,8},{24,0},{0,24},{9,17},{17,9},{25,1},{1,25},{10,18},{1... | collective-permute-start | bytes 49160 | tf_op jit(solution)/shard_map/ppermute | solution.py:723
  18.0 0.0 collective-permute-done.2.b
  18.0 0.0 collective-permute-done.3.a
  18.0 0.0 copy-done
  18.0 2.0 %middle_second.1 = (f32[14408,128]{1,0:T(8,128)S(1)}, f32[12968,128]{1,0:T(8,128)S(1)}, f32[2184,128]{1,0:T(8,128)S(1)}, f32[8,27,32,128]{3,2,1,0:T(8,128)S(1)}, f32[12968,128]{1,0:T(8,128)S(1)}) custom-call(f32[14408,128]{1,0:T(8,128)S(1)} %get-tuple-element.66._post, ...), custom_call_target="tpu_custom_call", output_to_operand_aliasing={{0}: (0, {}), {1}: (1, {}), {2}: (2, {})} | custom-call | bytes 12582912 | tf_op jit(solution)/shard_map/middle_second/pallas_call | solution.py:794
  20.0 0.0 collective-permute-done.4.first
  20.0 1.1 %collective-permute-done.5.second = f32[32,128]{1,0:T(8,128)S(1)} collective-permute-done((f32[32,128]{1,0:T(8,128)S(1)}, f32[32,128]{1,0:T(8,128)S(1)}, u32[]{:S(2)}, u32[]{:S(2)}) %collective-permute-start.5) | collective-permute-done | bytes 16416 | tf_op jit(solution)/shard_map/ppermute | solution.py:723
  21.1 1.4 %side_seed.1 = (f32[14408,128]{1,0:T(8,128)S(1)}, f32[12968,128]{1,0:T(8,128)S(1)}, f32[2184,128]{1,0:T(8,128)S(1)}, f32[8,27,32,128]{3,2,1,0:T(8,128)S(1)}, f32...) custom-call(f32[14408,128]{1,0:T(8,128)S(1)} %get-tuple-element.71._, ...), custom_call_target="tpu_custom_call", output_to_operand_aliasing={{0}: (0, {}), {1}: (1, {}), {2}: (2, {}), {3}: (3, {}), {4}... | custom-call | tf_op jit(solution)/shard_map/side_seed/pallas_call | solution.py:794
  22.5 0.1 collective-permute-start.6
  22.5 0.4 collective-permute-start.7
  22.9 0.9 %rim_seed.1 = (f32[8,27,32,128]{3,2,1,0:T(8,128)S(1)}, f32[12968,128]{1,0:T(8,128)S(1)}, f32[216,128]{1,0:T(8,128)S(1)}, f32[216,128]{1,0:T(8,128)S(1)}) custom-call(f32[8,27,32,128]{3,2,1,0:T(8,128)S(1)} %get-tuple-element.78._stage, f32[12968,128]{1,0:T(8,128)S(1)} %get-tuple-element.79._field, ...), custom_call_target="tpu_custom_call", output_to_operand_aliasing={{0}: (0, {}), {1}: (1, {})} | custom-call | bytes 12582912 | tf_op jit(solution)/shard_map/rim_seed/pallas_call | solution.py:794
  23.9 2.2 %collective-permute-start.8 = (f32[216,128]{1,0:T(8,128)S(1)}, f32[216,128]{1,0:T(8,128)S(1)}, u32[]{:S(2)}, u32[]{:S(2)}) collective-permute-start(f32[216,128]{1,0:T(8,128)S(1)} %get-tuple-element.92), channel_id=1, source_target_pairs={{8,16},{16,8},{24,0},{0,24},{9,17},{17,9},{25,1},{1,25},{10,18},{1... | collective-permute-start | bytes 331784 | tf_op jit(solution)/shard_map/ppermute | solution.py:723
  26.1 0.0 collective-permute-start.9
  26.1 1.9 %inner_seed.1 = (f32[8,27,32,128]{3,2,1,0:T(8,128)S(1)}, f32[12968,128]{1,0:T(8,128)S(1)}, f32[12968,128]{1,0:T(8,128)S(1)}, f32[312,128]{1,0:T(8,128)S(1)}, f32[27,32,1024]{2,1,0:T(8,128)}) custom-call(f32[8,27,32,128]{3,2,1,0:T(8,128)S(1)} %get-tuple-element.81.kept, ...), custom_call_target="tpu_custom_call", output_to_operand_aliasing={{0}: (0, {}), {1}: (1, {})} | custom-call | bytes 12582912 | tf_op jit(solution)/shard_map/inner_seed/pallas_call | solution.py:794
  28.0 2.6 %collective-permute-done.6.refs_1_ = f32[448,128]{1,0:T(8,128)S(1)} collective-permute-done((f32[448,128]{1,0:T(8,128)S(1)}, f32[448,128]{1,0:T(8,128)S(1)}, u32[]{:S(2)}, u32[]{:S(2)}) %collective-permute-start.6) | collective-permute-done | bytes 229408 | tf_op jit(solution)/shard_map/ppermute | solution.py:723
  30.6 0.0 collective-permute-done.7.refs_2_
  30.6 0.1 relay.3
  30.7 0.1 collective-permute-start.10
  30.8 2.5 %collective-permute-start.11 = (f32[32,128]{1,0:T(8,128)S(1)}, f32[32,128]{1,0:T(8,128)S(1)}, u32[]{:S(2)}, u32[]{:S(2)}) collective-permute-start(f32[32,128]{1,0:T(8,128)S(1)} %get-tuple-element.100), channel_id=1, source_target_pairs={{8,16},{16,8},{24,0},{0,24},{9,17},{17,9},{25,1},{1,25},{10,18},{1... | collective-permute-start | bytes 49160 | tf_op jit(solution)/shard_map/ppermute | solution.py:723
  33.4 0.0 collective-permute-done.8.b
  33.4 0.1 collective-permute-done.9.a
  33.4 1.9 %middle_adjoint.1 = (f32[12968,128]{1,0:T(8,128)S(1)}, f32[12968,128]{1,0:T(8,128)S(1)}, f32[312,128]{1,0:T(8,128)S(1)}, f32[256,128]{1,0:T(8,128)S(1)}, f32[1280,128]{1,0:T(8,128)S(1)}) custom-call(f32[12968,128]{1,0:T(8,128)S(1)} %get-tuple-element.88._field, ...), custom_call_target="tpu_custom_call", output_to_operand_aliasing={{0}: (0, {}), {1}: (1, {}), {2}: (2, {})} | custom-call | bytes 12582912 | tf_op jit(solution)/shard_map/middle_adjoint/pallas_call | solution.py:794
  35.3 0.0 collective-permute-done.10.refs_7_
  35.3 1.1 %collective-permute-done.11.refs_8_ = f32[32,128]{1,0:T(8,128)S(1)} collective-permute-done((f32[32,128]{1,0:T(8,128)S(1)}, f32[32,128]{1,0:T(8,128)S(1)}, u32[]{:S(2)}, u32[]{:S(2)}) %collective-permute-start.11) | collective-permute-done | bytes 16416 | tf_op jit(solution)/shard_map/ppermute | solution.py:723
  36.4 2.1 %total.1 = (f32[12968,128]{1,0:T(8,128)S(1)}, f32[12968,128]{1,0:T(8,128)S(1)}, f32[312,128]{1,0:T(8,128)S(1)}, f32[256,128]{1,0:T(8,128)S(1)}, f32[1280,128]{1,0:T(8,128)S(1)}, /*index=5*/f32[8,128]{1,0:T(8,128)S(1)}) custom-call(f32[12968,128]{1,0:T(8,128)S(1)} %get-tuple-element.94.r, ...), custom_call_target="tpu_custom_call", output_to_operand_aliasing={{0}: (0, {}), {1}: (1, {}), {2}: (2, {}), {3}: (3, {}), {4}... | custom-call | tf_op jit(solution)/shard_map/total/pallas_call | solution.py:794
  38.5 0.1 collective-permute-start.12
  38.6 1.2 %collective-permute-done.12 = f32[8,128]{1,0:T(8,128)S(1)} collective-permute-done((f32[8,128]{1,0:T(8,128)S(1)}, f32[8,128]{1,0:T(8,128)S(1)}, u32[]{:S(2)}, u32[]{:S(2)}) %collective-permute-start.12) | collective-permute-done | bytes 4128 | tf_op jit(solution)/shard_map/ppermute | solution.py:729
  39.7 2.1 %collective-permute-start.15 = (f32[8,128]{1,0:T(8,128)S(1)}, f32[8,128]{1,0:T(8,128)S(1)}, u32[]{:S(2)}, u32[]{:S(2)}) collective-permute-start(f32[8,128]{1,0:T(8,128)S(1)} %max.21.near), channel_id=1, source_target_pairs={{0,7},{1,6},{2,5},{3,4},{4,3},{5,2},{6,1},{7,0},{8,15},{9,14},{10,... | collective-permute-start | bytes 12296 | tf_op jit(solution)/shard_map/ppermute | solution.py:739
  41.8 0.7 %collective-permute-start.14 = (f32[8,128]{1,0:T(8,128)S(1)}, f32[8,128]{1,0:T(8,128)S(1)}, u32[]{:S(2)}, u32[]{:S(2)}) collective-permute-start(f32[8,128]{1,0:T(8,128)S(1)} %max.21.near), channel_id=1, source_target_pairs={{0,5},{1,4},{2,7},{3,6},{4,1},{5,0},{6,3},{7,2},{8,13},{9,12},{10,... | collective-permute-start | bytes 12296 | tf_op jit(solution)/shard_map/ppermute | solution.py:739
  42.5 0.3 collective-permute-start.13
  42.7 1.6 %adjoint_low.1 = (f32[8,128]{1,0:T(8,128)S(1)}, f32[27,32,1024]{2,1,0:T(8,128)}) custom-call(f32[12968,128]{1,0:T(8,128)S(1)} %get-tuple-element.101.buf, f32[1280,128]{1,0:T(8,128)S(1)} %get-tuple-element.102.fields, f32[8,128]{1,0:T(8,128)S(1)} %max.21.near), custom_call_target="tpu_custom_call" | custom-call | bytes 6291456 | tf_op jit(solution)/shard_map/adjoint_low/pallas_call | solution.py:794
  44.3 0.0 collective-permute-done.15
  44.3 0.5 collective-permute-done.14
  44.8 0.7 %collective-permute-done.13 = f32[8,128]{1,0:T(8,128)S(1)} collective-permute-done((f32[8,128]{1,0:T(8,128)S(1)}, f32[8,128]{1,0:T(8,128)S(1)}, u32[]{:S(2)}, u32[]{:S(2)}) %collective-permute-start.13) | collective-permute-done | bytes 4128 | tf_op jit(solution)/shard_map/ppermute | solution.py:739
  45.5 1.3 %collective-permute-start.18 = (f32[8,128]{1,0:T(8,128)S(1)}, f32[8,128]{1,0:T(8,128)S(1)}, u32[]{:S(2)}, u32[]{:S(2)}) collective-permute-start(f32[8,128]{1,0:T(8,128)S(1)} %maximum_maximum_fusion.1), channel_id=1, source_target_pairs={{0,25},{1,24},{2,27},{3,26},{4,29},{5,28},{6,31},{7,30},{8,17},{9,... | collective-permute-start | bytes 12296 | tf_op jit(solution)/shard_map/ppermute | solution.py:746
  46.8 0.0 collective-permute-start.17
  46.8 2.5 %collective-permute-start.16 = (f32[8,128]{1,0:T(8,128)S(1)}, f32[8,128]{1,0:T(8,128)S(1)}, u32[]{:S(2)}, u32[]{:S(2)}) collective-permute-start(f32[8,128]{1,0:T(8,128)S(1)} %maximum_maximum_fusion.1), channel_id=1, source_target_pairs={{0,9},{1,8},{2,11},{3,10},{4,13},{5,12},{6,15},{7,14},{8,1},{9,0},... | collective-permute-start | bytes 12296 | tf_op jit(solution)/shard_map/ppermute | solution.py:746
  49.4 1.6 %adjoint_high.1 = f32[27,32,1024]{2,1,0:T(8,128)} custom-call(f32[12968,128]{1,0:T(8,128)S(1)} %get-tuple-element.101.buf, f32[1280,128]{1,0:T(8,128)S(1)} %get-tuple-element.102.fields, f32[27,32,1024]{2,1,0:T(8,128)} %get-tuple-element.104._), custom_call_target="tpu_custom_call", output_to_operand_aliasing={{}: (2, {})} | custom-call | bytes 6291456 | tf_op jit(solution)/shard_map/adjoint_high/pallas_call | solution.py:794
  51.0 0.0 collective-permute-done.18
  51.0 0.0 collective-permute-done.17
  51.0 0.0 collective-permute-done.16
  51.0 0.8 %normalize.1 = f32[32,1024]{1,0:T(8,128)} custom-call(f32[256,128]{1,0:T(8,128)S(1)} %get-tuple-element.105.total, f32[8,128]{1,0:T(8,128)S(1)} %maximum_maximum_fusion.peak), custom_call_target="tpu_custom_call" | custom-call | tf_op jit(solution)/shard_map/normalize/pallas_call | solution.py:794
  (3 shorter events, 0.0 us)
Async XLA Ops:
  3.2 9.1 %collective-permute-start = (f32[480,128]{1,0:T(8,128)S(1)}, f32[480,128]{1,0:T(8,128)S(1)}, u32[]{:S(2)}, u32[]{:S(2)}) collective-permute-start(f32[480,128]{1,0:T(8,128)S(1)} %get-tuple-element.64), channel_id=1, source_target_pairs={{1,2},{2,1},{3,4},{4,3},{5,6},{6,5},{7,0},{0,7},{9,10},{10,9},{11,... | collective-permute-start | bytes 737288 | tf_op jit(solution)/shard_map/ppermute | solution.py:723
  6.6 5.7 %collective-permute-start.1 = (f32[480,128]{1,0:T(8,128)S(1)}, f32[480,128]{1,0:T(8,128)S(1)}, u32[]{:S(2)}, u32[]{:S(2)}) collective-permute-start(f32[480,128]{1,0:T(8,128)S(1)} %get-tuple-element.65), channel_id=1, source_target_pairs={{0,1},{1,0},{2,3},{3,2},{4,5},{5,4},{6,7},{7,6},{8,9},{9,8},{10,11... | collective-permute-start | bytes 737288 | tf_op jit(solution)/shard_map/ppermute | solution.py:722
  7.3 10.8 %collective-permute-start.2 = (f32[240,128]{1,0:T(8,128)S(1)}, f32[240,128]{1,0:T(8,128)S(1)}, u32[]{:S(2)}, u32[]{:S(2)}) collective-permute-start(f32[240,128]{1,0:T(8,128)S(1)} %get-tuple-element.69), channel_id=1, source_target_pairs={{8,16},{16,8},{24,0},{0,24},{9,17},{17,9},{25,1},{1,25},{10,18},{1... | collective-permute-start | bytes 368648 | tf_op jit(solution)/shard_map/ppermute | solution.py:723
  10.9 7.1 %collective-permute-start.3 = (f32[240,128]{1,0:T(8,128)S(1)}, f32[240,128]{1,0:T(8,128)S(1)}, u32[]{:S(2)}, u32[]{:S(2)}) collective-permute-start(f32[240,128]{1,0:T(8,128)S(1)} %get-tuple-element.70), channel_id=1, source_target_pairs={{0,8},{8,0},{16,24},{24,16},{1,9},{9,1},{17,25},{25,17},{2,10},{10... | collective-permute-start | bytes 368648 | tf_op jit(solution)/shard_map/ppermute | solution.py:722
  12.3 5.7 %copy-start = (f32[27,32,1024]{2,1,0:T(8,128)S(1)}, f32[27,32,1024]{2,1,0:T(8,128)}, u32[]{:S(2)}) copy-start(f32[27,32,1024]{2,1,0:T(8,128)} %refs_1_.3) | copy-start | bytes 10616836
  12.5 7.5 %collective-permute-start.4 = (f32[32,128]{1,0:T(8,128)S(1)}, f32[32,128]{1,0:T(8,128)S(1)}, u32[]{:S(2)}, u32[]{:S(2)}) collective-permute-start(f32[32,128]{1,0:T(8,128)S(1)} %get-tuple-element.76), channel_id=1, source_target_pairs={{0,8},{8,0},{16,24},{24,16},{1,9},{9,1},{17,25},{25,17},{2,10},{10... | collective-permute-start | bytes 49160 | tf_op jit(solution)/shard_map/ppermute | solution.py:722
  15.6 5.5 %collective-permute-start.5 = (f32[32,128]{1,0:T(8,128)S(1)}, f32[32,128]{1,0:T(8,128)S(1)}, u32[]{:S(2)}, u32[]{:S(2)}) collective-permute-start(f32[32,128]{1,0:T(8,128)S(1)} %get-tuple-element.77), channel_id=1, source_target_pairs={{8,16},{16,8},{24,0},{0,24},{9,17},{17,9},{25,1},{1,25},{10,18},{1... | collective-permute-start | bytes 49160 | tf_op jit(solution)/shard_map/ppermute | solution.py:723
  22.5 8.1 %collective-permute-start.6 = (f32[448,128]{1,0:T(8,128)S(1)}, f32[448,128]{1,0:T(8,128)S(1)}, u32[]{:S(2)}, u32[]{:S(2)}) collective-permute-start(f32[448,128]{1,0:T(8,128)S(1)} %get-tuple-element.86), channel_id=1, source_target_pairs={{1,2},{2,1},{3,4},{4,3},{5,6},{6,5},{7,0},{0,7},{9,10},{10,9},{11,... | collective-permute-start | bytes 688136 | tf_op jit(solution)/shard_map/ppermute | solution.py:723
  22.5 8.1 %collective-permute-start.7 = (f32[448,128]{1,0:T(8,128)S(1)}, f32[448,128]{1,0:T(8,128)S(1)}, u32[]{:S(2)}, u32[]{:S(2)}) collective-permute-start(f32[448,128]{1,0:T(8,128)S(1)} %get-tuple-element.87), channel_id=1, source_target_pairs={{0,1},{1,0},{2,3},{3,2},{4,5},{5,4},{6,7},{7,6},{8,9},{9,8},{10,11... | collective-permute-start | bytes 688136 | tf_op jit(solution)/shard_map/ppermute | solution.py:722
  23.9 9.5 %collective-permute-start.8 = (f32[216,128]{1,0:T(8,128)S(1)}, f32[216,128]{1,0:T(8,128)S(1)}, u32[]{:S(2)}, u32[]{:S(2)}) collective-permute-start(f32[216,128]{1,0:T(8,128)S(1)} %get-tuple-element.92), channel_id=1, source_target_pairs={{8,16},{16,8},{24,0},{0,24},{9,17},{17,9},{25,1},{1,25},{10,18},{1... | collective-permute-start | bytes 331784 | tf_op jit(solution)/shard_map/ppermute | solution.py:723
  26.1 7.3 %collective-permute-start.9 = (f32[216,128]{1,0:T(8,128)S(1)}, f32[216,128]{1,0:T(8,128)S(1)}, u32[]{:S(2)}, u32[]{:S(2)}) collective-permute-start(f32[216,128]{1,0:T(8,128)S(1)} %get-tuple-element.93), channel_id=1, source_target_pairs={{0,8},{8,0},{16,24},{24,16},{1,9},{9,1},{17,25},{25,17},{2,10},{10... | collective-permute-start | bytes 331784 | tf_op jit(solution)/shard_map/ppermute | solution.py:722
  30.7 4.6 %collective-permute-start.10 = (f32[32,128]{1,0:T(8,128)S(1)}, f32[32,128]{1,0:T(8,128)S(1)}, u32[]{:S(2)}, u32[]{:S(2)}) collective-permute-start(f32[32,128]{1,0:T(8,128)S(1)} %get-tuple-element.99), channel_id=1, source_target_pairs={{0,8},{8,0},{16,24},{24,16},{1,9},{9,1},{17,25},{25,17},{2,10},{10... | collective-permute-start | bytes 49160 | tf_op jit(solution)/shard_map/ppermute | solution.py:722
  30.8 5.6 %collective-permute-start.11 = (f32[32,128]{1,0:T(8,128)S(1)}, f32[32,128]{1,0:T(8,128)S(1)}, u32[]{:S(2)}, u32[]{:S(2)}) collective-permute-start(f32[32,128]{1,0:T(8,128)S(1)} %get-tuple-element.100), channel_id=1, source_target_pairs={{8,16},{16,8},{24,0},{0,24},{9,17},{17,9},{25,1},{1,25},{10,18},{1... | collective-permute-start | bytes 49160 | tf_op jit(solution)/shard_map/ppermute | solution.py:723
  38.5 1.2 %collective-permute-start.12 = (f32[8,128]{1,0:T(8,128)S(1)}, f32[8,128]{1,0:T(8,128)S(1)}, u32[]{:S(2)}, u32[]{:S(2)}) collective-permute-start(f32[8,128]{1,0:T(8,128)S(1)} %get-tuple-element.103), channel_id=1, source_target_pairs={{0,1},{1,0},{2,3},{3,2},{4,5},{5,4},{6,7},{7,6},{8,9},{9,8},{10,11... | collective-permute-start | bytes 12296 | tf_op jit(solution)/shard_map/ppermute | solution.py:729
  39.7 4.6 %collective-permute-start.15 = (f32[8,128]{1,0:T(8,128)S(1)}, f32[8,128]{1,0:T(8,128)S(1)}, u32[]{:S(2)}, u32[]{:S(2)}) collective-permute-start(f32[8,128]{1,0:T(8,128)S(1)} %max.21.near), channel_id=1, source_target_pairs={{0,7},{1,6},{2,5},{3,4},{4,3},{5,2},{6,1},{7,0},{8,15},{9,14},{10,... | collective-permute-start | bytes 12296 | tf_op jit(solution)/shard_map/ppermute | solution.py:739
  41.8 3.0 %collective-permute-start.14 = (f32[8,128]{1,0:T(8,128)S(1)}, f32[8,128]{1,0:T(8,128)S(1)}, u32[]{:S(2)}, u32[]{:S(2)}) collective-permute-start(f32[8,128]{1,0:T(8,128)S(1)} %max.21.near), channel_id=1, source_target_pairs={{0,5},{1,4},{2,7},{3,6},{4,1},{5,0},{6,3},{7,2},{8,13},{9,12},{10,... | collective-permute-start | bytes 12296 | tf_op jit(solution)/shard_map/ppermute | solution.py:739
  42.5 3.0 %collective-permute-start.13 = (f32[8,128]{1,0:T(8,128)S(1)}, f32[8,128]{1,0:T(8,128)S(1)}, u32[]{:S(2)}, u32[]{:S(2)}) collective-permute-start(f32[8,128]{1,0:T(8,128)S(1)} %max.21.near), channel_id=1, source_target_pairs={{0,3},{1,2},{2,1},{3,0},{4,7},{5,6},{6,5},{7,4},{8,11},{9,10},{10,... | collective-permute-start | bytes 12296 | tf_op jit(solution)/shard_map/ppermute | solution.py:739
  45.5 5.5 %collective-permute-start.18 = (f32[8,128]{1,0:T(8,128)S(1)}, f32[8,128]{1,0:T(8,128)S(1)}, u32[]{:S(2)}, u32[]{:S(2)}) collective-permute-start(f32[8,128]{1,0:T(8,128)S(1)} %maximum_maximum_fusion.1), channel_id=1, source_target_pairs={{0,25},{1,24},{2,27},{3,26},{4,29},{5,28},{6,31},{7,30},{8,17},{9,... | collective-permute-start | bytes 12296 | tf_op jit(solution)/shard_map/ppermute | solution.py:746
  46.8 4.1 %collective-permute-start.17 = (f32[8,128]{1,0:T(8,128)S(1)}, f32[8,128]{1,0:T(8,128)S(1)}, u32[]{:S(2)}, u32[]{:S(2)}) collective-permute-start(f32[8,128]{1,0:T(8,128)S(1)} %maximum_maximum_fusion.1), channel_id=1, source_target_pairs={{0,17},{1,16},{2,19},{3,18},{4,21},{5,20},{6,23},{7,22},{8,25},{9,... | collective-permute-start | bytes 12296 | tf_op jit(solution)/shard_map/ppermute | solution.py:746
  46.8 4.2 %collective-permute-start.16 = (f32[8,128]{1,0:T(8,128)S(1)}, f32[8,128]{1,0:T(8,128)S(1)}, u32[]{:S(2)}, u32[]{:S(2)}) collective-permute-start(f32[8,128]{1,0:T(8,128)S(1)} %maximum_maximum_fusion.1), channel_id=1, source_target_pairs={{0,9},{1,8},{2,11},{3,10},{4,13},{5,12},{6,15},{7,14},{8,1},{9,0},... | collective-permute-start | bytes 12296 | tf_op jit(solution)/shard_map/ppermute | solution.py:746

commit v7 on v6

--- a/solution.py
+++ b/solution.py
@@ -564,8 +564,11 @@
         refs[11:],
     )
 
-    def copy(k):
-        return pltpu.make_async_copy(block_of(pops, k), stage.at[k - 1], sems.at[k - 1])
+    def copy(k, r, n):
+        rows = pl.ds(r, n)
+        source = pops.at[:, rows, lanes_of(k)]
+        part = 1 if r else 0
+        return pltpu.make_async_copy(source, stage.at[k - 1, :, rows], sems.at[k - 1, part])
 
     flat_copies = [
         pltpu.make_async_copy(source, target, flat_sems.at[n])
@@ -573,18 +576,22 @@
     ]
     for each in flat_copies:
         each.start()
-    for k in (1, g.cols, *range(2, g.cols)):
-        copy(k).start()
+    for k in (1, g.cols):
+        copy(k, 0, g.rows).start()
+    for k in range(2, g.cols):
+        for piece in g.outer:
+            copy(k, *piece).start()
     for each in flat_copies:
         each.wait()
     for k in (1, g.cols):
         flat_fields(g, out, near, k)
-    copy(1).wait()
-    copy(g.cols).wait()
+    for k in (1, g.cols):
+        copy(k, 0, g.rows).wait()
     side_tiles(g, staged_tile(g, collide_first(g, state, out), stage))
     by_parity("gy", *faces, functools.partial(pack_y, g, out, 1, 30))
     for k in range(2, g.cols):
-        copy(k).wait()
+        for piece in g.outer:
+            copy(k, *piece).wait()
 
 
 def rim_first_kernel(g, _out, _state, stage, *refs):
@@ -595,8 +602,18 @@
     by_parity("gx", *faces, functools.partial(pack_x, g, out, 1, 30))
 
 
-def inner_first_kernel(g, _, _state, stage, post, state0, out, state1):
+def inner_first_kernel(g, _, _state, pops, post, state0, out, state1, stage, sems):
     masks = lane_masks(16)
+    middle = pl.ds(8, g.rows - 16)
+
+    def copy(k):
+        source = pops.at[:, middle, lanes_of(k)]
+        return pltpu.make_async_copy(source, stage.at[k - 1, :, middle], sems.at[k - 1])
+
+    for k in range(2, g.cols):
+        copy(k).start()
+    for k in range(2, g.cols):
+        copy(k).wait()
     interior_tiles(g, staged_tile(g, collide_first(g, state0, post), stage))
     interior_tiles(g, step_tile(g, post, out, 1, 30, masks, collide_second(g, state1)))
 
@@ -781,12 +798,14 @@
     stage = vmem(g.cols, 27, rows, LANES)
     sems = pltpu.SemaphoreType.DMA((g.cols,))
 
-    def call(name, kernel, operands, out_shape, scratch=(), kept=0, load=0, result=None):
+    def call(name, kernel, operands, out_shape, scratch=(), kept=0, load=0, result=None, far=()):
         out_shape = [pltpu.VMEM(x.shape, x.dtype) for x in operands[:kept]] + out_shape
         aliases = {n: n for n in range(kept)}
-        space = pltpu.HBM if name == "side_first" else pltpu.VMEM
-        pinned = [pltpu.with_memory_space_constraint(x, space) for x in operands]
-        in_specs = [pl.BlockSpec(memory_space=space)] * len(operands)
+        spaces = [pltpu.HBM if n in far else pltpu.VMEM for n in range(len(operands))]
+        pinned = [
+            pltpu.with_memory_space_constraint(x, space) for x, space in zip(operands, spaces)
+        ]
+        in_specs = [pl.BlockSpec(memory_space=space) for space in spaces]
         if result is not None:
             aliases[len(operands)] = len(out_shape) - 1
             pinned.append(pltpu.with_memory_space_constraint(result, pltpu.HBM))
@@ -821,7 +840,8 @@
         side_first_kernel,
         [populations, porosity, solid, labels],
         [padded(30), fields(7, g.local), stage] + flat_space + y_faces(30, 1),
-        [sems, pltpu.SemaphoreType.DMA((3,))],
+        [pltpu.SemaphoreType.DMA((g.cols, 2)), pltpu.SemaphoreType.DMA((3,))],
+        far=range(4),
     )
     along_y = swap_faces("gy", ny, rest[3:])
     post, state0, *parcels = call(
@@ -836,10 +856,12 @@
     post, state0, second, state1 = call(
         "inner_first",
         inner_first_kernel,
-        [post, state0, staged],
+        [post, state0, populations],
         [padded(27), fields(7, g.extended)],
+        [stage, sems],
         kept=2,
         load=FLIGHT,
+        far=(2,),
     )
     post, parcels = relay(post, along_y, 1, 30)
     post, second, state1, staged, field = call(

time: 52 us -> 52.3 us (level)
  starting transfers between devices: 24.8 us -> 22.8 us
  Pallas kernels: 18.9 us -> 20.2 us
  waiting for transfers between devices: 7.2 us -> 8.37 us
    ppermute x6, starting transfers between devices: 14.4 us -> 12.4 us  [swap(): lax.ppermute(second, axis, swap_pairs(count, 1))]
    pallas_call x14, Pallas kernels: 18.9 us -> 20.2 us  [call(): pl.pallas_call(functools.partial(kernel, g), in_specs=in_specs, out_shape...]
    ppermute x3, waiting for transfers between devices: 0.01 us -> 0.61 us  [largest_of_all(): parts.append(lax.ppermute(peak, ('gx', 'gy'), pairs))]
  transfers between devices with their start and end apart: 19 -> 19, of which waited for: 7 -> 8; matrix products, arithmetic and copies ran while one was open for 0% -> 0% of each run, Pallas kernels for 23% -> 26%
where the time goes in v7:
time: 52.3 us; the launch traced here: 52.2 us
  starting transfers between devices  22.8 us (44%)
  Pallas kernels  20.2 us (39%)
  waiting for transfers between devices  8.37 us (16%)
  between operations  0.83 us (2%)
    pallas_call x14, Pallas kernels, call(): pl.pallas_call(functools.partial(kernel, g), in_specs=in_specs, out_shape...  20.2 us
    ppermute x6, starting transfers between devices, swap(): lax.ppermute(second, axis, swap_pairs(count, 1))  12.4 us
    ppermute x6, waiting for transfers between devices, swap(): lax.ppermute(second, axis, swap_pairs(count, 1))  5 us
    ppermute x3, starting transfers between devices, largest_of_all(): parts.append(lax.ppermute(peak, ('gx', 'gy'), pairs))  3.88 us
    ppermute x6, starting transfers between devices, swap(): lax.ppermute(first, axis, swap_pairs(count, 0))  3.48 us
    ppermute x3, starting transfers between devices, largest_of_all(): parts.append(lax.ppermute(peak, 'gy', pairs))  2.98 us
    ppermute x1, waiting for transfers between devices, largest_of_all(): lax.ppermute(peak, 'gy', [(i, i ^ 1) for i in range(ny)])  1.15 us
    ppermute x3, waiting for transfers between devices, largest_of_all(): parts.append(lax.ppermute(peak, 'gy', pairs))  1.13 us
  transfers between devices with their start and end apart: 19, of which 8 were waited for; matrix products, arithmetic and copies ran while one was open for 0% of the time, Pallas kernels for 26%

profile of v7, /device:TPU:0, one launch (start us, length us, event | category | flops | bytes accessed | tf_op | source)
XLA Modules:
  0.0 52.2 jit_solution(12407545570882985112)
XLA Ops:
  0.6 2.3 %side_first.1 = (f32[14408,128]{1,0:T(8,128)S(1)}, f32[1792,128]{1,0:T(8,128)S(1)}, f32[8,27,32,128]{3,2,1,0:T(8,128)S(1)}, f32[32,1024]{1,0:T(8,128)S(1)}, s32[...) custom-call(f32[27,32,1024]{2,1,0:T(8,128)} %pops.3, ...), custom_call_target="tpu_custom_call" | custom-call | tf_op jit(solution)/shard_map/side_first/pallas_call | solution.py:813
  3.0 3.4 %collective-permute-start = (f32[480,128]{1,0:T(8,128)S(1)}, f32[480,128]{1,0:T(8,128)S(1)}, u32[]{:S(2)}, u32[]{:S(2)}) collective-permute-start(f32[480,128]{1,0:T(8,128)S(1)} %get-tuple-element.64), channel_id=1, source_target_pairs={{1,2},{2,1},{3,4},{4,3},{5,6},{6,5},{7,0},{0,7},{9,10},{10,9},{11,... | collective-permute-start | bytes 737288 | tf_op jit(solution)/shard_map/ppermute | solution.py:740
  6.4 0.0 collective-permute-start.1
  6.4 0.6 %rim_first.1 = (f32[14408,128]{1,0:T(8,128)S(1)}, f32[1792,128]{1,0:T(8,128)S(1)}, f32[240,128]{1,0:T(8,128)S(1)}, f32[240,128]{1,0:T(8,128)S(1)}) custom-call(f32[14408,128]{1,0:T(8,128)S(1)} %get-tuple-element.55._out, f32[1792,128]{1,0:T(8,128)S(1)} %get-tuple-element.56._state, ...), custom_call_target="tpu_custom_call", output_to_operand_aliasing={{0}: (0, {}), {1}: (1, {})} | custom-call | bytes 12582912 | tf_op jit(solution)/shard_map/rim_first/pallas_call | solution.py:813
  7.0 3.7 %collective-permute-start.2 = (f32[240,128]{1,0:T(8,128)S(1)}, f32[240,128]{1,0:T(8,128)S(1)}, u32[]{:S(2)}, u32[]{:S(2)}) collective-permute-start(f32[240,128]{1,0:T(8,128)S(1)} %get-tuple-element.69), channel_id=1, source_target_pairs={{8,16},{16,8},{24,0},{0,24},{9,17},{17,9},{25,1},{1,25},{10,18},{1... | collective-permute-start | bytes 368648 | tf_op jit(solution)/shard_map/ppermute | solution.py:740
  10.7 0.0 collective-permute-start.3
  10.7 2.9 %inner_first.1 = (f32[14408,128]{1,0:T(8,128)S(1)}, f32[1792,128]{1,0:T(8,128)S(1)}, f32[12968,128]{1,0:T(8,128)S(1)}, f32[2184,128]{1,0:T(8,128)S(1)}) custom-call(f32[14408,128]{1,0:T(8,128)S(1)} %get-tuple-element.61._, f32[1792,128]{1,0:T(8,128)S(1)} %get-tuple-element.62._state, f32[27,32,1024]{2,1,0:T(8,128)} %pops.3), custom_call_target="tpu_custom_call", output_to_operand_aliasing={{0}: (0, {}), {1}: (1, {})} | custom-call | bytes 12582912 | tf_op jit(solution)/shard_map/inner_first/pallas_call | solution.py:813
  13.6 0.0 copy-start
  13.6 0.0 collective-permute-done.refs_1_
  13.6 0.0 collective-permute-done.1.refs_2_
  13.6 0.1 relay.2
  13.7 2.1 %collective-permute-start.4 = (f32[32,128]{1,0:T(8,128)S(1)}, f32[32,128]{1,0:T(8,128)S(1)}, u32[]{:S(2)}, u32[]{:S(2)}) collective-permute-start(f32[32,128]{1,0:T(8,128)S(1)} %get-tuple-element.76), channel_id=1, source_target_pairs={{0,8},{8,0},{16,24},{24,16},{1,9},{9,1},{17,25},{25,17},{2,10},{10... | collective-permute-start | bytes 49160 | tf_op jit(solution)/shard_map/ppermute | solution.py:739
  15.8 2.0 %collective-permute-start.5 = (f32[32,128]{1,0:T(8,128)S(1)}, f32[32,128]{1,0:T(8,128)S(1)}, u32[]{:S(2)}, u32[]{:S(2)}) collective-permute-start(f32[32,128]{1,0:T(8,128)S(1)} %get-tuple-element.77), channel_id=1, source_target_pairs={{8,16},{16,8},{24,0},{0,24},{9,17},{17,9},{25,1},{1,25},{10,18},{1... | collective-permute-start | bytes 49160 | tf_op jit(solution)/shard_map/ppermute | solution.py:740
  17.8 0.0 collective-permute-done.2.b
  17.8 0.0 collective-permute-done.3.a
  17.8 0.0 copy-done
  17.8 2.0 %middle_second.1 = (f32[14408,128]{1,0:T(8,128)S(1)}, f32[12968,128]{1,0:T(8,128)S(1)}, f32[2184,128]{1,0:T(8,128)S(1)}, f32[8,27,32,128]{3,2,1,0:T(8,128)S(1)}, f32[12968,128]{1,0:T(8,128)S(1)}) custom-call(f32[14408,128]{1,0:T(8,128)S(1)} %get-tuple-element.66._post, ...), custom_call_target="tpu_custom_call", output_to_operand_aliasing={{0}: (0, {}), {1}: (1, {}), {2}: (2, {})} | custom-call | bytes 12582912 | tf_op jit(solution)/shard_map/middle_second/pallas_call | solution.py:813
  19.8 0.0 collective-permute-done.4.first
  19.8 1.6 %collective-permute-done.5.second = f32[32,128]{1,0:T(8,128)S(1)} collective-permute-done((f32[32,128]{1,0:T(8,128)S(1)}, f32[32,128]{1,0:T(8,128)S(1)}, u32[]{:S(2)}, u32[]{:S(2)}) %collective-permute-start.5) | collective-permute-done | bytes 16416 | tf_op jit(solution)/shard_map/ppermute | solution.py:740
  21.4 1.4 %side_seed.1 = (f32[14408,128]{1,0:T(8,128)S(1)}, f32[12968,128]{1,0:T(8,128)S(1)}, f32[2184,128]{1,0:T(8,128)S(1)}, f32[8,27,32,128]{3,2,1,0:T(8,128)S(1)}, f32...) custom-call(f32[14408,128]{1,0:T(8,128)S(1)} %get-tuple-element.71._, ...), custom_call_target="tpu_custom_call", output_to_operand_aliasing={{0}: (0, {}), {1}: (1, {}), {2}: (2, {}), {3}: (3, {}), {4}... | custom-call | tf_op jit(solution)/shard_map/side_seed/pallas_call | solution.py:813
  22.8 0.1 collective-permute-start.6
  22.8 1.3 %collective-permute-start.7 = (f32[448,128]{1,0:T(8,128)S(1)}, f32[448,128]{1,0:T(8,128)S(1)}, u32[]{:S(2)}, u32[]{:S(2)}) collective-permute-start(f32[448,128]{1,0:T(8,128)S(1)} %get-tuple-element.87), channel_id=1, source_target_pairs={{0,1},{1,0},{2,3},{3,2},{4,5},{5,4},{6,7},{7,6},{8,9},{9,8},{10,11... | collective-permute-start | bytes 688136 | tf_op jit(solution)/shard_map/ppermute | solution.py:739
  24.1 0.9 %rim_seed.1 = (f32[8,27,32,128]{3,2,1,0:T(8,128)S(1)}, f32[12968,128]{1,0:T(8,128)S(1)}, f32[216,128]{1,0:T(8,128)S(1)}, f32[216,128]{1,0:T(8,128)S(1)}) custom-call(f32[8,27,32,128]{3,2,1,0:T(8,128)S(1)} %get-tuple-element.78._stage, f32[12968,128]{1,0:T(8,128)S(1)} %get-tuple-element.79._field, ...), custom_call_target="tpu_custom_call", output_to_operand_aliasing={{0}: (0, {}), {1}: (1, {})} | custom-call | bytes 12582912 | tf_op jit(solution)/shard_map/rim_seed/pallas_call | solution.py:813
  25.1 0.8 %collective-permute-start.8 = (f32[216,128]{1,0:T(8,128)S(1)}, f32[216,128]{1,0:T(8,128)S(1)}, u32[]{:S(2)}, u32[]{:S(2)}) collective-permute-start(f32[216,128]{1,0:T(8,128)S(1)} %get-tuple-element.92), channel_id=1, source_target_pairs={{8,16},{16,8},{24,0},{0,24},{9,17},{17,9},{25,1},{1,25},{10,18},{1... | collective-permute-start | bytes 331784 | tf_op jit(solution)/shard_map/ppermute | solution.py:740
  25.9 0.0 collective-permute-start.9
  25.9 1.9 %inner_seed.1 = (f32[8,27,32,128]{3,2,1,0:T(8,128)S(1)}, f32[12968,128]{1,0:T(8,128)S(1)}, f32[12968,128]{1,0:T(8,128)S(1)}, f32[312,128]{1,0:T(8,128)S(1)}, f32[27,32,1024]{2,1,0:T(8,128)}) custom-call(f32[8,27,32,128]{3,2,1,0:T(8,128)S(1)} %get-tuple-element.81.kept, ...), custom_call_target="tpu_custom_call", output_to_operand_aliasing={{0}: (0, {}), {1}: (1, {})} | custom-call | bytes 12582912 | tf_op jit(solution)/shard_map/inner_seed/pallas_call | solution.py:813
  27.8 2.7 %collective-permute-done.6.refs_1_ = f32[448,128]{1,0:T(8,128)S(1)} collective-permute-done((f32[448,128]{1,0:T(8,128)S(1)}, f32[448,128]{1,0:T(8,128)S(1)}, u32[]{:S(2)}, u32[]{:S(2)}) %collective-permute-start.6) | collective-permute-done | bytes 229408 | tf_op jit(solution)/shard_map/ppermute | solution.py:740
  30.4 0.0 collective-permute-done.7.refs_2_
  30.4 0.1 relay.3
  30.6 0.1 collective-permute-start.10
  30.6 2.5 %collective-permute-start.11 = (f32[32,128]{1,0:T(8,128)S(1)}, f32[32,128]{1,0:T(8,128)S(1)}, u32[]{:S(2)}, u32[]{:S(2)}) collective-permute-start(f32[32,128]{1,0:T(8,128)S(1)} %get-tuple-element.100), channel_id=1, source_target_pairs={{8,16},{16,8},{24,0},{0,24},{9,17},{17,9},{25,1},{1,25},{10,18},{1... | collective-permute-start | bytes 49160 | tf_op jit(solution)/shard_map/ppermute | solution.py:740
  33.1 0.0 collective-permute-done.8.b
  33.1 0.5 collective-permute-done.9.a
  33.6 1.9 %middle_adjoint.1 = (f32[12968,128]{1,0:T(8,128)S(1)}, f32[12968,128]{1,0:T(8,128)S(1)}, f32[312,128]{1,0:T(8,128)S(1)}, f32[256,128]{1,0:T(8,128)S(1)}, f32[1280,128]{1,0:T(8,128)S(1)}) custom-call(f32[12968,128]{1,0:T(8,128)S(1)} %get-tuple-element.88._field, ...), custom_call_target="tpu_custom_call", output_to_operand_aliasing={{0}: (0, {}), {1}: (1, {}), {2}: (2, {})} | custom-call | bytes 12582912 | tf_op jit(solution)/shard_map/middle_adjoint/pallas_call | solution.py:813
  35.5 0.0 collective-permute-done.10.refs_7_
  35.5 0.8 %collective-permute-done.11.refs_8_ = f32[32,128]{1,0:T(8,128)S(1)} collective-permute-done((f32[32,128]{1,0:T(8,128)S(1)}, f32[32,128]{1,0:T(8,128)S(1)}, u32[]{:S(2)}, u32[]{:S(2)}) %collective-permute-start.11) | collective-permute-done | bytes 16416 | tf_op jit(solution)/shard_map/ppermute | solution.py:740
  36.2 2.1 %total.1 = (f32[12968,128]{1,0:T(8,128)S(1)}, f32[12968,128]{1,0:T(8,128)S(1)}, f32[312,128]{1,0:T(8,128)S(1)}, f32[256,128]{1,0:T(8,128)S(1)}, f32[1280,128]{1,0:T(8,128)S(1)}, /*index=5*/f32[8,128]{1,0:T(8,128)S(1)}) custom-call(f32[12968,128]{1,0:T(8,128)S(1)} %get-tuple-element.94.r, ...), custom_call_target="tpu_custom_call", output_to_operand_aliasing={{0}: (0, {}), {1}: (1, {}), {2}: (2, {}), {3}: (3, {}), {4}... | custom-call | tf_op jit(solution)/shard_map/total/pallas_call | solution.py:813
  38.3 0.1 collective-permute-start.12
  38.4 1.2 %collective-permute-done.12 = f32[8,128]{1,0:T(8,128)S(1)} collective-permute-done((f32[8,128]{1,0:T(8,128)S(1)}, f32[8,128]{1,0:T(8,128)S(1)}, u32[]{:S(2)}, u32[]{:S(2)}) %collective-permute-start.12) | collective-permute-done | bytes 4128 | tf_op jit(solution)/shard_map/ppermute | solution.py:746
  39.6 2.0 %collective-permute-start.15 = (f32[8,128]{1,0:T(8,128)S(1)}, f32[8,128]{1,0:T(8,128)S(1)}, u32[]{:S(2)}, u32[]{:S(2)}) collective-permute-start(f32[8,128]{1,0:T(8,128)S(1)} %max.21.near), channel_id=1, source_target_pairs={{0,7},{1,6},{2,5},{3,4},{4,3},{5,2},{6,1},{7,0},{8,15},{9,14},{10,... | collective-permute-start | bytes 12296 | tf_op jit(solution)/shard_map/ppermute | solution.py:756
  41.6 0.7 %collective-permute-start.14 = (f32[8,128]{1,0:T(8,128)S(1)}, f32[8,128]{1,0:T(8,128)S(1)}, u32[]{:S(2)}, u32[]{:S(2)}) collective-permute-start(f32[8,128]{1,0:T(8,128)S(1)} %max.21.near), channel_id=1, source_target_pairs={{0,5},{1,4},{2,7},{3,6},{4,1},{5,0},{6,3},{7,2},{8,13},{9,12},{10,... | collective-permute-start | bytes 12296 | tf_op jit(solution)/shard_map/ppermute | solution.py:756
  42.2 0.3 collective-permute-start.13
  42.5 1.6 %adjoint_low.1 = (f32[8,128]{1,0:T(8,128)S(1)}, f32[27,32,1024]{2,1,0:T(8,128)}) custom-call(f32[12968,128]{1,0:T(8,128)S(1)} %get-tuple-element.101.buf, f32[1280,128]{1,0:T(8,128)S(1)} %get-tuple-element.102.fields, f32[8,128]{1,0:T(8,128)S(1)} %max.21.near), custom_call_target="tpu_custom_call" | custom-call | bytes 6291456 | tf_op jit(solution)/shard_map/adjoint_low/pallas_call | solution.py:813
  44.1 0.0 collective-permute-done.15
  44.1 0.5 collective-permute-done.14
  44.6 0.7 %collective-permute-done.13 = f32[8,128]{1,0:T(8,128)S(1)} collective-permute-done((f32[8,128]{1,0:T(8,128)S(1)}, f32[8,128]{1,0:T(8,128)S(1)}, u32[]{:S(2)}, u32[]{:S(2)}) %collective-permute-start.13) | collective-permute-done | bytes 4128 | tf_op jit(solution)/shard_map/ppermute | solution.py:756
  45.3 2.2 %collective-permute-start.18 = (f32[8,128]{1,0:T(8,128)S(1)}, f32[8,128]{1,0:T(8,128)S(1)}, u32[]{:S(2)}, u32[]{:S(2)}) collective-permute-start(f32[8,128]{1,0:T(8,128)S(1)} %maximum_maximum_fusion.1), channel_id=1, source_target_pairs={{0,25},{1,24},{2,27},{3,26},{4,29},{5,28},{6,31},{7,30},{8,17},{9,... | collective-permute-start | bytes 12296 | tf_op jit(solution)/shard_map/ppermute | solution.py:763
  47.4 0.0 collective-permute-start.17
  47.4 1.7 %collective-permute-start.16 = (f32[8,128]{1,0:T(8,128)S(1)}, f32[8,128]{1,0:T(8,128)S(1)}, u32[]{:S(2)}, u32[]{:S(2)}) collective-permute-start(f32[8,128]{1,0:T(8,128)S(1)} %maximum_maximum_fusion.1), channel_id=1, source_target_pairs={{0,9},{1,8},{2,11},{3,10},{4,13},{5,12},{6,15},{7,14},{8,1},{9,0},... | collective-permute-start | bytes 12296 | tf_op jit(solution)/shard_map/ppermute | solution.py:763
  49.1 1.6 %adjoint_high.1 = f32[27,32,1024]{2,1,0:T(8,128)} custom-call(f32[12968,128]{1,0:T(8,128)S(1)} %get-tuple-element.101.buf, f32[1280,128]{1,0:T(8,128)S(1)} %get-tuple-element.102.fields, f32[27,32,1024]{2,1,0:T(8,128)} %get-tuple-element.104._), custom_call_target="tpu_custom_call", output_to_operand_aliasing={{}: (2, {})} | custom-call | bytes 6291456 | tf_op jit(solution)/shard_map/adjoint_high/pallas_call | solution.py:813
  50.7 0.0 collective-permute-done.18
  50.8 0.6 %collective-permute-done.17 = f32[8,128]{1,0:T(8,128)S(1)} collective-permute-done((f32[8,128]{1,0:T(8,128)S(1)}, f32[8,128]{1,0:T(8,128)S(1)}, u32[]{:S(2)}, u32[]{:S(2)}) %collective-permute-start.17) | collective-permute-done | bytes 4128 | tf_op jit(solution)/shard_map/ppermute | solution.py:763
  51.4 0.0 collective-permute-done.16
  51.4 0.8 %normalize.1 = f32[32,1024]{1,0:T(8,128)} custom-call(f32[256,128]{1,0:T(8,128)S(1)} %get-tuple-element.105.total, f32[8,128]{1,0:T(8,128)S(1)} %maximum_maximum_fusion.peak), custom_call_target="tpu_custom_call" | custom-call | tf_op jit(solution)/shard_map/normalize/pallas_call | solution.py:813
  (3 shorter events, 0.0 us)
Async XLA Ops:
  3.0 10.6 %collective-permute-start = (f32[480,128]{1,0:T(8,128)S(1)}, f32[480,128]{1,0:T(8,128)S(1)}, u32[]{:S(2)}, u32[]{:S(2)}) collective-permute-start(f32[480,128]{1,0:T(8,128)S(1)} %get-tuple-element.64), channel_id=1, source_target_pairs={{1,2},{2,1},{3,4},{4,3},{5,6},{6,5},{7,0},{0,7},{9,10},{10,9},{11,... | collective-permute-start | bytes 737288 | tf_op jit(solution)/shard_map/ppermute | solution.py:740
  6.4 7.2 %collective-permute-start.1 = (f32[480,128]{1,0:T(8,128)S(1)}, f32[480,128]{1,0:T(8,128)S(1)}, u32[]{:S(2)}, u32[]{:S(2)}) collective-permute-start(f32[480,128]{1,0:T(8,128)S(1)} %get-tuple-element.65), channel_id=1, source_target_pairs={{0,1},{1,0},{2,3},{3,2},{4,5},{5,4},{6,7},{7,6},{8,9},{9,8},{10,11... | collective-permute-start | bytes 737288 | tf_op jit(solution)/shard_map/ppermute | solution.py:739
  7.0 10.8 %collective-permute-start.2 = (f32[240,128]{1,0:T(8,128)S(1)}, f32[240,128]{1,0:T(8,128)S(1)}, u32[]{:S(2)}, u32[]{:S(2)}) collective-permute-start(f32[240,128]{1,0:T(8,128)S(1)} %get-tuple-element.69), channel_id=1, source_target_pairs={{8,16},{16,8},{24,0},{0,24},{9,17},{17,9},{25,1},{1,25},{10,18},{1... | collective-permute-start | bytes 368648 | tf_op jit(solution)/shard_map/ppermute | solution.py:740
  10.7 7.1 %collective-permute-start.3 = (f32[240,128]{1,0:T(8,128)S(1)}, f32[240,128]{1,0:T(8,128)S(1)}, u32[]{:S(2)}, u32[]{:S(2)}) collective-permute-start(f32[240,128]{1,0:T(8,128)S(1)} %get-tuple-element.70), channel_id=1, source_target_pairs={{0,8},{8,0},{16,24},{24,16},{1,9},{9,1},{17,25},{25,17},{2,10},{10... | collective-permute-start | bytes 368648 | tf_op jit(solution)/shard_map/ppermute | solution.py:739
  13.6 4.2 %copy-start = (f32[27,32,1024]{2,1,0:T(8,128)S(1)}, f32[27,32,1024]{2,1,0:T(8,128)}, u32[]{:S(2)}) copy-start(f32[27,32,1024]{2,1,0:T(8,128)} %refs_1_.3) | copy-start | bytes 10616836
  13.7 6.0 %collective-permute-start.4 = (f32[32,128]{1,0:T(8,128)S(1)}, f32[32,128]{1,0:T(8,128)S(1)}, u32[]{:S(2)}, u32[]{:S(2)}) collective-permute-start(f32[32,128]{1,0:T(8,128)S(1)} %get-tuple-element.76), channel_id=1, source_target_pairs={{0,8},{8,0},{16,24},{24,16},{1,9},{9,1},{17,25},{25,17},{2,10},{10... | collective-permute-start | bytes 49160 | tf_op jit(solution)/shard_map/ppermute | solution.py:739
  15.8 5.5 %collective-permute-start.5 = (f32[32,128]{1,0:T(8,128)S(1)}, f32[32,128]{1,0:T(8,128)S(1)}, u32[]{:S(2)}, u32[]{:S(2)}) collective-permute-start(f32[32,128]{1,0:T(8,128)S(1)} %get-tuple-element.77), channel_id=1, source_target_pairs={{8,16},{16,8},{24,0},{0,24},{9,17},{17,9},{25,1},{1,25},{10,18},{1... | collective-permute-start | bytes 49160 | tf_op jit(solution)/shard_map/ppermute | solution.py:740
  22.8 7.7 %collective-permute-start.6 = (f32[448,128]{1,0:T(8,128)S(1)}, f32[448,128]{1,0:T(8,128)S(1)}, u32[]{:S(2)}, u32[]{:S(2)}) collective-permute-start(f32[448,128]{1,0:T(8,128)S(1)} %get-tuple-element.86), channel_id=1, source_target_pairs={{1,2},{2,1},{3,4},{4,3},{5,6},{6,5},{7,0},{0,7},{9,10},{10,9},{11,... | collective-permute-start | bytes 688136 | tf_op jit(solution)/shard_map/ppermute | solution.py:740
  22.8 7.6 %collective-permute-start.7 = (f32[448,128]{1,0:T(8,128)S(1)}, f32[448,128]{1,0:T(8,128)S(1)}, u32[]{:S(2)}, u32[]{:S(2)}) collective-permute-start(f32[448,128]{1,0:T(8,128)S(1)} %get-tuple-element.87), channel_id=1, source_target_pairs={{0,1},{1,0},{2,3},{3,2},{4,5},{5,4},{6,7},{7,6},{8,9},{9,8},{10,11... | collective-permute-start | bytes 688136 | tf_op jit(solution)/shard_map/ppermute | solution.py:739
  25.1 8.1 %collective-permute-start.8 = (f32[216,128]{1,0:T(8,128)S(1)}, f32[216,128]{1,0:T(8,128)S(1)}, u32[]{:S(2)}, u32[]{:S(2)}) collective-permute-start(f32[216,128]{1,0:T(8,128)S(1)} %get-tuple-element.92), channel_id=1, source_target_pairs={{8,16},{16,8},{24,0},{0,24},{9,17},{17,9},{25,1},{1,25},{10,18},{1... | collective-permute-start | bytes 331784 | tf_op jit(solution)/shard_map/ppermute | solution.py:740
  25.9 7.7 %collective-permute-start.9 = (f32[216,128]{1,0:T(8,128)S(1)}, f32[216,128]{1,0:T(8,128)S(1)}, u32[]{:S(2)}, u32[]{:S(2)}) collective-permute-start(f32[216,128]{1,0:T(8,128)S(1)} %get-tuple-element.93), channel_id=1, source_target_pairs={{0,8},{8,0},{16,24},{24,16},{1,9},{9,1},{17,25},{25,17},{2,10},{10... | collective-permute-start | bytes 331784 | tf_op jit(solution)/shard_map/ppermute | solution.py:739
  30.6 4.9 %collective-permute-start.10 = (f32[32,128]{1,0:T(8,128)S(1)}, f32[32,128]{1,0:T(8,128)S(1)}, u32[]{:S(2)}, u32[]{:S(2)}) collective-permute-start(f32[32,128]{1,0:T(8,128)S(1)} %get-tuple-element.99), channel_id=1, source_target_pairs={{0,8},{8,0},{16,24},{24,16},{1,9},{9,1},{17,25},{25,17},{2,10},{10... | collective-permute-start | bytes 49160 | tf_op jit(solution)/shard_map/ppermute | solution.py:739
  30.6 5.6 %collective-permute-start.11 = (f32[32,128]{1,0:T(8,128)S(1)}, f32[32,128]{1,0:T(8,128)S(1)}, u32[]{:S(2)}, u32[]{:S(2)}) collective-permute-start(f32[32,128]{1,0:T(8,128)S(1)} %get-tuple-element.100), channel_id=1, source_target_pairs={{8,16},{16,8},{24,0},{0,24},{9,17},{17,9},{25,1},{1,25},{10,18},{1... | collective-permute-start | bytes 49160 | tf_op jit(solution)/shard_map/ppermute | solution.py:740
  38.3 1.2 %collective-permute-start.12 = (f32[8,128]{1,0:T(8,128)S(1)}, f32[8,128]{1,0:T(8,128)S(1)}, u32[]{:S(2)}, u32[]{:S(2)}) collective-permute-start(f32[8,128]{1,0:T(8,128)S(1)} %get-tuple-element.103), channel_id=1, source_target_pairs={{0,1},{1,0},{2,3},{3,2},{4,5},{5,4},{6,7},{7,6},{8,9},{9,8},{10,11... | collective-permute-start | bytes 12296 | tf_op jit(solution)/shard_map/ppermute | solution.py:746
  39.6 4.6 %collective-permute-start.15 = (f32[8,128]{1,0:T(8,128)S(1)}, f32[8,128]{1,0:T(8,128)S(1)}, u32[]{:S(2)}, u32[]{:S(2)}) collective-permute-start(f32[8,128]{1,0:T(8,128)S(1)} %max.21.near), channel_id=1, source_target_pairs={{0,7},{1,6},{2,5},{3,4},{4,3},{5,2},{6,1},{7,0},{8,15},{9,14},{10,... | collective-permute-start | bytes 12296 | tf_op jit(solution)/shard_map/ppermute | solution.py:756
  41.6 3.0 %collective-permute-start.14 = (f32[8,128]{1,0:T(8,128)S(1)}, f32[8,128]{1,0:T(8,128)S(1)}, u32[]{:S(2)}, u32[]{:S(2)}) collective-permute-start(f32[8,128]{1,0:T(8,128)S(1)} %max.21.near), channel_id=1, source_target_pairs={{0,5},{1,4},{2,7},{3,6},{4,1},{5,0},{6,3},{7,2},{8,13},{9,12},{10,... | collective-permute-start | bytes 12296 | tf_op jit(solution)/shard_map/ppermute | solution.py:756
  42.2 3.0 %collective-permute-start.13 = (f32[8,128]{1,0:T(8,128)S(1)}, f32[8,128]{1,0:T(8,128)S(1)}, u32[]{:S(2)}, u32[]{:S(2)}) collective-permute-start(f32[8,128]{1,0:T(8,128)S(1)} %max.21.near), channel_id=1, source_target_pairs={{0,3},{1,2},{2,1},{3,0},{4,7},{5,6},{6,5},{7,4},{8,11},{9,10},{10,... | collective-permute-start | bytes 12296 | tf_op jit(solution)/shard_map/ppermute | solution.py:756
  45.3 5.5 %collective-permute-start.18 = (f32[8,128]{1,0:T(8,128)S(1)}, f32[8,128]{1,0:T(8,128)S(1)}, u32[]{:S(2)}, u32[]{:S(2)}) collective-permute-start(f32[8,128]{1,0:T(8,128)S(1)} %maximum_maximum_fusion.1), channel_id=1, source_target_pairs={{0,25},{1,24},{2,27},{3,26},{4,29},{5,28},{6,31},{7,30},{8,17},{9,... | collective-permute-start | bytes 12296 | tf_op jit(solution)/shard_map/ppermute | solution.py:763
  47.4 3.9 %collective-permute-start.17 = (f32[8,128]{1,0:T(8,128)S(1)}, f32[8,128]{1,0:T(8,128)S(1)}, u32[]{:S(2)}, u32[]{:S(2)}) collective-permute-start(f32[8,128]{1,0:T(8,128)S(1)} %maximum_maximum_fusion.1), channel_id=1, source_target_pairs={{0,17},{1,16},{2,19},{3,18},{4,21},{5,20},{6,23},{7,22},{8,25},{9,... | collective-permute-start | bytes 12296 | tf_op jit(solution)/shard_map/ppermute | solution.py:763
  47.4 3.9 %collective-permute-start.16 = (f32[8,128]{1,0:T(8,128)S(1)}, f32[8,128]{1,0:T(8,128)S(1)}, u32[]{:S(2)}, u32[]{:S(2)}) collective-permute-start(f32[8,128]{1,0:T(8,128)S(1)} %maximum_maximum_fusion.1), channel_id=1, source_target_pairs={{0,9},{1,8},{2,11},{3,10},{4,13},{5,12},{6,15},{7,14},{8,1},{9,0},... | collective-permute-start | bytes 12296 | tf_op jit(solution)/shard_map/ppermute | solution.py:763

commit v8 on v6

--- a/solution.py
+++ b/solution.py
@@ -392,7 +392,7 @@
         return carry
 
     count = last + 1 - first
-    unroll = max(n for n in (1, 2, 3, 4) if count % n == 0)
+    unroll = max(n for n in (1, 2, 3, 4, 6, 8) if count % n == 0)
     lax.fori_loop(first, last + 1, step, 0, unroll=unroll)
 
 
@@ -614,7 +614,7 @@
     core_tiles(g, seed_tile(g, out, adjoint, stage, field, masks))
 
 
-def side_seed_kernel(g, _post, _out, _state, _stage, _field, first, second, adjoint, *refs):
+def side_seed_kernel(g, _post, _out, _state, _stage, _field, second, first, adjoint, *refs):
     post, out, state1, stage, field, *faces = refs
     masks = lane_masks(16)
     by_parity("gx", second, first, functools.partial(unpack_corners, g, post, 1, 30))
@@ -668,7 +668,7 @@
 
 
 def total_kernel(g, *refs):
-    state1, state0, first, second, field, out, before, total, parts, peak = refs[5:]
+    state1, state0, second, first, field, out, before, total, parts, peak = refs[5:]
     masks = lane_masks(16)
     by_parity("gx", second, first, functools.partial(unpack_corners, g, field, -1, 27))
     corner_tiles(g, field, out, -1, 27, masks, adjoint_second(g, state1, before))
@@ -813,7 +813,7 @@
             relay_kernel(grid, sign, count, *refs)
 
         buf, *parcels = call("relay", kernel, [buf, *parcels], corners(count), kept=1)
-        return buf, swap("gx", nx, *parcels)
+        return buf, swap("gx", nx, *parcels)[::-1]
 
     flat_space = [vmem(*porosity.shape)] + [pltpu.VMEM(porosity.shape, jnp.int32)] * 2
     post, state0, staged, *rest = call(

time: 52 us -> 51.3 us (0.987)
  waiting for transfers between devices: 7.2 us -> 8.71 us
  starting transfers between devices: 24.8 us -> 23.3 us
  Pallas kernels: 18.9 us -> 18.3 us
    ppermute x6, starting transfers between devices: 3.53 us -> 0.08 us  [swap(): lax.ppermute(first, axis, swap_pairs(count, 0))]
    ppermute x6, waiting for transfers between devices: 0.07 us -> 2.95 us  [swap(): lax.ppermute(first, axis, swap_pairs(count, 0))]
    ppermute x6, starting transfers between devices: 14.4 us -> 16.1 us  [swap(): lax.ppermute(second, axis, swap_pairs(count, 1))]
    ppermute x3, waiting for transfers between devices: 1.18 us -> 0.01 us  [largest_of_all(): parts.append(lax.ppermute(peak, 'gy', pairs))]
    pallas_call x14, Pallas kernels: 18.9 us -> 18.3 us  [call(): pl.pallas_call(functools.partial(kernel, g), in_specs=in_specs, out_shape...]
  transfers between devices with their start and end apart: 19 -> 19, of which waited for: 7 -> 9; matrix products, arithmetic and copies ran while one was open for 0% -> 0% of each run, Pallas kernels for 23% -> 23%
where the time goes in v8:
time: 51.3 us; the launch traced here: 51.2 us
  starting transfers between devices  23.3 us (45%)
  Pallas kernels  18.3 us (36%)
  waiting for transfers between devices  8.71 us (17%)
  between operations  0.83 us (2%)
    pallas_call x14, Pallas kernels, call(): pl.pallas_call(functools.partial(kernel, g), in_specs=in_specs, out_shape...  18.3 us
    ppermute x6, starting transfers between devices, swap(): lax.ppermute(second, axis, swap_pairs(count, 1))  16.1 us
    ppermute x6, waiting for transfers between devices, swap(): lax.ppermute(second, axis, swap_pairs(count, 1))  4.52 us
    ppermute x3, starting transfers between devices, largest_of_all(): parts.append(lax.ppermute(peak, ('gx', 'gy'), pairs))  4.12 us
    ppermute x3, starting transfers between devices, largest_of_all(): parts.append(lax.ppermute(peak, 'gy', pairs))  2.98 us
    ppermute x6, waiting for transfers between devices, swap(): lax.ppermute(first, axis, swap_pairs(count, 0))  2.95 us
    ppermute x1, waiting for transfers between devices, largest_of_all(): lax.ppermute(peak, 'gy', [(i, i ^ 1) for i in range(ny)])  1.15 us
  transfers between devices with their start and end apart: 19, of which 9 were waited for; matrix products, arithmetic and copies ran while one was open for 0% of the time, Pallas kernels for 23%

profile of v8, /device:TPU:0, one launch (start us, length us, event | category | flops | bytes accessed | tf_op | source)
XLA Modules:
  0.0 51.2 jit_solution(7671782442924696004)
XLA Ops:
  0.6 2.6 %side_first.1 = (f32[14408,128]{1,0:T(8,128)S(1)}, f32[1792,128]{1,0:T(8,128)S(1)}, f32[8,27,32,128]{3,2,1,0:T(8,128)S(1)}, f32[32,1024]{1,0:T(8,128)S(1)}, s32[...) custom-call(f32[27,32,1024]{2,1,0:T(8,128)} %pops.1, ...), custom_call_target="tpu_custom_call" | custom-call | tf_op jit(solution)/shard_map/side_first/pallas_call | solution.py:794
  3.2 3.4 %collective-permute-start = (f32[480,128]{1,0:T(8,128)S(1)}, f32[480,128]{1,0:T(8,128)S(1)}, u32[]{:S(2)}, u32[]{:S(2)}) collective-permute-start(f32[480,128]{1,0:T(8,128)S(1)} %get-tuple-element.64), channel_id=1, source_target_pairs={{1,2},{2,1},{3,4},{4,3},{5,6},{6,5},{7,0},{0,7},{9,10},{10,9},{11,... | collective-permute-start | bytes 737288 | tf_op jit(solution)/shard_map/ppermute | solution.py:723
  6.6 0.0 collective-permute-start.1
  6.6 0.6 %rim_first.1 = (f32[14408,128]{1,0:T(8,128)S(1)}, f32[1792,128]{1,0:T(8,128)S(1)}, f32[240,128]{1,0:T(8,128)S(1)}, f32[240,128]{1,0:T(8,128)S(1)}) custom-call(f32[14408,128]{1,0:T(8,128)S(1)} %get-tuple-element.55._out, f32[1792,128]{1,0:T(8,128)S(1)} %get-tuple-element.56._state, ...), custom_call_target="tpu_custom_call", output_to_operand_aliasing={{0}: (0, {}), {1}: (1, {})} | custom-call | bytes 12582912 | tf_op jit(solution)/shard_map/rim_first/pallas_call | solution.py:794
  7.2 3.7 %collective-permute-start.2 = (f32[240,128]{1,0:T(8,128)S(1)}, f32[240,128]{1,0:T(8,128)S(1)}, u32[]{:S(2)}, u32[]{:S(2)}) collective-permute-start(f32[240,128]{1,0:T(8,128)S(1)} %get-tuple-element.69), channel_id=1, source_target_pairs={{8,16},{16,8},{24,0},{0,24},{9,17},{17,9},{25,1},{1,25},{10,18},{1... | collective-permute-start | bytes 368648 | tf_op jit(solution)/shard_map/ppermute | solution.py:723
  10.9 0.0 collective-permute-start.3
  10.9 1.2 %inner_first.1 = (f32[14408,128]{1,0:T(8,128)S(1)}, f32[1792,128]{1,0:T(8,128)S(1)}, f32[12968,128]{1,0:T(8,128)S(1)}, f32[2184,128]{1,0:T(8,128)S(1)}) custom-call(f32[14408,128]{1,0:T(8,128)S(1)} %get-tuple-element.61._, f32[1792,128]{1,0:T(8,128)S(1)} %get-tuple-element.62._state, ...), custom_call_target="tpu_custom_call", output_to_operand_aliasing={{0}: (0, {}), {1}: (1, {})} | custom-call | bytes 12582912 | tf_op jit(solution)/shard_map/inner_first/pallas_call | solution.py:794
  12.1 0.0 copy-start
  12.1 0.2 collective-permute-done.refs_1_
  12.3 0.0 collective-permute-done.1.refs_2_
  12.3 0.1 relay.2
  12.4 5.2 %collective-permute-start.4 = (f32[32,128]{1,0:T(8,128)S(1)}, f32[32,128]{1,0:T(8,128)S(1)}, u32[]{:S(2)}, u32[]{:S(2)}) collective-permute-start(f32[32,128]{1,0:T(8,128)S(1)} %get-tuple-element.76), channel_id=1, source_target_pairs={{8,16},{16,8},{24,0},{0,24},{9,17},{17,9},{25,1},{1,25},{10,18},{1... | collective-permute-start | bytes 49160 | tf_op jit(solution)/shard_map/ppermute | solution.py:723
  17.6 0.0 collective-permute-start.5
  17.6 0.0 collective-permute-done.2.b
  17.6 0.2 collective-permute-done.3.a
  17.8 0.0 copy-done
  17.8 1.6 %middle_second.1 = (f32[14408,128]{1,0:T(8,128)S(1)}, f32[12968,128]{1,0:T(8,128)S(1)}, f32[2184,128]{1,0:T(8,128)S(1)}, f32[8,27,32,128]{3,2,1,0:T(8,128)S(1)}, f32[12968,128]{1,0:T(8,128)S(1)}) custom-call(f32[14408,128]{1,0:T(8,128)S(1)} %get-tuple-element.66._post, ...), custom_call_target="tpu_custom_call", output_to_operand_aliasing={{0}: (0, {}), {1}: (1, {}), {2}: (2, {})} | custom-call | bytes 12582912 | tf_op jit(solution)/shard_map/middle_second/pallas_call | solution.py:794
  19.4 0.0 collective-permute-done.4.second
  19.4 1.9 %collective-permute-done.5.first = f32[32,128]{1,0:T(8,128)S(1)} collective-permute-done((f32[32,128]{1,0:T(8,128)S(1)}, f32[32,128]{1,0:T(8,128)S(1)}, u32[]{:S(2)}, u32[]{:S(2)}) %collective-permute-start.5) | collective-permute-done | bytes 16416 | tf_op jit(solution)/shard_map/ppermute | solution.py:722
  21.3 1.4 %side_seed.1 = (f32[14408,128]{1,0:T(8,128)S(1)}, f32[12968,128]{1,0:T(8,128)S(1)}, f32[2184,128]{1,0:T(8,128)S(1)}, f32[8,27,32,128]{3,2,1,0:T(8,128)S(1)}, f32...) custom-call(f32[14408,128]{1,0:T(8,128)S(1)} %get-tuple-element.71._, ...), custom_call_target="tpu_custom_call", output_to_operand_aliasing={{0}: (0, {}), {1}: (1, {}), {2}: (2, {}), {3}: (3, {}), {4}... | custom-call | tf_op jit(solution)/shard_map/side_seed/pallas_call | solution.py:794
  22.7 0.1 collective-permute-start.6
  22.8 0.1 collective-permute-start.7
  22.9 0.8 %rim_seed.1 = (f32[8,27,32,128]{3,2,1,0:T(8,128)S(1)}, f32[12968,128]{1,0:T(8,128)S(1)}, f32[216,128]{1,0:T(8,128)S(1)}, f32[216,128]{1,0:T(8,128)S(1)}) custom-call(f32[8,27,32,128]{3,2,1,0:T(8,128)S(1)} %get-tuple-element.78._stage, f32[12968,128]{1,0:T(8,128)S(1)} %get-tuple-element.79._field, ...), custom_call_target="tpu_custom_call", output_to_operand_aliasing={{0}: (0, {}), {1}: (1, {})} | custom-call | bytes 12582912 | tf_op jit(solution)/shard_map/rim_seed/pallas_call | solution.py:794
  23.7 1.9 %collective-permute-start.8 = (f32[216,128]{1,0:T(8,128)S(1)}, f32[216,128]{1,0:T(8,128)S(1)}, u32[]{:S(2)}, u32[]{:S(2)}) collective-permute-start(f32[216,128]{1,0:T(8,128)S(1)} %get-tuple-element.92), channel_id=1, source_target_pairs={{8,16},{16,8},{24,0},{0,24},{9,17},{17,9},{25,1},{1,25},{10,18},{1... | collective-permute-start | bytes 331784 | tf_op jit(solution)/shard_map/ppermute | solution.py:723
  25.6 0.0 collective-permute-start.9
  25.6 2.4 %inner_seed.1 = (f32[8,27,32,128]{3,2,1,0:T(8,128)S(1)}, f32[12968,128]{1,0:T(8,128)S(1)}, f32[12968,128]{1,0:T(8,128)S(1)}, f32[312,128]{1,0:T(8,128)S(1)}, f32[27,32,1024]{2,1,0:T(8,128)}) custom-call(f32[8,27,32,128]{3,2,1,0:T(8,128)S(1)} %get-tuple-element.81.kept, ...), custom_call_target="tpu_custom_call", output_to_operand_aliasing={{0}: (0, {}), {1}: (1, {})} | custom-call | bytes 12582912 | tf_op jit(solution)/shard_map/inner_seed/pallas_call | solution.py:794
  28.0 2.8 %collective-permute-done.6.refs_1_ = f32[448,128]{1,0:T(8,128)S(1)} collective-permute-done((f32[448,128]{1,0:T(8,128)S(1)}, f32[448,128]{1,0:T(8,128)S(1)}, u32[]{:S(2)}, u32[]{:S(2)}) %collective-permute-start.6) | collective-permute-done | bytes 229408 | tf_op jit(solution)/shard_map/ppermute | solution.py:723
  30.8 0.0 collective-permute-done.7.refs_2_
  30.8 0.1 relay.3
  31.0 1.9 %collective-permute-start.10 = (f32[32,128]{1,0:T(8,128)S(1)}, f32[32,128]{1,0:T(8,128)S(1)}, u32[]{:S(2)}, u32[]{:S(2)}) collective-permute-start(f32[32,128]{1,0:T(8,128)S(1)} %get-tuple-element.99), channel_id=1, source_target_pairs={{8,16},{16,8},{24,0},{0,24},{9,17},{17,9},{25,1},{1,25},{10,18},{1... | collective-permute-start | bytes 49160 | tf_op jit(solution)/shard_map/ppermute | solution.py:723
  32.8 0.0 collective-permute-start.11
  32.8 0.0 collective-permute-done.8.b
  32.8 0.7 %collective-permute-done.9.a = f32[216,128]{1,0:T(8,128)S(1)} collective-permute-done((f32[216,128]{1,0:T(8,128)S(1)}, f32[216,128]{1,0:T(8,128)S(1)}, u32[]{:S(2)}, u32[]{:S(2)}) %collective-permute-start.9) | collective-permute-done | bytes 110624 | tf_op jit(solution)/shard_map/ppermute | solution.py:722
  33.5 1.5 %middle_adjoint.1 = (f32[12968,128]{1,0:T(8,128)S(1)}, f32[12968,128]{1,0:T(8,128)S(1)}, f32[312,128]{1,0:T(8,128)S(1)}, f32[256,128]{1,0:T(8,128)S(1)}, f32[1280,128]{1,0:T(8,128)S(1)}) custom-call(f32[12968,128]{1,0:T(8,128)S(1)} %get-tuple-element.88._field, ...), custom_call_target="tpu_custom_call", output_to_operand_aliasing={{0}: (0, {}), {1}: (1, {}), {2}: (2, {})} | custom-call | bytes 12582912 | tf_op jit(solution)/shard_map/middle_adjoint/pallas_call | solution.py:794
  35.1 1.5 %collective-permute-done.10.refs_7_ = f32[32,128]{1,0:T(8,128)S(1)} collective-permute-done((f32[32,128]{1,0:T(8,128)S(1)}, f32[32,128]{1,0:T(8,128)S(1)}, u32[]{:S(2)}, u32[]{:S(2)}) %collective-permute-start.10) | collective-permute-done | bytes 16416 | tf_op jit(solution)/shard_map/ppermute | solution.py:723
  36.6 0.2 collective-permute-done.11.refs_8_
  36.7 2.0 %total.1 = (f32[12968,128]{1,0:T(8,128)S(1)}, f32[12968,128]{1,0:T(8,128)S(1)}, f32[312,128]{1,0:T(8,128)S(1)}, f32[256,128]{1,0:T(8,128)S(1)}, f32[1280,128]{1,0:T(8,128)S(1)}, /*index=5*/f32[8,128]{1,0:T(8,128)S(1)}) custom-call(f32[12968,128]{1,0:T(8,128)S(1)} %get-tuple-element.94.r, ...), custom_call_target="tpu_custom_call", output_to_operand_aliasing={{0}: (0, {}), {1}: (1, {}), {2}: (2, {}), {3}: (3, {}), {4}... | custom-call | tf_op jit(solution)/shard_map/total/pallas_call | solution.py:794
  38.7 0.1 collective-permute-start.12
  38.8 1.2 %collective-permute-done.12 = f32[8,128]{1,0:T(8,128)S(1)} collective-permute-done((f32[8,128]{1,0:T(8,128)S(1)}, f32[8,128]{1,0:T(8,128)S(1)}, u32[]{:S(2)}, u32[]{:S(2)}) %collective-permute-start.12) | collective-permute-done | bytes 4128 | tf_op jit(solution)/shard_map/ppermute | solution.py:729
  40.0 1.0 %collective-permute-start.15 = (f32[8,128]{1,0:T(8,128)S(1)}, f32[8,128]{1,0:T(8,128)S(1)}, u32[]{:S(2)}, u32[]{:S(2)}) collective-permute-start(f32[8,128]{1,0:T(8,128)S(1)} %max.21.near), channel_id=1, source_target_pairs={{0,7},{1,6},{2,5},{3,4},{4,3},{5,2},{6,1},{7,0},{8,15},{9,14},{10,... | collective-permute-start | bytes 12296 | tf_op jit(solution)/shard_map/ppermute | solution.py:739
  41.0 0.0 collective-permute-start.14
  41.0 2.0 %collective-permute-start.13 = (f32[8,128]{1,0:T(8,128)S(1)}, f32[8,128]{1,0:T(8,128)S(1)}, u32[]{:S(2)}, u32[]{:S(2)}) collective-permute-start(f32[8,128]{1,0:T(8,128)S(1)} %max.21.near), channel_id=1, source_target_pairs={{0,3},{1,2},{2,1},{3,0},{4,7},{5,6},{6,5},{7,4},{8,11},{9,10},{10,... | collective-permute-start | bytes 12296 | tf_op jit(solution)/shard_map/ppermute | solution.py:739
  43.0 1.6 %adjoint_low.1 = (f32[8,128]{1,0:T(8,128)S(1)}, f32[27,32,1024]{2,1,0:T(8,128)}) custom-call(f32[12968,128]{1,0:T(8,128)S(1)} %get-tuple-element.101.buf, f32[1280,128]{1,0:T(8,128)S(1)} %get-tuple-element.102.fields, f32[8,128]{1,0:T(8,128)S(1)} %max.21.near), custom_call_target="tpu_custom_call" | custom-call | bytes 6291456 | tf_op jit(solution)/shard_map/adjoint_low/pallas_call | solution.py:794
  44.6 0.0 collective-permute-done.15
  44.6 0.0 collective-permute-done.14
  44.6 0.0 collective-permute-done.13
  44.6 1.9 %collective-permute-start.18 = (f32[8,128]{1,0:T(8,128)S(1)}, f32[8,128]{1,0:T(8,128)S(1)}, u32[]{:S(2)}, u32[]{:S(2)}) collective-permute-start(f32[8,128]{1,0:T(8,128)S(1)} %maximum_maximum_fusion.1), channel_id=1, source_target_pairs={{0,25},{1,24},{2,27},{3,26},{4,29},{5,28},{6,31},{7,30},{8,17},{9,... | collective-permute-start | bytes 12296 | tf_op jit(solution)/shard_map/ppermute | solution.py:746
  46.5 0.0 collective-permute-start.17
  46.5 2.3 %collective-permute-start.16 = (f32[8,128]{1,0:T(8,128)S(1)}, f32[8,128]{1,0:T(8,128)S(1)}, u32[]{:S(2)}, u32[]{:S(2)}) collective-permute-start(f32[8,128]{1,0:T(8,128)S(1)} %maximum_maximum_fusion.1), channel_id=1, source_target_pairs={{0,9},{1,8},{2,11},{3,10},{4,13},{5,12},{6,15},{7,14},{8,1},{9,0},... | collective-permute-start | bytes 12296 | tf_op jit(solution)/shard_map/ppermute | solution.py:746
  48.7 1.6 %adjoint_high.1 = f32[27,32,1024]{2,1,0:T(8,128)} custom-call(f32[12968,128]{1,0:T(8,128)S(1)} %get-tuple-element.101.buf, f32[1280,128]{1,0:T(8,128)S(1)} %get-tuple-element.102.fields, f32[27,32,1024]{2,1,0:T(8,128)} %get-tuple-element.104._), custom_call_target="tpu_custom_call", output_to_operand_aliasing={{}: (2, {})} | custom-call | bytes 6291456 | tf_op jit(solution)/shard_map/adjoint_high/pallas_call | solution.py:794
  50.3 0.0 collective-permute-done.18
  50.3 0.1 collective-permute-done.17
  50.4 0.0 collective-permute-done.16
  50.4 0.8 %normalize.1 = f32[32,1024]{1,0:T(8,128)} custom-call(f32[256,128]{1,0:T(8,128)S(1)} %get-tuple-element.105.total, f32[8,128]{1,0:T(8,128)S(1)} %maximum_maximum_fusion.peak), custom_call_target="tpu_custom_call" | custom-call | tf_op jit(solution)/shard_map/normalize/pallas_call | solution.py:794
  (3 shorter events, 0.0 us)
Async XLA Ops:
  3.2 9.1 %collective-permute-start = (f32[480,128]{1,0:T(8,128)S(1)}, f32[480,128]{1,0:T(8,128)S(1)}, u32[]{:S(2)}, u32[]{:S(2)}) collective-permute-start(f32[480,128]{1,0:T(8,128)S(1)} %get-tuple-element.64), channel_id=1, source_target_pairs={{1,2},{2,1},{3,4},{4,3},{5,6},{6,5},{7,0},{0,7},{9,10},{10,9},{11,... | collective-permute-start | bytes 737288 | tf_op jit(solution)/shard_map/ppermute | solution.py:723
  6.6 5.7 %collective-permute-start.1 = (f32[480,128]{1,0:T(8,128)S(1)}, f32[480,128]{1,0:T(8,128)S(1)}, u32[]{:S(2)}, u32[]{:S(2)}) collective-permute-start(f32[480,128]{1,0:T(8,128)S(1)} %get-tuple-element.65), channel_id=1, source_target_pairs={{0,1},{1,0},{2,3},{3,2},{4,5},{5,4},{6,7},{7,6},{8,9},{9,8},{10,11... | collective-permute-start | bytes 737288 | tf_op jit(solution)/shard_map/ppermute | solution.py:722
  7.2 10.4 %collective-permute-start.2 = (f32[240,128]{1,0:T(8,128)S(1)}, f32[240,128]{1,0:T(8,128)S(1)}, u32[]{:S(2)}, u32[]{:S(2)}) collective-permute-start(f32[240,128]{1,0:T(8,128)S(1)} %get-tuple-element.69), channel_id=1, source_target_pairs={{8,16},{16,8},{24,0},{0,24},{9,17},{17,9},{25,1},{1,25},{10,18},{1... | collective-permute-start | bytes 368648 | tf_op jit(solution)/shard_map/ppermute | solution.py:723
  10.9 6.9 %collective-permute-start.3 = (f32[240,128]{1,0:T(8,128)S(1)}, f32[240,128]{1,0:T(8,128)S(1)}, u32[]{:S(2)}, u32[]{:S(2)}) collective-permute-start(f32[240,128]{1,0:T(8,128)S(1)} %get-tuple-element.70), channel_id=1, source_target_pairs={{0,8},{8,0},{16,24},{24,16},{1,9},{9,1},{17,25},{25,17},{2,10},{10... | collective-permute-start | bytes 368648 | tf_op jit(solution)/shard_map/ppermute | solution.py:722
  12.1 5.7 %copy-start = (f32[27,32,1024]{2,1,0:T(8,128)S(1)}, f32[27,32,1024]{2,1,0:T(8,128)}, u32[]{:S(2)}) copy-start(f32[27,32,1024]{2,1,0:T(8,128)} %refs_1_.3) | copy-start | bytes 10616836
  12.4 7.0 %collective-permute-start.4 = (f32[32,128]{1,0:T(8,128)S(1)}, f32[32,128]{1,0:T(8,128)S(1)}, u32[]{:S(2)}, u32[]{:S(2)}) collective-permute-start(f32[32,128]{1,0:T(8,128)S(1)} %get-tuple-element.76), channel_id=1, source_target_pairs={{8,16},{16,8},{24,0},{0,24},{9,17},{17,9},{25,1},{1,25},{10,18},{1... | collective-permute-start | bytes 49160 | tf_op jit(solution)/shard_map/ppermute | solution.py:723
  17.6 3.7 %collective-permute-start.5 = (f32[32,128]{1,0:T(8,128)S(1)}, f32[32,128]{1,0:T(8,128)S(1)}, u32[]{:S(2)}, u32[]{:S(2)}) collective-permute-start(f32[32,128]{1,0:T(8,128)S(1)} %get-tuple-element.77), channel_id=1, source_target_pairs={{0,8},{8,0},{16,24},{24,16},{1,9},{9,1},{17,25},{25,17},{2,10},{10... | collective-permute-start | bytes 49160 | tf_op jit(solution)/shard_map/ppermute | solution.py:722
  22.7 8.1 %collective-permute-start.6 = (f32[448,128]{1,0:T(8,128)S(1)}, f32[448,128]{1,0:T(8,128)S(1)}, u32[]{:S(2)}, u32[]{:S(2)}) collective-permute-start(f32[448,128]{1,0:T(8,128)S(1)} %get-tuple-element.86), channel_id=1, source_target_pairs={{1,2},{2,1},{3,4},{4,3},{5,6},{6,5},{7,0},{0,7},{9,10},{10,9},{11,... | collective-permute-start | bytes 688136 | tf_op jit(solution)/shard_map/ppermute | solution.py:723
  22.8 8.1 %collective-permute-start.7 = (f32[448,128]{1,0:T(8,128)S(1)}, f32[448,128]{1,0:T(8,128)S(1)}, u32[]{:S(2)}, u32[]{:S(2)}) collective-permute-start(f32[448,128]{1,0:T(8,128)S(1)} %get-tuple-element.87), channel_id=1, source_target_pairs={{0,1},{1,0},{2,3},{3,2},{4,5},{5,4},{6,7},{7,6},{8,9},{9,8},{10,11... | collective-permute-start | bytes 688136 | tf_op jit(solution)/shard_map/ppermute | solution.py:722
  23.7 9.1 %collective-permute-start.8 = (f32[216,128]{1,0:T(8,128)S(1)}, f32[216,128]{1,0:T(8,128)S(1)}, u32[]{:S(2)}, u32[]{:S(2)}) collective-permute-start(f32[216,128]{1,0:T(8,128)S(1)} %get-tuple-element.92), channel_id=1, source_target_pairs={{8,16},{16,8},{24,0},{0,24},{9,17},{17,9},{25,1},{1,25},{10,18},{1... | collective-permute-start | bytes 331784 | tf_op jit(solution)/shard_map/ppermute | solution.py:723
  25.6 7.9 %collective-permute-start.9 = (f32[216,128]{1,0:T(8,128)S(1)}, f32[216,128]{1,0:T(8,128)S(1)}, u32[]{:S(2)}, u32[]{:S(2)}) collective-permute-start(f32[216,128]{1,0:T(8,128)S(1)} %get-tuple-element.93), channel_id=1, source_target_pairs={{0,8},{8,0},{16,24},{24,16},{1,9},{9,1},{17,25},{25,17},{2,10},{10... | collective-permute-start | bytes 331784 | tf_op jit(solution)/shard_map/ppermute | solution.py:722
  31.0 5.6 %collective-permute-start.10 = (f32[32,128]{1,0:T(8,128)S(1)}, f32[32,128]{1,0:T(8,128)S(1)}, u32[]{:S(2)}, u32[]{:S(2)}) collective-permute-start(f32[32,128]{1,0:T(8,128)S(1)} %get-tuple-element.99), channel_id=1, source_target_pairs={{8,16},{16,8},{24,0},{0,24},{9,17},{17,9},{25,1},{1,25},{10,18},{1... | collective-permute-start | bytes 49160 | tf_op jit(solution)/shard_map/ppermute | solution.py:723
  32.8 3.9 %collective-permute-start.11 = (f32[32,128]{1,0:T(8,128)S(1)}, f32[32,128]{1,0:T(8,128)S(1)}, u32[]{:S(2)}, u32[]{:S(2)}) collective-permute-start(f32[32,128]{1,0:T(8,128)S(1)} %get-tuple-element.100), channel_id=1, source_target_pairs={{0,8},{8,0},{16,24},{24,16},{1,9},{9,1},{17,25},{25,17},{2,10},{10... | collective-permute-start | bytes 49160 | tf_op jit(solution)/shard_map/ppermute | solution.py:722
  38.7 1.2 %collective-permute-start.12 = (f32[8,128]{1,0:T(8,128)S(1)}, f32[8,128]{1,0:T(8,128)S(1)}, u32[]{:S(2)}, u32[]{:S(2)}) collective-permute-start(f32[8,128]{1,0:T(8,128)S(1)} %get-tuple-element.103), channel_id=1, source_target_pairs={{0,1},{1,0},{2,3},{3,2},{4,5},{5,4},{6,7},{7,6},{8,9},{9,8},{10,11... | collective-permute-start | bytes 12296 | tf_op jit(solution)/shard_map/ppermute | solution.py:729
  40.0 4.6 %collective-permute-start.15 = (f32[8,128]{1,0:T(8,128)S(1)}, f32[8,128]{1,0:T(8,128)S(1)}, u32[]{:S(2)}, u32[]{:S(2)}) collective-permute-start(f32[8,128]{1,0:T(8,128)S(1)} %max.21.near), channel_id=1, source_target_pairs={{0,7},{1,6},{2,5},{3,4},{4,3},{5,2},{6,1},{7,0},{8,15},{9,14},{10,... | collective-permute-start | bytes 12296 | tf_op jit(solution)/shard_map/ppermute | solution.py:739
  41.0 3.6 %collective-permute-start.14 = (f32[8,128]{1,0:T(8,128)S(1)}, f32[8,128]{1,0:T(8,128)S(1)}, u32[]{:S(2)}, u32[]{:S(2)}) collective-permute-start(f32[8,128]{1,0:T(8,128)S(1)} %max.21.near), channel_id=1, source_target_pairs={{0,5},{1,4},{2,7},{3,6},{4,1},{5,0},{6,3},{7,2},{8,13},{9,12},{10,... | collective-permute-start | bytes 12296 | tf_op jit(solution)/shard_map/ppermute | solution.py:739
  41.0 3.6 %collective-permute-start.13 = (f32[8,128]{1,0:T(8,128)S(1)}, f32[8,128]{1,0:T(8,128)S(1)}, u32[]{:S(2)}, u32[]{:S(2)}) collective-permute-start(f32[8,128]{1,0:T(8,128)S(1)} %max.21.near), channel_id=1, source_target_pairs={{0,3},{1,2},{2,1},{3,0},{4,7},{5,6},{6,5},{7,4},{8,11},{9,10},{10,... | collective-permute-start | bytes 12296 | tf_op jit(solution)/shard_map/ppermute | solution.py:739
  44.6 5.7 %collective-permute-start.18 = (f32[8,128]{1,0:T(8,128)S(1)}, f32[8,128]{1,0:T(8,128)S(1)}, u32[]{:S(2)}, u32[]{:S(2)}) collective-permute-start(f32[8,128]{1,0:T(8,128)S(1)} %maximum_maximum_fusion.1), channel_id=1, source_target_pairs={{0,25},{1,24},{2,27},{3,26},{4,29},{5,28},{6,31},{7,30},{8,17},{9,... | collective-permute-start | bytes 12296 | tf_op jit(solution)/shard_map/ppermute | solution.py:746
  46.5 3.9 %collective-permute-start.17 = (f32[8,128]{1,0:T(8,128)S(1)}, f32[8,128]{1,0:T(8,128)S(1)}, u32[]{:S(2)}, u32[]{:S(2)}) collective-permute-start(f32[8,128]{1,0:T(8,128)S(1)} %maximum_maximum_fusion.1), channel_id=1, source_target_pairs={{0,17},{1,16},{2,19},{3,18},{4,21},{5,20},{6,23},{7,22},{8,25},{9,... | collective-permute-start | bytes 12296 | tf_op jit(solution)/shard_map/ppermute | solution.py:746
  46.5 3.9 %collective-permute-start.16 = (f32[8,128]{1,0:T(8,128)S(1)}, f32[8,128]{1,0:T(8,128)S(1)}, u32[]{:S(2)}, u32[]{:S(2)}) collective-permute-start(f32[8,128]{1,0:T(8,128)S(1)} %maximum_maximum_fusion.1), channel_id=1, source_target_pairs={{0,9},{1,8},{2,11},{3,10},{4,13},{5,12},{6,15},{7,14},{8,1},{9,0},... | collective-permute-start | bytes 12296 | tf_op jit(solution)/shard_map/ppermute | solution.py:746

commit v9 on v8

--- a/solution.py
+++ b/solution.py
@@ -637,12 +637,13 @@
     def copy(k):
         return pltpu.make_async_copy(stage.at[k - 1], block_of(final, k), sems.at[k - 1])
 
-    copy(1).start()
-    copy(g.cols).start()
+    for k in (1, g.cols, *range(3, g.cols - 1)):
+        copy(k).start()
     seed = seed_tile(g, post, adjoint, stage, field, masks)
 
     near_core_tiles(g, seed)
-    every(2, g.cols - 1, lambda k: copy(k).start())
+    for k in (2, g.cols - 1):
+        copy(k).start()
     interior_tiles(g, step_tile(g, field, out, -1, 27, masks, adjoint_second(g, state1, total)))
     every(1, g.cols, lambda k: copy(k).wait())
 
@@ -680,7 +681,8 @@
     for start in range(0, g.local, size):
         value = jnp.abs(total[start : start + size, :]).reshape(-1, 8, LANES)
         largest = jnp.maximum(largest, jnp.max(value, 0))
-    peak[...] = largest
+    for n in range(0, peak.shape[0], 8):
+        peak[n : n + 8, :] = largest
 
 
 def adjoint_kernel(g, first, last, buf, parts, result, stage, sems):
@@ -722,34 +724,6 @@
         lax.ppermute(first, axis, swap_pairs(count, 0)),
         lax.ppermute(second, axis, swap_pairs(count, 1)),
     )
-
-
-def largest_of_all(peak, sizes, beside):
-    nx, ny = sizes
-    peak = jnp.maximum(peak, lax.ppermute(peak, "gy", [(i, i ^ 1) for i in range(ny)]))
-    groups = 0
-    for axis, count, first, widths in (("gy", ny, 2, (4, 4)), ("gx", nx, 1, (4, 2))):
-        step = first
-        for width in widths:
-            width = min(width, count // step)
-            parts = []
-            for n in range(1, width):
-                if axis == "gy":
-                    pairs = [(i, i ^ (n * step) ^ 1) for i in range(ny)]
-                    parts.append(lax.ppermute(peak, "gy", pairs))
-                else:
-                    pairs = [
-                        (i * ny + y, (i ^ (n * step)) * ny + (y ^ 1))
-                        for i in range(nx)
-                        for y in range(ny)
-                    ]
-                    parts.append(lax.ppermute(peak, ("gx", "gy"), pairs))
-            groups += 1
-            if groups == 1:
-                peak = beside(peak)
-            peak = functools.reduce(jnp.maximum, parts, peak)
-            step *= width
-    return peak
 
 
 def on_device(sizes, populations, adjoint_in, porosity, solid, labels):
@@ -893,40 +867,17 @@
         "total",
         total_kernel,
         [field, pulled, before, total, parts, state1, state0, *parcels],
-        [vmem(8, LANES)],
+        [vmem(8 * nx * ny, LANES)],
         kept=5,
     )
-    half = g.cols // 2
-    scratch = [vmem(half, 27, rows, LANES), pltpu.SemaphoreType.DMA((half,))]
-    halves = []
-
-    def first_half(peak):
-        def kernel(grid, buf, fields, near, echo, *refs):
-            echo[...] = near[...]
-            adjoint_kernel(grid, 1, half, buf, fields, *refs)
-
-        echo, result = call(
-            "adjoint_low",
-            kernel,
-            [pulled, parts, peak],
-            [vmem(8, LANES), whole],
-            scratch,
-            load=FLIGHT // 2,
-        )
-        halves.append(result)
-        return echo
-
-    largest = largest_of_all(peak, sizes, first_half)
+    largest = lax.all_to_all(peak, ("gx", "gy"), 0, 0, tiled=True)
     (adjoint_out,) = call(
-        "adjoint_high",
-        lambda grid, buf, fields, _, *refs: adjoint_kernel(
-            grid, 1 + half, g.cols, buf, fields, *refs
-        ),
+        "adjoint_first",
+        lambda grid, buf, fields, *refs: adjoint_kernel(grid, 1, g.cols, buf, fields, *refs),
         [pulled, parts],
         [whole],
-        scratch,
-        load=FLIGHT // 2,
-        result=halves[0],
+        [stage, sems],
+        load=FLIGHT,
     )
     (sensitivity,) = call(
         "normalize",

time: 51.3 us -> 54.2 us (1.057)
  local copies, waits for them, and re-layouts: 0.01 us -> 5.68 us
  starting transfers between devices: 23.3 us -> 19.1 us
  waiting for transfers between devices: 8.71 us -> 11 us
  Pallas kernels: 18.3 us -> 17.4 us
    ppermute x7 -> x0, starting transfers between devices: 7.17 us -> none  [the longest x3 4.12 us: largest_of_all(): parts.append(lax.ppermute(peak, ('gx', 'gy'), pairs))]
    unnamed x2 -> x6, local copies, waits for them, and re-layouts: 0.01 us -> 5.68 us
    all_to_all x0 -> x1, waiting for transfers between devices: none -> 3.02 us  [on_device(): largest = lax.all_to_all(peak, ('gx', 'gy'), 0, 0, tiled=True)]
    all_to_all x0 -> x1, starting transfers between devices: none -> 2.97 us  [on_device(): largest = lax.all_to_all(peak, ('gx', 'gy'), 0, 0, tiled=True)]
    ppermute x7 -> x0, waiting for transfers between devices: 1.24 us -> none  [the longest x1 1.15 us: largest_of_all(): lax.ppermute(peak, 'gy', [(i, i ^ 1) for i in range(ny)])]
    pallas_call x14 -> x13, Pallas kernels: 18.3 us -> 17.4 us  [call(): pl.pallas_call(functools.partial(kernel, g), in_specs=in_specs, out_shape...]
  transfers between devices with their start and end apart: 19 -> 13, of which waited for: 9 -> 8; matrix products, arithmetic and copies ran while one was open for 0% -> 0% of each run, Pallas kernels for 23% -> 19%
where the time goes in v9:
time: 54.2 us; the launch traced here: 54 us
  starting transfers between devices  19.1 us (35%)
  Pallas kernels  17.4 us (32%)
  waiting for transfers between devices  11 us (20%)
  local copies, waits for them, and re-layouts  5.68 us (10%)
  between operations  0.78 us (1%)
    pallas_call x13, Pallas kernels, call(): pl.pallas_call(functools.partial(kernel, g), in_specs=in_specs, out_shape...  17.4 us
    ppermute x6, starting transfers between devices, swap(): lax.ppermute(second, axis, swap_pairs(count, 1))  16.1 us
    unnamed x6, local copies, waits for them, and re-layouts  5.68 us
    ppermute x6, waiting for transfers between devices, swap(): lax.ppermute(second, axis, swap_pairs(count, 1))  5.06 us
    all_to_all x1, waiting for transfers between devices, on_device(): largest = lax.all_to_all(peak, ('gx', 'gy'), 0, 0, tiled=True)  3.02 us
    all_to_all x1, starting transfers between devices, on_device(): largest = lax.all_to_all(peak, ('gx', 'gy'), 0, 0, tiled=True)  2.97 us
    ppermute x6, waiting for transfers between devices, swap(): lax.ppermute(first, axis, swap_pairs(count, 0))  2.95 us
  transfers between devices with their start and end apart: 13, of which 8 were waited for; matrix products, arithmetic and copies ran while one was open for 0% of the time, Pallas kernels for 19%

profile of v9, /device:TPU:0, one launch (start us, length us, event | category | flops | bytes accessed | tf_op | source)
XLA Modules:
  0.0 54.0 jit_solution(12417754002920001407)
XLA Ops:
  0.6 2.6 %side_first.1 = (f32[14408,128]{1,0:T(8,128)S(1)}, f32[1792,128]{1,0:T(8,128)S(1)}, f32[8,27,32,128]{3,2,1,0:T(8,128)S(1)}, f32[32,1024]{1,0:T(8,128)S(1)}, s32[...) custom-call(f32[27,32,1024]{2,1,0:T(8,128)} %pops.1, ...), custom_call_target="tpu_custom_call" | custom-call | tf_op jit(solution)/shard_map/side_first/pallas_call | solution.py:768
  3.2 3.4 %collective-permute-start = (f32[480,128]{1,0:T(8,128)S(1)}, f32[480,128]{1,0:T(8,128)S(1)}, u32[]{:S(2)}, u32[]{:S(2)}) collective-permute-start(f32[480,128]{1,0:T(8,128)S(1)} %get-tuple-element.62), channel_id=1, source_target_pairs={{1,2},{2,1},{3,4},{4,3},{5,6},{6,5},{7,0},{0,7},{9,10},{10,9},{11,... | collective-permute-start | bytes 737288 | tf_op jit(solution)/shard_map/ppermute | solution.py:725
  6.6 0.0 collective-permute-start.1
  6.6 0.6 %rim_first.1 = (f32[14408,128]{1,0:T(8,128)S(1)}, f32[1792,128]{1,0:T(8,128)S(1)}, f32[240,128]{1,0:T(8,128)S(1)}, f32[240,128]{1,0:T(8,128)S(1)}) custom-call(f32[14408,128]{1,0:T(8,128)S(1)} %get-tuple-element.53._out, f32[1792,128]{1,0:T(8,128)S(1)} %get-tuple-element.54._state, ...), custom_call_target="tpu_custom_call", output_to_operand_aliasing={{0}: (0, {}), {1}: (1, {})} | custom-call | bytes 12582912 | tf_op jit(solution)/shard_map/rim_first/pallas_call | solution.py:768
  7.2 3.7 %collective-permute-start.2 = (f32[240,128]{1,0:T(8,128)S(1)}, f32[240,128]{1,0:T(8,128)S(1)}, u32[]{:S(2)}, u32[]{:S(2)}) collective-permute-start(f32[240,128]{1,0:T(8,128)S(1)} %get-tuple-element.67), channel_id=1, source_target_pairs={{8,16},{16,8},{24,0},{0,24},{9,17},{17,9},{25,1},{1,25},{10,18},{1... | collective-permute-start | bytes 368648 | tf_op jit(solution)/shard_map/ppermute | solution.py:725
  10.9 0.0 collective-permute-start.3
  10.9 1.2 %inner_first.1 = (f32[14408,128]{1,0:T(8,128)S(1)}, f32[1792,128]{1,0:T(8,128)S(1)}, f32[12968,128]{1,0:T(8,128)S(1)}, f32[2184,128]{1,0:T(8,128)S(1)}) custom-call(f32[14408,128]{1,0:T(8,128)S(1)} %get-tuple-element.59._, f32[1792,128]{1,0:T(8,128)S(1)} %get-tuple-element.60._state, ...), custom_call_target="tpu_custom_call", output_to_operand_aliasing={{0}: (0, {}), {1}: (1, {})} | custom-call | bytes 12582912 | tf_op jit(solution)/shard_map/inner_first/pallas_call | solution.py:768
  12.1 0.0 copy-start.2
  12.1 0.2 collective-permute-done.refs_1_
  12.3 0.0 collective-permute-done.1.refs_2_
  12.3 0.1 relay.2
  12.4 5.2 %collective-permute-start.4 = (f32[32,128]{1,0:T(8,128)S(1)}, f32[32,128]{1,0:T(8,128)S(1)}, u32[]{:S(2)}, u32[]{:S(2)}) collective-permute-start(f32[32,128]{1,0:T(8,128)S(1)} %get-tuple-element.74), channel_id=1, source_target_pairs={{8,16},{16,8},{24,0},{0,24},{9,17},{17,9},{25,1},{1,25},{10,18},{1... | collective-permute-start | bytes 49160 | tf_op jit(solution)/shard_map/ppermute | solution.py:725
  17.6 0.0 collective-permute-start.5
  17.6 0.0 collective-permute-done.2.b
  17.6 0.2 collective-permute-done.3.a
  17.8 0.0 copy-done.2
  17.8 1.6 %middle_second.1 = (f32[14408,128]{1,0:T(8,128)S(1)}, f32[12968,128]{1,0:T(8,128)S(1)}, f32[2184,128]{1,0:T(8,128)S(1)}, f32[8,27,32,128]{3,2,1,0:T(8,128)S(1)}, f32[12968,128]{1,0:T(8,128)S(1)}) custom-call(f32[14408,128]{1,0:T(8,128)S(1)} %get-tuple-element.64._post, ...), custom_call_target="tpu_custom_call", output_to_operand_aliasing={{0}: (0, {}), {1}: (1, {}), {2}: (2, {})} | custom-call | bytes 12582912 | tf_op jit(solution)/shard_map/middle_second/pallas_call | solution.py:768
  19.4 0.0 collective-permute-done.4.second
  19.4 1.9 %collective-permute-done.5.first = f32[32,128]{1,0:T(8,128)S(1)} collective-permute-done((f32[32,128]{1,0:T(8,128)S(1)}, f32[32,128]{1,0:T(8,128)S(1)}, u32[]{:S(2)}, u32[]{:S(2)}) %collective-permute-start.5) | collective-permute-done | bytes 16416 | tf_op jit(solution)/shard_map/ppermute | solution.py:724
  21.3 1.4 %side_seed.1 = (f32[14408,128]{1,0:T(8,128)S(1)}, f32[12968,128]{1,0:T(8,128)S(1)}, f32[2184,128]{1,0:T(8,128)S(1)}, f32[8,27,32,128]{3,2,1,0:T(8,128)S(1)}, f32...) custom-call(f32[14408,128]{1,0:T(8,128)S(1)} %get-tuple-element.69._, ...), custom_call_target="tpu_custom_call", output_to_operand_aliasing={{0}: (0, {}), {1}: (1, {}), {2}: (2, {}), {3}: (3, {}), {4}... | custom-call | tf_op jit(solution)/shard_map/side_seed/pallas_call | solution.py:768
  22.7 0.1 collective-permute-start.6
  22.8 0.1 collective-permute-start.7
  22.9 0.8 %rim_seed.1 = (f32[8,27,32,128]{3,2,1,0:T(8,128)S(1)}, f32[12968,128]{1,0:T(8,128)S(1)}, f32[216,128]{1,0:T(8,128)S(1)}, f32[216,128]{1,0:T(8,128)S(1)}) custom-call(f32[8,27,32,128]{3,2,1,0:T(8,128)S(1)} %get-tuple-element.76._stage, f32[12968,128]{1,0:T(8,128)S(1)} %get-tuple-element.77._field, ...), custom_call_target="tpu_custom_call", output_to_operand_aliasing={{0}: (0, {}), {1}: (1, {})} | custom-call | bytes 12582912 | tf_op jit(solution)/shard_map/rim_seed/pallas_call | solution.py:768
  23.7 1.9 %collective-permute-start.8 = (f32[216,128]{1,0:T(8,128)S(1)}, f32[216,128]{1,0:T(8,128)S(1)}, u32[]{:S(2)}, u32[]{:S(2)}) collective-permute-start(f32[216,128]{1,0:T(8,128)S(1)} %get-tuple-element.90), channel_id=1, source_target_pairs={{8,16},{16,8},{24,0},{0,24},{9,17},{17,9},{25,1},{1,25},{10,18},{1... | collective-permute-start | bytes 331784 | tf_op jit(solution)/shard_map/ppermute | solution.py:725
  25.6 0.0 collective-permute-start.9
  25.6 1.9 %inner_seed.1 = (f32[8,27,32,128]{3,2,1,0:T(8,128)S(1)}, f32[12968,128]{1,0:T(8,128)S(1)}, f32[12968,128]{1,0:T(8,128)S(1)}, f32[312,128]{1,0:T(8,128)S(1)}, f32[27,32,1024]{2,1,0:T(8,128)}) custom-call(f32[8,27,32,128]{3,2,1,0:T(8,128)S(1)} %get-tuple-element.79.kept, ...), custom_call_target="tpu_custom_call", output_to_operand_aliasing={{0}: (0, {}), {1}: (1, {})} | custom-call | bytes 12582912 | tf_op jit(solution)/shard_map/inner_seed/pallas_call | solution.py:768
  27.5 3.3 %collective-permute-done.6.refs_1_ = f32[448,128]{1,0:T(8,128)S(1)} collective-permute-done((f32[448,128]{1,0:T(8,128)S(1)}, f32[448,128]{1,0:T(8,128)S(1)}, u32[]{:S(2)}, u32[]{:S(2)}) %collective-permute-start.6) | collective-permute-done | bytes 229408 | tf_op jit(solution)/shard_map/ppermute | solution.py:725
  30.8 0.0 collective-permute-done.7.refs_2_
  30.8 0.1 relay.3
  31.0 1.9 %collective-permute-start.10 = (f32[32,128]{1,0:T(8,128)S(1)}, f32[32,128]{1,0:T(8,128)S(1)}, u32[]{:S(2)}, u32[]{:S(2)}) collective-permute-start(f32[32,128]{1,0:T(8,128)S(1)} %get-tuple-element.97), channel_id=1, source_target_pairs={{8,16},{16,8},{24,0},{0,24},{9,17},{17,9},{25,1},{1,25},{10,18},{1... | collective-permute-start | bytes 49160 | tf_op jit(solution)/shard_map/ppermute | solution.py:725
  32.8 0.0 collective-permute-start.11
  32.8 0.0 collective-permute-done.8.b
  32.8 0.7 %collective-permute-done.9.a = f32[216,128]{1,0:T(8,128)S(1)} collective-permute-done((f32[216,128]{1,0:T(8,128)S(1)}, f32[216,128]{1,0:T(8,128)S(1)}, u32[]{:S(2)}, u32[]{:S(2)}) %collective-permute-start.9) | collective-permute-done | bytes 110624 | tf_op jit(solution)/shard_map/ppermute | solution.py:724
  33.5 1.5 %middle_adjoint.1 = (f32[12968,128]{1,0:T(8,128)S(1)}, f32[12968,128]{1,0:T(8,128)S(1)}, f32[312,128]{1,0:T(8,128)S(1)}, f32[256,128]{1,0:T(8,128)S(1)}, f32[1280,128]{1,0:T(8,128)S(1)}) custom-call(f32[12968,128]{1,0:T(8,128)S(1)} %get-tuple-element.86._field, ...), custom_call_target="tpu_custom_call", output_to_operand_aliasing={{0}: (0, {}), {1}: (1, {}), {2}: (2, {})} | custom-call | bytes 12582912 | tf_op jit(solution)/shard_map/middle_adjoint/pallas_call | solution.py:768
  35.1 1.5 %collective-permute-done.10.refs_7_ = f32[32,128]{1,0:T(8,128)S(1)} collective-permute-done((f32[32,128]{1,0:T(8,128)S(1)}, f32[32,128]{1,0:T(8,128)S(1)}, u32[]{:S(2)}, u32[]{:S(2)}) %collective-permute-start.10) | collective-permute-done | bytes 16416 | tf_op jit(solution)/shard_map/ppermute | solution.py:725
  36.6 0.2 collective-permute-done.11.refs_8_
  36.7 2.5 %total.1 = (f32[12968,128]{1,0:T(8,128)S(1)}, f32[12968,128]{1,0:T(8,128)S(1)}, f32[312,128]{1,0:T(8,128)S(1)}, f32[256,128]{1,0:T(8,128)S(1)}, f32[1280,128]{1,0:T(8,128)S(1)}, /*index=5*/f32[256,128]{1,0:T(8,128)}) custom-call(f32[12968,128]{1,0:T(8,128)S(1)} %get-tuple-element.92.re, ...), custom_call_target="tpu_custom_call", output_to_operand_aliasing={{0}: (0, {}), {1}: (1, {}), {2}: (2, {}), {3}: (3, {}), {4}... | custom-call | tf_op jit(solution)/shard_map/total/pallas_call | solution.py:768
  39.2 0.0 copy-start
  39.2 2.8 %copy-done = f32[12968,128]{1,0:T(8,128)} copy-done((f32[12968,128]{1,0:T(8,128)}, f32[12968,128]{1,0:T(8,128)S(1)}, u32[]{:S(2)}) %copy-start) | copy-done | bytes 6639640
  42.0 3.0 %all-to-all-start = ((f32[32,8,128]{2,1,0:T(8,128)}), f32[32,8,128]{2,1,0:T(8,128)S(1)}, u32[]{:S(2)}, u32[]{:S(2)}) async-start(f32[32,8,128]{2,1,0:T(8,128)} %bitcast), calls=%async_computation | async-start | bytes 262144 | tf_op jit(solution)/shard_map/all_to_all | solution.py:873
  45.0 0.0 copy-start.1
  45.0 2.9 %copy-done.1 = f32[12968,128]{1,0:T(8,128)S(1)} copy-done((f32[12968,128]{1,0:T(8,128)S(1)}, f32[12968,128]{1,0:T(8,128)}, u32[]{:S(2)}) %copy-start.1) | copy-done | bytes 6639640
  47.9 2.3 %adjoint_first.1 = f32[27,32,1024]{2,1,0:T(8,128)} custom-call(f32[12968,128]{1,0:T(8,128)S(1)} %copy-done.1, f32[1280,128]{1,0:T(8,128)S(1)} %get-tuple-element.100.fields), custom_call_target="tpu_custom_call" | custom-call | bytes 12582912 | tf_op jit(solution)/shard_map/adjoint_first/pallas_call | solution.py:768
  50.2 3.0 %all-to-all-done = f32[32,8,128]{2,1,0:T(8,128)S(1)} async-done(((f32[32,8,128]{2,1,0:T(8,128)}), f32[32,8,128]{2,1,0:T(8,128)S(1)}, u32[]{:S(2)}, u32[]{:S(2)}) %all-to-all-start) | async-done | bytes 131104 | tf_op jit(solution)/shard_map/all_to_all | solution.py:873
  53.2 0.8 %normalize.1 = f32[32,1024]{1,0:T(8,128)} custom-call(f32[256,128]{1,0:T(8,128)S(1)} %get-tuple-element.101.total, f32[256,128]{1,0:T(8,128)S(1)} %bitcast.2), custom_call_target="tpu_custom_call" | custom-call | tf_op jit(solution)/shard_map/normalize/pallas_call | solution.py:768
Async XLA Ops:
  3.2 9.1 %collective-permute-start = (f32[480,128]{1,0:T(8,128)S(1)}, f32[480,128]{1,0:T(8,128)S(1)}, u32[]{:S(2)}, u32[]{:S(2)}) collective-permute-start(f32[480,128]{1,0:T(8,128)S(1)} %get-tuple-element.62), channel_id=1, source_target_pairs={{1,2},{2,1},{3,4},{4,3},{5,6},{6,5},{7,0},{0,7},{9,10},{10,9},{11,... | collective-permute-start | bytes 737288 | tf_op jit(solution)/shard_map/ppermute | solution.py:725
  6.6 5.7 %collective-permute-start.1 = (f32[480,128]{1,0:T(8,128)S(1)}, f32[480,128]{1,0:T(8,128)S(1)}, u32[]{:S(2)}, u32[]{:S(2)}) collective-permute-start(f32[480,128]{1,0:T(8,128)S(1)} %get-tuple-element.63), channel_id=1, source_target_pairs={{0,1},{1,0},{2,3},{3,2},{4,5},{5,4},{6,7},{7,6},{8,9},{9,8},{10,11... | collective-permute-start | bytes 737288 | tf_op jit(solution)/shard_map/ppermute | solution.py:724
  7.2 10.4 %collective-permute-start.2 = (f32[240,128]{1,0:T(8,128)S(1)}, f32[240,128]{1,0:T(8,128)S(1)}, u32[]{:S(2)}, u32[]{:S(2)}) collective-permute-start(f32[240,128]{1,0:T(8,128)S(1)} %get-tuple-element.67), channel_id=1, source_target_pairs={{8,16},{16,8},{24,0},{0,24},{9,17},{17,9},{25,1},{1,25},{10,18},{1... | collective-permute-start | bytes 368648 | tf_op jit(solution)/shard_map/ppermute | solution.py:725
  10.9 6.9 %collective-permute-start.3 = (f32[240,128]{1,0:T(8,128)S(1)}, f32[240,128]{1,0:T(8,128)S(1)}, u32[]{:S(2)}, u32[]{:S(2)}) collective-permute-start(f32[240,128]{1,0:T(8,128)S(1)} %get-tuple-element.68), channel_id=1, source_target_pairs={{0,8},{8,0},{16,24},{24,16},{1,9},{9,1},{17,25},{25,17},{2,10},{10... | collective-permute-start | bytes 368648 | tf_op jit(solution)/shard_map/ppermute | solution.py:724
  12.1 5.7 %copy-start.2 = (f32[27,32,1024]{2,1,0:T(8,128)S(1)}, f32[27,32,1024]{2,1,0:T(8,128)}, u32[]{:S(2)}) copy-start(f32[27,32,1024]{2,1,0:T(8,128)} %refs_1_.3) | copy-start | bytes 10616836
  12.4 7.0 %collective-permute-start.4 = (f32[32,128]{1,0:T(8,128)S(1)}, f32[32,128]{1,0:T(8,128)S(1)}, u32[]{:S(2)}, u32[]{:S(2)}) collective-permute-start(f32[32,128]{1,0:T(8,128)S(1)} %get-tuple-element.74), channel_id=1, source_target_pairs={{8,16},{16,8},{24,0},{0,24},{9,17},{17,9},{25,1},{1,25},{10,18},{1... | collective-permute-start | bytes 49160 | tf_op jit(solution)/shard_map/ppermute | solution.py:725
  17.6 3.7 %collective-permute-start.5 = (f32[32,128]{1,0:T(8,128)S(1)}, f32[32,128]{1,0:T(8,128)S(1)}, u32[]{:S(2)}, u32[]{:S(2)}) collective-permute-start(f32[32,128]{1,0:T(8,128)S(1)} %get-tuple-element.75), channel_id=1, source_target_pairs={{0,8},{8,0},{16,24},{24,16},{1,9},{9,1},{17,25},{25,17},{2,10},{10... | collective-permute-start | bytes 49160 | tf_op jit(solution)/shard_map/ppermute | solution.py:724
  22.7 8.1 %collective-permute-start.6 = (f32[448,128]{1,0:T(8,128)S(1)}, f32[448,128]{1,0:T(8,128)S(1)}, u32[]{:S(2)}, u32[]{:S(2)}) collective-permute-start(f32[448,128]{1,0:T(8,128)S(1)} %get-tuple-element.84), channel_id=1, source_target_pairs={{1,2},{2,1},{3,4},{4,3},{5,6},{6,5},{7,0},{0,7},{9,10},{10,9},{11,... | collective-permute-start | bytes 688136 | tf_op jit(solution)/shard_map/ppermute | solution.py:725
  22.8 8.1 %collective-permute-start.7 = (f32[448,128]{1,0:T(8,128)S(1)}, f32[448,128]{1,0:T(8,128)S(1)}, u32[]{:S(2)}, u32[]{:S(2)}) collective-permute-start(f32[448,128]{1,0:T(8,128)S(1)} %get-tuple-element.85), channel_id=1, source_target_pairs={{0,1},{1,0},{2,3},{3,2},{4,5},{5,4},{6,7},{7,6},{8,9},{9,8},{10,11... | collective-permute-start | bytes 688136 | tf_op jit(solution)/shard_map/ppermute | solution.py:724
  23.7 9.1 %collective-permute-start.8 = (f32[216,128]{1,0:T(8,128)S(1)}, f32[216,128]{1,0:T(8,128)S(1)}, u32[]{:S(2)}, u32[]{:S(2)}) collective-permute-start(f32[216,128]{1,0:T(8,128)S(1)} %get-tuple-element.90), channel_id=1, source_target_pairs={{8,16},{16,8},{24,0},{0,24},{9,17},{17,9},{25,1},{1,25},{10,18},{1... | collective-permute-start | bytes 331784 | tf_op jit(solution)/shard_map/ppermute | solution.py:725
  25.6 7.9 %collective-permute-start.9 = (f32[216,128]{1,0:T(8,128)S(1)}, f32[216,128]{1,0:T(8,128)S(1)}, u32[]{:S(2)}, u32[]{:S(2)}) collective-permute-start(f32[216,128]{1,0:T(8,128)S(1)} %get-tuple-element.91), channel_id=1, source_target_pairs={{0,8},{8,0},{16,24},{24,16},{1,9},{9,1},{17,25},{25,17},{2,10},{10... | collective-permute-start | bytes 331784 | tf_op jit(solution)/shard_map/ppermute | solution.py:724
  31.0 5.6 %collective-permute-start.10 = (f32[32,128]{1,0:T(8,128)S(1)}, f32[32,128]{1,0:T(8,128)S(1)}, u32[]{:S(2)}, u32[]{:S(2)}) collective-permute-start(f32[32,128]{1,0:T(8,128)S(1)} %get-tuple-element.97), channel_id=1, source_target_pairs={{8,16},{16,8},{24,0},{0,24},{9,17},{17,9},{25,1},{1,25},{10,18},{1... | collective-permute-start | bytes 49160 | tf_op jit(solution)/shard_map/ppermute | solution.py:725
  32.8 3.9 %collective-permute-start.11 = (f32[32,128]{1,0:T(8,128)S(1)}, f32[32,128]{1,0:T(8,128)S(1)}, u32[]{:S(2)}, u32[]{:S(2)}) collective-permute-start(f32[32,128]{1,0:T(8,128)S(1)} %get-tuple-element.98), channel_id=1, source_target_pairs={{0,8},{8,0},{16,24},{24,16},{1,9},{9,1},{17,25},{25,17},{2,10},{10... | collective-permute-start | bytes 49160 | tf_op jit(solution)/shard_map/ppermute | solution.py:724
  39.2 2.8 %copy-start = (f32[12968,128]{1,0:T(8,128)}, f32[12968,128]{1,0:T(8,128)S(1)}, u32[]{:S(2)}) copy-start(f32[12968,128]{1,0:T(8,128)S(1)} %get-tuple-element.99.buf) | copy-start | bytes 19918852
  42.0 11.2 %all-to-all-start = ((f32[32,8,128]{2,1,0:T(8,128)}), f32[32,8,128]{2,1,0:T(8,128)S(1)}, u32[]{:S(2)}, u32[]{:S(2)}) async-start(f32[32,8,128]{2,1,0:T(8,128)} %bitcast), calls=%async_computation | async-start | bytes 262144 | tf_op jit(solution)/shard_map/all_to_all | solution.py:873
  45.0 2.9 %copy-start.1 = (f32[12968,128]{1,0:T(8,128)S(1)}, f32[12968,128]{1,0:T(8,128)}, u32[]{:S(2)}) copy-start(f32[12968,128]{1,0:T(8,128)} %copy-done) | copy-start | bytes 19918852

commit v10 on v9

--- a/solution.py
+++ b/solution.py
@@ -427,12 +427,6 @@
         return carry
 
     lax.fori_loop(0, 2, step, 0, unroll=2)
-
-
-def rim_tiles(g, act):
-    every(1, g.cols, functools.partial(act, pieces=g.outer))
-    for pieces in g.inner:
-        side_panels(g, functools.partial(act, pieces=pieces), 2)
 
 
 def step_tile(g, buf, out, sign, fields, masks, compute):
@@ -648,34 +642,47 @@
     every(1, g.cols, lambda k: copy(k).wait())
 
 
-def total_tile(g, out, before, state0, total, parts, masks):
+def total_tile(g, out, before, state0, total, stage, masks):
     def act(k, pieces):
         p = pull_block(g, out, -1, k, pieces, masks)
         spot = spot_of(g, k)
         *flow, wall = load_fields(state0, g.local, spot, pieces, 7)
-        *spread, porous = adjoint_scalars(p, *flow, wall > 0.5)
+        solid = wall > 0.5
+        *spread, porous = adjoint_scalars(p, *flow, solid)
         here = load_fields(before, g.extended, spot, pieces, 1)[0] + porous
         save_fields(total, g.local, spot, pieces, [here])
-        save_fields(parts, g.local, spot, pieces, spread + [wall])
+        for i, value in enumerate(adjoint_spread(p, *spread, solid)):
+            write_rows(stage.at[k - 1, i], 0, pieces, value)
 
     return act
 
 
-def middle_adjoint_kernel(g, field, out, before, total, parts, state1, state0, x_second, x_first):
+def middle_adjoint_kernel(g, field, out, before, total, stage, state1, state0, x_second, x_first):
     masks = lane_masks(16)
     by_parity("gx", x_second, x_first, functools.partial(unpack_x, g, field, -1, 27))
     middle_tiles(g, step_tile(g, field, out, -1, 27, masks, adjoint_second(g, state1, before)))
-    core_tiles(g, total_tile(g, out, before, state0, total, parts, masks))
+    core_tiles(g, total_tile(g, out, before, state0, total, stage, masks))
 
 
 def total_kernel(g, *refs):
-    state1, state0, second, first, field, out, before, total, parts, peak = refs[5:]
+    state1, state0, second, first, field, out, before, total, stage, peak, result, sems = refs[5:]
     masks = lane_masks(16)
+
+    def copy(k):
+        return pltpu.make_async_copy(stage.at[k - 1], block_of(result, k), sems.at[k - 1])
+
     by_parity("gx", second, first, functools.partial(unpack_corners, g, field, -1, 27))
     corner_tiles(g, field, out, -1, 27, masks, adjoint_second(g, state1, before))
-    act = total_tile(g, out, before, state0, total, parts, masks)
+    act = total_tile(g, out, before, state0, total, stage, masks)
     near_core_tiles(g, act)
-    rim_tiles(g, act)
+    for pieces in g.inner:
+        side_panels(g, functools.partial(act, pieces=pieces), 2)
+
+    def column(k):
+        act(k, g.outer)
+        copy(k).start()
+
+    every(1, g.cols, column)
     size = 8 * (g.local // 64)
     largest = jnp.zeros((8, LANES), F32)
     for start in range(0, g.local, size):
@@ -683,24 +690,7 @@
         largest = jnp.maximum(largest, jnp.max(value, 0))
     for n in range(0, peak.shape[0], 8):
         peak[n : n + 8, :] = largest
-
-
-def adjoint_kernel(g, first, last, buf, parts, result, stage, sems):
-    masks = lane_masks(16)
-
-    def copy(k):
-        return pltpu.make_async_copy(stage.at[k - first], block_of(result, k), sems.at[k - first])
-
-    def column(k):
-        for pieces in (g.outer,) + g.inner:
-            p = pull_block(g, buf, -1, k, pieces, masks)
-            *spread, wall = load_fields(parts, g.local, spot_of(g, k), pieces, 5)
-            for i, value in enumerate(adjoint_spread(p, *spread, wall > 0.5)):
-                write_rows(stage.at[k - first, i], 0, pieces, value)
-        copy(k).start()
-
-    every(first, last, column)
-    every(first, last, lambda k: copy(k).wait())
+    every(1, g.cols, lambda k: copy(k).wait())
 
 
 def scale_kernel(g, total, peak, out):
@@ -761,10 +751,6 @@
         space = pltpu.HBM if name == "side_first" else pltpu.VMEM
         pinned = [pltpu.with_memory_space_constraint(x, space) for x in operands]
         in_specs = [pl.BlockSpec(memory_space=space)] * len(operands)
-        if result is not None:
-            aliases[len(operands)] = len(out_shape) - 1
-            pinned.append(pltpu.with_memory_space_constraint(result, pltpu.HBM))
-            in_specs.append(in_hbm)
         return pl.pallas_call(
             functools.partial(kernel, g),
             in_specs=in_specs,
@@ -853,32 +839,25 @@
         load=FLIGHT,
     )
     field, parcels = relay(field, along_y, -1, 27)
-    field, pulled, before, total, parts = call(
+    field, pulled, before, total, staged = call(
         "middle_adjoint",
         lambda grid, _field, _out, _before, near, far, b, a, *refs: middle_adjoint_kernel(
             grid, *refs, near, far, b, a
         ),
         [field, pulled, before, state1, state0, *along_x],
-        [fields(1, g.local), fields(5, g.local)],
+        [fields(1, g.local), stage],
         kept=3,
         load=FLIGHT,
     )
-    _, pulled, _, total, parts, peak = call(
+    _, _, _, total, _, peak, adjoint_out = call(
         "total",
         total_kernel,
-        [field, pulled, before, total, parts, state1, state0, *parcels],
-        [vmem(8 * nx * ny, LANES)],
+        [field, pulled, before, total, staged, state1, state0, *parcels],
+        [vmem(8 * nx * ny, LANES), whole],
+        [sems],
         kept=5,
     )
     largest = lax.all_to_all(peak, ("gx", "gy"), 0, 0, tiled=True)
-    (adjoint_out,) = call(
-        "adjoint_first",
-        lambda grid, buf, fields, *refs: adjoint_kernel(grid, 1, g.cols, buf, fields, *refs),
-        [pulled, parts],
-        [whole],
-        [stage, sems],
-        load=FLIGHT,
-    )
     (sensitivity,) = call(
         "normalize",
         scale_kernel,

time: 54.2 us -> 51.9 us (0.958)
  blocking collectives: 0 us -> 11 us
  local copies, waits for them, and re-layouts: 5.68 us -> 0.01 us
  waiting for transfers between devices: 11 us -> 7.92 us
  starting transfers between devices: 19.1 us -> 16.2 us
  Pallas kernels: 17.4 us -> 15.8 us
    all_to_all x0 -> x1, blocking collectives: none -> 11 us  [on_device(): largest = lax.all_to_all(peak, ('gx', 'gy'), 0, 0, tiled=True)]
    unnamed x6 -> x2, local copies, waits for them, and re-layouts: 5.68 us -> 0.01 us
    all_to_all x1 -> x0, waiting for transfers between devices: 3.02 us -> none  [on_device(): largest = lax.all_to_all(peak, ('gx', 'gy'), 0, 0, tiled=True)]
    all_to_all x1 -> x0, starting transfers between devices: 2.97 us -> none  [on_device(): largest = lax.all_to_all(peak, ('gx', 'gy'), 0, 0, tiled=True)]
    pallas_call x13 -> x12, Pallas kernels: 17.4 us -> 15.8 us  [call(): pl.pallas_call(functools.partial(kernel, g), in_specs=in_specs, out_shape...]
  transfers between devices with their start and end apart: 13 -> 12, of which waited for: 8 -> 7; matrix products, arithmetic and copies ran while one was open for 0% -> 0% of each run, Pallas kernels for 19% -> 15%
where the time goes in v10:
time: 51.9 us; the launch traced here: 51.7 us
  starting transfers between devices  16.2 us (31%)
  Pallas kernels  15.8 us (30%)
  blocking collectives  11 us (21%)
  waiting for transfers between devices  7.92 us (15%)
  between operations  0.76 us (1%)
    ppermute x6, starting transfers between devices, swap(): lax.ppermute(second, axis, swap_pairs(count, 1))  16.1 us
    pallas_call x12, Pallas kernels, call(): pl.pallas_call(functools.partial(kernel, g), in_specs=in_specs, out_shape...  15.8 us
    all_to_all x1, blocking collectives, on_device(): largest = lax.all_to_all(peak, ('gx', 'gy'), 0, 0, tiled=True)  11 us
    ppermute x6, waiting for transfers between devices, swap(): lax.ppermute(second, axis, swap_pairs(count, 1))  4.97 us
    ppermute x6, waiting for transfers between devices, swap(): lax.ppermute(first, axis, swap_pairs(count, 0))  2.95 us
  transfers between devices with their start and end apart: 12, of which 7 were waited for; matrix products, arithmetic and copies ran while one was open for 0% of the time, Pallas kernels for 15%

profile of v10, /device:TPU:0, one launch (start us, length us, event | category | flops | bytes accessed | tf_op | source)
XLA Modules:
  0.0 51.7 jit_solution(9723996397634839089)
XLA Ops:
  0.6 2.5 %side_first.1 = (f32[14408,128]{1,0:T(8,128)S(1)}, f32[1792,128]{1,0:T(8,128)S(1)}, f32[8,27,32,128]{3,2,1,0:T(8,128)S(1)}, f32[32,1024]{1,0:T(8,128)S(1)}, s32[...) custom-call(f32[27,32,1024]{2,1,0:T(8,128)} %pops.1, ...), custom_call_target="tpu_custom_call" | custom-call | tf_op jit(solution)/shard_map/side_first/pallas_call | solution.py:754
  3.2 3.4 %collective-permute-start = (f32[480,128]{1,0:T(8,128)S(1)}, f32[480,128]{1,0:T(8,128)S(1)}, u32[]{:S(2)}, u32[]{:S(2)}) collective-permute-start(f32[480,128]{1,0:T(8,128)S(1)} %get-tuple-element.61), channel_id=1, source_target_pairs={{1,2},{2,1},{3,4},{4,3},{5,6},{6,5},{7,0},{0,7},{9,10},{10,9},{11,... | collective-permute-start | bytes 737288 | tf_op jit(solution)/shard_map/ppermute | solution.py:715
  6.6 0.0 collective-permute-start.1
  6.6 0.6 %rim_first.1 = (f32[14408,128]{1,0:T(8,128)S(1)}, f32[1792,128]{1,0:T(8,128)S(1)}, f32[240,128]{1,0:T(8,128)S(1)}, f32[240,128]{1,0:T(8,128)S(1)}) custom-call(f32[14408,128]{1,0:T(8,128)S(1)} %get-tuple-element.52._out, f32[1792,128]{1,0:T(8,128)S(1)} %get-tuple-element.53._state, ...), custom_call_target="tpu_custom_call", output_to_operand_aliasing={{0}: (0, {}), {1}: (1, {})} | custom-call | bytes 12582912 | tf_op jit(solution)/shard_map/rim_first/pallas_call | solution.py:754
  7.2 3.7 %collective-permute-start.2 = (f32[240,128]{1,0:T(8,128)S(1)}, f32[240,128]{1,0:T(8,128)S(1)}, u32[]{:S(2)}, u32[]{:S(2)}) collective-permute-start(f32[240,128]{1,0:T(8,128)S(1)} %get-tuple-element.66), channel_id=1, source_target_pairs={{8,16},{16,8},{24,0},{0,24},{9,17},{17,9},{25,1},{1,25},{10,18},{1... | collective-permute-start | bytes 368648 | tf_op jit(solution)/shard_map/ppermute | solution.py:715
  10.8 0.0 collective-permute-start.3
  10.8 1.2 %inner_first.1 = (f32[14408,128]{1,0:T(8,128)S(1)}, f32[1792,128]{1,0:T(8,128)S(1)}, f32[12968,128]{1,0:T(8,128)S(1)}, f32[2184,128]{1,0:T(8,128)S(1)}) custom-call(f32[14408,128]{1,0:T(8,128)S(1)} %get-tuple-element.58._, f32[1792,128]{1,0:T(8,128)S(1)} %get-tuple-element.59._state, ...), custom_call_target="tpu_custom_call", output_to_operand_aliasing={{0}: (0, {}), {1}: (1, {})} | custom-call | bytes 12582912 | tf_op jit(solution)/shard_map/inner_first/pallas_call | solution.py:754
  12.1 0.0 copy-start
  12.1 0.2 collective-permute-done.refs_1_
  12.2 0.0 collective-permute-done.1.refs_2_
  12.3 0.1 relay.2
  12.4 5.2 %collective-permute-start.4 = (f32[32,128]{1,0:T(8,128)S(1)}, f32[32,128]{1,0:T(8,128)S(1)}, u32[]{:S(2)}, u32[]{:S(2)}) collective-permute-start(f32[32,128]{1,0:T(8,128)S(1)} %get-tuple-element.73), channel_id=1, source_target_pairs={{8,16},{16,8},{24,0},{0,24},{9,17},{17,9},{25,1},{1,25},{10,18},{1... | collective-permute-start | bytes 49160 | tf_op jit(solution)/shard_map/ppermute | solution.py:715
  17.6 0.0 collective-permute-start.5
  17.6 0.0 collective-permute-done.2.b
  17.6 0.2 collective-permute-done.3.a
  17.7 0.0 copy-done
  17.7 1.6 %middle_second.1 = (f32[14408,128]{1,0:T(8,128)S(1)}, f32[12968,128]{1,0:T(8,128)S(1)}, f32[2184,128]{1,0:T(8,128)S(1)}, f32[8,27,32,128]{3,2,1,0:T(8,128)S(1)}, f32[12968,128]{1,0:T(8,128)S(1)}) custom-call(f32[14408,128]{1,0:T(8,128)S(1)} %get-tuple-element.63._post, ...), custom_call_target="tpu_custom_call", output_to_operand_aliasing={{0}: (0, {}), {1}: (1, {}), {2}: (2, {})} | custom-call | bytes 12582912 | tf_op jit(solution)/shard_map/middle_second/pallas_call | solution.py:754
  19.4 0.0 collective-permute-done.4.second
  19.4 1.9 %collective-permute-done.5.first = f32[32,128]{1,0:T(8,128)S(1)} collective-permute-done((f32[32,128]{1,0:T(8,128)S(1)}, f32[32,128]{1,0:T(8,128)S(1)}, u32[]{:S(2)}, u32[]{:S(2)}) %collective-permute-start.5) | collective-permute-done | bytes 16416 | tf_op jit(solution)/shard_map/ppermute | solution.py:714
  21.3 1.4 %side_seed.1 = (f32[14408,128]{1,0:T(8,128)S(1)}, f32[12968,128]{1,0:T(8,128)S(1)}, f32[2184,128]{1,0:T(8,128)S(1)}, f32[8,27,32,128]{3,2,1,0:T(8,128)S(1)}, f32...) custom-call(f32[14408,128]{1,0:T(8,128)S(1)} %get-tuple-element.68._, ...), custom_call_target="tpu_custom_call", output_to_operand_aliasing={{0}: (0, {}), {1}: (1, {}), {2}: (2, {}), {3}: (3, {}), {4}... | custom-call | tf_op jit(solution)/shard_map/side_seed/pallas_call | solution.py:754
  22.7 0.1 collective-permute-start.6
  22.8 0.1 collective-permute-start.7
  22.8 0.8 %rim_seed.1 = (f32[8,27,32,128]{3,2,1,0:T(8,128)S(1)}, f32[12968,128]{1,0:T(8,128)S(1)}, f32[216,128]{1,0:T(8,128)S(1)}, f32[216,128]{1,0:T(8,128)S(1)}) custom-call(f32[8,27,32,128]{3,2,1,0:T(8,128)S(1)} %get-tuple-element.75._stage, f32[12968,128]{1,0:T(8,128)S(1)} %get-tuple-element.76._field, ...), custom_call_target="tpu_custom_call", output_to_operand_aliasing={{0}: (0, {}), {1}: (1, {})} | custom-call | bytes 12582912 | tf_op jit(solution)/shard_map/rim_seed/pallas_call | solution.py:754
  23.7 1.9 %collective-permute-start.8 = (f32[216,128]{1,0:T(8,128)S(1)}, f32[216,128]{1,0:T(8,128)S(1)}, u32[]{:S(2)}, u32[]{:S(2)}) collective-permute-start(f32[216,128]{1,0:T(8,128)S(1)} %get-tuple-element.89), channel_id=1, source_target_pairs={{8,16},{16,8},{24,0},{0,24},{9,17},{17,9},{25,1},{1,25},{10,18},{1... | collective-permute-start | bytes 331784 | tf_op jit(solution)/shard_map/ppermute | solution.py:715
  25.6 0.0 collective-permute-start.9
  25.6 1.9 %inner_seed.1 = (f32[8,27,32,128]{3,2,1,0:T(8,128)S(1)}, f32[12968,128]{1,0:T(8,128)S(1)}, f32[12968,128]{1,0:T(8,128)S(1)}, f32[312,128]{1,0:T(8,128)S(1)}, f32[27,32,1024]{2,1,0:T(8,128)}) custom-call(f32[8,27,32,128]{3,2,1,0:T(8,128)S(1)} %get-tuple-element.78.kept, ...), custom_call_target="tpu_custom_call", output_to_operand_aliasing={{0}: (0, {}), {1}: (1, {})} | custom-call | bytes 12582912 | tf_op jit(solution)/shard_map/inner_seed/pallas_call | solution.py:754
  27.5 3.3 %collective-permute-done.6.refs_1_ = f32[448,128]{1,0:T(8,128)S(1)} collective-permute-done((f32[448,128]{1,0:T(8,128)S(1)}, f32[448,128]{1,0:T(8,128)S(1)}, u32[]{:S(2)}, u32[]{:S(2)}) %collective-permute-start.6) | collective-permute-done | bytes 229408 | tf_op jit(solution)/shard_map/ppermute | solution.py:715
  30.8 0.0 collective-permute-done.7.refs_2_
  30.8 0.1 relay.3
  30.9 1.9 %collective-permute-start.10 = (f32[32,128]{1,0:T(8,128)S(1)}, f32[32,128]{1,0:T(8,128)S(1)}, u32[]{:S(2)}, u32[]{:S(2)}) collective-permute-start(f32[32,128]{1,0:T(8,128)S(1)} %get-tuple-element.96), channel_id=1, source_target_pairs={{8,16},{16,8},{24,0},{0,24},{9,17},{17,9},{25,1},{1,25},{10,18},{1... | collective-permute-start | bytes 49160 | tf_op jit(solution)/shard_map/ppermute | solution.py:715
  32.8 0.0 collective-permute-start.11
  32.8 0.0 collective-permute-done.8.b
  32.8 0.7 %collective-permute-done.9.a = f32[216,128]{1,0:T(8,128)S(1)} collective-permute-done((f32[216,128]{1,0:T(8,128)S(1)}, f32[216,128]{1,0:T(8,128)S(1)}, u32[]{:S(2)}, u32[]{:S(2)}) %collective-permute-start.9) | collective-permute-done | bytes 110624 | tf_op jit(solution)/shard_map/ppermute | solution.py:714
  33.5 1.6 %middle_adjoint.1 = (f32[12968,128]{1,0:T(8,128)S(1)}, f32[12968,128]{1,0:T(8,128)S(1)}, f32[312,128]{1,0:T(8,128)S(1)}, f32[256,128]{1,0:T(8,128)S(1)}, f32[8,27,32,128]{3,2,1,0:T(8,128)S(1)}) custom-call(f32[12968,128]{1,0:T(8,128)S(1)} %get-tuple-element.85._field, ...), custom_call_target="tpu_custom_call", output_to_operand_aliasing={{0}: (0, {}), {1}: (1, {}), {2}: (2, {})} | custom-call | bytes 12582912 | tf_op jit(solution)/shard_map/middle_adjoint/pallas_call | solution.py:754
  35.1 1.4 %collective-permute-done.10.refs_7_ = f32[32,128]{1,0:T(8,128)S(1)} collective-permute-done((f32[32,128]{1,0:T(8,128)S(1)}, f32[32,128]{1,0:T(8,128)S(1)}, u32[]{:S(2)}, u32[]{:S(2)}) %collective-permute-start.10) | collective-permute-done | bytes 16416 | tf_op jit(solution)/shard_map/ppermute | solution.py:715
  36.6 0.2 collective-permute-done.11.refs_8_
  36.7 3.2 %total.1 = (f32[12968,128]{1,0:T(8,128)S(1)}, f32[12968,128]{1,0:T(8,128)S(1)}, f32[312,128]{1,0:T(8,128)S(1)}, f32[256,128]{1,0:T(8,128)S(1)}, f32[8,27,32,128]...) custom-call(f32[12968,128]{1,0:T(8,128)S(1)} %get-tuple-element.91.r, ...), custom_call_target="tpu_custom_call", output_to_operand_aliasing={{0}: (0, {}), {1}: (1, {}), {2}: (2, {}), {3}: (3, {}), {4}... | custom-call | tf_op jit(solution)/shard_map/total/pallas_call | solution.py:754
  39.9 11.0 %all_to_all.11 = f32[32,8,128]{2,1,0:T(8,128)S(1)} all-to-all(f32[32,8,128]{2,1,0:T(8,128)S(1)} %bitcast.3), channel_id=1, replica_groups=mesh['gx'=4,'gy'=8] {'gx','gy'}, dimensions={0} | all-to-all | bytes 262144 | tf_op jit(solution)/shard_map/all_to_all | solution.py:860
  50.9 0.8 %normalize.1 = f32[32,1024]{1,0:T(8,128)} custom-call(f32[256,128]{1,0:T(8,128)S(1)} %get-tuple-element.99.total, f32[256,128]{1,0:T(8,128)S(1)} %bitcast.2), custom_call_target="tpu_custom_call" | custom-call | tf_op jit(solution)/shard_map/normalize/pallas_call | solution.py:754
Async XLA Ops:
  3.2 9.1 %collective-permute-start = (f32[480,128]{1,0:T(8,128)S(1)}, f32[480,128]{1,0:T(8,128)S(1)}, u32[]{:S(2)}, u32[]{:S(2)}) collective-permute-start(f32[480,128]{1,0:T(8,128)S(1)} %get-tuple-element.61), channel_id=1, source_target_pairs={{1,2},{2,1},{3,4},{4,3},{5,6},{6,5},{7,0},{0,7},{9,10},{10,9},{11,... | collective-permute-start | bytes 737288 | tf_op jit(solution)/shard_map/ppermute | solution.py:715
  6.6 5.7 %collective-permute-start.1 = (f32[480,128]{1,0:T(8,128)S(1)}, f32[480,128]{1,0:T(8,128)S(1)}, u32[]{:S(2)}, u32[]{:S(2)}) collective-permute-start(f32[480,128]{1,0:T(8,128)S(1)} %get-tuple-element.62), channel_id=1, source_target_pairs={{0,1},{1,0},{2,3},{3,2},{4,5},{5,4},{6,7},{7,6},{8,9},{9,8},{10,11... | collective-permute-start | bytes 737288 | tf_op jit(solution)/shard_map/ppermute | solution.py:714
  7.2 10.4 %collective-permute-start.2 = (f32[240,128]{1,0:T(8,128)S(1)}, f32[240,128]{1,0:T(8,128)S(1)}, u32[]{:S(2)}, u32[]{:S(2)}) collective-permute-start(f32[240,128]{1,0:T(8,128)S(1)} %get-tuple-element.66), channel_id=1, source_target_pairs={{8,16},{16,8},{24,0},{0,24},{9,17},{17,9},{25,1},{1,25},{10,18},{1... | collective-permute-start | bytes 368648 | tf_op jit(solution)/shard_map/ppermute | solution.py:715
  10.8 6.9 %collective-permute-start.3 = (f32[240,128]{1,0:T(8,128)S(1)}, f32[240,128]{1,0:T(8,128)S(1)}, u32[]{:S(2)}, u32[]{:S(2)}) collective-permute-start(f32[240,128]{1,0:T(8,128)S(1)} %get-tuple-element.67), channel_id=1, source_target_pairs={{0,8},{8,0},{16,24},{24,16},{1,9},{9,1},{17,25},{25,17},{2,10},{10... | collective-permute-start | bytes 368648 | tf_op jit(solution)/shard_map/ppermute | solution.py:714
  12.1 5.7 %copy-start = (f32[27,32,1024]{2,1,0:T(8,128)S(1)}, f32[27,32,1024]{2,1,0:T(8,128)}, u32[]{:S(2)}) copy-start(f32[27,32,1024]{2,1,0:T(8,128)} %refs_1_.3) | copy-start | bytes 10616836
  12.4 7.0 %collective-permute-start.4 = (f32[32,128]{1,0:T(8,128)S(1)}, f32[32,128]{1,0:T(8,128)S(1)}, u32[]{:S(2)}, u32[]{:S(2)}) collective-permute-start(f32[32,128]{1,0:T(8,128)S(1)} %get-tuple-element.73), channel_id=1, source_target_pairs={{8,16},{16,8},{24,0},{0,24},{9,17},{17,9},{25,1},{1,25},{10,18},{1... | collective-permute-start | bytes 49160 | tf_op jit(solution)/shard_map/ppermute | solution.py:715
  17.6 3.7 %collective-permute-start.5 = (f32[32,128]{1,0:T(8,128)S(1)}, f32[32,128]{1,0:T(8,128)S(1)}, u32[]{:S(2)}, u32[]{:S(2)}) collective-permute-start(f32[32,128]{1,0:T(8,128)S(1)} %get-tuple-element.74), channel_id=1, source_target_pairs={{0,8},{8,0},{16,24},{24,16},{1,9},{9,1},{17,25},{25,17},{2,10},{10... | collective-permute-start | bytes 49160 | tf_op jit(solution)/shard_map/ppermute | solution.py:714
  22.7 8.1 %collective-permute-start.6 = (f32[448,128]{1,0:T(8,128)S(1)}, f32[448,128]{1,0:T(8,128)S(1)}, u32[]{:S(2)}, u32[]{:S(2)}) collective-permute-start(f32[448,128]{1,0:T(8,128)S(1)} %get-tuple-element.83), channel_id=1, source_target_pairs={{1,2},{2,1},{3,4},{4,3},{5,6},{6,5},{7,0},{0,7},{9,10},{10,9},{11,... | collective-permute-start | bytes 688136 | tf_op jit(solution)/shard_map/ppermute | solution.py:715
  22.8 8.1 %collective-permute-start.7 = (f32[448,128]{1,0:T(8,128)S(1)}, f32[448,128]{1,0:T(8,128)S(1)}, u32[]{:S(2)}, u32[]{:S(2)}) collective-permute-start(f32[448,128]{1,0:T(8,128)S(1)} %get-tuple-element.84), channel_id=1, source_target_pairs={{0,1},{1,0},{2,3},{3,2},{4,5},{5,4},{6,7},{7,6},{8,9},{9,8},{10,11... | collective-permute-start | bytes 688136 | tf_op jit(solution)/shard_map/ppermute | solution.py:714
  23.7 9.1 %collective-permute-start.8 = (f32[216,128]{1,0:T(8,128)S(1)}, f32[216,128]{1,0:T(8,128)S(1)}, u32[]{:S(2)}, u32[]{:S(2)}) collective-permute-start(f32[216,128]{1,0:T(8,128)S(1)} %get-tuple-element.89), channel_id=1, source_target_pairs={{8,16},{16,8},{24,0},{0,24},{9,17},{17,9},{25,1},{1,25},{10,18},{1... | collective-permute-start | bytes 331784 | tf_op jit(solution)/shard_map/ppermute | solution.py:715
  25.6 7.9 %collective-permute-start.9 = (f32[216,128]{1,0:T(8,128)S(1)}, f32[216,128]{1,0:T(8,128)S(1)}, u32[]{:S(2)}, u32[]{:S(2)}) collective-permute-start(f32[216,128]{1,0:T(8,128)S(1)} %get-tuple-element.90), channel_id=1, source_target_pairs={{0,8},{8,0},{16,24},{24,16},{1,9},{9,1},{17,25},{25,17},{2,10},{10... | collective-permute-start | bytes 331784 | tf_op jit(solution)/shard_map/ppermute | solution.py:714
  30.9 5.6 %collective-permute-start.10 = (f32[32,128]{1,0:T(8,128)S(1)}, f32[32,128]{1,0:T(8,128)S(1)}, u32[]{:S(2)}, u32[]{:S(2)}) collective-permute-start(f32[32,128]{1,0:T(8,128)S(1)} %get-tuple-element.96), channel_id=1, source_target_pairs={{8,16},{16,8},{24,0},{0,24},{9,17},{17,9},{25,1},{1,25},{10,18},{1... | collective-permute-start | bytes 49160 | tf_op jit(solution)/shard_map/ppermute | solution.py:715
  32.8 3.9 %collective-permute-start.11 = (f32[32,128]{1,0:T(8,128)S(1)}, f32[32,128]{1,0:T(8,128)S(1)}, u32[]{:S(2)}, u32[]{:S(2)}) collective-permute-start(f32[32,128]{1,0:T(8,128)S(1)} %get-tuple-element.97), channel_id=1, source_target_pairs={{0,8},{8,0},{16,24},{24,16},{1,9},{9,1},{17,25},{25,17},{2,10},{10... | collective-permute-start | bytes 49160 | tf_op jit(solution)/shard_map/ppermute | solution.py:714

commit v11 on v8

--- a/solution.py
+++ b/solution.py
@@ -55,20 +55,18 @@
 
 def lane_masks(height):
     lane = lax.broadcasted_iota(jnp.int32, (height, LANES), 1)
-    return lane >= NZ, lane % NZ == 0, lane % NZ == NZ - 1
+    level = lane % NZ
+    below = jnp.where(level == 0, lane + (NZ - 1), lane - 1)
+    above = jnp.where(level == NZ - 1, lane - (NZ - 1), lane + 1)
+    return lane >= NZ, below, above, below ^ NZ, above ^ NZ
 
 
 def shift_lanes(here, d, masks):
-    first, last = masks[1:]
     dy, dz = d[1:]
     if dz == 0:
         return here if dy == 0 else pltpu.roll(here, NZ, 1)
-    if dz == 1:
-        one, other, edge = 1, NZ + 1, first
-    else:
-        one, other, edge = LANES - 1, NZ - 1, last
-    inner, wrapped = (one, other) if dy == 0 else (other, one)
-    return jnp.where(edge, pltpu.roll(here, wrapped, 1), pltpu.roll(here, inner, 1))
+    source = masks[(1 if dz == 1 else 2) + (0 if dy == 0 else 2)]
+    return jnp.take_along_axis(here, source, axis=1, mode="promise_in_bounds")
 
 
 def pull(load, d, masks):
@@ -637,12 +635,13 @@
     def copy(k):
         return pltpu.make_async_copy(stage.at[k - 1], block_of(final, k), sems.at[k - 1])
 
-    copy(1).start()
-    copy(g.cols).start()
+    for k in (1, g.cols, *range(3, g.cols - 1)):
+        copy(k).start()
     seed = seed_tile(g, post, adjoint, stage, field, masks)
 
     near_core_tiles(g, seed)
-    every(2, g.cols - 1, lambda k: copy(k).start())
+    for k in (2, g.cols - 1):
+        copy(k).start()
     interior_tiles(g, step_tile(g, field, out, -1, 27, masks, adjoint_second(g, state1, total)))
     every(1, g.cols, lambda k: copy(k).wait())
 

time: 51.3 us -> 51.8 us (level)
  Pallas kernels: 18.3 us -> 18.9 us
    pallas_call x14, Pallas kernels: 18.3 us -> 18.9 us  [call(): pl.pallas_call(functools.partial(kernel, g), in_specs=in_specs, out_shape...]
  transfers between devices with their start and end apart: 19 -> 19, of which waited for: 9 -> 8; matrix products, arithmetic and copies ran while one was open for 0% -> 0% of each run, Pallas kernels for 23% -> 23%
where the time goes in v11:
time: 51.8 us; the launch traced here: 51.7 us
  starting transfers between devices  23.3 us (45%)
  Pallas kernels  18.9 us (36%)
  waiting for transfers between devices  8.59 us (17%)
  between operations  0.85 us (2%)
    pallas_call x14, Pallas kernels, call(): pl.pallas_call(functools.partial(kernel, g), in_specs=in_specs, out_shape...  18.9 us
    ppermute x6, starting transfers between devices, swap(): lax.ppermute(second, axis, swap_pairs(count, 1))  16.1 us
    ppermute x6, waiting for transfers between devices, swap(): lax.ppermute(second, axis, swap_pairs(count, 1))  4.7 us
    ppermute x3, starting transfers between devices, largest_of_all(): parts.append(lax.ppermute(peak, ('gx', 'gy'), pairs))  4.12 us
    ppermute x3, starting transfers between devices, largest_of_all(): parts.append(lax.ppermute(peak, 'gy', pairs))  2.98 us
    ppermute x6, waiting for transfers between devices, swap(): lax.ppermute(first, axis, swap_pairs(count, 0))  2.73 us
    ppermute x1, waiting for transfers between devices, largest_of_all(): lax.ppermute(peak, 'gy', [(i, i ^ 1) for i in range(ny)])  1.15 us
  transfers between devices with their start and end apart: 19, of which 8 were waited for; matrix products, arithmetic and copies ran while one was open for 0% of the time, Pallas kernels for 23%

profile of v11, /device:TPU:0, one launch (start us, length us, event | category | flops | bytes accessed | tf_op | source)
XLA Modules:
  0.0 51.7 jit_solution(3212119673282397453)
XLA Ops:
  0.6 2.6 %side_first.1 = (f32[14408,128]{1,0:T(8,128)S(1)}, f32[1792,128]{1,0:T(8,128)S(1)}, f32[8,27,32,128]{3,2,1,0:T(8,128)S(1)}, f32[32,1024]{1,0:T(8,128)S(1)}, s32[...) custom-call(f32[27,32,1024]{2,1,0:T(8,128)} %pops.1, ...), custom_call_target="tpu_custom_call" | custom-call | tf_op jit(solution)/shard_map/side_first/pallas_call | solution.py:793
  3.2 3.4 %collective-permute-start = (f32[480,128]{1,0:T(8,128)S(1)}, f32[480,128]{1,0:T(8,128)S(1)}, u32[]{:S(2)}, u32[]{:S(2)}) collective-permute-start(f32[480,128]{1,0:T(8,128)S(1)} %get-tuple-element.64), channel_id=1, source_target_pairs={{1,2},{2,1},{3,4},{4,3},{5,6},{6,5},{7,0},{0,7},{9,10},{10,9},{11,... | collective-permute-start | bytes 737288 | tf_op jit(solution)/shard_map/ppermute | solution.py:722
  6.6 0.0 collective-permute-start.1
  6.6 0.6 %rim_first.1 = (f32[14408,128]{1,0:T(8,128)S(1)}, f32[1792,128]{1,0:T(8,128)S(1)}, f32[240,128]{1,0:T(8,128)S(1)}, f32[240,128]{1,0:T(8,128)S(1)}) custom-call(f32[14408,128]{1,0:T(8,128)S(1)} %get-tuple-element.55._out, f32[1792,128]{1,0:T(8,128)S(1)} %get-tuple-element.56._state, ...), custom_call_target="tpu_custom_call", output_to_operand_aliasing={{0}: (0, {}), {1}: (1, {})} | custom-call | bytes 12582912 | tf_op jit(solution)/shard_map/rim_first/pallas_call | solution.py:793
  7.2 3.7 %collective-permute-start.2 = (f32[240,128]{1,0:T(8,128)S(1)}, f32[240,128]{1,0:T(8,128)S(1)}, u32[]{:S(2)}, u32[]{:S(2)}) collective-permute-start(f32[240,128]{1,0:T(8,128)S(1)} %get-tuple-element.69), channel_id=1, source_target_pairs={{8,16},{16,8},{24,0},{0,24},{9,17},{17,9},{25,1},{1,25},{10,18},{1... | collective-permute-start | bytes 368648 | tf_op jit(solution)/shard_map/ppermute | solution.py:722
  10.9 0.0 collective-permute-start.3
  10.9 1.2 %inner_first.1 = (f32[14408,128]{1,0:T(8,128)S(1)}, f32[1792,128]{1,0:T(8,128)S(1)}, f32[12968,128]{1,0:T(8,128)S(1)}, f32[2184,128]{1,0:T(8,128)S(1)}) custom-call(f32[14408,128]{1,0:T(8,128)S(1)} %get-tuple-element.61._, f32[1792,128]{1,0:T(8,128)S(1)} %get-tuple-element.62._state, ...), custom_call_target="tpu_custom_call", output_to_operand_aliasing={{0}: (0, {}), {1}: (1, {})} | custom-call | bytes 12582912 | tf_op jit(solution)/shard_map/inner_first/pallas_call | solution.py:793
  12.1 0.0 copy-start
  12.1 0.2 collective-permute-done.refs_1_
  12.3 0.0 collective-permute-done.1.refs_2_
  12.3 0.1 relay.2
  12.4 5.2 %collective-permute-start.4 = (f32[32,128]{1,0:T(8,128)S(1)}, f32[32,128]{1,0:T(8,128)S(1)}, u32[]{:S(2)}, u32[]{:S(2)}) collective-permute-start(f32[32,128]{1,0:T(8,128)S(1)} %get-tuple-element.76), channel_id=1, source_target_pairs={{8,16},{16,8},{24,0},{0,24},{9,17},{17,9},{25,1},{1,25},{10,18},{1... | collective-permute-start | bytes 49160 | tf_op jit(solution)/shard_map/ppermute | solution.py:722
  17.6 0.0 collective-permute-start.5
  17.6 0.0 collective-permute-done.2.b
  17.6 0.2 collective-permute-done.3.a
  17.8 0.0 copy-done
  17.8 1.9 %middle_second.1 = (f32[14408,128]{1,0:T(8,128)S(1)}, f32[12968,128]{1,0:T(8,128)S(1)}, f32[2184,128]{1,0:T(8,128)S(1)}, f32[8,27,32,128]{3,2,1,0:T(8,128)S(1)}, f32[12968,128]{1,0:T(8,128)S(1)}) custom-call(f32[14408,128]{1,0:T(8,128)S(1)} %get-tuple-element.66._post, ...), custom_call_target="tpu_custom_call", output_to_operand_aliasing={{0}: (0, {}), {1}: (1, {}), {2}: (2, {})} | custom-call | bytes 12582912 | tf_op jit(solution)/shard_map/middle_second/pallas_call | solution.py:793
  19.7 0.0 collective-permute-done.4.second
  19.7 1.7 %collective-permute-done.5.first = f32[32,128]{1,0:T(8,128)S(1)} collective-permute-done((f32[32,128]{1,0:T(8,128)S(1)}, f32[32,128]{1,0:T(8,128)S(1)}, u32[]{:S(2)}, u32[]{:S(2)}) %collective-permute-start.5) | collective-permute-done | bytes 16416 | tf_op jit(solution)/shard_map/ppermute | solution.py:721
  21.3 1.4 %side_seed.1 = (f32[14408,128]{1,0:T(8,128)S(1)}, f32[12968,128]{1,0:T(8,128)S(1)}, f32[2184,128]{1,0:T(8,128)S(1)}, f32[8,27,32,128]{3,2,1,0:T(8,128)S(1)}, f32...) custom-call(f32[14408,128]{1,0:T(8,128)S(1)} %get-tuple-element.71._, ...), custom_call_target="tpu_custom_call", output_to_operand_aliasing={{0}: (0, {}), {1}: (1, {}), {2}: (2, {}), {3}: (3, {}), {4}... | custom-call | tf_op jit(solution)/shard_map/side_seed/pallas_call | solution.py:793
  22.7 0.1 collective-permute-start.6
  22.8 0.1 collective-permute-start.7
  22.9 0.9 %rim_seed.1 = (f32[8,27,32,128]{3,2,1,0:T(8,128)S(1)}, f32[12968,128]{1,0:T(8,128)S(1)}, f32[216,128]{1,0:T(8,128)S(1)}, f32[216,128]{1,0:T(8,128)S(1)}) custom-call(f32[8,27,32,128]{3,2,1,0:T(8,128)S(1)} %get-tuple-element.78._stage, f32[12968,128]{1,0:T(8,128)S(1)} %get-tuple-element.79._field, ...), custom_call_target="tpu_custom_call", output_to_operand_aliasing={{0}: (0, {}), {1}: (1, {})} | custom-call | bytes 12582912 | tf_op jit(solution)/shard_map/rim_seed/pallas_call | solution.py:793
  23.8 1.9 %collective-permute-start.8 = (f32[216,128]{1,0:T(8,128)S(1)}, f32[216,128]{1,0:T(8,128)S(1)}, u32[]{:S(2)}, u32[]{:S(2)}) collective-permute-start(f32[216,128]{1,0:T(8,128)S(1)} %get-tuple-element.92), channel_id=1, source_target_pairs={{8,16},{16,8},{24,0},{0,24},{9,17},{17,9},{25,1},{1,25},{10,18},{1... | collective-permute-start | bytes 331784 | tf_op jit(solution)/shard_map/ppermute | solution.py:722
  25.7 0.0 collective-permute-start.9
  25.7 1.9 %inner_seed.1 = (f32[8,27,32,128]{3,2,1,0:T(8,128)S(1)}, f32[12968,128]{1,0:T(8,128)S(1)}, f32[12968,128]{1,0:T(8,128)S(1)}, f32[312,128]{1,0:T(8,128)S(1)}, f32[27,32,1024]{2,1,0:T(8,128)}) custom-call(f32[8,27,32,128]{3,2,1,0:T(8,128)S(1)} %get-tuple-element.81.kept, ...), custom_call_target="tpu_custom_call", output_to_operand_aliasing={{0}: (0, {}), {1}: (1, {})} | custom-call | bytes 12582912 | tf_op jit(solution)/shard_map/inner_seed/pallas_call | solution.py:793
  27.6 3.3 %collective-permute-done.6.refs_1_ = f32[448,128]{1,0:T(8,128)S(1)} collective-permute-done((f32[448,128]{1,0:T(8,128)S(1)}, f32[448,128]{1,0:T(8,128)S(1)}, u32[]{:S(2)}, u32[]{:S(2)}) %collective-permute-start.6) | collective-permute-done | bytes 229408 | tf_op jit(solution)/shard_map/ppermute | solution.py:722
  30.9 0.0 collective-permute-done.7.refs_2_
  30.9 0.1 relay.3
  31.0 1.9 %collective-permute-start.10 = (f32[32,128]{1,0:T(8,128)S(1)}, f32[32,128]{1,0:T(8,128)S(1)}, u32[]{:S(2)}, u32[]{:S(2)}) collective-permute-start(f32[32,128]{1,0:T(8,128)S(1)} %get-tuple-element.99), channel_id=1, source_target_pairs={{8,16},{16,8},{24,0},{0,24},{9,17},{17,9},{25,1},{1,25},{10,18},{1... | collective-permute-start | bytes 49160 | tf_op jit(solution)/shard_map/ppermute | solution.py:722
  32.9 0.0 collective-permute-start.11
  32.9 0.0 collective-permute-done.8.b
  32.9 0.7 %collective-permute-done.9.a = f32[216,128]{1,0:T(8,128)S(1)} collective-permute-done((f32[216,128]{1,0:T(8,128)S(1)}, f32[216,128]{1,0:T(8,128)S(1)}, u32[]{:S(2)}, u32[]{:S(2)}) %collective-permute-start.9) | collective-permute-done | bytes 110624 | tf_op jit(solution)/shard_map/ppermute | solution.py:721
  33.6 1.8 %middle_adjoint.1 = (f32[12968,128]{1,0:T(8,128)S(1)}, f32[12968,128]{1,0:T(8,128)S(1)}, f32[312,128]{1,0:T(8,128)S(1)}, f32[256,128]{1,0:T(8,128)S(1)}, f32[1280,128]{1,0:T(8,128)S(1)}) custom-call(f32[12968,128]{1,0:T(8,128)S(1)} %get-tuple-element.88._field, ...), custom_call_target="tpu_custom_call", output_to_operand_aliasing={{0}: (0, {}), {1}: (1, {}), {2}: (2, {})} | custom-call | bytes 12582912 | tf_op jit(solution)/shard_map/middle_adjoint/pallas_call | solution.py:793
  35.4 1.2 %collective-permute-done.10.refs_7_ = f32[32,128]{1,0:T(8,128)S(1)} collective-permute-done((f32[32,128]{1,0:T(8,128)S(1)}, f32[32,128]{1,0:T(8,128)S(1)}, u32[]{:S(2)}, u32[]{:S(2)}) %collective-permute-start.10) | collective-permute-done | bytes 16416 | tf_op jit(solution)/shard_map/ppermute | solution.py:722
  36.6 0.2 collective-permute-done.11.refs_8_
  36.8 2.2 %total.1 = (f32[12968,128]{1,0:T(8,128)S(1)}, f32[12968,128]{1,0:T(8,128)S(1)}, f32[312,128]{1,0:T(8,128)S(1)}, f32[256,128]{1,0:T(8,128)S(1)}, f32[1280,128]{1,0:T(8,128)S(1)}, /*index=5*/f32[8,128]{1,0:T(8,128)S(1)}) custom-call(f32[12968,128]{1,0:T(8,128)S(1)} %get-tuple-element.94.r, ...), custom_call_target="tpu_custom_call", output_to_operand_aliasing={{0}: (0, {}), {1}: (1, {}), {2}: (2, {}), {3}: (3, {}), {4}... | custom-call | tf_op jit(solution)/shard_map/total/pallas_call | solution.py:793
  39.0 0.1 collective-permute-start.12
  39.1 1.2 %collective-permute-done.12 = f32[8,128]{1,0:T(8,128)S(1)} collective-permute-done((f32[8,128]{1,0:T(8,128)S(1)}, f32[8,128]{1,0:T(8,128)S(1)}, u32[]{:S(2)}, u32[]{:S(2)}) %collective-permute-start.12) | collective-permute-done | bytes 4128 | tf_op jit(solution)/shard_map/ppermute | solution.py:728
  40.2 1.0 %collective-permute-start.15 = (f32[8,128]{1,0:T(8,128)S(1)}, f32[8,128]{1,0:T(8,128)S(1)}, u32[]{:S(2)}, u32[]{:S(2)}) collective-permute-start(f32[8,128]{1,0:T(8,128)S(1)} %max.21.near), channel_id=1, source_target_pairs={{0,7},{1,6},{2,5},{3,4},{4,3},{5,2},{6,1},{7,0},{8,15},{9,14},{10,... | collective-permute-start | bytes 12296 | tf_op jit(solution)/shard_map/ppermute | solution.py:738
  41.3 0.1 collective-permute-start.14
  41.4 1.9 %collective-permute-start.13 = (f32[8,128]{1,0:T(8,128)S(1)}, f32[8,128]{1,0:T(8,128)S(1)}, u32[]{:S(2)}, u32[]{:S(2)}) collective-permute-start(f32[8,128]{1,0:T(8,128)S(1)} %max.21.near), channel_id=1, source_target_pairs={{0,3},{1,2},{2,1},{3,0},{4,7},{5,6},{6,5},{7,4},{8,11},{9,10},{10,... | collective-permute-start | bytes 12296 | tf_op jit(solution)/shard_map/ppermute | solution.py:738
  43.2 1.7 %adjoint_low.1 = (f32[8,128]{1,0:T(8,128)S(1)}, f32[27,32,1024]{2,1,0:T(8,128)}) custom-call(f32[12968,128]{1,0:T(8,128)S(1)} %get-tuple-element.101.buf, f32[1280,128]{1,0:T(8,128)S(1)} %get-tuple-element.102.fields, f32[8,128]{1,0:T(8,128)S(1)} %max.21.near), custom_call_target="tpu_custom_call" | custom-call | bytes 6291456 | tf_op jit(solution)/shard_map/adjoint_low/pallas_call | solution.py:793
  44.9 0.0 collective-permute-done.15
  45.0 0.0 collective-permute-done.14
  45.0 0.0 collective-permute-done.13
  45.0 1.9 %collective-permute-start.18 = (f32[8,128]{1,0:T(8,128)S(1)}, f32[8,128]{1,0:T(8,128)S(1)}, u32[]{:S(2)}, u32[]{:S(2)}) collective-permute-start(f32[8,128]{1,0:T(8,128)S(1)} %maximum_maximum_fusion.1), channel_id=1, source_target_pairs={{0,25},{1,24},{2,27},{3,26},{4,29},{5,28},{6,31},{7,30},{8,17},{9,... | collective-permute-start | bytes 12296 | tf_op jit(solution)/shard_map/ppermute | solution.py:745
  46.8 0.0 collective-permute-start.17
  46.8 2.3 %collective-permute-start.16 = (f32[8,128]{1,0:T(8,128)S(1)}, f32[8,128]{1,0:T(8,128)S(1)}, u32[]{:S(2)}, u32[]{:S(2)}) collective-permute-start(f32[8,128]{1,0:T(8,128)S(1)} %maximum_maximum_fusion.1), channel_id=1, source_target_pairs={{0,9},{1,8},{2,11},{3,10},{4,13},{5,12},{6,15},{7,14},{8,1},{9,0},... | collective-permute-start | bytes 12296 | tf_op jit(solution)/shard_map/ppermute | solution.py:745
  49.1 1.7 %adjoint_high.1 = f32[27,32,1024]{2,1,0:T(8,128)} custom-call(f32[12968,128]{1,0:T(8,128)S(1)} %get-tuple-element.101.buf, f32[1280,128]{1,0:T(8,128)S(1)} %get-tuple-element.102.fields, f32[27,32,1024]{2,1,0:T(8,128)} %get-tuple-element.104._), custom_call_target="tpu_custom_call", output_to_operand_aliasing={{}: (2, {})} | custom-call | bytes 6291456 | tf_op jit(solution)/shard_map/adjoint_high/pallas_call | solution.py:793
  50.8 0.0 collective-permute-done.18
  50.8 0.0 collective-permute-done.17
  50.8 0.0 collective-permute-done.16
  50.9 0.8 %normalize.1 = f32[32,1024]{1,0:T(8,128)} custom-call(f32[256,128]{1,0:T(8,128)S(1)} %get-tuple-element.105.total, f32[8,128]{1,0:T(8,128)S(1)} %maximum_maximum_fusion.peak), custom_call_target="tpu_custom_call" | custom-call | tf_op jit(solution)/shard_map/normalize/pallas_call | solution.py:793
  (3 shorter events, 0.0 us)
Async XLA Ops:
  3.2 9.1 %collective-permute-start = (f32[480,128]{1,0:T(8,128)S(1)}, f32[480,128]{1,0:T(8,128)S(1)}, u32[]{:S(2)}, u32[]{:S(2)}) collective-permute-start(f32[480,128]{1,0:T(8,128)S(1)} %get-tuple-element.64), channel_id=1, source_target_pairs={{1,2},{2,1},{3,4},{4,3},{5,6},{6,5},{7,0},{0,7},{9,10},{10,9},{11,... | collective-permute-start | bytes 737288 | tf_op jit(solution)/shard_map/ppermute | solution.py:722
  6.6 5.7 %collective-permute-start.1 = (f32[480,128]{1,0:T(8,128)S(1)}, f32[480,128]{1,0:T(8,128)S(1)}, u32[]{:S(2)}, u32[]{:S(2)}) collective-permute-start(f32[480,128]{1,0:T(8,128)S(1)} %get-tuple-element.65), channel_id=1, source_target_pairs={{0,1},{1,0},{2,3},{3,2},{4,5},{5,4},{6,7},{7,6},{8,9},{9,8},{10,11... | collective-permute-start | bytes 737288 | tf_op jit(solution)/shard_map/ppermute | solution.py:721
  7.2 10.4 %collective-permute-start.2 = (f32[240,128]{1,0:T(8,128)S(1)}, f32[240,128]{1,0:T(8,128)S(1)}, u32[]{:S(2)}, u32[]{:S(2)}) collective-permute-start(f32[240,128]{1,0:T(8,128)S(1)} %get-tuple-element.69), channel_id=1, source_target_pairs={{8,16},{16,8},{24,0},{0,24},{9,17},{17,9},{25,1},{1,25},{10,18},{1... | collective-permute-start | bytes 368648 | tf_op jit(solution)/shard_map/ppermute | solution.py:722
  10.9 6.9 %collective-permute-start.3 = (f32[240,128]{1,0:T(8,128)S(1)}, f32[240,128]{1,0:T(8,128)S(1)}, u32[]{:S(2)}, u32[]{:S(2)}) collective-permute-start(f32[240,128]{1,0:T(8,128)S(1)} %get-tuple-element.70), channel_id=1, source_target_pairs={{0,8},{8,0},{16,24},{24,16},{1,9},{9,1},{17,25},{25,17},{2,10},{10... | collective-permute-start | bytes 368648 | tf_op jit(solution)/shard_map/ppermute | solution.py:721
  12.1 5.7 %copy-start = (f32[27,32,1024]{2,1,0:T(8,128)S(1)}, f32[27,32,1024]{2,1,0:T(8,128)}, u32[]{:S(2)}) copy-start(f32[27,32,1024]{2,1,0:T(8,128)} %refs_1_.3) | copy-start | bytes 10616836
  12.4 7.2 %collective-permute-start.4 = (f32[32,128]{1,0:T(8,128)S(1)}, f32[32,128]{1,0:T(8,128)S(1)}, u32[]{:S(2)}, u32[]{:S(2)}) collective-permute-start(f32[32,128]{1,0:T(8,128)S(1)} %get-tuple-element.76), channel_id=1, source_target_pairs={{8,16},{16,8},{24,0},{0,24},{9,17},{17,9},{25,1},{1,25},{10,18},{1... | collective-permute-start | bytes 49160 | tf_op jit(solution)/shard_map/ppermute | solution.py:722
  17.6 3.7 %collective-permute-start.5 = (f32[32,128]{1,0:T(8,128)S(1)}, f32[32,128]{1,0:T(8,128)S(1)}, u32[]{:S(2)}, u32[]{:S(2)}) collective-permute-start(f32[32,128]{1,0:T(8,128)S(1)} %get-tuple-element.77), channel_id=1, source_target_pairs={{0,8},{8,0},{16,24},{24,16},{1,9},{9,1},{17,25},{25,17},{2,10},{10... | collective-permute-start | bytes 49160 | tf_op jit(solution)/shard_map/ppermute | solution.py:721
  22.7 8.1 %collective-permute-start.6 = (f32[448,128]{1,0:T(8,128)S(1)}, f32[448,128]{1,0:T(8,128)S(1)}, u32[]{:S(2)}, u32[]{:S(2)}) collective-permute-start(f32[448,128]{1,0:T(8,128)S(1)} %get-tuple-element.86), channel_id=1, source_target_pairs={{1,2},{2,1},{3,4},{4,3},{5,6},{6,5},{7,0},{0,7},{9,10},{10,9},{11,... | collective-permute-start | bytes 688136 | tf_op jit(solution)/shard_map/ppermute | solution.py:722
  22.8 8.1 %collective-permute-start.7 = (f32[448,128]{1,0:T(8,128)S(1)}, f32[448,128]{1,0:T(8,128)S(1)}, u32[]{:S(2)}, u32[]{:S(2)}) collective-permute-start(f32[448,128]{1,0:T(8,128)S(1)} %get-tuple-element.87), channel_id=1, source_target_pairs={{0,1},{1,0},{2,3},{3,2},{4,5},{5,4},{6,7},{7,6},{8,9},{9,8},{10,11... | collective-permute-start | bytes 688136 | tf_op jit(solution)/shard_map/ppermute | solution.py:721
  23.8 9.1 %collective-permute-start.8 = (f32[216,128]{1,0:T(8,128)S(1)}, f32[216,128]{1,0:T(8,128)S(1)}, u32[]{:S(2)}, u32[]{:S(2)}) collective-permute-start(f32[216,128]{1,0:T(8,128)S(1)} %get-tuple-element.92), channel_id=1, source_target_pairs={{8,16},{16,8},{24,0},{0,24},{9,17},{17,9},{25,1},{1,25},{10,18},{1... | collective-permute-start | bytes 331784 | tf_op jit(solution)/shard_map/ppermute | solution.py:722
  25.7 7.9 %collective-permute-start.9 = (f32[216,128]{1,0:T(8,128)S(1)}, f32[216,128]{1,0:T(8,128)S(1)}, u32[]{:S(2)}, u32[]{:S(2)}) collective-permute-start(f32[216,128]{1,0:T(8,128)S(1)} %get-tuple-element.93), channel_id=1, source_target_pairs={{0,8},{8,0},{16,24},{24,16},{1,9},{9,1},{17,25},{25,17},{2,10},{10... | collective-permute-start | bytes 331784 | tf_op jit(solution)/shard_map/ppermute | solution.py:721
  31.0 5.6 %collective-permute-start.10 = (f32[32,128]{1,0:T(8,128)S(1)}, f32[32,128]{1,0:T(8,128)S(1)}, u32[]{:S(2)}, u32[]{:S(2)}) collective-permute-start(f32[32,128]{1,0:T(8,128)S(1)} %get-tuple-element.99), channel_id=1, source_target_pairs={{8,16},{16,8},{24,0},{0,24},{9,17},{17,9},{25,1},{1,25},{10,18},{1... | collective-permute-start | bytes 49160 | tf_op jit(solution)/shard_map/ppermute | solution.py:722
  32.9 3.9 %collective-permute-start.11 = (f32[32,128]{1,0:T(8,128)S(1)}, f32[32,128]{1,0:T(8,128)S(1)}, u32[]{:S(2)}, u32[]{:S(2)}) collective-permute-start(f32[32,128]{1,0:T(8,128)S(1)} %get-tuple-element.100), channel_id=1, source_target_pairs={{0,8},{8,0},{16,24},{24,16},{1,9},{9,1},{17,25},{25,17},{2,10},{10... | collective-permute-start | bytes 49160 | tf_op jit(solution)/shard_map/ppermute | solution.py:721
  39.0 1.2 %collective-permute-start.12 = (f32[8,128]{1,0:T(8,128)S(1)}, f32[8,128]{1,0:T(8,128)S(1)}, u32[]{:S(2)}, u32[]{:S(2)}) collective-permute-start(f32[8,128]{1,0:T(8,128)S(1)} %get-tuple-element.103), channel_id=1, source_target_pairs={{0,1},{1,0},{2,3},{3,2},{4,5},{5,4},{6,7},{7,6},{8,9},{9,8},{10,11... | collective-permute-start | bytes 12296 | tf_op jit(solution)/shard_map/ppermute | solution.py:728
  40.2 4.7 %collective-permute-start.15 = (f32[8,128]{1,0:T(8,128)S(1)}, f32[8,128]{1,0:T(8,128)S(1)}, u32[]{:S(2)}, u32[]{:S(2)}) collective-permute-start(f32[8,128]{1,0:T(8,128)S(1)} %max.21.near), channel_id=1, source_target_pairs={{0,7},{1,6},{2,5},{3,4},{4,3},{5,2},{6,1},{7,0},{8,15},{9,14},{10,... | collective-permute-start | bytes 12296 | tf_op jit(solution)/shard_map/ppermute | solution.py:738
  41.3 3.7 %collective-permute-start.14 = (f32[8,128]{1,0:T(8,128)S(1)}, f32[8,128]{1,0:T(8,128)S(1)}, u32[]{:S(2)}, u32[]{:S(2)}) collective-permute-start(f32[8,128]{1,0:T(8,128)S(1)} %max.21.near), channel_id=1, source_target_pairs={{0,5},{1,4},{2,7},{3,6},{4,1},{5,0},{6,3},{7,2},{8,13},{9,12},{10,... | collective-permute-start | bytes 12296 | tf_op jit(solution)/shard_map/ppermute | solution.py:738
  41.4 3.6 %collective-permute-start.13 = (f32[8,128]{1,0:T(8,128)S(1)}, f32[8,128]{1,0:T(8,128)S(1)}, u32[]{:S(2)}, u32[]{:S(2)}) collective-permute-start(f32[8,128]{1,0:T(8,128)S(1)} %max.21.near), channel_id=1, source_target_pairs={{0,3},{1,2},{2,1},{3,0},{4,7},{5,6},{6,5},{7,4},{8,11},{9,10},{10,... | collective-permute-start | bytes 12296 | tf_op jit(solution)/shard_map/ppermute | solution.py:738
  45.0 5.8 %collective-permute-start.18 = (f32[8,128]{1,0:T(8,128)S(1)}, f32[8,128]{1,0:T(8,128)S(1)}, u32[]{:S(2)}, u32[]{:S(2)}) collective-permute-start(f32[8,128]{1,0:T(8,128)S(1)} %maximum_maximum_fusion.1), channel_id=1, source_target_pairs={{0,25},{1,24},{2,27},{3,26},{4,29},{5,28},{6,31},{7,30},{8,17},{9,... | collective-permute-start | bytes 12296 | tf_op jit(solution)/shard_map/ppermute | solution.py:745
  46.8 4.0 %collective-permute-start.17 = (f32[8,128]{1,0:T(8,128)S(1)}, f32[8,128]{1,0:T(8,128)S(1)}, u32[]{:S(2)}, u32[]{:S(2)}) collective-permute-start(f32[8,128]{1,0:T(8,128)S(1)} %maximum_maximum_fusion.1), channel_id=1, source_target_pairs={{0,17},{1,16},{2,19},{3,18},{4,21},{5,20},{6,23},{7,22},{8,25},{9,... | collective-permute-start | bytes 12296 | tf_op jit(solution)/shard_map/ppermute | solution.py:745
  46.8 4.0 %collective-permute-start.16 = (f32[8,128]{1,0:T(8,128)S(1)}, f32[8,128]{1,0:T(8,128)S(1)}, u32[]{:S(2)}, u32[]{:S(2)}) collective-permute-start(f32[8,128]{1,0:T(8,128)S(1)} %maximum_maximum_fusion.1), channel_id=1, source_target_pairs={{0,9},{1,8},{2,11},{3,10},{4,13},{5,12},{6,15},{7,14},{8,1},{9,0},... | collective-permute-start | bytes 12296 | tf_op jit(solution)/shard_map/ppermute | solution.py:745

commit v12 on v11

--- a/solution.py
+++ b/solution.py
@@ -55,28 +55,50 @@
 
 def lane_masks(height):
     lane = lax.broadcasted_iota(jnp.int32, (height, LANES), 1)
-    level = lane % NZ
-    below = jnp.where(level == 0, lane + (NZ - 1), lane - 1)
-    above = jnp.where(level == NZ - 1, lane - (NZ - 1), lane + 1)
-    return lane >= NZ, below, above, below ^ NZ, above ^ NZ
-
-
-def shift_lanes(here, d, masks):
-    dy, dz = d[1:]
+    return lane >= NZ, lane % NZ == 0, lane % NZ == NZ - 1
+
+
+def halves(load, d, masks):
+    high = masks[0]
+    if d[1] == 1:
+        return jnp.where(high, load(-1), load(0))
+    if d[1] == -1:
+        return jnp.where(high, load(0), load(1))
+    return load(0)
+
+
+def turns(dz):
+    return (1, NZ + 1) if dz == 1 else (LANES - 1, NZ - 1)
+
+
+def shift_pair(flat, steep, dz, masks):
+    edge, source = (masks[1], masks[2]) if dz == 1 else (masks[2], masks[1])
+    near, far = turns(dz)
+    one = pltpu.roll(jnp.where(source, steep, flat), near, 1)
+    two = pltpu.roll(jnp.where(source, flat, steep), far, 1)
+    return jnp.where(edge, two, one), jnp.where(edge, one, two)
+
+
+def shift_steep(tile, dz, masks):
     if dz == 0:
-        return here if dy == 0 else pltpu.roll(here, NZ, 1)
-    source = masks[(1 if dz == 1 else 2) + (0 if dy == 0 else 2)]
-    return jnp.take_along_axis(here, source, axis=1, mode="promise_in_bounds")
-
-
-def pull(load, d, masks):
-    high = masks[0]
-    here = load(0)
-    if d[1] == 1:
-        here = jnp.where(high, load(-1), here)
-    elif d[1] == -1:
-        here = jnp.where(high, here, load(1))
-    return shift_lanes(here, d, masks)
+        return pltpu.roll(tile, NZ, 1)
+    near, far = turns(dz)
+    edge = masks[1] if dz == 1 else masks[2]
+    return jnp.where(edge, pltpu.roll(tile, near, 1), pltpu.roll(tile, far, 1))
+
+
+def shift_lanes(tiles, sign, masks):
+    out = list(tiles)
+    place = {velocity(i, sign): i for i in range(27)}
+    for dx in (-1, 0, 1):
+        for dy in (-1, 1):
+            i = place[dx, dy, 0]
+            out[i] = shift_steep(tiles[i], 0, masks)
+        for dz in (-1, 1):
+            i, j, k = (place[dx, dy, dz] for dy in (0, 1, -1))
+            out[i], out[j] = shift_pair(tiles[i], tiles[j], dz, masks)
+            out[k] = shift_steep(tiles[k], dz, masks)
+    return out
 
 
 def stacked(parts):
@@ -105,8 +127,8 @@
             start = {-1: base - g.panel, 0: base, 1: after}[n]
             return read_rows(buf, start + (g.field(i) - d[0]), pieces)
 
-        out.append(pull(load, d, masks))
-    return out
+        out.append(halves(load, d, masks))
+    return shift_lanes(out, sign, masks)
 
 
 def pull_edge(g, buf, sign, side, masks, fields=27):
@@ -121,8 +143,8 @@
         def load(n, i=i, row=row):
             return buf[pl.ds(g.at(i, 1 + n, row), g.cols, stride=g.panel), :]
 
-        out.append(pull(load, d, masks))
-    return out
+        out.append(halves(load, d, masks))
+    return shift_lanes(out, sign, masks)
 
 
 def moments(f):

time: 51.8 us -> 50.8 us (0.981)
  Pallas kernels: 18.9 us -> 16.7 us
  waiting for transfers between devices: 8.59 us -> 9.73 us
    pallas_call x14, Pallas kernels: 18.9 us -> 16.7 us  [call(): pl.pallas_call(functools.partial(kernel, g), in_specs=in_specs, out_shape...]
    ppermute x6, waiting for transfers between devices: 4.7 us -> 5.44 us  [swap(): lax.ppermute(second, axis, swap_pairs(count, 1))]
  transfers between devices with their start and end apart: 19 -> 19, of which waited for: 8 -> 9; matrix products, arithmetic and copies ran while one was open for 0% -> 0% of each run, Pallas kernels for 23% -> 21%
where the time goes in v12:
time: 50.8 us; the launch traced here: 50.6 us
  starting transfers between devices  23.3 us (46%)
  Pallas kernels  16.7 us (33%)
  waiting for transfers between devices  9.73 us (19%)
  between operations  0.82 us (2%)
    pallas_call x14, Pallas kernels, call(): pl.pallas_call(functools.partial(kernel, g), in_specs=in_specs, out_shape...  16.7 us
    ppermute x6, starting transfers between devices, swap(): lax.ppermute(second, axis, swap_pairs(count, 1))  16.1 us
    ppermute x6, waiting for transfers between devices, swap(): lax.ppermute(second, axis, swap_pairs(count, 1))  5.44 us
    ppermute x3, starting transfers between devices, largest_of_all(): parts.append(lax.ppermute(peak, ('gx', 'gy'), pairs))  4.12 us
    ppermute x3, starting transfers between devices, largest_of_all(): parts.append(lax.ppermute(peak, 'gy', pairs))  2.98 us
    ppermute x6, waiting for transfers between devices, swap(): lax.ppermute(first, axis, swap_pairs(count, 0))  2.9 us
    ppermute x1, waiting for transfers between devices, largest_of_all(): lax.ppermute(peak, 'gy', [(i, i ^ 1) for i in range(ny)])  1.15 us
  transfers between devices with their start and end apart: 19, of which 9 were waited for; matrix products, arithmetic and copies ran while one was open for 0% of the time, Pallas kernels for 21%

profile of v12, /device:TPU:0, one launch (start us, length us, event | category | flops | bytes accessed | tf_op | source)
XLA Modules:
  0.0 50.6 jit_solution(12572772960704380375)
XLA Ops:
  0.6 2.6 %side_first.1 = (f32[14408,128]{1,0:T(8,128)S(1)}, f32[1792,128]{1,0:T(8,128)S(1)}, f32[8,27,32,128]{3,2,1,0:T(8,128)S(1)}, f32[32,1024]{1,0:T(8,128)S(1)}, s32[...) custom-call(f32[27,32,1024]{2,1,0:T(8,128)} %pops.1, ...), custom_call_target="tpu_custom_call" | custom-call | tf_op jit(solution)/shard_map/side_first/pallas_call | solution.py:815
  3.2 3.4 %collective-permute-start = (f32[480,128]{1,0:T(8,128)S(1)}, f32[480,128]{1,0:T(8,128)S(1)}, u32[]{:S(2)}, u32[]{:S(2)}) collective-permute-start(f32[480,128]{1,0:T(8,128)S(1)} %get-tuple-element.64), channel_id=1, source_target_pairs={{1,2},{2,1},{3,4},{4,3},{5,6},{6,5},{7,0},{0,7},{9,10},{10,9},{11,... | collective-permute-start | bytes 737288 | tf_op jit(solution)/shard_map/ppermute | solution.py:744
  6.6 0.0 collective-permute-start.1
  6.6 0.6 %rim_first.1 = (f32[14408,128]{1,0:T(8,128)S(1)}, f32[1792,128]{1,0:T(8,128)S(1)}, f32[240,128]{1,0:T(8,128)S(1)}, f32[240,128]{1,0:T(8,128)S(1)}) custom-call(f32[14408,128]{1,0:T(8,128)S(1)} %get-tuple-element.55._out, f32[1792,128]{1,0:T(8,128)S(1)} %get-tuple-element.56._state, ...), custom_call_target="tpu_custom_call", output_to_operand_aliasing={{0}: (0, {}), {1}: (1, {})} | custom-call | bytes 12582912 | tf_op jit(solution)/shard_map/rim_first/pallas_call | solution.py:815
  7.2 3.7 %collective-permute-start.2 = (f32[240,128]{1,0:T(8,128)S(1)}, f32[240,128]{1,0:T(8,128)S(1)}, u32[]{:S(2)}, u32[]{:S(2)}) collective-permute-start(f32[240,128]{1,0:T(8,128)S(1)} %get-tuple-element.69), channel_id=1, source_target_pairs={{8,16},{16,8},{24,0},{0,24},{9,17},{17,9},{25,1},{1,25},{10,18},{1... | collective-permute-start | bytes 368648 | tf_op jit(solution)/shard_map/ppermute | solution.py:744
  10.9 0.0 collective-permute-start.3
  10.9 1.2 %inner_first.1 = (f32[14408,128]{1,0:T(8,128)S(1)}, f32[1792,128]{1,0:T(8,128)S(1)}, f32[12968,128]{1,0:T(8,128)S(1)}, f32[2184,128]{1,0:T(8,128)S(1)}) custom-call(f32[14408,128]{1,0:T(8,128)S(1)} %get-tuple-element.61._, f32[1792,128]{1,0:T(8,128)S(1)} %get-tuple-element.62._state, ...), custom_call_target="tpu_custom_call", output_to_operand_aliasing={{0}: (0, {}), {1}: (1, {})} | custom-call | bytes 12582912 | tf_op jit(solution)/shard_map/inner_first/pallas_call | solution.py:815
  12.1 0.0 copy-start
  12.1 0.2 collective-permute-done.refs_1_
  12.3 0.0 collective-permute-done.1.refs_2_
  12.3 0.1 relay.2
  12.4 5.2 %collective-permute-start.4 = (f32[32,128]{1,0:T(8,128)S(1)}, f32[32,128]{1,0:T(8,128)S(1)}, u32[]{:S(2)}, u32[]{:S(2)}) collective-permute-start(f32[32,128]{1,0:T(8,128)S(1)} %get-tuple-element.76), channel_id=1, source_target_pairs={{8,16},{16,8},{24,0},{0,24},{9,17},{17,9},{25,1},{1,25},{10,18},{1... | collective-permute-start | bytes 49160 | tf_op jit(solution)/shard_map/ppermute | solution.py:744
  17.6 0.0 collective-permute-start.5
  17.6 0.0 collective-permute-done.2.b
  17.6 0.2 collective-permute-done.3.a
  17.8 0.0 copy-done
  17.8 1.5 %middle_second.1 = (f32[14408,128]{1,0:T(8,128)S(1)}, f32[12968,128]{1,0:T(8,128)S(1)}, f32[2184,128]{1,0:T(8,128)S(1)}, f32[8,27,32,128]{3,2,1,0:T(8,128)S(1)}, f32[12968,128]{1,0:T(8,128)S(1)}) custom-call(f32[14408,128]{1,0:T(8,128)S(1)} %get-tuple-element.66._post, ...), custom_call_target="tpu_custom_call", output_to_operand_aliasing={{0}: (0, {}), {1}: (1, {}), {2}: (2, {})} | custom-call | bytes 12582912 | tf_op jit(solution)/shard_map/middle_second/pallas_call | solution.py:815
  19.3 0.0 collective-permute-done.4.second
  19.3 2.0 %collective-permute-done.5.first = f32[32,128]{1,0:T(8,128)S(1)} collective-permute-done((f32[32,128]{1,0:T(8,128)S(1)}, f32[32,128]{1,0:T(8,128)S(1)}, u32[]{:S(2)}, u32[]{:S(2)}) %collective-permute-start.5) | collective-permute-done | bytes 16416 | tf_op jit(solution)/shard_map/ppermute | solution.py:743
  21.3 1.2 %side_seed.1 = (f32[14408,128]{1,0:T(8,128)S(1)}, f32[12968,128]{1,0:T(8,128)S(1)}, f32[2184,128]{1,0:T(8,128)S(1)}, f32[8,27,32,128]{3,2,1,0:T(8,128)S(1)}, f32...) custom-call(f32[14408,128]{1,0:T(8,128)S(1)} %get-tuple-element.71._, ...), custom_call_target="tpu_custom_call", output_to_operand_aliasing={{0}: (0, {}), {1}: (1, {}), {2}: (2, {}), {3}: (3, {}), {4}... | custom-call | tf_op jit(solution)/shard_map/side_seed/pallas_call | solution.py:815
  22.6 0.1 collective-permute-start.6
  22.6 0.1 collective-permute-start.7
  22.7 0.7 %rim_seed.1 = (f32[8,27,32,128]{3,2,1,0:T(8,128)S(1)}, f32[12968,128]{1,0:T(8,128)S(1)}, f32[216,128]{1,0:T(8,128)S(1)}, f32[216,128]{1,0:T(8,128)S(1)}) custom-call(f32[8,27,32,128]{3,2,1,0:T(8,128)S(1)} %get-tuple-element.78._stage, f32[12968,128]{1,0:T(8,128)S(1)} %get-tuple-element.79._field, ...), custom_call_target="tpu_custom_call", output_to_operand_aliasing={{0}: (0, {}), {1}: (1, {})} | custom-call | bytes 12582912 | tf_op jit(solution)/shard_map/rim_seed/pallas_call | solution.py:815
  23.4 1.9 %collective-permute-start.8 = (f32[216,128]{1,0:T(8,128)S(1)}, f32[216,128]{1,0:T(8,128)S(1)}, u32[]{:S(2)}, u32[]{:S(2)}) collective-permute-start(f32[216,128]{1,0:T(8,128)S(1)} %get-tuple-element.92), channel_id=1, source_target_pairs={{8,16},{16,8},{24,0},{0,24},{9,17},{17,9},{25,1},{1,25},{10,18},{1... | collective-permute-start | bytes 331784 | tf_op jit(solution)/shard_map/ppermute | solution.py:744
  25.3 0.0 collective-permute-start.9
  25.3 1.9 %inner_seed.1 = (f32[8,27,32,128]{3,2,1,0:T(8,128)S(1)}, f32[12968,128]{1,0:T(8,128)S(1)}, f32[12968,128]{1,0:T(8,128)S(1)}, f32[312,128]{1,0:T(8,128)S(1)}, f32[27,32,1024]{2,1,0:T(8,128)}) custom-call(f32[8,27,32,128]{3,2,1,0:T(8,128)S(1)} %get-tuple-element.81.kept, ...), custom_call_target="tpu_custom_call", output_to_operand_aliasing={{0}: (0, {}), {1}: (1, {})} | custom-call | bytes 12582912 | tf_op jit(solution)/shard_map/inner_seed/pallas_call | solution.py:815
  27.2 3.5 %collective-permute-done.6.refs_1_ = f32[448,128]{1,0:T(8,128)S(1)} collective-permute-done((f32[448,128]{1,0:T(8,128)S(1)}, f32[448,128]{1,0:T(8,128)S(1)}, u32[]{:S(2)}, u32[]{:S(2)}) %collective-permute-start.6) | collective-permute-done | bytes 229408 | tf_op jit(solution)/shard_map/ppermute | solution.py:744
  30.7 0.0 collective-permute-done.7.refs_2_
  30.7 0.1 relay.3
  30.8 1.9 %collective-permute-start.10 = (f32[32,128]{1,0:T(8,128)S(1)}, f32[32,128]{1,0:T(8,128)S(1)}, u32[]{:S(2)}, u32[]{:S(2)}) collective-permute-start(f32[32,128]{1,0:T(8,128)S(1)} %get-tuple-element.99), channel_id=1, source_target_pairs={{8,16},{16,8},{24,0},{0,24},{9,17},{17,9},{25,1},{1,25},{10,18},{1... | collective-permute-start | bytes 49160 | tf_op jit(solution)/shard_map/ppermute | solution.py:744
  32.7 0.0 collective-permute-start.11
  32.7 0.0 collective-permute-done.8.b
  32.7 0.5 %collective-permute-done.9.a = f32[216,128]{1,0:T(8,128)S(1)} collective-permute-done((f32[216,128]{1,0:T(8,128)S(1)}, f32[216,128]{1,0:T(8,128)S(1)}, u32[]{:S(2)}, u32[]{:S(2)}) %collective-permute-start.9) | collective-permute-done | bytes 110624 | tf_op jit(solution)/shard_map/ppermute | solution.py:743
  33.2 1.4 %middle_adjoint.1 = (f32[12968,128]{1,0:T(8,128)S(1)}, f32[12968,128]{1,0:T(8,128)S(1)}, f32[312,128]{1,0:T(8,128)S(1)}, f32[256,128]{1,0:T(8,128)S(1)}, f32[1280,128]{1,0:T(8,128)S(1)}) custom-call(f32[12968,128]{1,0:T(8,128)S(1)} %get-tuple-element.88._field, ...), custom_call_target="tpu_custom_call", output_to_operand_aliasing={{0}: (0, {}), {1}: (1, {}), {2}: (2, {})} | custom-call | bytes 12582912 | tf_op jit(solution)/shard_map/middle_adjoint/pallas_call | solution.py:815
  34.7 1.7 %collective-permute-done.10.refs_7_ = f32[32,128]{1,0:T(8,128)S(1)} collective-permute-done((f32[32,128]{1,0:T(8,128)S(1)}, f32[32,128]{1,0:T(8,128)S(1)}, u32[]{:S(2)}, u32[]{:S(2)}) %collective-permute-start.10) | collective-permute-done | bytes 16416 | tf_op jit(solution)/shard_map/ppermute | solution.py:744
  36.4 0.2 collective-permute-done.11.refs_8_
  36.6 1.7 %total.1 = (f32[12968,128]{1,0:T(8,128)S(1)}, f32[12968,128]{1,0:T(8,128)S(1)}, f32[312,128]{1,0:T(8,128)S(1)}, f32[256,128]{1,0:T(8,128)S(1)}, f32[1280,128]{1,0:T(8,128)S(1)}, /*index=5*/f32[8,128]{1,0:T(8,128)S(1)}) custom-call(f32[12968,128]{1,0:T(8,128)S(1)} %get-tuple-element.94.r, ...), custom_call_target="tpu_custom_call", output_to_operand_aliasing={{0}: (0, {}), {1}: (1, {}), {2}: (2, {}), {3}: (3, {}), {4}... | custom-call | tf_op jit(solution)/shard_map/total/pallas_call | solution.py:815
  38.3 0.1 collective-permute-start.12
  38.4 1.2 %collective-permute-done.12 = f32[8,128]{1,0:T(8,128)S(1)} collective-permute-done((f32[8,128]{1,0:T(8,128)S(1)}, f32[8,128]{1,0:T(8,128)S(1)}, u32[]{:S(2)}, u32[]{:S(2)}) %collective-permute-start.12) | collective-permute-done | bytes 4128 | tf_op jit(solution)/shard_map/ppermute | solution.py:750
  39.6 1.0 %collective-permute-start.15 = (f32[8,128]{1,0:T(8,128)S(1)}, f32[8,128]{1,0:T(8,128)S(1)}, u32[]{:S(2)}, u32[]{:S(2)}) collective-permute-start(f32[8,128]{1,0:T(8,128)S(1)} %max.21.near), channel_id=1, source_target_pairs={{0,7},{1,6},{2,5},{3,4},{4,3},{5,2},{6,1},{7,0},{8,15},{9,14},{10,... | collective-permute-start | bytes 12296 | tf_op jit(solution)/shard_map/ppermute | solution.py:760
  40.6 0.0 collective-permute-start.14
  40.6 2.0 %collective-permute-start.13 = (f32[8,128]{1,0:T(8,128)S(1)}, f32[8,128]{1,0:T(8,128)S(1)}, u32[]{:S(2)}, u32[]{:S(2)}) collective-permute-start(f32[8,128]{1,0:T(8,128)S(1)} %max.21.near), channel_id=1, source_target_pairs={{0,3},{1,2},{2,1},{3,0},{4,7},{5,6},{6,5},{7,4},{8,11},{9,10},{10,... | collective-permute-start | bytes 12296 | tf_op jit(solution)/shard_map/ppermute | solution.py:760
  42.5 1.4 %adjoint_low.1 = (f32[8,128]{1,0:T(8,128)S(1)}, f32[27,32,1024]{2,1,0:T(8,128)}) custom-call(f32[12968,128]{1,0:T(8,128)S(1)} %get-tuple-element.101.buf, f32[1280,128]{1,0:T(8,128)S(1)} %get-tuple-element.102.fields, f32[8,128]{1,0:T(8,128)S(1)} %max.21.near), custom_call_target="tpu_custom_call" | custom-call | bytes 6291456 | tf_op jit(solution)/shard_map/adjoint_low/pallas_call | solution.py:815
  44.0 0.0 collective-permute-done.15
  44.0 0.0 collective-permute-done.14
  44.0 0.0 collective-permute-done.13
  44.0 1.9 %collective-permute-start.18 = (f32[8,128]{1,0:T(8,128)S(1)}, f32[8,128]{1,0:T(8,128)S(1)}, u32[]{:S(2)}, u32[]{:S(2)}) collective-permute-start(f32[8,128]{1,0:T(8,128)S(1)} %maximum_maximum_fusion.1), channel_id=1, source_target_pairs={{0,25},{1,24},{2,27},{3,26},{4,29},{5,28},{6,31},{7,30},{8,17},{9,... | collective-permute-start | bytes 12296 | tf_op jit(solution)/shard_map/ppermute | solution.py:767
  45.9 0.0 collective-permute-start.17
  45.9 2.3 %collective-permute-start.16 = (f32[8,128]{1,0:T(8,128)S(1)}, f32[8,128]{1,0:T(8,128)S(1)}, u32[]{:S(2)}, u32[]{:S(2)}) collective-permute-start(f32[8,128]{1,0:T(8,128)S(1)} %maximum_maximum_fusion.1), channel_id=1, source_target_pairs={{0,9},{1,8},{2,11},{3,10},{4,13},{5,12},{6,15},{7,14},{8,1},{9,0},... | collective-permute-start | bytes 12296 | tf_op jit(solution)/shard_map/ppermute | solution.py:767
  48.2 1.4 %adjoint_high.1 = f32[27,32,1024]{2,1,0:T(8,128)} custom-call(f32[12968,128]{1,0:T(8,128)S(1)} %get-tuple-element.101.buf, f32[1280,128]{1,0:T(8,128)S(1)} %get-tuple-element.102.fields, f32[27,32,1024]{2,1,0:T(8,128)} %get-tuple-element.104._), custom_call_target="tpu_custom_call", output_to_operand_aliasing={{}: (2, {})} | custom-call | bytes 6291456 | tf_op jit(solution)/shard_map/adjoint_high/pallas_call | solution.py:815
  49.6 0.0 collective-permute-done.18
  49.6 0.2 collective-permute-done.17
  49.8 0.0 collective-permute-done.16
  49.8 0.8 %normalize.1 = f32[32,1024]{1,0:T(8,128)} custom-call(f32[256,128]{1,0:T(8,128)S(1)} %get-tuple-element.105.total, f32[8,128]{1,0:T(8,128)S(1)} %maximum_maximum_fusion.peak), custom_call_target="tpu_custom_call" | custom-call | tf_op jit(solution)/shard_map/normalize/pallas_call | solution.py:815
  (3 shorter events, 0.0 us)
Async XLA Ops:
  3.2 9.1 %collective-permute-start = (f32[480,128]{1,0:T(8,128)S(1)}, f32[480,128]{1,0:T(8,128)S(1)}, u32[]{:S(2)}, u32[]{:S(2)}) collective-permute-start(f32[480,128]{1,0:T(8,128)S(1)} %get-tuple-element.64), channel_id=1, source_target_pairs={{1,2},{2,1},{3,4},{4,3},{5,6},{6,5},{7,0},{0,7},{9,10},{10,9},{11,... | collective-permute-start | bytes 737288 | tf_op jit(solution)/shard_map/ppermute | solution.py:744
  6.6 5.7 %collective-permute-start.1 = (f32[480,128]{1,0:T(8,128)S(1)}, f32[480,128]{1,0:T(8,128)S(1)}, u32[]{:S(2)}, u32[]{:S(2)}) collective-permute-start(f32[480,128]{1,0:T(8,128)S(1)} %get-tuple-element.65), channel_id=1, source_target_pairs={{0,1},{1,0},{2,3},{3,2},{4,5},{5,4},{6,7},{7,6},{8,9},{9,8},{10,11... | collective-permute-start | bytes 737288 | tf_op jit(solution)/shard_map/ppermute | solution.py:743
  7.2 10.4 %collective-permute-start.2 = (f32[240,128]{1,0:T(8,128)S(1)}, f32[240,128]{1,0:T(8,128)S(1)}, u32[]{:S(2)}, u32[]{:S(2)}) collective-permute-start(f32[240,128]{1,0:T(8,128)S(1)} %get-tuple-element.69), channel_id=1, source_target_pairs={{8,16},{16,8},{24,0},{0,24},{9,17},{17,9},{25,1},{1,25},{10,18},{1... | collective-permute-start | bytes 368648 | tf_op jit(solution)/shard_map/ppermute | solution.py:744
  10.9 6.9 %collective-permute-start.3 = (f32[240,128]{1,0:T(8,128)S(1)}, f32[240,128]{1,0:T(8,128)S(1)}, u32[]{:S(2)}, u32[]{:S(2)}) collective-permute-start(f32[240,128]{1,0:T(8,128)S(1)} %get-tuple-element.70), channel_id=1, source_target_pairs={{0,8},{8,0},{16,24},{24,16},{1,9},{9,1},{17,25},{25,17},{2,10},{10... | collective-permute-start | bytes 368648 | tf_op jit(solution)/shard_map/ppermute | solution.py:743
  12.1 5.7 %copy-start = (f32[27,32,1024]{2,1,0:T(8,128)S(1)}, f32[27,32,1024]{2,1,0:T(8,128)}, u32[]{:S(2)}) copy-start(f32[27,32,1024]{2,1,0:T(8,128)} %refs_1_.3) | copy-start | bytes 10616836
  12.4 6.9 %collective-permute-start.4 = (f32[32,128]{1,0:T(8,128)S(1)}, f32[32,128]{1,0:T(8,128)S(1)}, u32[]{:S(2)}, u32[]{:S(2)}) collective-permute-start(f32[32,128]{1,0:T(8,128)S(1)} %get-tuple-element.76), channel_id=1, source_target_pairs={{8,16},{16,8},{24,0},{0,24},{9,17},{17,9},{25,1},{1,25},{10,18},{1... | collective-permute-start | bytes 49160 | tf_op jit(solution)/shard_map/ppermute | solution.py:744
  17.6 3.7 %collective-permute-start.5 = (f32[32,128]{1,0:T(8,128)S(1)}, f32[32,128]{1,0:T(8,128)S(1)}, u32[]{:S(2)}, u32[]{:S(2)}) collective-permute-start(f32[32,128]{1,0:T(8,128)S(1)} %get-tuple-element.77), channel_id=1, source_target_pairs={{0,8},{8,0},{16,24},{24,16},{1,9},{9,1},{17,25},{25,17},{2,10},{10... | collective-permute-start | bytes 49160 | tf_op jit(solution)/shard_map/ppermute | solution.py:743
  22.6 8.1 %collective-permute-start.6 = (f32[448,128]{1,0:T(8,128)S(1)}, f32[448,128]{1,0:T(8,128)S(1)}, u32[]{:S(2)}, u32[]{:S(2)}) collective-permute-start(f32[448,128]{1,0:T(8,128)S(1)} %get-tuple-element.86), channel_id=1, source_target_pairs={{1,2},{2,1},{3,4},{4,3},{5,6},{6,5},{7,0},{0,7},{9,10},{10,9},{11,... | collective-permute-start | bytes 688136 | tf_op jit(solution)/shard_map/ppermute | solution.py:744
  22.6 8.1 %collective-permute-start.7 = (f32[448,128]{1,0:T(8,128)S(1)}, f32[448,128]{1,0:T(8,128)S(1)}, u32[]{:S(2)}, u32[]{:S(2)}) collective-permute-start(f32[448,128]{1,0:T(8,128)S(1)} %get-tuple-element.87), channel_id=1, source_target_pairs={{0,1},{1,0},{2,3},{3,2},{4,5},{5,4},{6,7},{7,6},{8,9},{9,8},{10,11... | collective-permute-start | bytes 688136 | tf_op jit(solution)/shard_map/ppermute | solution.py:743
  23.4 9.3 %collective-permute-start.8 = (f32[216,128]{1,0:T(8,128)S(1)}, f32[216,128]{1,0:T(8,128)S(1)}, u32[]{:S(2)}, u32[]{:S(2)}) collective-permute-start(f32[216,128]{1,0:T(8,128)S(1)} %get-tuple-element.92), channel_id=1, source_target_pairs={{8,16},{16,8},{24,0},{0,24},{9,17},{17,9},{25,1},{1,25},{10,18},{1... | collective-permute-start | bytes 331784 | tf_op jit(solution)/shard_map/ppermute | solution.py:744
  25.3 7.9 %collective-permute-start.9 = (f32[216,128]{1,0:T(8,128)S(1)}, f32[216,128]{1,0:T(8,128)S(1)}, u32[]{:S(2)}, u32[]{:S(2)}) collective-permute-start(f32[216,128]{1,0:T(8,128)S(1)} %get-tuple-element.93), channel_id=1, source_target_pairs={{0,8},{8,0},{16,24},{24,16},{1,9},{9,1},{17,25},{25,17},{2,10},{10... | collective-permute-start | bytes 331784 | tf_op jit(solution)/shard_map/ppermute | solution.py:743
  30.8 5.6 %collective-permute-start.10 = (f32[32,128]{1,0:T(8,128)S(1)}, f32[32,128]{1,0:T(8,128)S(1)}, u32[]{:S(2)}, u32[]{:S(2)}) collective-permute-start(f32[32,128]{1,0:T(8,128)S(1)} %get-tuple-element.99), channel_id=1, source_target_pairs={{8,16},{16,8},{24,0},{0,24},{9,17},{17,9},{25,1},{1,25},{10,18},{1... | collective-permute-start | bytes 49160 | tf_op jit(solution)/shard_map/ppermute | solution.py:744
  32.7 3.9 %collective-permute-start.11 = (f32[32,128]{1,0:T(8,128)S(1)}, f32[32,128]{1,0:T(8,128)S(1)}, u32[]{:S(2)}, u32[]{:S(2)}) collective-permute-start(f32[32,128]{1,0:T(8,128)S(1)} %get-tuple-element.100), channel_id=1, source_target_pairs={{0,8},{8,0},{16,24},{24,16},{1,9},{9,1},{17,25},{25,17},{2,10},{10... | collective-permute-start | bytes 49160 | tf_op jit(solution)/shard_map/ppermute | solution.py:743
  38.3 1.2 %collective-permute-start.12 = (f32[8,128]{1,0:T(8,128)S(1)}, f32[8,128]{1,0:T(8,128)S(1)}, u32[]{:S(2)}, u32[]{:S(2)}) collective-permute-start(f32[8,128]{1,0:T(8,128)S(1)} %get-tuple-element.103), channel_id=1, source_target_pairs={{0,1},{1,0},{2,3},{3,2},{4,5},{5,4},{6,7},{7,6},{8,9},{9,8},{10,11... | collective-permute-start | bytes 12296 | tf_op jit(solution)/shard_map/ppermute | solution.py:750
  39.6 4.4 %collective-permute-start.15 = (f32[8,128]{1,0:T(8,128)S(1)}, f32[8,128]{1,0:T(8,128)S(1)}, u32[]{:S(2)}, u32[]{:S(2)}) collective-permute-start(f32[8,128]{1,0:T(8,128)S(1)} %max.21.near), channel_id=1, source_target_pairs={{0,7},{1,6},{2,5},{3,4},{4,3},{5,2},{6,1},{7,0},{8,15},{9,14},{10,... | collective-permute-start | bytes 12296 | tf_op jit(solution)/shard_map/ppermute | solution.py:760
  40.6 3.4 %collective-permute-start.14 = (f32[8,128]{1,0:T(8,128)S(1)}, f32[8,128]{1,0:T(8,128)S(1)}, u32[]{:S(2)}, u32[]{:S(2)}) collective-permute-start(f32[8,128]{1,0:T(8,128)S(1)} %max.21.near), channel_id=1, source_target_pairs={{0,5},{1,4},{2,7},{3,6},{4,1},{5,0},{6,3},{7,2},{8,13},{9,12},{10,... | collective-permute-start | bytes 12296 | tf_op jit(solution)/shard_map/ppermute | solution.py:760
  40.6 3.4 %collective-permute-start.13 = (f32[8,128]{1,0:T(8,128)S(1)}, f32[8,128]{1,0:T(8,128)S(1)}, u32[]{:S(2)}, u32[]{:S(2)}) collective-permute-start(f32[8,128]{1,0:T(8,128)S(1)} %max.21.near), channel_id=1, source_target_pairs={{0,3},{1,2},{2,1},{3,0},{4,7},{5,6},{6,5},{7,4},{8,11},{9,10},{10,... | collective-permute-start | bytes 12296 | tf_op jit(solution)/shard_map/ppermute | solution.py:760
  44.0 5.6 %collective-permute-start.18 = (f32[8,128]{1,0:T(8,128)S(1)}, f32[8,128]{1,0:T(8,128)S(1)}, u32[]{:S(2)}, u32[]{:S(2)}) collective-permute-start(f32[8,128]{1,0:T(8,128)S(1)} %maximum_maximum_fusion.1), channel_id=1, source_target_pairs={{0,25},{1,24},{2,27},{3,26},{4,29},{5,28},{6,31},{7,30},{8,17},{9,... | collective-permute-start | bytes 12296 | tf_op jit(solution)/shard_map/ppermute | solution.py:767
  45.9 3.9 %collective-permute-start.17 = (f32[8,128]{1,0:T(8,128)S(1)}, f32[8,128]{1,0:T(8,128)S(1)}, u32[]{:S(2)}, u32[]{:S(2)}) collective-permute-start(f32[8,128]{1,0:T(8,128)S(1)} %maximum_maximum_fusion.1), channel_id=1, source_target_pairs={{0,17},{1,16},{2,19},{3,18},{4,21},{5,20},{6,23},{7,22},{8,25},{9,... | collective-permute-start | bytes 12296 | tf_op jit(solution)/shard_map/ppermute | solution.py:767
  45.9 3.9 %collective-permute-start.16 = (f32[8,128]{1,0:T(8,128)S(1)}, f32[8,128]{1,0:T(8,128)S(1)}, u32[]{:S(2)}, u32[]{:S(2)}) collective-permute-start(f32[8,128]{1,0:T(8,128)S(1)} %maximum_maximum_fusion.1), channel_id=1, source_target_pairs={{0,9},{1,8},{2,11},{3,10},{4,13},{5,12},{6,15},{7,14},{8,1},{9,0},... | collective-permute-start | bytes 12296 | tf_op jit(solution)/shard_map/ppermute | solution.py:767

commit v13 on v12

--- a/solution.py
+++ b/solution.py
@@ -649,6 +649,10 @@
     by_parity("gx", *faces, functools.partial(pack_x, g, field, -1, 27))
 
 
+def early_panels(g):
+    return (1, g.cols, *range(3, g.cols // 2 + 1))
+
+
 def inner_seed_kernel(
     g, post, _stage, _field, state1, adjoint, stage, field, out, total, final, sems
 ):
@@ -657,15 +661,14 @@
     def copy(k):
         return pltpu.make_async_copy(stage.at[k - 1], block_of(final, k), sems.at[k - 1])
 
-    for k in (1, g.cols, *range(3, g.cols - 1)):
+    for k in early_panels(g):
         copy(k).start()
     seed = seed_tile(g, post, adjoint, stage, field, masks)
 
     near_core_tiles(g, seed)
-    for k in (2, g.cols - 1):
-        copy(k).start()
     interior_tiles(g, step_tile(g, field, out, -1, 27, masks, adjoint_second(g, state1, total)))
-    every(1, g.cols, lambda k: copy(k).wait())
+    for k in early_panels(g):
+        copy(k).wait()
 
 
 def total_tile(g, out, before, state0, total, parts, masks):
@@ -681,11 +684,22 @@
     return act
 
 
-def middle_adjoint_kernel(g, field, out, before, total, parts, state1, state0, x_second, x_first):
+def middle_adjoint_kernel(
+    g, state1, state0, x_second, x_first, stage, _, field, out, before, total, parts, final, sems
+):
     masks = lane_masks(16)
+    copies = [
+        pltpu.make_async_copy(stage.at[k - 1], block_of(final, k), sems.at[k - 1])
+        for k in range(1, g.cols + 1)
+        if k not in early_panels(g)
+    ]
+    for each in copies:
+        each.start()
     by_parity("gx", x_second, x_first, functools.partial(unpack_x, g, field, -1, 27))
     middle_tiles(g, step_tile(g, field, out, -1, 27, masks, adjoint_second(g, state1, before)))
     core_tiles(g, total_tile(g, out, before, state0, total, parts, masks))
+    for each in copies:
+        each.wait()
 
 
 def total_kernel(g, *refs):
@@ -890,7 +904,7 @@
         load=FLIGHT,
     )
     along_x = swap_faces("gx", nx, parcels)
-    _, field, pulled, before, final = call(
+    staged, field, pulled, before, final = call(
         "inner_seed",
         lambda grid, kept, into, buf, *refs: inner_seed_kernel(grid, buf, kept, into, *refs),
         [staged, field, second, state1, adjoint_in],
@@ -900,15 +914,15 @@
         load=FLIGHT,
     )
     field, parcels = relay(field, along_y, -1, 27)
-    field, pulled, before, total, parts = call(
+    field, pulled, before, total, parts, final = call(
         "middle_adjoint",
-        lambda grid, _field, _out, _before, near, far, b, a, *refs: middle_adjoint_kernel(
-            grid, *refs, near, far, b, a
-        ),
-        [field, pulled, before, state1, state0, *along_x],
-        [fields(1, g.local), fields(5, g.local)],
+        lambda grid, _field, _out, _before, *refs: middle_adjoint_kernel(grid, *refs),
+        [field, pulled, before, state1, state0, *along_x, staged],
+        [fields(1, g.local), fields(5, g.local), whole],
+        [sems],
         kept=3,
         load=FLIGHT,
+        result=final,
     )
     _, pulled, _, total, parts, peak = call(
         "total",

time: 50.8 us -> 50.7 us (level)
    pallas_call x14, Pallas kernels: 16.7 us -> 16.2 us  [call(): pl.pallas_call(functools.partial(kernel, g), in_specs=in_specs, out_shape...]
  transfers between devices with their start and end apart: 19 -> 19, of which waited for: 9 -> 9; matrix products, arithmetic and copies ran while one was open for 0% -> 0% of each run, Pallas kernels for 21% -> 20%
where the time goes in v13:
time: 50.7 us; the launch traced here: 50.6 us
  starting transfers between devices  23.3 us (46%)
  Pallas kernels  16.2 us (32%)
  waiting for transfers between devices  10.2 us (20%)
  between operations  0.82 us (2%)
    pallas_call x14, Pallas kernels, call(): pl.pallas_call(functools.partial(kernel, g), in_specs=in_specs, out_shape...  16.2 us
    ppermute x6, starting transfers between devices, swap(): lax.ppermute(second, axis, swap_pairs(count, 1))  16.1 us
    ppermute x6, waiting for transfers between devices, swap(): lax.ppermute(second, axis, swap_pairs(count, 1))  5.91 us
    ppermute x3, starting transfers between devices, largest_of_all(): parts.append(lax.ppermute(peak, ('gx', 'gy'), pairs))  4.12 us
    ppermute x3, starting transfers between devices, largest_of_all(): parts.append(lax.ppermute(peak, 'gy', pairs))  2.98 us
    ppermute x6, waiting for transfers between devices, swap(): lax.ppermute(first, axis, swap_pairs(count, 0))  2.92 us
    ppermute x1, waiting for transfers between devices, largest_of_all(): lax.ppermute(peak, 'gy', [(i, i ^ 1) for i in range(ny)])  1.15 us
  transfers between devices with their start and end apart: 19, of which 9 were waited for; matrix products, arithmetic and copies ran while one was open for 0% of the time, Pallas kernels for 20%

profile of v13, /device:TPU:0, one launch (start us, length us, event | category | flops | bytes accessed | tf_op | source)
XLA Modules:
  0.0 50.6 jit_solution(3351922142815166419)
XLA Ops:
  0.6 2.6 %side_first.1 = (f32[14408,128]{1,0:T(8,128)S(1)}, f32[1792,128]{1,0:T(8,128)S(1)}, f32[8,27,32,128]{3,2,1,0:T(8,128)S(1)}, f32[32,1024]{1,0:T(8,128)S(1)}, s32[...) custom-call(f32[27,32,1024]{2,1,0:T(8,128)} %pops.1, ...), custom_call_target="tpu_custom_call" | custom-call | tf_op jit(solution)/shard_map/side_first/pallas_call | solution.py:829
  3.2 3.4 %collective-permute-start = (f32[480,128]{1,0:T(8,128)S(1)}, f32[480,128]{1,0:T(8,128)S(1)}, u32[]{:S(2)}, u32[]{:S(2)}) collective-permute-start(f32[480,128]{1,0:T(8,128)S(1)} %get-tuple-element.66), channel_id=1, source_target_pairs={{1,2},{2,1},{3,4},{4,3},{5,6},{6,5},{7,0},{0,7},{9,10},{10,9},{11,... | collective-permute-start | bytes 737288 | tf_op jit(solution)/shard_map/ppermute | solution.py:758
  6.6 0.0 collective-permute-start.1
  6.6 0.6 %rim_first.1 = (f32[14408,128]{1,0:T(8,128)S(1)}, f32[1792,128]{1,0:T(8,128)S(1)}, f32[240,128]{1,0:T(8,128)S(1)}, f32[240,128]{1,0:T(8,128)S(1)}) custom-call(f32[14408,128]{1,0:T(8,128)S(1)} %get-tuple-element.57._out, f32[1792,128]{1,0:T(8,128)S(1)} %get-tuple-element.58._state, ...), custom_call_target="tpu_custom_call", output_to_operand_aliasing={{0}: (0, {}), {1}: (1, {})} | custom-call | bytes 12582912 | tf_op jit(solution)/shard_map/rim_first/pallas_call | solution.py:829
  7.2 3.7 %collective-permute-start.2 = (f32[240,128]{1,0:T(8,128)S(1)}, f32[240,128]{1,0:T(8,128)S(1)}, u32[]{:S(2)}, u32[]{:S(2)}) collective-permute-start(f32[240,128]{1,0:T(8,128)S(1)} %get-tuple-element.71), channel_id=1, source_target_pairs={{8,16},{16,8},{24,0},{0,24},{9,17},{17,9},{25,1},{1,25},{10,18},{1... | collective-permute-start | bytes 368648 | tf_op jit(solution)/shard_map/ppermute | solution.py:758
  10.9 0.0 collective-permute-start.3
  10.9 1.2 %inner_first.1 = (f32[14408,128]{1,0:T(8,128)S(1)}, f32[1792,128]{1,0:T(8,128)S(1)}, f32[12968,128]{1,0:T(8,128)S(1)}, f32[2184,128]{1,0:T(8,128)S(1)}) custom-call(f32[14408,128]{1,0:T(8,128)S(1)} %get-tuple-element.63._, f32[1792,128]{1,0:T(8,128)S(1)} %get-tuple-element.64._state, ...), custom_call_target="tpu_custom_call", output_to_operand_aliasing={{0}: (0, {}), {1}: (1, {})} | custom-call | bytes 12582912 | tf_op jit(solution)/shard_map/inner_first/pallas_call | solution.py:829
  12.1 0.0 copy-start
  12.1 0.2 collective-permute-done.refs_1_
  12.3 0.0 collective-permute-done.1.refs_2_
  12.3 0.1 relay.2
  12.4 5.2 %collective-permute-start.4 = (f32[32,128]{1,0:T(8,128)S(1)}, f32[32,128]{1,0:T(8,128)S(1)}, u32[]{:S(2)}, u32[]{:S(2)}) collective-permute-start(f32[32,128]{1,0:T(8,128)S(1)} %get-tuple-element.78), channel_id=1, source_target_pairs={{8,16},{16,8},{24,0},{0,24},{9,17},{17,9},{25,1},{1,25},{10,18},{1... | collective-permute-start | bytes 49160 | tf_op jit(solution)/shard_map/ppermute | solution.py:758
  17.6 0.0 collective-permute-start.5
  17.6 0.0 collective-permute-done.2.b
  17.6 0.2 collective-permute-done.3.a
  17.8 0.0 copy-done
  17.8 1.5 %middle_second.1 = (f32[14408,128]{1,0:T(8,128)S(1)}, f32[12968,128]{1,0:T(8,128)S(1)}, f32[2184,128]{1,0:T(8,128)S(1)}, f32[8,27,32,128]{3,2,1,0:T(8,128)S(1)}, f32[12968,128]{1,0:T(8,128)S(1)}) custom-call(f32[14408,128]{1,0:T(8,128)S(1)} %get-tuple-element.68._post, ...), custom_call_target="tpu_custom_call", output_to_operand_aliasing={{0}: (0, {}), {1}: (1, {}), {2}: (2, {})} | custom-call | bytes 12582912 | tf_op jit(solution)/shard_map/middle_second/pallas_call | solution.py:829
  19.3 0.0 collective-permute-done.4.second
  19.3 2.0 %collective-permute-done.5.first = f32[32,128]{1,0:T(8,128)S(1)} collective-permute-done((f32[32,128]{1,0:T(8,128)S(1)}, f32[32,128]{1,0:T(8,128)S(1)}, u32[]{:S(2)}, u32[]{:S(2)}) %collective-permute-start.5) | collective-permute-done | bytes 16416 | tf_op jit(solution)/shard_map/ppermute | solution.py:757
  21.3 1.2 %side_seed.1 = (f32[14408,128]{1,0:T(8,128)S(1)}, f32[12968,128]{1,0:T(8,128)S(1)}, f32[2184,128]{1,0:T(8,128)S(1)}, f32[8,27,32,128]{3,2,1,0:T(8,128)S(1)}, f32...) custom-call(f32[14408,128]{1,0:T(8,128)S(1)} %get-tuple-element.73._, ...), custom_call_target="tpu_custom_call", output_to_operand_aliasing={{0}: (0, {}), {1}: (1, {}), {2}: (2, {}), {3}: (3, {}), {4}... | custom-call | tf_op jit(solution)/shard_map/side_seed/pallas_call | solution.py:829
  22.5 0.1 collective-permute-start.6
  22.6 0.1 collective-permute-start.7
  22.7 0.7 %rim_seed.1 = (f32[8,27,32,128]{3,2,1,0:T(8,128)S(1)}, f32[12968,128]{1,0:T(8,128)S(1)}, f32[216,128]{1,0:T(8,128)S(1)}, f32[216,128]{1,0:T(8,128)S(1)}) custom-call(f32[8,27,32,128]{3,2,1,0:T(8,128)S(1)} %get-tuple-element.80._stage, f32[12968,128]{1,0:T(8,128)S(1)} %get-tuple-element.81._field, ...), custom_call_target="tpu_custom_call", output_to_operand_aliasing={{0}: (0, {}), {1}: (1, {})} | custom-call | bytes 12582912 | tf_op jit(solution)/shard_map/rim_seed/pallas_call | solution.py:829
  23.4 1.9 %collective-permute-start.8 = (f32[216,128]{1,0:T(8,128)S(1)}, f32[216,128]{1,0:T(8,128)S(1)}, u32[]{:S(2)}, u32[]{:S(2)}) collective-permute-start(f32[216,128]{1,0:T(8,128)S(1)} %get-tuple-element.93), channel_id=1, source_target_pairs={{8,16},{16,8},{24,0},{0,24},{9,17},{17,9},{25,1},{1,25},{10,18},{1... | collective-permute-start | bytes 331784 | tf_op jit(solution)/shard_map/ppermute | solution.py:758
  25.3 0.0 collective-permute-start.9
  25.3 1.3 %inner_seed.1 = (f32[8,27,32,128]{3,2,1,0:T(8,128)S(1)}, f32[12968,128]{1,0:T(8,128)S(1)}, f32[12968,128]{1,0:T(8,128)S(1)}, f32[312,128]{1,0:T(8,128)S(1)}, f32[27,32,1024]{2,1,0:T(8,128)}) custom-call(f32[8,27,32,128]{3,2,1,0:T(8,128)S(1)} %get-tuple-element.83.kept, ...), custom_call_target="tpu_custom_call", output_to_operand_aliasing={{0}: (0, {}), {1}: (1, {})} | custom-call | bytes 12582912 | tf_op jit(solution)/shard_map/inner_seed/pallas_call | solution.py:829
  26.6 4.1 %collective-permute-done.6.refs_1_ = f32[448,128]{1,0:T(8,128)S(1)} collective-permute-done((f32[448,128]{1,0:T(8,128)S(1)}, f32[448,128]{1,0:T(8,128)S(1)}, u32[]{:S(2)}, u32[]{:S(2)}) %collective-permute-start.6) | collective-permute-done | bytes 229408 | tf_op jit(solution)/shard_map/ppermute | solution.py:758
  30.7 0.0 collective-permute-done.7.refs_2_
  30.7 0.1 relay.3
  30.8 1.9 %collective-permute-start.10 = (f32[32,128]{1,0:T(8,128)S(1)}, f32[32,128]{1,0:T(8,128)S(1)}, u32[]{:S(2)}, u32[]{:S(2)}) collective-permute-start(f32[32,128]{1,0:T(8,128)S(1)} %get-tuple-element.103), channel_id=1, source_target_pairs={{8,16},{16,8},{24,0},{0,24},{9,17},{17,9},{25,1},{1,25},{10,18},{1... | collective-permute-start | bytes 49160 | tf_op jit(solution)/shard_map/ppermute | solution.py:758
  32.7 0.0 collective-permute-start.11
  32.7 0.0 collective-permute-done.8.refs_2_
  32.7 0.6 %collective-permute-done.9.refs_3_ = f32[216,128]{1,0:T(8,128)S(1)} collective-permute-done((f32[216,128]{1,0:T(8,128)S(1)}, f32[216,128]{1,0:T(8,128)S(1)}, u32[]{:S(2)}, u32[]{:S(2)}) %collective-permute-start.9) | collective-permute-done | bytes 110624 | tf_op jit(solution)/shard_map/ppermute | solution.py:757
  33.2 1.5 %middle_adjoint.1 = (f32[12968,128]{1,0:T(8,128)S(1)}, f32[12968,128]{1,0:T(8,128)S(1)}, f32[312,128]{1,0:T(8,128)S(1)}, f32[256,128]{1,0:T(8,128)S(1)}, f32[128...) custom-call(f32[12968,128]{1,0:T(8,128)S(1)} %get-tuple-element.89._, ...), custom_call_target="tpu_custom_call", output_to_operand_aliasing={{0}: (0, {}), {1}: (1, {}), {2}: (2, {}), {5}: (8, {})} | custom-call | bytes 12582912 | tf_op jit(solution)/shard_map/middle_adjoint/pallas_call | solution.py:829
  34.8 1.7 %collective-permute-done.10.refs_7_ = f32[32,128]{1,0:T(8,128)S(1)} collective-permute-done((f32[32,128]{1,0:T(8,128)S(1)}, f32[32,128]{1,0:T(8,128)S(1)}, u32[]{:S(2)}, u32[]{:S(2)}) %collective-permute-start.10) | collective-permute-done | bytes 16416 | tf_op jit(solution)/shard_map/ppermute | solution.py:758
  36.4 0.2 collective-permute-done.11.refs_8_
  36.6 1.7 %total.1 = (f32[12968,128]{1,0:T(8,128)S(1)}, f32[12968,128]{1,0:T(8,128)S(1)}, f32[312,128]{1,0:T(8,128)S(1)}, f32[256,128]{1,0:T(8,128)S(1)}, f32[1280,128]{1,0:T(8,128)S(1)}, /*index=5*/f32[8,128]{1,0:T(8,128)S(1)}) custom-call(f32[12968,128]{1,0:T(8,128)S(1)} %get-tuple-element.98.r, ...), custom_call_target="tpu_custom_call", output_to_operand_aliasing={{0}: (0, {}), {1}: (1, {}), {2}: (2, {}), {3}: (3, {}), {4}... | custom-call | tf_op jit(solution)/shard_map/total/pallas_call | solution.py:829
  38.3 0.1 collective-permute-start.12
  38.4 1.2 %collective-permute-done.12 = f32[8,128]{1,0:T(8,128)S(1)} collective-permute-done((f32[8,128]{1,0:T(8,128)S(1)}, f32[8,128]{1,0:T(8,128)S(1)}, u32[]{:S(2)}, u32[]{:S(2)}) %collective-permute-start.12) | collective-permute-done | bytes 4128 | tf_op jit(solution)/shard_map/ppermute | solution.py:764
  39.5 1.0 %collective-permute-start.15 = (f32[8,128]{1,0:T(8,128)S(1)}, f32[8,128]{1,0:T(8,128)S(1)}, u32[]{:S(2)}, u32[]{:S(2)}) collective-permute-start(f32[8,128]{1,0:T(8,128)S(1)} %max.21.near), channel_id=1, source_target_pairs={{0,7},{1,6},{2,5},{3,4},{4,3},{5,2},{6,1},{7,0},{8,15},{9,14},{10,... | collective-permute-start | bytes 12296 | tf_op jit(solution)/shard_map/ppermute | solution.py:774
  40.5 0.0 collective-permute-start.14
  40.5 2.0 %collective-permute-start.13 = (f32[8,128]{1,0:T(8,128)S(1)}, f32[8,128]{1,0:T(8,128)S(1)}, u32[]{:S(2)}, u32[]{:S(2)}) collective-permute-start(f32[8,128]{1,0:T(8,128)S(1)} %max.21.near), channel_id=1, source_target_pairs={{0,3},{1,2},{2,1},{3,0},{4,7},{5,6},{6,5},{7,4},{8,11},{9,10},{10,... | collective-permute-start | bytes 12296 | tf_op jit(solution)/shard_map/ppermute | solution.py:774
  42.5 1.4 %adjoint_low.1 = (f32[8,128]{1,0:T(8,128)S(1)}, f32[27,32,1024]{2,1,0:T(8,128)}) custom-call(f32[12968,128]{1,0:T(8,128)S(1)} %get-tuple-element.105.buf, f32[1280,128]{1,0:T(8,128)S(1)} %get-tuple-element.106.fields, f32[8,128]{1,0:T(8,128)S(1)} %max.21.near), custom_call_target="tpu_custom_call" | custom-call | bytes 6291456 | tf_op jit(solution)/shard_map/adjoint_low/pallas_call | solution.py:829
  43.9 0.0 collective-permute-done.15
  44.0 0.0 collective-permute-done.14
  44.0 0.0 collective-permute-done.13
  44.0 1.9 %collective-permute-start.18 = (f32[8,128]{1,0:T(8,128)S(1)}, f32[8,128]{1,0:T(8,128)S(1)}, u32[]{:S(2)}, u32[]{:S(2)}) collective-permute-start(f32[8,128]{1,0:T(8,128)S(1)} %maximum_maximum_fusion.1), channel_id=1, source_target_pairs={{0,25},{1,24},{2,27},{3,26},{4,29},{5,28},{6,31},{7,30},{8,17},{9,... | collective-permute-start | bytes 12296 | tf_op jit(solution)/shard_map/ppermute | solution.py:781
  45.9 0.0 collective-permute-start.17
  45.9 2.3 %collective-permute-start.16 = (f32[8,128]{1,0:T(8,128)S(1)}, f32[8,128]{1,0:T(8,128)S(1)}, u32[]{:S(2)}, u32[]{:S(2)}) collective-permute-start(f32[8,128]{1,0:T(8,128)S(1)} %maximum_maximum_fusion.1), channel_id=1, source_target_pairs={{0,9},{1,8},{2,11},{3,10},{4,13},{5,12},{6,15},{7,14},{8,1},{9,0},... | collective-permute-start | bytes 12296 | tf_op jit(solution)/shard_map/ppermute | solution.py:781
  48.1 1.4 %adjoint_high.1 = f32[27,32,1024]{2,1,0:T(8,128)} custom-call(f32[12968,128]{1,0:T(8,128)S(1)} %get-tuple-element.105.buf, f32[1280,128]{1,0:T(8,128)S(1)} %get-tuple-element.106.fields, f32[27,32,1024]{2,1,0:T(8,128)} %get-tuple-element.108._), custom_call_target="tpu_custom_call", output_to_operand_aliasing={{}: (2, {})} | custom-call | bytes 6291456 | tf_op jit(solution)/shard_map/adjoint_high/pallas_call | solution.py:829
  49.6 0.0 collective-permute-done.18
  49.6 0.2 collective-permute-done.17
  49.8 0.0 collective-permute-done.16
  49.8 0.8 %normalize.1 = f32[32,1024]{1,0:T(8,128)} custom-call(f32[256,128]{1,0:T(8,128)S(1)} %get-tuple-element.109.total, f32[8,128]{1,0:T(8,128)S(1)} %maximum_maximum_fusion.peak), custom_call_target="tpu_custom_call" | custom-call | tf_op jit(solution)/shard_map/normalize/pallas_call | solution.py:829
  (3 shorter events, 0.0 us)
Async XLA Ops:
  3.2 9.1 %collective-permute-start = (f32[480,128]{1,0:T(8,128)S(1)}, f32[480,128]{1,0:T(8,128)S(1)}, u32[]{:S(2)}, u32[]{:S(2)}) collective-permute-start(f32[480,128]{1,0:T(8,128)S(1)} %get-tuple-element.66), channel_id=1, source_target_pairs={{1,2},{2,1},{3,4},{4,3},{5,6},{6,5},{7,0},{0,7},{9,10},{10,9},{11,... | collective-permute-start | bytes 737288 | tf_op jit(solution)/shard_map/ppermute | solution.py:758
  6.6 5.7 %collective-permute-start.1 = (f32[480,128]{1,0:T(8,128)S(1)}, f32[480,128]{1,0:T(8,128)S(1)}, u32[]{:S(2)}, u32[]{:S(2)}) collective-permute-start(f32[480,128]{1,0:T(8,128)S(1)} %get-tuple-element.67), channel_id=1, source_target_pairs={{0,1},{1,0},{2,3},{3,2},{4,5},{5,4},{6,7},{7,6},{8,9},{9,8},{10,11... | collective-permute-start | bytes 737288 | tf_op jit(solution)/shard_map/ppermute | solution.py:757
  7.2 10.4 %collective-permute-start.2 = (f32[240,128]{1,0:T(8,128)S(1)}, f32[240,128]{1,0:T(8,128)S(1)}, u32[]{:S(2)}, u32[]{:S(2)}) collective-permute-start(f32[240,128]{1,0:T(8,128)S(1)} %get-tuple-element.71), channel_id=1, source_target_pairs={{8,16},{16,8},{24,0},{0,24},{9,17},{17,9},{25,1},{1,25},{10,18},{1... | collective-permute-start | bytes 368648 | tf_op jit(solution)/shard_map/ppermute | solution.py:758
  10.9 6.9 %collective-permute-start.3 = (f32[240,128]{1,0:T(8,128)S(1)}, f32[240,128]{1,0:T(8,128)S(1)}, u32[]{:S(2)}, u32[]{:S(2)}) collective-permute-start(f32[240,128]{1,0:T(8,128)S(1)} %get-tuple-element.72), channel_id=1, source_target_pairs={{0,8},{8,0},{16,24},{24,16},{1,9},{9,1},{17,25},{25,17},{2,10},{10... | collective-permute-start | bytes 368648 | tf_op jit(solution)/shard_map/ppermute | solution.py:757
  12.1 5.7 %copy-start = (f32[27,32,1024]{2,1,0:T(8,128)S(1)}, f32[27,32,1024]{2,1,0:T(8,128)}, u32[]{:S(2)}) copy-start(f32[27,32,1024]{2,1,0:T(8,128)} %refs_1_.3) | copy-start | bytes 10616836
  12.4 6.9 %collective-permute-start.4 = (f32[32,128]{1,0:T(8,128)S(1)}, f32[32,128]{1,0:T(8,128)S(1)}, u32[]{:S(2)}, u32[]{:S(2)}) collective-permute-start(f32[32,128]{1,0:T(8,128)S(1)} %get-tuple-element.78), channel_id=1, source_target_pairs={{8,16},{16,8},{24,0},{0,24},{9,17},{17,9},{25,1},{1,25},{10,18},{1... | collective-permute-start | bytes 49160 | tf_op jit(solution)/shard_map/ppermute | solution.py:758
  17.6 3.7 %collective-permute-start.5 = (f32[32,128]{1,0:T(8,128)S(1)}, f32[32,128]{1,0:T(8,128)S(1)}, u32[]{:S(2)}, u32[]{:S(2)}) collective-permute-start(f32[32,128]{1,0:T(8,128)S(1)} %get-tuple-element.79), channel_id=1, source_target_pairs={{0,8},{8,0},{16,24},{24,16},{1,9},{9,1},{17,25},{25,17},{2,10},{10... | collective-permute-start | bytes 49160 | tf_op jit(solution)/shard_map/ppermute | solution.py:757
  22.5 8.1 %collective-permute-start.6 = (f32[448,128]{1,0:T(8,128)S(1)}, f32[448,128]{1,0:T(8,128)S(1)}, u32[]{:S(2)}, u32[]{:S(2)}) collective-permute-start(f32[448,128]{1,0:T(8,128)S(1)} %get-tuple-element.87), channel_id=1, source_target_pairs={{1,2},{2,1},{3,4},{4,3},{5,6},{6,5},{7,0},{0,7},{9,10},{10,9},{11,... | collective-permute-start | bytes 688136 | tf_op jit(solution)/shard_map/ppermute | solution.py:758
  22.6 8.1 %collective-permute-start.7 = (f32[448,128]{1,0:T(8,128)S(1)}, f32[448,128]{1,0:T(8,128)S(1)}, u32[]{:S(2)}, u32[]{:S(2)}) collective-permute-start(f32[448,128]{1,0:T(8,128)S(1)} %get-tuple-element.88), channel_id=1, source_target_pairs={{0,1},{1,0},{2,3},{3,2},{4,5},{5,4},{6,7},{7,6},{8,9},{9,8},{10,11... | collective-permute-start | bytes 688136 | tf_op jit(solution)/shard_map/ppermute | solution.py:757
  23.4 9.3 %collective-permute-start.8 = (f32[216,128]{1,0:T(8,128)S(1)}, f32[216,128]{1,0:T(8,128)S(1)}, u32[]{:S(2)}, u32[]{:S(2)}) collective-permute-start(f32[216,128]{1,0:T(8,128)S(1)} %get-tuple-element.93), channel_id=1, source_target_pairs={{8,16},{16,8},{24,0},{0,24},{9,17},{17,9},{25,1},{1,25},{10,18},{1... | collective-permute-start | bytes 331784 | tf_op jit(solution)/shard_map/ppermute | solution.py:758
  25.3 7.9 %collective-permute-start.9 = (f32[216,128]{1,0:T(8,128)S(1)}, f32[216,128]{1,0:T(8,128)S(1)}, u32[]{:S(2)}, u32[]{:S(2)}) collective-permute-start(f32[216,128]{1,0:T(8,128)S(1)} %get-tuple-element.94), channel_id=1, source_target_pairs={{0,8},{8,0},{16,24},{24,16},{1,9},{9,1},{17,25},{25,17},{2,10},{10... | collective-permute-start | bytes 331784 | tf_op jit(solution)/shard_map/ppermute | solution.py:757
  30.8 5.6 %collective-permute-start.10 = (f32[32,128]{1,0:T(8,128)S(1)}, f32[32,128]{1,0:T(8,128)S(1)}, u32[]{:S(2)}, u32[]{:S(2)}) collective-permute-start(f32[32,128]{1,0:T(8,128)S(1)} %get-tuple-element.103), channel_id=1, source_target_pairs={{8,16},{16,8},{24,0},{0,24},{9,17},{17,9},{25,1},{1,25},{10,18},{1... | collective-permute-start | bytes 49160 | tf_op jit(solution)/shard_map/ppermute | solution.py:758
  32.7 3.9 %collective-permute-start.11 = (f32[32,128]{1,0:T(8,128)S(1)}, f32[32,128]{1,0:T(8,128)S(1)}, u32[]{:S(2)}, u32[]{:S(2)}) collective-permute-start(f32[32,128]{1,0:T(8,128)S(1)} %get-tuple-element.104), channel_id=1, source_target_pairs={{0,8},{8,0},{16,24},{24,16},{1,9},{9,1},{17,25},{25,17},{2,10},{10... | collective-permute-start | bytes 49160 | tf_op jit(solution)/shard_map/ppermute | solution.py:757
  38.3 1.2 %collective-permute-start.12 = (f32[8,128]{1,0:T(8,128)S(1)}, f32[8,128]{1,0:T(8,128)S(1)}, u32[]{:S(2)}, u32[]{:S(2)}) collective-permute-start(f32[8,128]{1,0:T(8,128)S(1)} %get-tuple-element.107), channel_id=1, source_target_pairs={{0,1},{1,0},{2,3},{3,2},{4,5},{5,4},{6,7},{7,6},{8,9},{9,8},{10,11... | collective-permute-start | bytes 12296 | tf_op jit(solution)/shard_map/ppermute | solution.py:764
  39.5 4.4 %collective-permute-start.15 = (f32[8,128]{1,0:T(8,128)S(1)}, f32[8,128]{1,0:T(8,128)S(1)}, u32[]{:S(2)}, u32[]{:S(2)}) collective-permute-start(f32[8,128]{1,0:T(8,128)S(1)} %max.21.near), channel_id=1, source_target_pairs={{0,7},{1,6},{2,5},{3,4},{4,3},{5,2},{6,1},{7,0},{8,15},{9,14},{10,... | collective-permute-start | bytes 12296 | tf_op jit(solution)/shard_map/ppermute | solution.py:774
  40.5 3.4 %collective-permute-start.14 = (f32[8,128]{1,0:T(8,128)S(1)}, f32[8,128]{1,0:T(8,128)S(1)}, u32[]{:S(2)}, u32[]{:S(2)}) collective-permute-start(f32[8,128]{1,0:T(8,128)S(1)} %max.21.near), channel_id=1, source_target_pairs={{0,5},{1,4},{2,7},{3,6},{4,1},{5,0},{6,3},{7,2},{8,13},{9,12},{10,... | collective-permute-start | bytes 12296 | tf_op jit(solution)/shard_map/ppermute | solution.py:774
  40.5 3.4 %collective-permute-start.13 = (f32[8,128]{1,0:T(8,128)S(1)}, f32[8,128]{1,0:T(8,128)S(1)}, u32[]{:S(2)}, u32[]{:S(2)}) collective-permute-start(f32[8,128]{1,0:T(8,128)S(1)} %max.21.near), channel_id=1, source_target_pairs={{0,3},{1,2},{2,1},{3,0},{4,7},{5,6},{6,5},{7,4},{8,11},{9,10},{10,... | collective-permute-start | bytes 12296 | tf_op jit(solution)/shard_map/ppermute | solution.py:774
  44.0 5.6 %collective-permute-start.18 = (f32[8,128]{1,0:T(8,128)S(1)}, f32[8,128]{1,0:T(8,128)S(1)}, u32[]{:S(2)}, u32[]{:S(2)}) collective-permute-start(f32[8,128]{1,0:T(8,128)S(1)} %maximum_maximum_fusion.1), channel_id=1, source_target_pairs={{0,25},{1,24},{2,27},{3,26},{4,29},{5,28},{6,31},{7,30},{8,17},{9,... | collective-permute-start | bytes 12296 | tf_op jit(solution)/shard_map/ppermute | solution.py:781
  45.9 3.9 %collective-permute-start.17 = (f32[8,128]{1,0:T(8,128)S(1)}, f32[8,128]{1,0:T(8,128)S(1)}, u32[]{:S(2)}, u32[]{:S(2)}) collective-permute-start(f32[8,128]{1,0:T(8,128)S(1)} %maximum_maximum_fusion.1), channel_id=1, source_target_pairs={{0,17},{1,16},{2,19},{3,18},{4,21},{5,20},{6,23},{7,22},{8,25},{9,... | collective-permute-start | bytes 12296 | tf_op jit(solution)/shard_map/ppermute | solution.py:781
  45.9 3.9 %collective-permute-start.16 = (f32[8,128]{1,0:T(8,128)S(1)}, f32[8,128]{1,0:T(8,128)S(1)}, u32[]{:S(2)}, u32[]{:S(2)}) collective-permute-start(f32[8,128]{1,0:T(8,128)S(1)} %maximum_maximum_fusion.1), channel_id=1, source_target_pairs={{0,9},{1,8},{2,11},{3,10},{4,13},{5,12},{6,15},{7,14},{8,1},{9,0},... | collective-permute-start | bytes 12296 | tf_op jit(solution)/shard_map/ppermute | solution.py:781

commit v14 on v13

--- a/solution.py
+++ b/solution.py
@@ -42,7 +42,7 @@
         return i * (self.cols + 2) * self.panel + 8
 
     def padded(self, fields):
-        return (fields * (self.cols + 2) * self.panel + 8, LANES)
+        return (fields * (self.cols + 2) * self.panel + 64, LANES)
 
 
 def velocity(i, sign):

time: 50.7 us -> 50.8 us (level)
  no operation moved by 1% of the time
where the time goes in v14:
time: 50.8 us; the launch traced here: 50.7 us
  starting transfers between devices  23.3 us (46%)
  Pallas kernels  16.3 us (32%)
  waiting for transfers between devices  10.2 us (20%)
  between operations  0.82 us (2%)
    pallas_call x14, Pallas kernels, call(): pl.pallas_call(functools.partial(kernel, g), in_specs=in_specs, out_shape...  16.3 us
    ppermute x6, starting transfers between devices, swap(): lax.ppermute(second, axis, swap_pairs(count, 1))  16.1 us
    ppermute x6, waiting for transfers between devices, swap(): lax.ppermute(second, axis, swap_pairs(count, 1))  5.87 us
    ppermute x3, starting transfers between devices, largest_of_all(): parts.append(lax.ppermute(peak, ('gx', 'gy'), pairs))  4.12 us
    ppermute x3, starting transfers between devices, largest_of_all(): parts.append(lax.ppermute(peak, 'gy', pairs))  2.98 us
    ppermute x6, waiting for transfers between devices, swap(): lax.ppermute(first, axis, swap_pairs(count, 0))  2.92 us
    ppermute x1, waiting for transfers between devices, largest_of_all(): lax.ppermute(peak, 'gy', [(i, i ^ 1) for i in range(ny)])  1.15 us
  transfers between devices with their start and end apart: 19, of which 9 were waited for; matrix products, arithmetic and copies ran while one was open for 0% of the time, Pallas kernels for 20%

profile of v14, /device:TPU:0, one launch (start us, length us, event | category | flops | bytes accessed | tf_op | source)
XLA Modules:
  0.0 50.7 jit_solution(1781109594101010639)
XLA Ops:
  0.6 2.6 %side_first.1 = (f32[14464,128]{1,0:T(8,128)S(1)}, f32[1792,128]{1,0:T(8,128)S(1)}, f32[8,27,32,128]{3,2,1,0:T(8,128)S(1)}, f32[32,1024]{1,0:T(8,128)S(1)}, s32[...) custom-call(f32[27,32,1024]{2,1,0:T(8,128)} %pops.1, ...), custom_call_target="tpu_custom_call" | custom-call | tf_op jit(solution)/shard_map/side_first/pallas_call | solution.py:829
  3.2 3.4 %collective-permute-start = (f32[480,128]{1,0:T(8,128)S(1)}, f32[480,128]{1,0:T(8,128)S(1)}, u32[]{:S(2)}, u32[]{:S(2)}) collective-permute-start(f32[480,128]{1,0:T(8,128)S(1)} %get-tuple-element.66), channel_id=1, source_target_pairs={{1,2},{2,1},{3,4},{4,3},{5,6},{6,5},{7,0},{0,7},{9,10},{10,9},{11,... | collective-permute-start | bytes 737288 | tf_op jit(solution)/shard_map/ppermute | solution.py:758
  6.6 0.0 collective-permute-start.1
  6.6 0.6 %rim_first.1 = (f32[14464,128]{1,0:T(8,128)S(1)}, f32[1792,128]{1,0:T(8,128)S(1)}, f32[240,128]{1,0:T(8,128)S(1)}, f32[240,128]{1,0:T(8,128)S(1)}) custom-call(f32[14464,128]{1,0:T(8,128)S(1)} %get-tuple-element.57._out, f32[1792,128]{1,0:T(8,128)S(1)} %get-tuple-element.58._state, ...), custom_call_target="tpu_custom_call", output_to_operand_aliasing={{0}: (0, {}), {1}: (1, {})} | custom-call | bytes 12582912 | tf_op jit(solution)/shard_map/rim_first/pallas_call | solution.py:829
  7.2 3.7 %collective-permute-start.2 = (f32[240,128]{1,0:T(8,128)S(1)}, f32[240,128]{1,0:T(8,128)S(1)}, u32[]{:S(2)}, u32[]{:S(2)}) collective-permute-start(f32[240,128]{1,0:T(8,128)S(1)} %get-tuple-element.71), channel_id=1, source_target_pairs={{8,16},{16,8},{24,0},{0,24},{9,17},{17,9},{25,1},{1,25},{10,18},{1... | collective-permute-start | bytes 368648 | tf_op jit(solution)/shard_map/ppermute | solution.py:758
  10.9 0.0 collective-permute-start.3
  10.9 1.2 %inner_first.1 = (f32[14464,128]{1,0:T(8,128)S(1)}, f32[1792,128]{1,0:T(8,128)S(1)}, f32[13024,128]{1,0:T(8,128)S(1)}, f32[2184,128]{1,0:T(8,128)S(1)}) custom-call(f32[14464,128]{1,0:T(8,128)S(1)} %get-tuple-element.63._, f32[1792,128]{1,0:T(8,128)S(1)} %get-tuple-element.64._state, ...), custom_call_target="tpu_custom_call", output_to_operand_aliasing={{0}: (0, {}), {1}: (1, {})} | custom-call | bytes 12582912 | tf_op jit(solution)/shard_map/inner_first/pallas_call | solution.py:829
  12.1 0.0 copy-start
  12.1 0.1 collective-permute-done.refs_1_
  12.3 0.0 collective-permute-done.1.refs_2_
  12.3 0.1 relay.2
  12.4 5.2 %collective-permute-start.4 = (f32[32,128]{1,0:T(8,128)S(1)}, f32[32,128]{1,0:T(8,128)S(1)}, u32[]{:S(2)}, u32[]{:S(2)}) collective-permute-start(f32[32,128]{1,0:T(8,128)S(1)} %get-tuple-element.78), channel_id=1, source_target_pairs={{8,16},{16,8},{24,0},{0,24},{9,17},{17,9},{25,1},{1,25},{10,18},{1... | collective-permute-start | bytes 49160 | tf_op jit(solution)/shard_map/ppermute | solution.py:758
  17.6 0.0 collective-permute-start.5
  17.6 0.0 collective-permute-done.2.b
  17.6 0.2 collective-permute-done.3.a
  17.8 0.0 copy-done
  17.8 1.5 %middle_second.1 = (f32[14464,128]{1,0:T(8,128)S(1)}, f32[13024,128]{1,0:T(8,128)S(1)}, f32[2184,128]{1,0:T(8,128)S(1)}, f32[8,27,32,128]{3,2,1,0:T(8,128)S(1)}, f32[13024,128]{1,0:T(8,128)S(1)}) custom-call(f32[14464,128]{1,0:T(8,128)S(1)} %get-tuple-element.68._post, ...), custom_call_target="tpu_custom_call", output_to_operand_aliasing={{0}: (0, {}), {1}: (1, {}), {2}: (2, {})} | custom-call | bytes 12582912 | tf_op jit(solution)/shard_map/middle_second/pallas_call | solution.py:829
  19.3 0.0 collective-permute-done.4.second
  19.3 2.0 %collective-permute-done.5.first = f32[32,128]{1,0:T(8,128)S(1)} collective-permute-done((f32[32,128]{1,0:T(8,128)S(1)}, f32[32,128]{1,0:T(8,128)S(1)}, u32[]{:S(2)}, u32[]{:S(2)}) %collective-permute-start.5) | collective-permute-done | bytes 16416 | tf_op jit(solution)/shard_map/ppermute | solution.py:757
  21.3 1.2 %side_seed.1 = (f32[14464,128]{1,0:T(8,128)S(1)}, f32[13024,128]{1,0:T(8,128)S(1)}, f32[2184,128]{1,0:T(8,128)S(1)}, f32[8,27,32,128]{3,2,1,0:T(8,128)S(1)}, f32...) custom-call(f32[14464,128]{1,0:T(8,128)S(1)} %get-tuple-element.73._, ...), custom_call_target="tpu_custom_call", output_to_operand_aliasing={{0}: (0, {}), {1}: (1, {}), {2}: (2, {}), {3}: (3, {}), {4}... | custom-call | tf_op jit(solution)/shard_map/side_seed/pallas_call | solution.py:829
  22.6 0.1 collective-permute-start.6
  22.6 0.1 collective-permute-start.7
  22.7 0.7 %rim_seed.1 = (f32[8,27,32,128]{3,2,1,0:T(8,128)S(1)}, f32[13024,128]{1,0:T(8,128)S(1)}, f32[216,128]{1,0:T(8,128)S(1)}, f32[216,128]{1,0:T(8,128)S(1)}) custom-call(f32[8,27,32,128]{3,2,1,0:T(8,128)S(1)} %get-tuple-element.80._stage, f32[13024,128]{1,0:T(8,128)S(1)} %get-tuple-element.81._field, ...), custom_call_target="tpu_custom_call", output_to_operand_aliasing={{0}: (0, {}), {1}: (1, {})} | custom-call | bytes 12582912 | tf_op jit(solution)/shard_map/rim_seed/pallas_call | solution.py:829
  23.4 1.9 %collective-permute-start.8 = (f32[216,128]{1,0:T(8,128)S(1)}, f32[216,128]{1,0:T(8,128)S(1)}, u32[]{:S(2)}, u32[]{:S(2)}) collective-permute-start(f32[216,128]{1,0:T(8,128)S(1)} %get-tuple-element.93), channel_id=1, source_target_pairs={{8,16},{16,8},{24,0},{0,24},{9,17},{17,9},{25,1},{1,25},{10,18},{1... | collective-permute-start | bytes 331784 | tf_op jit(solution)/shard_map/ppermute | solution.py:758
  25.3 0.0 collective-permute-start.9
  25.3 1.3 %inner_seed.1 = (f32[8,27,32,128]{3,2,1,0:T(8,128)S(1)}, f32[13024,128]{1,0:T(8,128)S(1)}, f32[13024,128]{1,0:T(8,128)S(1)}, f32[312,128]{1,0:T(8,128)S(1)}, f32[27,32,1024]{2,1,0:T(8,128)}) custom-call(f32[8,27,32,128]{3,2,1,0:T(8,128)S(1)} %get-tuple-element.83.kept, ...), custom_call_target="tpu_custom_call", output_to_operand_aliasing={{0}: (0, {}), {1}: (1, {})} | custom-call | bytes 12582912 | tf_op jit(solution)/shard_map/inner_seed/pallas_call | solution.py:829
  26.6 4.1 %collective-permute-done.6.refs_1_ = f32[448,128]{1,0:T(8,128)S(1)} collective-permute-done((f32[448,128]{1,0:T(8,128)S(1)}, f32[448,128]{1,0:T(8,128)S(1)}, u32[]{:S(2)}, u32[]{:S(2)}) %collective-permute-start.6) | collective-permute-done | bytes 229408 | tf_op jit(solution)/shard_map/ppermute | solution.py:758
  30.7 0.0 collective-permute-done.7.refs_2_
  30.7 0.1 relay.3
  30.8 1.9 %collective-permute-start.10 = (f32[32,128]{1,0:T(8,128)S(1)}, f32[32,128]{1,0:T(8,128)S(1)}, u32[]{:S(2)}, u32[]{:S(2)}) collective-permute-start(f32[32,128]{1,0:T(8,128)S(1)} %get-tuple-element.103), channel_id=1, source_target_pairs={{8,16},{16,8},{24,0},{0,24},{9,17},{17,9},{25,1},{1,25},{10,18},{1... | collective-permute-start | bytes 49160 | tf_op jit(solution)/shard_map/ppermute | solution.py:758
  32.7 0.0 collective-permute-start.11
  32.7 0.0 collective-permute-done.8.refs_2_
  32.7 0.6 %collective-permute-done.9.refs_3_ = f32[216,128]{1,0:T(8,128)S(1)} collective-permute-done((f32[216,128]{1,0:T(8,128)S(1)}, f32[216,128]{1,0:T(8,128)S(1)}, u32[]{:S(2)}, u32[]{:S(2)}) %collective-permute-start.9) | collective-permute-done | bytes 110624 | tf_op jit(solution)/shard_map/ppermute | solution.py:757
  33.2 1.5 %middle_adjoint.1 = (f32[13024,128]{1,0:T(8,128)S(1)}, f32[13024,128]{1,0:T(8,128)S(1)}, f32[312,128]{1,0:T(8,128)S(1)}, f32[256,128]{1,0:T(8,128)S(1)}, f32[128...) custom-call(f32[13024,128]{1,0:T(8,128)S(1)} %get-tuple-element.89._, ...), custom_call_target="tpu_custom_call", output_to_operand_aliasing={{0}: (0, {}), {1}: (1, {}), {2}: (2, {}), {5}: (8, {})} | custom-call | bytes 12582912 | tf_op jit(solution)/shard_map/middle_adjoint/pallas_call | solution.py:829
  34.8 1.6 %collective-permute-done.10.refs_7_ = f32[32,128]{1,0:T(8,128)S(1)} collective-permute-done((f32[32,128]{1,0:T(8,128)S(1)}, f32[32,128]{1,0:T(8,128)S(1)}, u32[]{:S(2)}, u32[]{:S(2)}) %collective-permute-start.10) | collective-permute-done | bytes 16416 | tf_op jit(solution)/shard_map/ppermute | solution.py:758
  36.4 0.2 collective-permute-done.11.refs_8_
  36.6 1.7 %total.1 = (f32[13024,128]{1,0:T(8,128)S(1)}, f32[13024,128]{1,0:T(8,128)S(1)}, f32[312,128]{1,0:T(8,128)S(1)}, f32[256,128]{1,0:T(8,128)S(1)}, f32[1280,128]{1,0:T(8,128)S(1)}, /*index=5*/f32[8,128]{1,0:T(8,128)S(1)}) custom-call(f32[13024,128]{1,0:T(8,128)S(1)} %get-tuple-element.98.r, ...), custom_call_target="tpu_custom_call", output_to_operand_aliasing={{0}: (0, {}), {1}: (1, {}), {2}: (2, {}), {3}: (3, {}), {4}... | custom-call | tf_op jit(solution)/shard_map/total/pallas_call | solution.py:829
  38.3 0.1 collective-permute-start.12
  38.4 1.2 %collective-permute-done.12 = f32[8,128]{1,0:T(8,128)S(1)} collective-permute-done((f32[8,128]{1,0:T(8,128)S(1)}, f32[8,128]{1,0:T(8,128)S(1)}, u32[]{:S(2)}, u32[]{:S(2)}) %collective-permute-start.12) | collective-permute-done | bytes 4128 | tf_op jit(solution)/shard_map/ppermute | solution.py:764
  39.6 1.0 %collective-permute-start.15 = (f32[8,128]{1,0:T(8,128)S(1)}, f32[8,128]{1,0:T(8,128)S(1)}, u32[]{:S(2)}, u32[]{:S(2)}) collective-permute-start(f32[8,128]{1,0:T(8,128)S(1)} %max.21.near), channel_id=1, source_target_pairs={{0,7},{1,6},{2,5},{3,4},{4,3},{5,2},{6,1},{7,0},{8,15},{9,14},{10,... | collective-permute-start | bytes 12296 | tf_op jit(solution)/shard_map/ppermute | solution.py:774
  40.6 0.0 collective-permute-start.14
  40.6 2.0 %collective-permute-start.13 = (f32[8,128]{1,0:T(8,128)S(1)}, f32[8,128]{1,0:T(8,128)S(1)}, u32[]{:S(2)}, u32[]{:S(2)}) collective-permute-start(f32[8,128]{1,0:T(8,128)S(1)} %max.21.near), channel_id=1, source_target_pairs={{0,3},{1,2},{2,1},{3,0},{4,7},{5,6},{6,5},{7,4},{8,11},{9,10},{10,... | collective-permute-start | bytes 12296 | tf_op jit(solution)/shard_map/ppermute | solution.py:774
  42.6 1.4 %adjoint_low.1 = (f32[8,128]{1,0:T(8,128)S(1)}, f32[27,32,1024]{2,1,0:T(8,128)}) custom-call(f32[13024,128]{1,0:T(8,128)S(1)} %get-tuple-element.105.buf, f32[1280,128]{1,0:T(8,128)S(1)} %get-tuple-element.106.fields, f32[8,128]{1,0:T(8,128)S(1)} %max.21.near), custom_call_target="tpu_custom_call" | custom-call | bytes 6291456 | tf_op jit(solution)/shard_map/adjoint_low/pallas_call | solution.py:829
  44.0 0.0 collective-permute-done.15
  44.0 0.0 collective-permute-done.14
  44.0 0.0 collective-permute-done.13
  44.1 1.9 %collective-permute-start.18 = (f32[8,128]{1,0:T(8,128)S(1)}, f32[8,128]{1,0:T(8,128)S(1)}, u32[]{:S(2)}, u32[]{:S(2)}) collective-permute-start(f32[8,128]{1,0:T(8,128)S(1)} %maximum_maximum_fusion.1), channel_id=1, source_target_pairs={{0,25},{1,24},{2,27},{3,26},{4,29},{5,28},{6,31},{7,30},{8,17},{9,... | collective-permute-start | bytes 12296 | tf_op jit(solution)/shard_map/ppermute | solution.py:781
  45.9 0.0 collective-permute-start.17
  45.9 2.3 %collective-permute-start.16 = (f32[8,128]{1,0:T(8,128)S(1)}, f32[8,128]{1,0:T(8,128)S(1)}, u32[]{:S(2)}, u32[]{:S(2)}) collective-permute-start(f32[8,128]{1,0:T(8,128)S(1)} %maximum_maximum_fusion.1), channel_id=1, source_target_pairs={{0,9},{1,8},{2,11},{3,10},{4,13},{5,12},{6,15},{7,14},{8,1},{9,0},... | collective-permute-start | bytes 12296 | tf_op jit(solution)/shard_map/ppermute | solution.py:781
  48.2 1.4 %adjoint_high.1 = f32[27,32,1024]{2,1,0:T(8,128)} custom-call(f32[13024,128]{1,0:T(8,128)S(1)} %get-tuple-element.105.buf, f32[1280,128]{1,0:T(8,128)S(1)} %get-tuple-element.106.fields, f32[27,32,1024]{2,1,0:T(8,128)} %get-tuple-element.108._), custom_call_target="tpu_custom_call", output_to_operand_aliasing={{}: (2, {})} | custom-call | bytes 6291456 | tf_op jit(solution)/shard_map/adjoint_high/pallas_call | solution.py:829
  49.6 0.0 collective-permute-done.18
  49.6 0.2 collective-permute-done.17
  49.9 0.0 collective-permute-done.16
  49.9 0.8 %normalize.1 = f32[32,1024]{1,0:T(8,128)} custom-call(f32[256,128]{1,0:T(8,128)S(1)} %get-tuple-element.109.total, f32[8,128]{1,0:T(8,128)S(1)} %maximum_maximum_fusion.peak), custom_call_target="tpu_custom_call" | custom-call | tf_op jit(solution)/shard_map/normalize/pallas_call | solution.py:829
  (3 shorter events, 0.0 us)
Async XLA Ops:
  3.2 9.1 %collective-permute-start = (f32[480,128]{1,0:T(8,128)S(1)}, f32[480,128]{1,0:T(8,128)S(1)}, u32[]{:S(2)}, u32[]{:S(2)}) collective-permute-start(f32[480,128]{1,0:T(8,128)S(1)} %get-tuple-element.66), channel_id=1, source_target_pairs={{1,2},{2,1},{3,4},{4,3},{5,6},{6,5},{7,0},{0,7},{9,10},{10,9},{11,... | collective-permute-start | bytes 737288 | tf_op jit(solution)/shard_map/ppermute | solution.py:758
  6.6 5.7 %collective-permute-start.1 = (f32[480,128]{1,0:T(8,128)S(1)}, f32[480,128]{1,0:T(8,128)S(1)}, u32[]{:S(2)}, u32[]{:S(2)}) collective-permute-start(f32[480,128]{1,0:T(8,128)S(1)} %get-tuple-element.67), channel_id=1, source_target_pairs={{0,1},{1,0},{2,3},{3,2},{4,5},{5,4},{6,7},{7,6},{8,9},{9,8},{10,11... | collective-permute-start | bytes 737288 | tf_op jit(solution)/shard_map/ppermute | solution.py:757
  7.2 10.4 %collective-permute-start.2 = (f32[240,128]{1,0:T(8,128)S(1)}, f32[240,128]{1,0:T(8,128)S(1)}, u32[]{:S(2)}, u32[]{:S(2)}) collective-permute-start(f32[240,128]{1,0:T(8,128)S(1)} %get-tuple-element.71), channel_id=1, source_target_pairs={{8,16},{16,8},{24,0},{0,24},{9,17},{17,9},{25,1},{1,25},{10,18},{1... | collective-permute-start | bytes 368648 | tf_op jit(solution)/shard_map/ppermute | solution.py:758
  10.9 6.9 %collective-permute-start.3 = (f32[240,128]{1,0:T(8,128)S(1)}, f32[240,128]{1,0:T(8,128)S(1)}, u32[]{:S(2)}, u32[]{:S(2)}) collective-permute-start(f32[240,128]{1,0:T(8,128)S(1)} %get-tuple-element.72), channel_id=1, source_target_pairs={{0,8},{8,0},{16,24},{24,16},{1,9},{9,1},{17,25},{25,17},{2,10},{10... | collective-permute-start | bytes 368648 | tf_op jit(solution)/shard_map/ppermute | solution.py:757
  12.1 5.6 %copy-start = (f32[27,32,1024]{2,1,0:T(8,128)S(1)}, f32[27,32,1024]{2,1,0:T(8,128)}, u32[]{:S(2)}) copy-start(f32[27,32,1024]{2,1,0:T(8,128)} %refs_1_.3) | copy-start | bytes 10616836
  12.4 6.9 %collective-permute-start.4 = (f32[32,128]{1,0:T(8,128)S(1)}, f32[32,128]{1,0:T(8,128)S(1)}, u32[]{:S(2)}, u32[]{:S(2)}) collective-permute-start(f32[32,128]{1,0:T(8,128)S(1)} %get-tuple-element.78), channel_id=1, source_target_pairs={{8,16},{16,8},{24,0},{0,24},{9,17},{17,9},{25,1},{1,25},{10,18},{1... | collective-permute-start | bytes 49160 | tf_op jit(solution)/shard_map/ppermute | solution.py:758
  17.6 3.7 %collective-permute-start.5 = (f32[32,128]{1,0:T(8,128)S(1)}, f32[32,128]{1,0:T(8,128)S(1)}, u32[]{:S(2)}, u32[]{:S(2)}) collective-permute-start(f32[32,128]{1,0:T(8,128)S(1)} %get-tuple-element.79), channel_id=1, source_target_pairs={{0,8},{8,0},{16,24},{24,16},{1,9},{9,1},{17,25},{25,17},{2,10},{10... | collective-permute-start | bytes 49160 | tf_op jit(solution)/shard_map/ppermute | solution.py:757
  22.6 8.1 %collective-permute-start.6 = (f32[448,128]{1,0:T(8,128)S(1)}, f32[448,128]{1,0:T(8,128)S(1)}, u32[]{:S(2)}, u32[]{:S(2)}) collective-permute-start(f32[448,128]{1,0:T(8,128)S(1)} %get-tuple-element.87), channel_id=1, source_target_pairs={{1,2},{2,1},{3,4},{4,3},{5,6},{6,5},{7,0},{0,7},{9,10},{10,9},{11,... | collective-permute-start | bytes 688136 | tf_op jit(solution)/shard_map/ppermute | solution.py:758
  22.6 8.1 %collective-permute-start.7 = (f32[448,128]{1,0:T(8,128)S(1)}, f32[448,128]{1,0:T(8,128)S(1)}, u32[]{:S(2)}, u32[]{:S(2)}) collective-permute-start(f32[448,128]{1,0:T(8,128)S(1)} %get-tuple-element.88), channel_id=1, source_target_pairs={{0,1},{1,0},{2,3},{3,2},{4,5},{5,4},{6,7},{7,6},{8,9},{9,8},{10,11... | collective-permute-start | bytes 688136 | tf_op jit(solution)/shard_map/ppermute | solution.py:757
  23.4 9.3 %collective-permute-start.8 = (f32[216,128]{1,0:T(8,128)S(1)}, f32[216,128]{1,0:T(8,128)S(1)}, u32[]{:S(2)}, u32[]{:S(2)}) collective-permute-start(f32[216,128]{1,0:T(8,128)S(1)} %get-tuple-element.93), channel_id=1, source_target_pairs={{8,16},{16,8},{24,0},{0,24},{9,17},{17,9},{25,1},{1,25},{10,18},{1... | collective-permute-start | bytes 331784 | tf_op jit(solution)/shard_map/ppermute | solution.py:758
  25.3 7.9 %collective-permute-start.9 = (f32[216,128]{1,0:T(8,128)S(1)}, f32[216,128]{1,0:T(8,128)S(1)}, u32[]{:S(2)}, u32[]{:S(2)}) collective-permute-start(f32[216,128]{1,0:T(8,128)S(1)} %get-tuple-element.94), channel_id=1, source_target_pairs={{0,8},{8,0},{16,24},{24,16},{1,9},{9,1},{17,25},{25,17},{2,10},{10... | collective-permute-start | bytes 331784 | tf_op jit(solution)/shard_map/ppermute | solution.py:757
  30.8 5.6 %collective-permute-start.10 = (f32[32,128]{1,0:T(8,128)S(1)}, f32[32,128]{1,0:T(8,128)S(1)}, u32[]{:S(2)}, u32[]{:S(2)}) collective-permute-start(f32[32,128]{1,0:T(8,128)S(1)} %get-tuple-element.103), channel_id=1, source_target_pairs={{8,16},{16,8},{24,0},{0,24},{9,17},{17,9},{25,1},{1,25},{10,18},{1... | collective-permute-start | bytes 49160 | tf_op jit(solution)/shard_map/ppermute | solution.py:758
  32.7 3.9 %collective-permute-start.11 = (f32[32,128]{1,0:T(8,128)S(1)}, f32[32,128]{1,0:T(8,128)S(1)}, u32[]{:S(2)}, u32[]{:S(2)}) collective-permute-start(f32[32,128]{1,0:T(8,128)S(1)} %get-tuple-element.104), channel_id=1, source_target_pairs={{0,8},{8,0},{16,24},{24,16},{1,9},{9,1},{17,25},{25,17},{2,10},{10... | collective-permute-start | bytes 49160 | tf_op jit(solution)/shard_map/ppermute | solution.py:757
  38.3 1.2 %collective-permute-start.12 = (f32[8,128]{1,0:T(8,128)S(1)}, f32[8,128]{1,0:T(8,128)S(1)}, u32[]{:S(2)}, u32[]{:S(2)}) collective-permute-start(f32[8,128]{1,0:T(8,128)S(1)} %get-tuple-element.107), channel_id=1, source_target_pairs={{0,1},{1,0},{2,3},{3,2},{4,5},{5,4},{6,7},{7,6},{8,9},{9,8},{10,11... | collective-permute-start | bytes 12296 | tf_op jit(solution)/shard_map/ppermute | solution.py:764
  39.6 4.4 %collective-permute-start.15 = (f32[8,128]{1,0:T(8,128)S(1)}, f32[8,128]{1,0:T(8,128)S(1)}, u32[]{:S(2)}, u32[]{:S(2)}) collective-permute-start(f32[8,128]{1,0:T(8,128)S(1)} %max.21.near), channel_id=1, source_target_pairs={{0,7},{1,6},{2,5},{3,4},{4,3},{5,2},{6,1},{7,0},{8,15},{9,14},{10,... | collective-permute-start | bytes 12296 | tf_op jit(solution)/shard_map/ppermute | solution.py:774
  40.6 3.4 %collective-permute-start.14 = (f32[8,128]{1,0:T(8,128)S(1)}, f32[8,128]{1,0:T(8,128)S(1)}, u32[]{:S(2)}, u32[]{:S(2)}) collective-permute-start(f32[8,128]{1,0:T(8,128)S(1)} %max.21.near), channel_id=1, source_target_pairs={{0,5},{1,4},{2,7},{3,6},{4,1},{5,0},{6,3},{7,2},{8,13},{9,12},{10,... | collective-permute-start | bytes 12296 | tf_op jit(solution)/shard_map/ppermute | solution.py:774
  40.6 3.4 %collective-permute-start.13 = (f32[8,128]{1,0:T(8,128)S(1)}, f32[8,128]{1,0:T(8,128)S(1)}, u32[]{:S(2)}, u32[]{:S(2)}) collective-permute-start(f32[8,128]{1,0:T(8,128)S(1)} %max.21.near), channel_id=1, source_target_pairs={{0,3},{1,2},{2,1},{3,0},{4,7},{5,6},{6,5},{7,4},{8,11},{9,10},{10,... | collective-permute-start | bytes 12296 | tf_op jit(solution)/shard_map/ppermute | solution.py:774
  44.1 5.6 %collective-permute-start.18 = (f32[8,128]{1,0:T(8,128)S(1)}, f32[8,128]{1,0:T(8,128)S(1)}, u32[]{:S(2)}, u32[]{:S(2)}) collective-permute-start(f32[8,128]{1,0:T(8,128)S(1)} %maximum_maximum_fusion.1), channel_id=1, source_target_pairs={{0,25},{1,24},{2,27},{3,26},{4,29},{5,28},{6,31},{7,30},{8,17},{9,... | collective-permute-start | bytes 12296 | tf_op jit(solution)/shard_map/ppermute | solution.py:781
  45.9 3.9 %collective-permute-start.17 = (f32[8,128]{1,0:T(8,128)S(1)}, f32[8,128]{1,0:T(8,128)S(1)}, u32[]{:S(2)}, u32[]{:S(2)}) collective-permute-start(f32[8,128]{1,0:T(8,128)S(1)} %maximum_maximum_fusion.1), channel_id=1, source_target_pairs={{0,17},{1,16},{2,19},{3,18},{4,21},{5,20},{6,23},{7,22},{8,25},{9,... | collective-permute-start | bytes 12296 | tf_op jit(solution)/shard_map/ppermute | solution.py:781
  45.9 3.9 %collective-permute-start.16 = (f32[8,128]{1,0:T(8,128)S(1)}, f32[8,128]{1,0:T(8,128)S(1)}, u32[]{:S(2)}, u32[]{:S(2)}) collective-permute-start(f32[8,128]{1,0:T(8,128)S(1)} %maximum_maximum_fusion.1), channel_id=1, source_target_pairs={{0,9},{1,8},{2,11},{3,10},{4,13},{5,12},{6,15},{7,14},{8,1},{9,0},... | collective-permute-start | bytes 12296 | tf_op jit(solution)/shard_map/ppermute | solution.py:781

commit v15 on v14

--- a/solution.py
+++ b/solution.py
@@ -584,8 +584,11 @@
         refs[11:],
     )
 
-    def copy(k):
-        return pltpu.make_async_copy(block_of(pops, k), stage.at[k - 1], sems.at[k - 1])
+    def copy(k, r, n):
+        rows = pl.ds(r, n)
+        source = pops.at[:, rows, lanes_of(k)]
+        part = 1 if r else 0
+        return pltpu.make_async_copy(source, stage.at[k - 1, :, rows], sems.at[k - 1, part])
 
     flat_copies = [
         pltpu.make_async_copy(source, target, flat_sems.at[n])
@@ -593,18 +596,22 @@
     ]
     for each in flat_copies:
         each.start()
-    for k in (1, g.cols, *range(2, g.cols)):
-        copy(k).start()
+    for k in (1, g.cols):
+        copy(k, 0, g.rows).start()
+    for k in range(2, g.cols):
+        for piece in g.outer:
+            copy(k, *piece).start()
     for each in flat_copies:
         each.wait()
     for k in (1, g.cols):
         flat_fields(g, out, near, k)
-    copy(1).wait()
-    copy(g.cols).wait()
+    for k in (1, g.cols):
+        copy(k, 0, g.rows).wait()
     side_tiles(g, staged_tile(g, collide_first(g, state, out), stage))
     by_parity("gy", *faces, functools.partial(pack_y, g, out, 1, 30))
     for k in range(2, g.cols):
-        copy(k).wait()
+        for piece in g.outer:
+            copy(k, *piece).wait()
 
 
 def rim_first_kernel(g, _out, _state, stage, *refs):
@@ -615,9 +622,16 @@
     by_parity("gx", *faces, functools.partial(pack_x, g, out, 1, 30))
 
 
-def inner_first_kernel(g, _, _state, stage, post, state0, out, state1):
+def inner_first_kernel(g, _, _state, pops, post, state0, out, state1):
     masks = lane_masks(16)
-    interior_tiles(g, staged_tile(g, collide_first(g, state0, post), stage))
+    collide = collide_first(g, state0, post)
+
+    def act(k, pieces):
+        lanes = lanes_of(k)
+        f = [stacked([pops[i, pl.ds(r, n), lanes] for r, n in pieces]) for i in range(27)]
+        collide(k, pieces, f)
+
+    interior_tiles(g, act)
     interior_tiles(g, step_tile(g, post, out, 1, 30, masks, collide_second(g, state1)))
 
 
@@ -856,7 +870,7 @@
         side_first_kernel,
         [populations, porosity, solid, labels],
         [padded(30), fields(7, g.local), stage] + flat_space + y_faces(30, 1),
-        [sems, pltpu.SemaphoreType.DMA((3,))],
+        [pltpu.SemaphoreType.DMA((g.cols, 2)), pltpu.SemaphoreType.DMA((3,))],
     )
     along_y = swap_faces("gy", ny, rest[3:])
     post, state0, *parcels = call(
@@ -871,7 +885,7 @@
     post, state0, second, state1 = call(
         "inner_first",
         inner_first_kernel,
-        [post, state0, staged],
+        [post, state0, populations],
         [padded(27), fields(7, g.extended)],
         kept=2,
         load=FLIGHT,

time: 50.8 us -> 50.6 us (level)
  no operation moved by 1% of the time
where the time goes in v15:
time: 50.6 us; the launch traced here: 50.4 us
  starting transfers between devices  23.3 us (46%)
  Pallas kernels  16.1 us (32%)
  waiting for transfers between devices  10.1 us (20%)
  between operations  0.83 us (2%)
    pallas_call x14, Pallas kernels, call(): pl.pallas_call(functools.partial(kernel, g), in_specs=in_specs, out_shape...  16.1 us
    ppermute x6, starting transfers between devices, swap(): lax.ppermute(second, axis, swap_pairs(count, 1))  16.1 us
    ppermute x6, waiting for transfers between devices, swap(): lax.ppermute(second, axis, swap_pairs(count, 1))  5.86 us
    ppermute x3, starting transfers between devices, largest_of_all(): parts.append(lax.ppermute(peak, ('gx', 'gy'), pairs))  4.12 us
    ppermute x3, starting transfers between devices, largest_of_all(): parts.append(lax.ppermute(peak, 'gy', pairs))  2.98 us
    ppermute x6, waiting for transfers between devices, swap(): lax.ppermute(first, axis, swap_pairs(count, 0))  2.91 us
    ppermute x1, waiting for transfers between devices, largest_of_all(): lax.ppermute(peak, 'gy', [(i, i ^ 1) for i in range(ny)])  1.15 us
  transfers between devices with their start and end apart: 19, of which 9 were waited for; matrix products, arithmetic and copies ran while one was open for 0% of the time, Pallas kernels for 20%

profile of v15, /device:TPU:0, one launch (start us, length us, event | category | flops | bytes accessed | tf_op | source)
XLA Modules:
  0.0 50.4 jit_solution(17258625808684711871)
XLA Ops:
  0.6 2.3 %side_first.1 = (f32[14464,128]{1,0:T(8,128)S(1)}, f32[1792,128]{1,0:T(8,128)S(1)}, f32[8,27,32,128]{3,2,1,0:T(8,128)S(1)}, f32[32,1024]{1,0:T(8,128)S(1)}, s32[...) custom-call(f32[27,32,1024]{2,1,0:T(8,128)} %pops.3, ...), custom_call_target="tpu_custom_call" | custom-call | tf_op jit(solution)/shard_map/side_first/pallas_call | solution.py:843
  3.0 0.0 copy-start.1
  3.0 3.4 %collective-permute-start = (f32[480,128]{1,0:T(8,128)S(1)}, f32[480,128]{1,0:T(8,128)S(1)}, u32[]{:S(2)}, u32[]{:S(2)}) collective-permute-start(f32[480,128]{1,0:T(8,128)S(1)} %get-tuple-element.66), channel_id=1, source_target_pairs={{1,2},{2,1},{3,4},{4,3},{5,6},{6,5},{7,0},{0,7},{9,10},{10,9},{11,... | collective-permute-start | bytes 737288 | tf_op jit(solution)/shard_map/ppermute | solution.py:772
  6.4 0.0 collective-permute-start.1
  6.4 0.6 %rim_first.1 = (f32[14464,128]{1,0:T(8,128)S(1)}, f32[1792,128]{1,0:T(8,128)S(1)}, f32[240,128]{1,0:T(8,128)S(1)}, f32[240,128]{1,0:T(8,128)S(1)}) custom-call(f32[14464,128]{1,0:T(8,128)S(1)} %get-tuple-element.57._out, f32[1792,128]{1,0:T(8,128)S(1)} %get-tuple-element.58._state, ...), custom_call_target="tpu_custom_call", output_to_operand_aliasing={{0}: (0, {}), {1}: (1, {})} | custom-call | bytes 12582912 | tf_op jit(solution)/shard_map/rim_first/pallas_call | solution.py:843
  7.0 3.7 %collective-permute-start.2 = (f32[240,128]{1,0:T(8,128)S(1)}, f32[240,128]{1,0:T(8,128)S(1)}, u32[]{:S(2)}, u32[]{:S(2)}) collective-permute-start(f32[240,128]{1,0:T(8,128)S(1)} %get-tuple-element.71), channel_id=1, source_target_pairs={{8,16},{16,8},{24,0},{0,24},{9,17},{17,9},{25,1},{1,25},{10,18},{1... | collective-permute-start | bytes 368648 | tf_op jit(solution)/shard_map/ppermute | solution.py:772
  10.6 0.0 collective-permute-start.3
  10.7 0.0 copy-done.1
  10.7 1.3 %inner_first.1 = (f32[14464,128]{1,0:T(8,128)S(1)}, f32[1792,128]{1,0:T(8,128)S(1)}, f32[13024,128]{1,0:T(8,128)S(1)}, f32[2184,128]{1,0:T(8,128)S(1)}) custom-call(f32[14464,128]{1,0:T(8,128)S(1)} %get-tuple-element.63._, f32[1792,128]{1,0:T(8,128)S(1)} %get-tuple-element.64._state, ...), custom_call_target="tpu_custom_call", output_to_operand_aliasing={{0}: (0, {}), {1}: (1, {})} | custom-call | bytes 12582912 | tf_op jit(solution)/shard_map/inner_first/pallas_call | solution.py:843
  11.9 0.0 copy-start
  12.0 0.1 collective-permute-done.refs_1_
  12.1 0.0 collective-permute-done.1.refs_2_
  12.1 0.1 relay.2
  12.2 5.2 %collective-permute-start.4 = (f32[32,128]{1,0:T(8,128)S(1)}, f32[32,128]{1,0:T(8,128)S(1)}, u32[]{:S(2)}, u32[]{:S(2)}) collective-permute-start(f32[32,128]{1,0:T(8,128)S(1)} %get-tuple-element.78), channel_id=1, source_target_pairs={{8,16},{16,8},{24,0},{0,24},{9,17},{17,9},{25,1},{1,25},{10,18},{1... | collective-permute-start | bytes 49160 | tf_op jit(solution)/shard_map/ppermute | solution.py:772
  17.4 0.0 collective-permute-start.5
  17.4 0.0 collective-permute-done.2.b
  17.4 0.2 collective-permute-done.3.a
  17.5 0.0 copy-done
  17.6 1.5 %middle_second.1 = (f32[14464,128]{1,0:T(8,128)S(1)}, f32[13024,128]{1,0:T(8,128)S(1)}, f32[2184,128]{1,0:T(8,128)S(1)}, f32[8,27,32,128]{3,2,1,0:T(8,128)S(1)}, f32[13024,128]{1,0:T(8,128)S(1)}) custom-call(f32[14464,128]{1,0:T(8,128)S(1)} %get-tuple-element.68._post, ...), custom_call_target="tpu_custom_call", output_to_operand_aliasing={{0}: (0, {}), {1}: (1, {}), {2}: (2, {})} | custom-call | bytes 12582912 | tf_op jit(solution)/shard_map/middle_second/pallas_call | solution.py:843
  19.0 0.0 collective-permute-done.4.second
  19.1 2.0 %collective-permute-done.5.first = f32[32,128]{1,0:T(8,128)S(1)} collective-permute-done((f32[32,128]{1,0:T(8,128)S(1)}, f32[32,128]{1,0:T(8,128)S(1)}, u32[]{:S(2)}, u32[]{:S(2)}) %collective-permute-start.5) | collective-permute-done | bytes 16416 | tf_op jit(solution)/shard_map/ppermute | solution.py:771
  21.1 1.2 %side_seed.1 = (f32[14464,128]{1,0:T(8,128)S(1)}, f32[13024,128]{1,0:T(8,128)S(1)}, f32[2184,128]{1,0:T(8,128)S(1)}, f32[8,27,32,128]{3,2,1,0:T(8,128)S(1)}, f32...) custom-call(f32[14464,128]{1,0:T(8,128)S(1)} %get-tuple-element.73._, ...), custom_call_target="tpu_custom_call", output_to_operand_aliasing={{0}: (0, {}), {1}: (1, {}), {2}: (2, {}), {3}: (3, {}), {4}... | custom-call | tf_op jit(solution)/shard_map/side_seed/pallas_call | solution.py:843
  22.3 0.1 collective-permute-start.6
  22.4 0.1 collective-permute-start.7
  22.5 0.7 %rim_seed.1 = (f32[8,27,32,128]{3,2,1,0:T(8,128)S(1)}, f32[13024,128]{1,0:T(8,128)S(1)}, f32[216,128]{1,0:T(8,128)S(1)}, f32[216,128]{1,0:T(8,128)S(1)}) custom-call(f32[8,27,32,128]{3,2,1,0:T(8,128)S(1)} %get-tuple-element.80._stage, f32[13024,128]{1,0:T(8,128)S(1)} %get-tuple-element.81._field, ...), custom_call_target="tpu_custom_call", output_to_operand_aliasing={{0}: (0, {}), {1}: (1, {})} | custom-call | bytes 12582912 | tf_op jit(solution)/shard_map/rim_seed/pallas_call | solution.py:843
  23.2 1.9 %collective-permute-start.8 = (f32[216,128]{1,0:T(8,128)S(1)}, f32[216,128]{1,0:T(8,128)S(1)}, u32[]{:S(2)}, u32[]{:S(2)}) collective-permute-start(f32[216,128]{1,0:T(8,128)S(1)} %get-tuple-element.93), channel_id=1, source_target_pairs={{8,16},{16,8},{24,0},{0,24},{9,17},{17,9},{25,1},{1,25},{10,18},{1... | collective-permute-start | bytes 331784 | tf_op jit(solution)/shard_map/ppermute | solution.py:772
  25.1 0.0 collective-permute-start.9
  25.1 1.3 %inner_seed.1 = (f32[8,27,32,128]{3,2,1,0:T(8,128)S(1)}, f32[13024,128]{1,0:T(8,128)S(1)}, f32[13024,128]{1,0:T(8,128)S(1)}, f32[312,128]{1,0:T(8,128)S(1)}, f32[27,32,1024]{2,1,0:T(8,128)}) custom-call(f32[8,27,32,128]{3,2,1,0:T(8,128)S(1)} %get-tuple-element.83.kept, ...), custom_call_target="tpu_custom_call", output_to_operand_aliasing={{0}: (0, {}), {1}: (1, {})} | custom-call | bytes 12582912 | tf_op jit(solution)/shard_map/inner_seed/pallas_call | solution.py:843
  26.4 4.1 %collective-permute-done.6.refs_1_ = f32[448,128]{1,0:T(8,128)S(1)} collective-permute-done((f32[448,128]{1,0:T(8,128)S(1)}, f32[448,128]{1,0:T(8,128)S(1)}, u32[]{:S(2)}, u32[]{:S(2)}) %collective-permute-start.6) | collective-permute-done | bytes 229408 | tf_op jit(solution)/shard_map/ppermute | solution.py:772
  30.5 0.0 collective-permute-done.7.refs_2_
  30.5 0.1 relay.3
  30.6 1.9 %collective-permute-start.10 = (f32[32,128]{1,0:T(8,128)S(1)}, f32[32,128]{1,0:T(8,128)S(1)}, u32[]{:S(2)}, u32[]{:S(2)}) collective-permute-start(f32[32,128]{1,0:T(8,128)S(1)} %get-tuple-element.103), channel_id=1, source_target_pairs={{8,16},{16,8},{24,0},{0,24},{9,17},{17,9},{25,1},{1,25},{10,18},{1... | collective-permute-start | bytes 49160 | tf_op jit(solution)/shard_map/ppermute | solution.py:772
  32.5 0.0 collective-permute-start.11
  32.5 0.0 collective-permute-done.8.refs_2_
  32.5 0.5 %collective-permute-done.9.refs_3_ = f32[216,128]{1,0:T(8,128)S(1)} collective-permute-done((f32[216,128]{1,0:T(8,128)S(1)}, f32[216,128]{1,0:T(8,128)S(1)}, u32[]{:S(2)}, u32[]{:S(2)}) %collective-permute-start.9) | collective-permute-done | bytes 110624 | tf_op jit(solution)/shard_map/ppermute | solution.py:771
  33.0 1.5 %middle_adjoint.1 = (f32[13024,128]{1,0:T(8,128)S(1)}, f32[13024,128]{1,0:T(8,128)S(1)}, f32[312,128]{1,0:T(8,128)S(1)}, f32[256,128]{1,0:T(8,128)S(1)}, f32[128...) custom-call(f32[13024,128]{1,0:T(8,128)S(1)} %get-tuple-element.89._, ...), custom_call_target="tpu_custom_call", output_to_operand_aliasing={{0}: (0, {}), {1}: (1, {}), {2}: (2, {}), {5}: (8, {})} | custom-call | bytes 12582912 | tf_op jit(solution)/shard_map/middle_adjoint/pallas_call | solution.py:843
  34.6 1.6 %collective-permute-done.10.refs_7_ = f32[32,128]{1,0:T(8,128)S(1)} collective-permute-done((f32[32,128]{1,0:T(8,128)S(1)}, f32[32,128]{1,0:T(8,128)S(1)}, u32[]{:S(2)}, u32[]{:S(2)}) %collective-permute-start.10) | collective-permute-done | bytes 16416 | tf_op jit(solution)/shard_map/ppermute | solution.py:772
  36.2 0.2 collective-permute-done.11.refs_8_
  36.4 1.7 %total.1 = (f32[13024,128]{1,0:T(8,128)S(1)}, f32[13024,128]{1,0:T(8,128)S(1)}, f32[312,128]{1,0:T(8,128)S(1)}, f32[256,128]{1,0:T(8,128)S(1)}, f32[1280,128]{1,0:T(8,128)S(1)}, /*index=5*/f32[8,128]{1,0:T(8,128)S(1)}) custom-call(f32[13024,128]{1,0:T(8,128)S(1)} %get-tuple-element.98.r, ...), custom_call_target="tpu_custom_call", output_to_operand_aliasing={{0}: (0, {}), {1}: (1, {}), {2}: (2, {}), {3}: (3, {}), {4}... | custom-call | tf_op jit(solution)/shard_map/total/pallas_call | solution.py:843
  38.1 0.1 collective-permute-start.12
  38.2 1.2 %collective-permute-done.12 = f32[8,128]{1,0:T(8,128)S(1)} collective-permute-done((f32[8,128]{1,0:T(8,128)S(1)}, f32[8,128]{1,0:T(8,128)S(1)}, u32[]{:S(2)}, u32[]{:S(2)}) %collective-permute-start.12) | collective-permute-done | bytes 4128 | tf_op jit(solution)/shard_map/ppermute | solution.py:778
  39.4 1.0 %collective-permute-start.15 = (f32[8,128]{1,0:T(8,128)S(1)}, f32[8,128]{1,0:T(8,128)S(1)}, u32[]{:S(2)}, u32[]{:S(2)}) collective-permute-start(f32[8,128]{1,0:T(8,128)S(1)} %max.21.near), channel_id=1, source_target_pairs={{0,7},{1,6},{2,5},{3,4},{4,3},{5,2},{6,1},{7,0},{8,15},{9,14},{10,... | collective-permute-start | bytes 12296 | tf_op jit(solution)/shard_map/ppermute | solution.py:788
  40.4 0.0 collective-permute-start.14
  40.4 2.0 %collective-permute-start.13 = (f32[8,128]{1,0:T(8,128)S(1)}, f32[8,128]{1,0:T(8,128)S(1)}, u32[]{:S(2)}, u32[]{:S(2)}) collective-permute-start(f32[8,128]{1,0:T(8,128)S(1)} %max.21.near), channel_id=1, source_target_pairs={{0,3},{1,2},{2,1},{3,0},{4,7},{5,6},{6,5},{7,4},{8,11},{9,10},{10,... | collective-permute-start | bytes 12296 | tf_op jit(solution)/shard_map/ppermute | solution.py:788
  42.4 1.4 %adjoint_low.1 = (f32[8,128]{1,0:T(8,128)S(1)}, f32[27,32,1024]{2,1,0:T(8,128)}) custom-call(f32[13024,128]{1,0:T(8,128)S(1)} %get-tuple-element.105.buf, f32[1280,128]{1,0:T(8,128)S(1)} %get-tuple-element.106.fields, f32[8,128]{1,0:T(8,128)S(1)} %max.21.near), custom_call_target="tpu_custom_call" | custom-call | bytes 6291456 | tf_op jit(solution)/shard_map/adjoint_low/pallas_call | solution.py:843
  43.8 0.0 collective-permute-done.15
  43.8 0.0 collective-permute-done.14
  43.8 0.0 collective-permute-done.13
  43.9 1.9 %collective-permute-start.18 = (f32[8,128]{1,0:T(8,128)S(1)}, f32[8,128]{1,0:T(8,128)S(1)}, u32[]{:S(2)}, u32[]{:S(2)}) collective-permute-start(f32[8,128]{1,0:T(8,128)S(1)} %maximum_maximum_fusion.1), channel_id=1, source_target_pairs={{0,25},{1,24},{2,27},{3,26},{4,29},{5,28},{6,31},{7,30},{8,17},{9,... | collective-permute-start | bytes 12296 | tf_op jit(solution)/shard_map/ppermute | solution.py:795
  45.7 0.0 collective-permute-start.17
  45.7 2.3 %collective-permute-start.16 = (f32[8,128]{1,0:T(8,128)S(1)}, f32[8,128]{1,0:T(8,128)S(1)}, u32[]{:S(2)}, u32[]{:S(2)}) collective-permute-start(f32[8,128]{1,0:T(8,128)S(1)} %maximum_maximum_fusion.1), channel_id=1, source_target_pairs={{0,9},{1,8},{2,11},{3,10},{4,13},{5,12},{6,15},{7,14},{8,1},{9,0},... | collective-permute-start | bytes 12296 | tf_op jit(solution)/shard_map/ppermute | solution.py:795
  48.0 1.4 %adjoint_high.1 = f32[27,32,1024]{2,1,0:T(8,128)} custom-call(f32[13024,128]{1,0:T(8,128)S(1)} %get-tuple-element.105.buf, f32[1280,128]{1,0:T(8,128)S(1)} %get-tuple-element.106.fields, f32[27,32,1024]{2,1,0:T(8,128)} %get-tuple-element.108._), custom_call_target="tpu_custom_call", output_to_operand_aliasing={{}: (2, {})} | custom-call | bytes 6291456 | tf_op jit(solution)/shard_map/adjoint_high/pallas_call | solution.py:843
  49.4 0.0 collective-permute-done.18
  49.4 0.2 collective-permute-done.17
  49.6 0.0 collective-permute-done.16
  49.7 0.8 %normalize.1 = f32[32,1024]{1,0:T(8,128)} custom-call(f32[256,128]{1,0:T(8,128)S(1)} %get-tuple-element.109.total, f32[8,128]{1,0:T(8,128)S(1)} %maximum_maximum_fusion.peak), custom_call_target="tpu_custom_call" | custom-call | tf_op jit(solution)/shard_map/normalize/pallas_call | solution.py:843
  (3 shorter events, 0.0 us)
Async XLA Ops:
  3.0 7.7 %copy-start.1 = (f32[27,32,1024]{2,1,0:T(8,128)S(1)}, f32[27,32,1024]{2,1,0:T(8,128)}, u32[]{:S(2)}) copy-start(f32[27,32,1024]{2,1,0:T(8,128)} %pops.3) | copy-start | bytes 10616836
  3.0 9.1 %collective-permute-start = (f32[480,128]{1,0:T(8,128)S(1)}, f32[480,128]{1,0:T(8,128)S(1)}, u32[]{:S(2)}, u32[]{:S(2)}) collective-permute-start(f32[480,128]{1,0:T(8,128)S(1)} %get-tuple-element.66), channel_id=1, source_target_pairs={{1,2},{2,1},{3,4},{4,3},{5,6},{6,5},{7,0},{0,7},{9,10},{10,9},{11,... | collective-permute-start | bytes 737288 | tf_op jit(solution)/shard_map/ppermute | solution.py:772
  6.4 5.7 %collective-permute-start.1 = (f32[480,128]{1,0:T(8,128)S(1)}, f32[480,128]{1,0:T(8,128)S(1)}, u32[]{:S(2)}, u32[]{:S(2)}) collective-permute-start(f32[480,128]{1,0:T(8,128)S(1)} %get-tuple-element.67), channel_id=1, source_target_pairs={{0,1},{1,0},{2,3},{3,2},{4,5},{5,4},{6,7},{7,6},{8,9},{9,8},{10,11... | collective-permute-start | bytes 737288 | tf_op jit(solution)/shard_map/ppermute | solution.py:771
  7.0 10.4 %collective-permute-start.2 = (f32[240,128]{1,0:T(8,128)S(1)}, f32[240,128]{1,0:T(8,128)S(1)}, u32[]{:S(2)}, u32[]{:S(2)}) collective-permute-start(f32[240,128]{1,0:T(8,128)S(1)} %get-tuple-element.71), channel_id=1, source_target_pairs={{8,16},{16,8},{24,0},{0,24},{9,17},{17,9},{25,1},{1,25},{10,18},{1... | collective-permute-start | bytes 368648 | tf_op jit(solution)/shard_map/ppermute | solution.py:772
  10.6 6.9 %collective-permute-start.3 = (f32[240,128]{1,0:T(8,128)S(1)}, f32[240,128]{1,0:T(8,128)S(1)}, u32[]{:S(2)}, u32[]{:S(2)}) collective-permute-start(f32[240,128]{1,0:T(8,128)S(1)} %get-tuple-element.72), channel_id=1, source_target_pairs={{0,8},{8,0},{16,24},{24,16},{1,9},{9,1},{17,25},{25,17},{2,10},{10... | collective-permute-start | bytes 368648 | tf_op jit(solution)/shard_map/ppermute | solution.py:771
  11.9 5.6 %copy-start = (f32[27,32,1024]{2,1,0:T(8,128)S(1)}, f32[27,32,1024]{2,1,0:T(8,128)}, u32[]{:S(2)}) copy-start(f32[27,32,1024]{2,1,0:T(8,128)} %refs_1_.3) | copy-start | bytes 10616836
  12.2 6.9 %collective-permute-start.4 = (f32[32,128]{1,0:T(8,128)S(1)}, f32[32,128]{1,0:T(8,128)S(1)}, u32[]{:S(2)}, u32[]{:S(2)}) collective-permute-start(f32[32,128]{1,0:T(8,128)S(1)} %get-tuple-element.78), channel_id=1, source_target_pairs={{8,16},{16,8},{24,0},{0,24},{9,17},{17,9},{25,1},{1,25},{10,18},{1... | collective-permute-start | bytes 49160 | tf_op jit(solution)/shard_map/ppermute | solution.py:772
  17.4 3.7 %collective-permute-start.5 = (f32[32,128]{1,0:T(8,128)S(1)}, f32[32,128]{1,0:T(8,128)S(1)}, u32[]{:S(2)}, u32[]{:S(2)}) collective-permute-start(f32[32,128]{1,0:T(8,128)S(1)} %get-tuple-element.79), channel_id=1, source_target_pairs={{0,8},{8,0},{16,24},{24,16},{1,9},{9,1},{17,25},{25,17},{2,10},{10... | collective-permute-start | bytes 49160 | tf_op jit(solution)/shard_map/ppermute | solution.py:771
  22.3 8.1 %collective-permute-start.6 = (f32[448,128]{1,0:T(8,128)S(1)}, f32[448,128]{1,0:T(8,128)S(1)}, u32[]{:S(2)}, u32[]{:S(2)}) collective-permute-start(f32[448,128]{1,0:T(8,128)S(1)} %get-tuple-element.87), channel_id=1, source_target_pairs={{1,2},{2,1},{3,4},{4,3},{5,6},{6,5},{7,0},{0,7},{9,10},{10,9},{11,... | collective-permute-start | bytes 688136 | tf_op jit(solution)/shard_map/ppermute | solution.py:772
  22.4 8.1 %collective-permute-start.7 = (f32[448,128]{1,0:T(8,128)S(1)}, f32[448,128]{1,0:T(8,128)S(1)}, u32[]{:S(2)}, u32[]{:S(2)}) collective-permute-start(f32[448,128]{1,0:T(8,128)S(1)} %get-tuple-element.88), channel_id=1, source_target_pairs={{0,1},{1,0},{2,3},{3,2},{4,5},{5,4},{6,7},{7,6},{8,9},{9,8},{10,11... | collective-permute-start | bytes 688136 | tf_op jit(solution)/shard_map/ppermute | solution.py:771
  23.2 9.3 %collective-permute-start.8 = (f32[216,128]{1,0:T(8,128)S(1)}, f32[216,128]{1,0:T(8,128)S(1)}, u32[]{:S(2)}, u32[]{:S(2)}) collective-permute-start(f32[216,128]{1,0:T(8,128)S(1)} %get-tuple-element.93), channel_id=1, source_target_pairs={{8,16},{16,8},{24,0},{0,24},{9,17},{17,9},{25,1},{1,25},{10,18},{1... | collective-permute-start | bytes 331784 | tf_op jit(solution)/shard_map/ppermute | solution.py:772
  25.1 7.9 %collective-permute-start.9 = (f32[216,128]{1,0:T(8,128)S(1)}, f32[216,128]{1,0:T(8,128)S(1)}, u32[]{:S(2)}, u32[]{:S(2)}) collective-permute-start(f32[216,128]{1,0:T(8,128)S(1)} %get-tuple-element.94), channel_id=1, source_target_pairs={{0,8},{8,0},{16,24},{24,16},{1,9},{9,1},{17,25},{25,17},{2,10},{10... | collective-permute-start | bytes 331784 | tf_op jit(solution)/shard_map/ppermute | solution.py:771
  30.6 5.6 %collective-permute-start.10 = (f32[32,128]{1,0:T(8,128)S(1)}, f32[32,128]{1,0:T(8,128)S(1)}, u32[]{:S(2)}, u32[]{:S(2)}) collective-permute-start(f32[32,128]{1,0:T(8,128)S(1)} %get-tuple-element.103), channel_id=1, source_target_pairs={{8,16},{16,8},{24,0},{0,24},{9,17},{17,9},{25,1},{1,25},{10,18},{1... | collective-permute-start | bytes 49160 | tf_op jit(solution)/shard_map/ppermute | solution.py:772
  32.5 3.9 %collective-permute-start.11 = (f32[32,128]{1,0:T(8,128)S(1)}, f32[32,128]{1,0:T(8,128)S(1)}, u32[]{:S(2)}, u32[]{:S(2)}) collective-permute-start(f32[32,128]{1,0:T(8,128)S(1)} %get-tuple-element.104), channel_id=1, source_target_pairs={{0,8},{8,0},{16,24},{24,16},{1,9},{9,1},{17,25},{25,17},{2,10},{10... | collective-permute-start | bytes 49160 | tf_op jit(solution)/shard_map/ppermute | solution.py:771
  38.1 1.2 %collective-permute-start.12 = (f32[8,128]{1,0:T(8,128)S(1)}, f32[8,128]{1,0:T(8,128)S(1)}, u32[]{:S(2)}, u32[]{:S(2)}) collective-permute-start(f32[8,128]{1,0:T(8,128)S(1)} %get-tuple-element.107), channel_id=1, source_target_pairs={{0,1},{1,0},{2,3},{3,2},{4,5},{5,4},{6,7},{7,6},{8,9},{9,8},{10,11... | collective-permute-start | bytes 12296 | tf_op jit(solution)/shard_map/ppermute | solution.py:778
  39.4 4.4 %collective-permute-start.15 = (f32[8,128]{1,0:T(8,128)S(1)}, f32[8,128]{1,0:T(8,128)S(1)}, u32[]{:S(2)}, u32[]{:S(2)}) collective-permute-start(f32[8,128]{1,0:T(8,128)S(1)} %max.21.near), channel_id=1, source_target_pairs={{0,7},{1,6},{2,5},{3,4},{4,3},{5,2},{6,1},{7,0},{8,15},{9,14},{10,... | collective-permute-start | bytes 12296 | tf_op jit(solution)/shard_map/ppermute | solution.py:788
  40.4 3.4 %collective-permute-start.14 = (f32[8,128]{1,0:T(8,128)S(1)}, f32[8,128]{1,0:T(8,128)S(1)}, u32[]{:S(2)}, u32[]{:S(2)}) collective-permute-start(f32[8,128]{1,0:T(8,128)S(1)} %max.21.near), channel_id=1, source_target_pairs={{0,5},{1,4},{2,7},{3,6},{4,1},{5,0},{6,3},{7,2},{8,13},{9,12},{10,... | collective-permute-start | bytes 12296 | tf_op jit(solution)/shard_map/ppermute | solution.py:788
  40.4 3.4 %collective-permute-start.13 = (f32[8,128]{1,0:T(8,128)S(1)}, f32[8,128]{1,0:T(8,128)S(1)}, u32[]{:S(2)}, u32[]{:S(2)}) collective-permute-start(f32[8,128]{1,0:T(8,128)S(1)} %max.21.near), channel_id=1, source_target_pairs={{0,3},{1,2},{2,1},{3,0},{4,7},{5,6},{6,5},{7,4},{8,11},{9,10},{10,... | collective-permute-start | bytes 12296 | tf_op jit(solution)/shard_map/ppermute | solution.py:788
  43.9 5.6 %collective-permute-start.18 = (f32[8,128]{1,0:T(8,128)S(1)}, f32[8,128]{1,0:T(8,128)S(1)}, u32[]{:S(2)}, u32[]{:S(2)}) collective-permute-start(f32[8,128]{1,0:T(8,128)S(1)} %maximum_maximum_fusion.1), channel_id=1, source_target_pairs={{0,25},{1,24},{2,27},{3,26},{4,29},{5,28},{6,31},{7,30},{8,17},{9,... | collective-permute-start | bytes 12296 | tf_op jit(solution)/shard_map/ppermute | solution.py:795
  45.7 3.9 %collective-permute-start.17 = (f32[8,128]{1,0:T(8,128)S(1)}, f32[8,128]{1,0:T(8,128)S(1)}, u32[]{:S(2)}, u32[]{:S(2)}) collective-permute-start(f32[8,128]{1,0:T(8,128)S(1)} %maximum_maximum_fusion.1), channel_id=1, source_target_pairs={{0,17},{1,16},{2,19},{3,18},{4,21},{5,20},{6,23},{7,22},{8,25},{9,... | collective-permute-start | bytes 12296 | tf_op jit(solution)/shard_map/ppermute | solution.py:795
  45.7 3.9 %collective-permute-start.16 = (f32[8,128]{1,0:T(8,128)S(1)}, f32[8,128]{1,0:T(8,128)S(1)}, u32[]{:S(2)}, u32[]{:S(2)}) collective-permute-start(f32[8,128]{1,0:T(8,128)S(1)} %maximum_maximum_fusion.1), channel_id=1, source_target_pairs={{0,9},{1,8},{2,11},{3,10},{4,13},{5,12},{6,15},{7,14},{8,1},{9,0},... | collective-permute-start | bytes 12296 | tf_op jit(solution)/shard_map/ppermute | solution.py:795
